TPU v7x, 512 devices: a whole 4x4x16 slice. The times are simulated.
512 devices in a mesh: row: 16 (over x, z_hi), col: 32 (over z_lo, y, core).
Axes of the slice: x: 4, y: 4, z: 16 (z_hi: 4, z_lo: 4; z = z_hi * 4 + z_lo), core: 2. Of those that a mesh axis runs over, the one named last changes fastest.
Arguments:
- iterate: bfloat16 [5120, 25600], P('row', 'col'), may hold values from -0.0175 to 0.0175
Outputs:
- update: float32 [5120, 25600], P('row', 'col')
All inputs are finite; a program needn't handle non-finite values.
Results may differ from a plain program's by a relative error of at most 0.0035.
Values may be sent and summed in bfloat16 or wider, within the bound.
No kernel may reach another device: no remote copies, remote signals or barrier semaphores. Data moves between devices by JAX's collectives and lax.ppermute only.
A program may use at most 128 MiB of HBM per device.

v0:
```python
import math

import jax
import jax.numpy as jnp
from jax import lax
from jax.sharding import PartitionSpec as P

QUINTIC_A = 3.4445
QUINTIC_B = -4.775
QUINTIC_C = 2.0315


def from_behind(block, axis, distance):
    devices = range(lax.axis_size(axis))
    route = [((i - distance) % len(devices), i) for i in devices]
    return lax.ppermute(block, axis, route)


def from_root(value, axis, root):
    mine = lax.axis_index(axis) == root
    return lax.psum(jnp.where(mine, value, jnp.zeros_like(value)), axis)


def local(iterate):
    n_row = lax.axis_size("row")
    n_col = lax.axis_size("col")
    row_index = lax.axis_index("row")
    col_index = lax.axis_index("col")
    tile_rows, col_width = iterate.shape
    full_rows = tile_rows * n_row
    half_count = n_row // 2
    slab_ratio = n_col // n_row
    slab_rows = full_rows // n_col
    column = lax.all_gather(iterate, "row", axis=0, tiled=True)
    upper = [iterate] + [
        lax.dynamic_slice_in_dim(column, (row_index + offset) % n_row * tile_rows, tile_rows, 0)
        for offset in range(1, half_count + 1)
    ]
    stacked = jnp.stack(upper)
    partial_value = jnp.einsum("tn,kun->ktu", iterate, stacked, preferred_element_type=jnp.float32)
    own = lax.psum(partial_value, "col").astype(jnp.bfloat16)
    mirrored = jnp.stack(
        [from_behind(own[offset], "row", offset) for offset in range(1, half_count)]
    )
    offset_tiles = [own[offset] for offset in range(half_count + 1)]
    offset_tiles = offset_tiles + [
        mirrored[n_row - offset - 1].T for offset in range(half_count + 1, n_row)
    ]
    offset_row = jnp.concatenate(offset_tiles, axis=1)
    gram_row = jnp.roll(offset_row, row_index * tile_rows, axis=1)
    own_slab = lax.dynamic_slice_in_dim(gram_row, col_index * slab_rows, slab_rows, 1)
    piece = lax.dynamic_slice_in_dim(gram_row, col_index % slab_ratio * slab_rows, slab_rows, 0)
    matching = from_root(piece, "row", col_index // slab_ratio)
    square = jnp.einsum("tm,sm->ts", gram_row, matching, preferred_element_type=jnp.float32)
    polynomial = (QUINTIC_B * own_slab.astype(jnp.float32) + QUINTIC_C * square).astype(
        jnp.bfloat16
    )
    product = jnp.dot(
        lax.all_gather(polynomial, "col", axis=1, tiled=True),
        column,
        preferred_element_type=jnp.float32,
    )
    scale = 0.2 * math.sqrt(col_width * n_col)
    return scale * (QUINTIC_A * iterate.astype(jnp.float32) + product)


def solution(mesh):
    in_specs = (P("row", "col"),)
    out_specs = P("row", "col")
    return jax.shard_map(local, mesh=mesh, in_specs=in_specs, out_specs=out_specs, check_vma=False)
```

profile of v0, /device:TPU:1, one launch (start us, length us, event | category | flops | bytes accessed | tf_op | source)
XLA Modules:
  0.0 940.3 jit_solution(3538453069716015068)
XLA Ops:
  7.5 1.9 bitcast_dynamic-update-slice_fusion.8
  9.4 238.3 %all-gather.3.cloned.1.call-done = bf16[5120,800]{1,0:T(8,128)(2,1)} async-done(((bf16[320,800]{1,0:T(8,128)(2,1)}), bf16[5120,800]{1,0:T(8,128)(2,1)}) %all-gather.3.cloned.1.call-update) | async-done | bytes 8192016 | tf_op jit(solution)/shard_map/all_gather | solution.py:34
  247.7 1.9 bitcast_dynamic-update-slice_fusion.7
  249.6 1.9 bitcast_dynamic-update-slice_fusion.6
  251.5 1.9 bitcast_dynamic-update-slice_fusion.5
  253.5 1.9 bitcast_dynamic-update-slice_fusion.4
  255.4 1.9 bitcast_dynamic-update-slice_fusion.3
  257.3 2.0 bitcast_dynamic-update-slice_fusion.2
  259.2 1.9 bitcast_dynamic-update-slice_fusion.1
  261.2 1.9 bitcast_dynamic-update-slice_fusion
  263.1 7.5 convolution_bitcast_fusion
  270.6 165.3 %all-reduce.4 = bf16[9,320,320]{1,2,0:T(8,128)(2,1)S(1)} all-reduce(f32[9,320,320]{1,2,0:T(8,128)} %convolution_bitcast_fusion), channel_id=1, replica_groups=mesh['row'=16,'col'=32] {'col'}, use_global_device_ids=true, to_apply=%region_0.1 | all-reduce | flops 921600 | bytes 5529600 | tf_op jit(solution)/shard_map/psum | solution.py:41
  435.9 0.7 fusion.7
  436.6 1.0 fusion.14
  442.0 0.7 bitcast_dynamic-update-slice_fusion.9
  442.7 0.8 copy.29
  443.6 20.6 %collective-permute-start = (bf16[320,320]{1,0:T(8,128)(2,1)}, bf16[320,320]{1,0:T(8,128)(2,1)S(1)}, u32[]{:S(2)}, u32[]{:S(2)}) collective-permute-start(bf16[320,320]{1,0:T(8,128)(2,1)} %bitcast.94), channel_id=1, source_target_pairs={{288,0},{320,32},{352,64},{384,96},{416,128},{448,160},{480,192},{... | collective-permute-start | bytes 614408 | tf_op jit(solution)/shard_map/ppermute | solution.py:16
  464.2 0.9 copy.28
  465.0 1.9 collective-permute-start.1
  466.9 0.9 copy.27
  467.8 1.9 collective-permute-start.2
  469.7 1.8 copy.26
  471.5 8.9 collective-permute-start.3
  480.4 1.8 copy.25
  482.2 2.5 collective-permute-start.4
  484.8 1.8 copy.24
  486.5 1.8 copy.23
  489.0 6.5 collective-permute-done
  495.6 7.5 collective-permute-start.5
  503.8 6.8 collective-permute-start.6
  512.0 1.7 bitcast_dynamic-update-slice_fusion.29
  513.7 1.7 bitcast_dynamic-update-slice_fusion.27
  515.4 2.0 collective-permute-done.5
  517.4 0.7 bitcast_dynamic-update-slice_fusion.25
  518.1 2.3 collective-permute-done.6
  520.3 0.7 bitcast_dynamic-update-slice_fusion.23
  522.5 0.7 bitcast_dynamic-update-slice_fusion.20
  523.2 0.7 bitcast_dynamic-update-slice_fusion.18
  525.4 0.7 bitcast_dynamic-update-slice_fusion.12
  527.6 0.7 bitcast_dynamic-update-slice_fusion.36
  528.3 0.7 bitcast_dynamic-update-slice_fusion.34
  529.8 1.7 bitcast_dynamic-update-slice_fusion.30
  531.4 1.7 bitcast_dynamic-update-slice_fusion.28
  534.5 4.9 dynamic-slice_select_fusion
  539.7 312.4 %all-reduce.3.cloned.1.call-done = bf16[160,5120]{0,1:T(8,128)(2,1)} async-done(((bf16[160,5120]{0,1:T(8,128)(2,1)}), bf16[160,5120]{0,1:T(8,128)(2,1)}) %all-reduce.3.cloned.1.call-update) | async-done | bytes 1638416 | tf_op jit(solution)/shard_map/psum | solution.py:21
  852.1 5.0 add_convert_fusion
  857.1 67.3 %all-gather.5.cloned.1.call-done = bf16[320,5120]{0,1:T(8,128)(2,1)} async-done(((bf16[320,160]{0,1:T(8,128)(2,1)}), bf16[320,5120]{0,1:T(8,128)(2,1)}) %all-gather.5.cloned.1.call-update) | async-done | bytes 3276816 | tf_op jit(solution)/shard_map/all_gather | solution.py:59
  924.4 9.4 fusion.2
  (31 shorter events, 14.6 us)
Async XLA Ops:
  6.5 256.6 %copy-start = (bf16[320,800]{1,0:T(8,128)(2,1)S(1)}, bf16[320,800]{1,0:T(8,128)(2,1)}, u32[]{:S(2)}) copy-start(bf16[320,800]{1,0:T(8,128)(2,1)} %param.1) | copy-start | bytes 1536004
  6.5 241.2 %all-gather.3.cloned.1.call-start = ((), (), s32[]{:S(2)}) async-start(), calls=%async_computation | async-start | bytes 9748480 | tf_op jit(solution)/shard_map/all_gather | solution.py:34
  7.3 844.8 %all-reduce.3.cloned.1.call-start = ((), (), s32[]{:S(2)}) async-start(), calls=%async_computation.1 | async-start | bytes 5242880 | tf_op jit(solution)/shard_map/psum | solution.py:21
  443.6 52.0 %collective-permute-start = (bf16[320,320]{1,0:T(8,128)(2,1)}, bf16[320,320]{1,0:T(8,128)(2,1)S(1)}, u32[]{:S(2)}, u32[]{:S(2)}) collective-permute-start(bf16[320,320]{1,0:T(8,128)(2,1)} %bitcast.94), channel_id=1, source_target_pairs={{288,0},{320,32},{352,64},{384,96},{416,128},{448,160},{480,192},{... | collective-permute-start | bytes 614408 | tf_op jit(solution)/shard_map/ppermute | solution.py:16
  465.0 38.8 %collective-permute-start.1 = (bf16[320,320]{1,0:T(8,128)(2,1)}, bf16[320,320]{1,0:T(8,128)(2,1)S(1)}, u32[]{:S(2)}, u32[]{:S(2)}) collective-permute-start(bf16[320,320]{1,0:T(8,128)(2,1)} %bitcast.93), channel_id=1, source_target_pairs={{320,0},{352,32},{384,64},{416,96},{448,128},{480,160},{0,192},{32... | collective-permute-start | bytes 614408 | tf_op jit(solution)/shard_map/ppermute | solution.py:16
  467.8 43.5 %collective-permute-start.2 = (bf16[320,320]{1,0:T(8,128)(2,1)}, bf16[320,320]{1,0:T(8,128)(2,1)S(1)}, u32[]{:S(2)}, u32[]{:S(2)}) collective-permute-start(bf16[320,320]{1,0:T(8,128)(2,1)} %bitcast.89), channel_id=1, source_target_pairs={{352,0},{384,32},{416,64},{448,96},{480,128},{0,160},{32,192},{64,... | collective-permute-start | bytes 614408 | tf_op jit(solution)/shard_map/ppermute | solution.py:16
  471.5 40.5 %collective-permute-start.3 = (bf16[320,320]{1,0:T(8,128)(2,1)}, bf16[320,320]{1,0:T(8,128)(2,1)}, u32[]{:S(2)}, u32[]{:S(2)}) collective-permute-start(bf16[320,320]{1,0:T(8,128)(2,1)} %bitcast.90), channel_id=1, source_target_pairs={{384,0},{416,32},{448,64},{480,96},{0,128},{32,160},{64,192},{96,2... | collective-permute-start | bytes 614408 | tf_op jit(solution)/shard_map/ppermute | solution.py:16
  482.2 31.5 %collective-permute-start.4 = (bf16[320,320]{1,0:T(8,128)(2,1)}, bf16[320,320]{1,0:T(8,128)(2,1)}, u32[]{:S(2)}, u32[]{:S(2)}) collective-permute-start(bf16[320,320]{1,0:T(8,128)(2,1)} %bitcast.91), channel_id=1, source_target_pairs={{416,0},{448,32},{480,64},{0,96},{32,128},{64,160},{96,192},{128,2... | collective-permute-start | bytes 614408 | tf_op jit(solution)/shard_map/ppermute | solution.py:16
  495.6 21.8 %collective-permute-start.5 = (bf16[320,320]{1,0:T(8,128)(2,1)}, bf16[320,320]{1,0:T(8,128)(2,1)S(1)}, u32[]{:S(2)}, u32[]{:S(2)}) collective-permute-start(bf16[320,320]{1,0:T(8,128)(2,1)} %bitcast.92), channel_id=1, source_target_pairs={{448,0},{480,32},{0,64},{32,96},{64,128},{96,160},{128,192},{160,2... | collective-permute-start | bytes 614408 | tf_op jit(solution)/shard_map/ppermute | solution.py:16
  503.8 16.6 %collective-permute-start.6 = (bf16[320,320]{1,0:T(8,128)(2,1)}, bf16[320,320]{1,0:T(8,128)(2,1)S(1)}, u32[]{:S(2)}, u32[]{:S(2)}) collective-permute-start(bf16[320,320]{1,0:T(8,128)(2,1)} %bitcast.88), channel_id=1, source_target_pairs={{480,0},{0,32},{32,64},{64,96},{96,128},{128,160},{160,192},{192,2... | collective-permute-start | bytes 614408 | tf_op jit(solution)/shard_map/ppermute | solution.py:16
  539.4 385.0 %all-gather.5.cloned.1.call-start = ((), (), s32[]{:S(2)}) async-start(), calls=%async_computation.2 | async-start | bytes 4055040 | tf_op jit(solution)/shard_map/all_gather | solution.py:59
Sparse Core Ops, SparseCore 0:
  10.4 237.2 all-gather.2
  539.6 312.4 all-reduce.2
  857.2 67.1 all-gather.4
where the time goes:
time: 941 us; the launch traced here: 940 us
  waiting for transfers between devices  630 us (67%)
  blocking collectives  165 us (18%)
  local copies, waits for them, and re-layouts  55 us (6%)
  starting transfers between devices  50.4 us (5%)
  matrix products  21.9 us (2%)
  between operations  13.4 us (1%)
    psum x1, waiting for transfers between devices, from_root(): return lax.psum(jnp.where(mine, value, jnp.zeros_like(value)), axis)  312 us
    all_gather x1, waiting for transfers between devices, local(): column = lax.all_gather(iterate, 'row', axis=0, tiled=True)  238 us
    psum x1, blocking collectives, local(): own = lax.psum(partial_value, 'col').astype(jnp.bfloat16)  165 us
    all_gather x1, waiting for transfers between devices, local(): lax.all_gather(polynomial, 'col', axis=1, tiled=True)  67.3 us
    unnamed x48, local copies, waits for them, and re-layouts  51.3 us
    ppermute x7, starting transfers between devices, from_behind(): return lax.ppermute(block, axis, route)  50.1 us
  transfers between devices with their start and end apart: 10, of which 6 were waited for; matrix products, arithmetic and copies ran while one was open for 2% of the time, Pallas kernels for 0%

commit v1 on v0

v1 whole, which is shorter than its diff:
```python
import math

import jax
import jax.numpy as jnp
from jax import lax
from jax.sharding import Mesh
from jax.sharding import PartitionSpec as P

QUINTIC_A = 3.4445
QUINTIC_B = -4.775
QUINTIC_C = 2.0315

SIZES = {"x": 4, "zh": 4, "zl": 4, "y": 4, "c": 2}
F32 = jnp.float32
BF16 = jnp.bfloat16


def take(value, axis, distance):
    n = lax.axis_size(axis)
    return lax.ppermute(value, axis, [((i + distance) % n, i) for i in range(n)])


def rolled(parts, start):
    stacked = jnp.stack(parts + parts[:-1])
    return lax.dynamic_slice_in_dim(stacked, start, len(parts), 0)


def ring(value, axis):
    cut = value.shape[0] // 2
    ahead = take(value, axis, 1)
    behind = take(value, axis, -1)
    first = take(ahead[:cut], axis, 1)
    second = take(behind[cut:], axis, -1)
    return [value, ahead, jnp.concatenate([first, second], 0), behind]


def gathered(value, axis):
    return rolled(ring(value, axis), (4 - lax.axis_index(axis)) % 4)


def exchanged_sum(value, axis):
    received = lax.all_to_all(value, axis, split_axis=0, concat_axis=0, tiled=True)
    return received.astype(F32).sum(0)


def local(iterate):
    rows, width = iterate.shape
    h, l = lax.axis_index("zh"), lax.axis_index("zl")
    x, c = lax.axis_index("x"), lax.axis_index("c")
    slab = rows // 4
    pair = 2 * rows

    mine = lax.all_gather(iterate, "x", axis=0, tiled=True)
    upper, lower = take(iterate, "zh", 1), take(iterate, "zh", -1)
    cut = rows // 2
    opposite = jnp.concatenate(
        [take(upper[:cut], "zh", 1), take(lower[cut:], "zh", -1)], 0
    )
    blocks = [iterate, upper, opposite, lower]
    keep = lax.dynamic_slice_in_dim(mine, c * pair, pair, 0)
    give = lax.dynamic_slice_in_dim(mine, (1 - c) * pair, pair, 0)

    def tile(block):
        sent = jnp.einsum("rn,sn->rs", block, give, preferred_element_type=F32).astype(BF16)
        other = take(sent, "c", 1)
        kept = jnp.einsum("rn,sn->rs", block, keep, preferred_element_type=F32)
        both = (kept + other.astype(F32)).astype(BF16)
        return exchanged_sum(both.reshape(4, slab, pair), "y").astype(BF16)

    tiles = {}
    for e in (0, 1, 3, 2):
        tiles[e] = tile(blocks[e])
    by_h = rolled([tiles[e] for e in range(4)], (4 - h) % 4)
    gram = exchanged_sum(by_h, "zl").astype(BF16)

    right_rows = jnp.concatenate(ring(gram, "zh"), axis=1)
    right = gathered(right_rows, "x").reshape(rows, 4 * pair)
    left_parts = []
    for t in range(4):
        route = [
            (((q + t) % 4) * 4 + p, p * 4 + q) for p in range(4) for q in range(4)
        ]
        left_parts.append(lax.ppermute(gram, ("zh", "zl"), route))
    left_rows = rolled(left_parts, (h - l) % 4)
    left = gathered(left_rows, "y")
    left = left.transpose(0, 2, 1, 3).reshape(rows, 4 * pair)
    square = jnp.einsum("jk,ik->ji", right, left, preferred_element_type=F32)
    own = jnp.where(x % 2 == 0, right[:, :rows], right[:, rows:pair]).astype(F32)
    own = jnp.where(x // 2 == c, own, 0.0)
    partial = QUINTIC_B * own + QUINTIC_C * square
    kept = lax.dynamic_slice_in_dim(partial, c * 2 * slab, 2 * slab, 0)
    sent = lax.dynamic_slice_in_dim(partial, (1 - c) * 2 * slab, 2 * slab, 0)
    polynomial = (kept + take(sent, "c", 1)).astype(BF16)

    spread = jnp.broadcast_to(polynomial[None], (4,) + polynomial.shape)
    by_l = lax.all_to_all(spread, "zl", split_axis=0, concat_axis=0, tiled=True)
    by_y = gathered(by_l, "y")
    by_c = lax.all_gather(by_y, "c", axis=0, tiled=False)
    polynomial_all = by_c.reshape(16 * rows, rows)

    by_e = rolled(blocks, (4 - h) % 4)
    column = lax.all_gather(by_e, "x", axis=0, tiled=False)
    column = column.reshape(2, 2, 4, 4, slab, width).transpose(0, 3, 2, 1, 4, 5)
    column = column.reshape(16 * rows, width)
    product = jnp.einsum("km,kn->mn", polynomial_all, column, preferred_element_type=F32)
    scale = 0.2 * math.sqrt(width * 32)
    return scale * (QUINTIC_A * iterate.astype(F32) + product)


def solution(mesh):
    fine = Mesh(mesh.devices.reshape(tuple(SIZES.values())), tuple(SIZES))
    spec = P(("x", "zh"), ("zl", "y", "c"))
    return jax.shard_map(local, mesh=fine, in_specs=(spec,), out_specs=spec, check_vma=False)
```

time: 941 us -> 370 us (0.39)
  waiting for transfers between devices: 630 us -> 132 us
  blocking collectives: 165 us -> 18.4 us
  starting transfers between devices: 50.4 us -> 151 us
  local copies, waits for them, and re-layouts: 55 us -> 23.1 us
    psum x1 -> x0, waiting for transfers between devices: 312 us -> none  [from_root(): return lax.psum(jnp.where(mine, value, jnp.zeros_like(value)), axis)]
    all_gather x2 -> x3, waiting for transfers between devices: 306 us -> 18.2 us  [the longest x1 18.1 us: local(): by_c = lax.all_gather(by_y, 'c', axis=0, tiled=False)]
    psum x1 -> x0, blocking collectives: 165 us -> none  [local(): own = lax.psum(partial_value, 'col').astype(jnp.bfloat16)]
    ppermute x7 -> x29, waiting for transfers between devices: 10.7 us -> 94.8 us  [the longest x25 94.8 us: take(): lax.ppermute(value, axis, [((i + distance) % n, i) for i in range(n)])]
    ppermute x7 -> x29, starting transfers between devices: 50.1 us -> 127 us  [the longest x25 109 us: take(): lax.ppermute(value, axis, [((i + distance) % n, i) for i in range(n)])]
    unnamed x48 -> x37, local copies, waits for them, and re-layouts: 51.3 us -> 7.46 us
    all_to_all x0 -> x5, starting transfers between devices: none -> 23.6 us  [exchanged_sum(): lax.all_to_all(value, axis, split_axis=0, concat_axis=0, tiled=True)]
    all_to_all x0 -> x5, waiting for transfers between devices: none -> 18.5 us  [exchanged_sum(): lax.all_to_all(value, axis, split_axis=0, concat_axis=0, tiled=True)]
  transfers between devices with their start and end apart: 10 -> 37, of which waited for: 6 -> 16; matrix products, arithmetic and copies ran while one was open for 2% -> 11% of each run, Pallas kernels for 0% -> 0%
where the time goes in v1:
time: 370 us; the launch traced here: 369 us
  starting transfers between devices  151 us (41%)
  waiting for transfers between devices  132 us (36%)
  matrix products  29.3 us (8%)
  local copies, waits for them, and re-layouts  23.1 us (6%)
  blocking collectives  18.4 us (5%)
  between operations  14 us (4%)
    ppermute x25, starting transfers between devices, take(): lax.ppermute(value, axis, [((i + distance) % n, i) for i in range(n)])  109 us
    ppermute x25, waiting for transfers between devices, take(): lax.ppermute(value, axis, [((i + distance) % n, i) for i in range(n)])  94.8 us
    all_to_all x5, starting transfers between devices, exchanged_sum(): lax.all_to_all(value, axis, split_axis=0, concat_axis=0, tiled=True)  23.6 us
    all_to_all x5, waiting for transfers between devices, exchanged_sum(): lax.all_to_all(value, axis, split_axis=0, concat_axis=0, tiled=True)  18.5 us
    all_to_all x1, blocking collectives, local(): by_l = lax.all_to_all(spread, 'zl', split_axis=0, concat_axis=0, tiled=True)  18.4 us
    all_gather x1, waiting for transfers between devices, local(): by_c = lax.all_gather(by_y, 'c', axis=0, tiled=False)  18.1 us
    ppermute x4, starting transfers between devices, local(): left_parts.append(lax.ppermute(gram, ('zh', 'zl'), route))  18.1 us
    dot_general x4, matrix products, tile(): kept = jnp.einsum('rn,sn->rs', block, keep, preferred_element_type=F32)  9.83 us
  transfers between devices with their start and end apart: 37, of which 16 were waited for; matrix products, arithmetic and copies ran while one was open for 11% of the time, Pallas kernels for 0%

profile of v1, /device:TPU:1, one launch (start us, length us, event | category | flops | bytes accessed | tf_op | source)
XLA Modules:
  0.0 368.8 jit_solution(1714902115825595553)
XLA Ops:
  7.3 13.3 %collective-permute-start.1 = (bf16[320,800]{1,0:T(8,128)(2,1)}, bf16[320,800]{1,0:T(8,128)(2,1)S(1)}, u32[]{:S(2)}, u32[]{:S(2)}) collective-permute-start(bf16[320,800]{1,0:T(8,128)(2,1)} %param.1), channel_id=1, source_target_pairs={{32,0},{64,32},{96,64},{0,96},{33,1},{65,33},{97,65},{1,97},{34,2}... | collective-permute-start | bytes 1536008 | tf_op jit(solution)/shard_map/ppermute | solution.py:20
  20.6 1.9 collective-permute-start.4
  22.5 45.3 %collective-permute-done.1 = bf16[320,800]{1,0:T(8,128)(2,1)S(1)} collective-permute-done((bf16[320,800]{1,0:T(8,128)(2,1)}, bf16[320,800]{1,0:T(8,128)(2,1)S(1)}, u32[]{:S(2)}, u32[]{:S(2)}) %collective-permute-start.1) | collective-permute-done | bytes 512032 | tf_op jit(solution)/shard_map/ppermute | solution.py:20
  67.8 13.2 %collective-permute-start.3 = (bf16[160,800]{1,0:T(8,128)(2,1)S(1)}, bf16[160,800]{1,0:T(8,128)(2,1)S(1)}, u32[]{:S(2)}, u32[]{:S(2)}) collective-permute-start(bf16[160,800]{1,0:T(8,128)(2,1)S(1)} %slice.48), channel_id=1, source_target_pairs={{32,0},{64,32},{96,64},{0,96},{33,1},{65,33},{97,65},{1,97},{34,2}... | collective-permute-start | bytes 768008 | tf_op jit(solution)/shard_map/ppermute | solution.py:20
  82.9 2.1 collective-permute-start.5
  85.9 12.2 %collective-permute-done.3 = bf16[160,800]{1,0:T(8,128)(2,1)S(1)} collective-permute-done((bf16[160,800]{1,0:T(8,128)(2,1)S(1)}, bf16[160,800]{1,0:T(8,128)(2,1)S(1)}, u32[]{:S(2)}, u32[]{:S(2)}) %collective-permute-start.3) | collective-permute-done | bytes 256032 | tf_op jit(solution)/shard_map/ppermute | solution.py:20
  98.2 9.1 %collective-permute-done.5 = bf16[160,800]{1,0:T(8,128)(2,1)S(1)} collective-permute-done((bf16[160,800]{1,0:T(8,128)(2,1)S(1)}, bf16[160,800]{1,0:T(8,128)(2,1)S(1)}, u32[]{:S(2)}, u32[]{:S(2)}) %collective-permute-start.5) | collective-permute-done | bytes 256032 | tf_op jit(solution)/shard_map/ppermute | solution.py:20
  109.9 2.1 fusion.7
  112.1 2.4 collective-permute-start
  114.5 2.8 fusion.8
  120.7 2.4 collective-permute-start.7
  124.6 4.2 %all-to-all-start = ((bf16[4,80,640]{2,1,0:T(8,128)(2,1)}), bf16[4,80,640]{2,1,0:T(8,128)(2,1)S(1)}, u32[]{:S(2)}, u32[]{:S(2)}) async-start(bf16[4,80,640]{2,1,0:T(8,128)(2,1)} %bitcast.2), calls=%async_computation | async-start | bytes 819200 | tf_op jit(solution)/shard_map/all_to_all | solution.py:42
  128.7 2.7 convolution_convert_fusion.1
  131.5 2.2 collective-permute-start.6
  133.7 2.8 fusion.5
  136.8 4.2 %all-to-all-start.1 = ((bf16[4,80,640]{2,1,0:T(8,128)(2,1)}), bf16[4,80,640]{2,1,0:T(8,128)(2,1)S(1)}, u32[]{:S(2)}, u32[]{:S(2)}) async-start(bf16[4,80,640]{2,1,0:T(8,128)(2,1)} %bitcast.6), calls=%async_computation.1 | async-start | bytes 819200 | tf_op jit(solution)/shard_map/all_to_all | solution.py:42
  141.8 2.8 fusion.3
  144.7 4.3 %all-to-all-done.1 = bf16[4,80,640]{2,1,0:T(8,128)(2,1)S(1)} async-done(((bf16[4,80,640]{2,1,0:T(8,128)(2,1)}), bf16[4,80,640]{2,1,0:T(8,128)(2,1)S(1)}, u32[]{:S(2)}, u32[]{:S(2)}) %all-to-all-start.1) | async-done | bytes 409632 | tf_op jit(solution)/shard_map/all_to_all | solution.py:42
  149.0 3.5 all-to-all-start.2
  152.4 2.8 fusion.4
  155.4 3.8 %all-to-all-done.2 = bf16[4,80,640]{2,1,0:T(8,128)(2,1)S(1)} async-done(((bf16[4,80,640]{2,1,0:T(8,128)(2,1)}), bf16[4,80,640]{2,1,0:T(8,128)(2,1)S(1)}, u32[]{:S(2)}, u32[]{:S(2)}) %all-to-all-start.2) | async-done | bytes 409632 | tf_op jit(solution)/shard_map/all_to_all | solution.py:42
  159.2 3.5 all-to-all-start.3
  162.8 6.2 %all-to-all-done.3 = bf16[4,80,640]{2,1,0:T(8,128)(2,1)S(1)} async-done(((bf16[4,80,640]{2,1,0:T(8,128)(2,1)}), bf16[4,80,640]{2,1,0:T(8,128)(2,1)S(1)}, u32[]{:S(2)}, u32[]{:S(2)}) %all-to-all-start.3) | async-done | bytes 409632 | tf_op jit(solution)/shard_map/all_to_all | solution.py:42
  169.9 8.3 %all-to-all-start.4 = ((bf16[4,80,640]{2,1,0:T(8,128)(2,1)}), bf16[4,80,640]{2,1,0:T(8,128)(2,1)S(1)}, u32[]{:S(2)}, u32[]{:S(2)}) async-start(bf16[4,80,640]{2,1,0:T(8,128)(2,1)} %constant_dynamic-slice_fusion.5), calls=%async_computation.4 | async-start | bytes 819200 | tf_op jit(solution)/shard_map/all_to_all | solution.py:42
  179.0 3.2 constant_dynamic-slice_fusion
  182.3 3.9 %all-to-all-done.4 = bf16[4,80,640]{2,1,0:T(8,128)(2,1)S(1)} async-done(((bf16[4,80,640]{2,1,0:T(8,128)(2,1)}), bf16[4,80,640]{2,1,0:T(8,128)(2,1)S(1)}, u32[]{:S(2)}, u32[]{:S(2)}) %all-to-all-start.4) | async-done | bytes 409632 | tf_op jit(solution)/shard_map/all_to_all | solution.py:42
  186.3 1.9 collective-permute-start.10
  188.2 7.3 %collective-permute-start.8 = (bf16[80,640]{1,0:T(8,128)(2,1)S(1)}, bf16[80,640]{1,0:T(8,128)(2,1)S(1)}, u32[]{:S(2)}, u32[]{:S(2)}) collective-permute-start(bf16[80,640]{1,0:T(8,128)(2,1)S(1)} %reduce_sum.64), channel_id=1, source_target_pairs={{32,0},{64,32},{96,64},{0,96},{33,1},{65,33},{97,65},{1,97},{34,2}... | collective-permute-start | bytes 307208 | tf_op jit(solution)/shard_map/ppermute | solution.py:20
  196.2 3.4 collective-permute-start.19
  199.7 4.9 %collective-permute-start.18 = (bf16[80,640]{1,0:T(8,128)(2,1)S(1)}, bf16[80,640]{1,0:T(8,128)(2,1)S(1)}, u32[]{:S(2)}, u32[]{:S(2)}) collective-permute-start(bf16[80,640]{1,0:T(8,128)(2,1)S(1)} %reduce_sum.64), channel_id=1, source_target_pairs={{64,0},{96,8},{0,16},{32,24},{72,32},{104,40},{8,48},{40,56},{80,6... | collective-permute-start | bytes 307208 | tf_op jit(solution)/shard_map/ppermute | solution.py:83
  204.6 9.1 %collective-permute-start.17 = (bf16[80,640]{1,0:T(8,128)(2,1)S(1)}, bf16[80,640]{1,0:T(8,128)(2,1)S(1)}, u32[]{:S(2)}, u32[]{:S(2)}) collective-permute-start(bf16[80,640]{1,0:T(8,128)(2,1)S(1)} %reduce_sum.64), channel_id=1, source_target_pairs={{32,0},{64,8},{96,16},{0,24},{40,32},{72,40},{104,48},{8,56},{48,6... | collective-permute-start | bytes 307208 | tf_op jit(solution)/shard_map/ppermute | solution.py:83
  215.7 7.3 %collective-permute-start.9 = (bf16[40,640]{1,0:T(8,128)(2,1)S(1)}, bf16[40,640]{1,0:T(8,128)(2,1)S(1)}, u32[]{:S(2)}, u32[]{:S(2)}) collective-permute-start(bf16[40,640]{1,0:T(8,128)(2,1)S(1)} %slice.50), channel_id=1, source_target_pairs={{32,0},{64,32},{96,64},{0,96},{33,1},{65,33},{97,65},{1,97},{34,2}... | collective-permute-start | bytes 153608 | tf_op jit(solution)/shard_map/ppermute | solution.py:20
  223.2 2.2 collective-permute-start.22
  225.4 4.3 %collective-permute-start.20 = (bf16[4,80,640]{2,1,0:T(8,128)(2,1)S(1)}, bf16[4,80,640]{2,1,0:T(8,128)(2,1)S(1)}, u32[]{:S(2)}, u32[]{:S(2)}) collective-permute-start(bf16[4,80,640]{2,1,0:T(8,128)(2,1)S(1)} %get-tuple-element.6), channel_id=1, source_target_pairs={{2,0},{4,2},{6,4},{0,6},{3,1},{5,3},{7,5},{1,7},{10,8},{12,10},{14... | collective-permute-start | bytes 1228808 | tf_op jit(solution)/shard_map/ppermute | solution.py:20
  229.8 4.4 %collective-permute-start.12 = (bf16[80,2560]{1,0:T(8,128)(2,1)S(1)}, bf16[80,2560]{1,0:T(8,128)(2,1)S(1)}, u32[]{:S(2)}, u32[]{:S(2)}) collective-permute-start(bf16[80,2560]{1,0:T(8,128)(2,1)S(1)} %pad_maximum_fusion), channel_id=1, source_target_pairs={{128,0},{256,128},{384,256},{0,384},{129,1},{257,129},{385,257},{1... | collective-permute-start | bytes 1228808 | tf_op jit(solution)/shard_map/ppermute | solution.py:20
  238.2 4.6 %collective-permute-start.21 = (bf16[2,80,640]{2,1,0:T(8,128)(2,1)S(1)}, bf16[2,80,640]{2,1,0:T(8,128)(2,1)S(1)}, u32[]{:S(2)}, u32[]{:S(2)}) collective-permute-start(bf16[2,80,640]{2,1,0:T(8,128)(2,1)S(1)} %slice.56), channel_id=1, source_target_pairs={{2,0},{4,2},{6,4},{0,6},{3,1},{5,3},{7,5},{1,7},{10,8},{12,10},{14... | collective-permute-start | bytes 614408 | tf_op jit(solution)/shard_map/ppermute | solution.py:20
  242.8 6.6 %collective-permute-done.12 = bf16[80,2560]{1,0:T(8,128)(2,1)S(1)} collective-permute-done((bf16[80,2560]{1,0:T(8,128)(2,1)S(1)}, bf16[80,2560]{1,0:T(8,128)(2,1)S(1)}, u32[]{:S(2)}, u32[]{:S(2)}) %collective-permute-start.12) | collective-permute-done | bytes 409632 | tf_op jit(solution)/shard_map/ppermute | solution.py:20
  249.4 5.4 %collective-permute-start.13 = (bf16[40,2560]{1,0:T(8,128)(2,1)S(1)}, bf16[40,2560]{1,0:T(8,128)(2,1)S(1)}, u32[]{:S(2)}, u32[]{:S(2)}) collective-permute-start(bf16[40,2560]{1,0:T(8,128)(2,1)S(1)} %slice.52), channel_id=1, source_target_pairs={{128,0},{256,128},{384,256},{0,384},{129,1},{257,129},{385,257},{1... | collective-permute-start | bytes 614408 | tf_op jit(solution)/shard_map/ppermute | solution.py:20
  258.3 4.4 %collective-permute-done.13 = bf16[40,2560]{1,0:T(8,128)(2,1)S(1)} collective-permute-done((bf16[40,2560]{1,0:T(8,128)(2,1)S(1)}, bf16[40,2560]{1,0:T(8,128)(2,1)S(1)}, u32[]{:S(2)}, u32[]{:S(2)}) %collective-permute-start.13) | collective-permute-done | bytes 204832 | tf_op jit(solution)/shard_map/ppermute | solution.py:20
  262.7 5.5 %collective-permute-done.15 = bf16[40,2560]{1,0:T(8,128)(2,1)S(1)} collective-permute-done((bf16[40,2560]{1,0:T(8,128)(2,1)S(1)}, bf16[40,2560]{1,0:T(8,128)(2,1)S(1)}, u32[]{:S(2)}, u32[]{:S(2)}) %collective-permute-start.15) | collective-permute-done | bytes 204832 | tf_op jit(solution)/shard_map/ppermute | solution.py:20
  269.6 11.5 %collective-permute-start.24 = (f32[160,320]{1,0:T(8,128)S(1)}, f32[160,320]{1,0:T(8,128)S(1)}, u32[]{:S(2)}, u32[]{:S(2)}) collective-permute-start(f32[160,320]{1,0:T(8,128)S(1)} %constant_dynamic-slice_fusion.2), channel_id=1, source_target_pairs={{1,0},{0,1},{3,2},{2,3},{5,4},{4,5},{7,6},{6,7},{9,8},{8,9},{11,10... | collective-permute-start | bytes 614408 | tf_op jit(solution)/shard_map/ppermute | solution.py:20
  282.3 18.4 %all_to_all.30 = bf16[4,160,320]{2,1,0:T(8,128)(2,1)S(1)} all-to-all(bf16[4,160,320]{2,1,0:T(8,128)(2,1)S(1)} %broadcast_in_dim.11), channel_id=1, replica_groups=mesh['x'=4,'zh'=4,'zl'=4,'y'=4,'c'=2] {'zl'}, dimensions={0} | all-to-all | bytes 819200 | tf_op jit(solution)/shard_map/all_to_all | solution.py:96
  302.7 4.8 %collective-permute-start.25 = (bf16[4,160,320]{2,1,0:T(8,128)(2,1)S(1)}, bf16[4,160,320]{2,1,0:T(8,128)(2,1)S(1)}, u32[]{:S(2)}, u32[]{:S(2)}) collective-permute-start(bf16[4,160,320]{2,1,0:T(8,128)(2,1)S(1)} %all_to_all.30), channel_id=1, source_target_pairs={{2,0},{4,2},{6,4},{0,6},{3,1},{5,3},{7,5},{1,7},{10,8},{12,10},{14... | collective-permute-start | bytes 1228808 | tf_op jit(solution)/shard_map/ppermute | solution.py:20
  307.5 7.4 %collective-permute-done.27 = bf16[4,160,320]{2,1,0:T(8,128)(2,1)S(1)} collective-permute-done((bf16[4,160,320]{2,1,0:T(8,128)(2,1)S(1)}, bf16[4,160,320]{2,1,0:T(8,128)(2,1)S(1)}, u32[]{:S(2)}, u32[]{:S(2)}) %collective-permute-start.27) | collective-permute-done | bytes 409632 | tf_op jit(solution)/shard_map/ppermute | solution.py:20
  316.9 4.6 %collective-permute-start.26 = (bf16[2,160,320]{2,1,0:T(8,128)(2,1)S(1)}, bf16[2,160,320]{2,1,0:T(8,128)(2,1)S(1)}, u32[]{:S(2)}, u32[]{:S(2)}) collective-permute-start(bf16[2,160,320]{2,1,0:T(8,128)(2,1)S(1)} %slice.58), channel_id=1, source_target_pairs={{2,0},{4,2},{6,4},{0,6},{3,1},{5,3},{7,5},{1,7},{10,8},{12,10},{14... | collective-permute-start | bytes 614408 | tf_op jit(solution)/shard_map/ppermute | solution.py:20
  326.6 8.1 %copy.13 = bf16[2,2,4,4,80,800]{5,4,1,2,3,0:T(8,128)(2,1)} copy(bf16[2,2,4,4,80,800]{5,4,3,2,1,0:T(8,128)(2,1)} %bitcast.125) | data formatting | bytes 16384000 | tf_op jit(solution)/shard_map/reshape | solution.py:103
  334.7 18.1 %all-gather.8.cloned.1.call-done = bf16[8,4,160,320]{3,2,1,0:T(8,128)(2,1)} async-done(((bf16[4,4,160,320]{3,2,1,0:T(8,128)(2,1)}), bf16[8,4,160,320]{3,2,1,0:T(8,128)(2,1)}) %all-gather.8.cloned.1.call-update) | async-done | bytes 3276816 | tf_op jit(solution)/shard_map/all_gather | solution.py:98
  352.8 9.4 %fusion = f32[320,800]{1,0:T(8,128)} fusion(bf16[5120,320]{1,0:T(8,128)(2,1)} %bitcast.126, bf16[5120,800]{1,0:T(8,128)(2,1)} %bitcast.124, bf16[320,800]{1,0:T(8,128)(2,1)S(1)} %copy-done), kind=kOutput, calls=%fused_computation.2 | convolution fusion | flops 2622464000 | bytes 13004800 | tf_op jit(solution)/shard_map/km,kn->mn/dot_general | solution.py:105
  (115 shorter events, 36.1 us)
Async XLA Ops:
  6.5 103.4 %all-gather.6.cloned.1.call-start = ((), (), s32[]{:S(2)}) async-start(), calls=%async_computation.6 | async-start | bytes 2867200 | tf_op jit(solution)/shard_map/all_gather | solution.py:53
  7.3 60.5 %collective-permute-start.1 = (bf16[320,800]{1,0:T(8,128)(2,1)}, bf16[320,800]{1,0:T(8,128)(2,1)S(1)}, u32[]{:S(2)}, u32[]{:S(2)}) collective-permute-start(bf16[320,800]{1,0:T(8,128)(2,1)} %param.1), channel_id=1, source_target_pairs={{32,0},{64,32},{96,64},{0,96},{33,1},{65,33},{97,65},{1,97},{34,2}... | collective-permute-start | bytes 1536008 | tf_op jit(solution)/shard_map/ppermute | solution.py:20
  20.6 62.4 %collective-permute-start.4 = (bf16[320,800]{1,0:T(8,128)(2,1)}, bf16[320,800]{1,0:T(8,128)(2,1)S(1)}, u32[]{:S(2)}, u32[]{:S(2)}) collective-permute-start(bf16[320,800]{1,0:T(8,128)(2,1)} %param.1), channel_id=1, source_target_pairs={{96,0},{0,32},{32,64},{64,96},{97,1},{1,33},{33,65},{65,97},{98,2}... | collective-permute-start | bytes 1536008 | tf_op jit(solution)/shard_map/ppermute | solution.py:20
  67.8 30.4 %collective-permute-start.3 = (bf16[160,800]{1,0:T(8,128)(2,1)S(1)}, bf16[160,800]{1,0:T(8,128)(2,1)S(1)}, u32[]{:S(2)}, u32[]{:S(2)}) collective-permute-start(bf16[160,800]{1,0:T(8,128)(2,1)S(1)} %slice.48), channel_id=1, source_target_pairs={{32,0},{64,32},{96,64},{0,96},{33,1},{65,33},{97,65},{1,97},{34,2}... | collective-permute-start | bytes 768008 | tf_op jit(solution)/shard_map/ppermute | solution.py:20
  82.9 26.2 %copy-start = (bf16[320,800]{1,0:T(8,128)(2,1)S(1)}, bf16[320,800]{1,0:T(8,128)(2,1)}, u32[]{:S(2)}) copy-start(bf16[320,800]{1,0:T(8,128)(2,1)} %param.1) | copy-start | bytes 1536004
  82.9 24.3 %collective-permute-start.5 = (bf16[160,800]{1,0:T(8,128)(2,1)S(1)}, bf16[160,800]{1,0:T(8,128)(2,1)S(1)}, u32[]{:S(2)}, u32[]{:S(2)}) collective-permute-start(bf16[160,800]{1,0:T(8,128)(2,1)S(1)} %slice.49), channel_id=1, source_target_pairs={{96,0},{0,32},{32,64},{64,96},{97,1},{1,33},{33,65},{65,97},{98,2}... | collective-permute-start | bytes 768008 | tf_op jit(solution)/shard_map/ppermute | solution.py:20
  109.9 9.2 %copy-start.1 = (bf16[1280,800]{1,0:T(8,128)(2,1)S(1)}, bf16[1280,800]{1,0:T(8,128)(2,1)}, u32[]{:S(2)}) copy-start(bf16[1280,800]{1,0:T(8,128)(2,1)} %all-gather.6.cloned.1.call-done) | copy-start | bytes 6144004
  112.1 11.0 %collective-permute-start = (bf16[320,640]{1,0:T(8,128)(2,1)S(1)}, bf16[320,640]{1,0:T(8,128)(2,1)S(1)}, u32[]{:S(2)}, u32[]{:S(2)}) collective-permute-start(bf16[320,640]{1,0:T(8,128)(2,1)S(1)} %fusion.7), channel_id=1, source_target_pairs={{1,0},{0,1},{3,2},{2,3},{5,4},{4,5},{7,6},{6,7},{9,8},{8,9},{11,10... | collective-permute-start | bytes 1228808 | tf_op jit(solution)/shard_map/ppermute | solution.py:20
  117.3 16.4 %collective-permute-start.2 = (bf16[320,640]{1,0:T(8,128)(2,1)}, bf16[320,640]{1,0:T(8,128)(2,1)S(1)}, u32[]{:S(2)}, u32[]{:S(2)}) collective-permute-start(bf16[320,640]{1,0:T(8,128)(2,1)} %fusion.8), channel_id=1, source_target_pairs={{1,0},{0,1},{3,2},{2,3},{5,4},{4,5},{7,6},{6,7},{9,8},{8,9},{11,10... | collective-permute-start | bytes 1228808 | tf_op jit(solution)/shard_map/ppermute | solution.py:20
  120.7 31.8 %collective-permute-start.7 = (bf16[320,640]{1,0:T(8,128)(2,1)}, bf16[320,640]{1,0:T(8,128)(2,1)S(1)}, u32[]{:S(2)}, u32[]{:S(2)}) collective-permute-start(bf16[320,640]{1,0:T(8,128)(2,1)} %fusion.9), channel_id=1, source_target_pairs={{1,0},{0,1},{3,2},{2,3},{5,4},{4,5},{7,6},{6,7},{9,8},{8,9},{11,10... | collective-permute-start | bytes 1228808 | tf_op jit(solution)/shard_map/ppermute | solution.py:20
  124.6 12.3 %all-to-all-start = ((bf16[4,80,640]{2,1,0:T(8,128)(2,1)}), bf16[4,80,640]{2,1,0:T(8,128)(2,1)S(1)}, u32[]{:S(2)}, u32[]{:S(2)}) async-start(bf16[4,80,640]{2,1,0:T(8,128)(2,1)} %bitcast.2), calls=%async_computation | async-start | bytes 819200 | tf_op jit(solution)/shard_map/all_to_all | solution.py:42
  131.5 10.4 %collective-permute-start.6 = (bf16[320,640]{1,0:T(8,128)(2,1)}, bf16[320,640]{1,0:T(8,128)(2,1)}, u32[]{:S(2)}, u32[]{:S(2)}) collective-permute-start(bf16[320,640]{1,0:T(8,128)(2,1)} %convolution_convert_fusion.1), channel_id=1, source_target_pairs={{1,0},{0,1},{3,2},{2,3},{5,4},{4,5},{7,6},{6,7},{9,8},{8,9},{11,10... | collective-permute-start | bytes 1228808 | tf_op jit(solution)/shard_map/ppermute | solution.py:20
  136.8 12.2 %all-to-all-start.1 = ((bf16[4,80,640]{2,1,0:T(8,128)(2,1)}), bf16[4,80,640]{2,1,0:T(8,128)(2,1)S(1)}, u32[]{:S(2)}, u32[]{:S(2)}) async-start(bf16[4,80,640]{2,1,0:T(8,128)(2,1)} %bitcast.6), calls=%async_computation.1 | async-start | bytes 819200 | tf_op jit(solution)/shard_map/all_to_all | solution.py:42
  149.0 10.2 %all-to-all-start.2 = ((bf16[4,80,640]{2,1,0:T(8,128)(2,1)}), bf16[4,80,640]{2,1,0:T(8,128)(2,1)S(1)}, u32[]{:S(2)}, u32[]{:S(2)}) async-start(bf16[4,80,640]{2,1,0:T(8,128)(2,1)} %bitcast.8), calls=%async_computation.2 | async-start | bytes 819200 | tf_op jit(solution)/shard_map/all_to_all | solution.py:42
  159.2 9.8 %all-to-all-start.3 = ((bf16[4,80,640]{2,1,0:T(8,128)(2,1)}), bf16[4,80,640]{2,1,0:T(8,128)(2,1)S(1)}, u32[]{:S(2)}, u32[]{:S(2)}) async-start(bf16[4,80,640]{2,1,0:T(8,128)(2,1)} %bitcast.12), calls=%async_computation.3 | async-start | bytes 819200 | tf_op jit(solution)/shard_map/all_to_all | solution.py:42
  169.9 16.3 %all-to-all-start.4 = ((bf16[4,80,640]{2,1,0:T(8,128)(2,1)}), bf16[4,80,640]{2,1,0:T(8,128)(2,1)S(1)}, u32[]{:S(2)}, u32[]{:S(2)}) async-start(bf16[4,80,640]{2,1,0:T(8,128)(2,1)} %constant_dynamic-slice_fusion.5), calls=%async_computation.4 | async-start | bytes 819200 | tf_op jit(solution)/shard_map/all_to_all | solution.py:42
  178.2 148.4 %all-gather.10.cloned.1.call-start = ((), (), s32[]{:S(2)}) async-start(), calls=%async_computation.8 | async-start | bytes 11468800 | tf_op jit(solution)/shard_map/all_gather | solution.py:102
  182.3 170.6 %all-gather.8.cloned.1.call-start = ((), (), s32[]{:S(2)}) async-start(), calls=%async_computation.7 | async-start | bytes 5898240 | tf_op jit(solution)/shard_map/all_gather | solution.py:98
  186.3 18.3 %collective-permute-start.10 = (bf16[80,640]{1,0:T(8,128)(2,1)S(1)}, bf16[80,640]{1,0:T(8,128)(2,1)S(1)}, u32[]{:S(2)}, u32[]{:S(2)}) collective-permute-start(bf16[80,640]{1,0:T(8,128)(2,1)S(1)} %reduce_sum.64), channel_id=1, source_target_pairs={{96,0},{0,32},{32,64},{64,96},{97,1},{1,33},{33,65},{65,97},{98,2}... | collective-permute-start | bytes 307208 | tf_op jit(solution)/shard_map/ppermute | solution.py:20
  188.2 25.5 %collective-permute-start.8 = (bf16[80,640]{1,0:T(8,128)(2,1)S(1)}, bf16[80,640]{1,0:T(8,128)(2,1)S(1)}, u32[]{:S(2)}, u32[]{:S(2)}) collective-permute-start(bf16[80,640]{1,0:T(8,128)(2,1)S(1)} %reduce_sum.64), channel_id=1, source_target_pairs={{32,0},{64,32},{96,64},{0,96},{33,1},{65,33},{97,65},{1,97},{34,2}... | collective-permute-start | bytes 307208 | tf_op jit(solution)/shard_map/ppermute | solution.py:20
  195.5 20.2 %collective-permute-start.16 = (bf16[80,640]{1,0:T(8,128)(2,1)S(1)}, bf16[80,640]{1,0:T(8,128)(2,1)S(1)}, u32[]{:S(2)}, u32[]{:S(2)}) collective-permute-start(bf16[80,640]{1,0:T(8,128)(2,1)S(1)} %reduce_sum.64), channel_id=1, source_target_pairs={{0,0},{32,8},{64,16},{96,24},{8,32},{40,40},{72,48},{104,56},{16,6... | collective-permute-start | bytes 307208 | tf_op jit(solution)/shard_map/ppermute | solution.py:83
  196.2 26.8 %collective-permute-start.19 = (bf16[80,640]{1,0:T(8,128)(2,1)S(1)}, bf16[80,640]{1,0:T(8,128)(2,1)S(1)}, u32[]{:S(2)}, u32[]{:S(2)}) collective-permute-start(bf16[80,640]{1,0:T(8,128)(2,1)S(1)} %reduce_sum.64), channel_id=1, source_target_pairs={{96,0},{0,8},{32,16},{64,24},{104,32},{8,40},{40,48},{72,56},{112,... | collective-permute-start | bytes 307208 | tf_op jit(solution)/shard_map/ppermute | solution.py:83
  199.7 23.3 %collective-permute-start.18 = (bf16[80,640]{1,0:T(8,128)(2,1)S(1)}, bf16[80,640]{1,0:T(8,128)(2,1)S(1)}, u32[]{:S(2)}, u32[]{:S(2)}) collective-permute-start(bf16[80,640]{1,0:T(8,128)(2,1)S(1)} %reduce_sum.64), channel_id=1, source_target_pairs={{64,0},{96,8},{0,16},{32,24},{72,32},{104,40},{8,48},{40,56},{80,6... | collective-permute-start | bytes 307208 | tf_op jit(solution)/shard_map/ppermute | solution.py:83
  204.6 18.4 %collective-permute-start.17 = (bf16[80,640]{1,0:T(8,128)(2,1)S(1)}, bf16[80,640]{1,0:T(8,128)(2,1)S(1)}, u32[]{:S(2)}, u32[]{:S(2)}) collective-permute-start(bf16[80,640]{1,0:T(8,128)(2,1)S(1)} %reduce_sum.64), channel_id=1, source_target_pairs={{32,0},{64,8},{96,16},{0,24},{40,32},{72,40},{104,48},{8,56},{48,6... | collective-permute-start | bytes 307208 | tf_op jit(solution)/shard_map/ppermute | solution.py:83
  213.7 16.0 %collective-permute-start.11 = (bf16[40,640]{1,0:T(8,128)(2,1)S(1)}, bf16[40,640]{1,0:T(8,128)(2,1)S(1)}, u32[]{:S(2)}, u32[]{:S(2)}) collective-permute-start(bf16[40,640]{1,0:T(8,128)(2,1)S(1)} %slice.51), channel_id=1, source_target_pairs={{96,0},{0,32},{32,64},{64,96},{97,1},{1,33},{33,65},{65,97},{98,2}... | collective-permute-start | bytes 153608 | tf_op jit(solution)/shard_map/ppermute | solution.py:20
  215.7 14.1 %collective-permute-start.9 = (bf16[40,640]{1,0:T(8,128)(2,1)S(1)}, bf16[40,640]{1,0:T(8,128)(2,1)S(1)}, u32[]{:S(2)}, u32[]{:S(2)}) collective-permute-start(bf16[40,640]{1,0:T(8,128)(2,1)S(1)} %slice.50), channel_id=1, source_target_pairs={{32,0},{64,32},{96,64},{0,96},{33,1},{65,33},{97,65},{1,97},{34,2}... | collective-permute-start | bytes 153608 | tf_op jit(solution)/shard_map/ppermute | solution.py:20
  223.2 13.0 %collective-permute-start.22 = (bf16[4,80,640]{2,1,0:T(8,128)(2,1)S(1)}, bf16[4,80,640]{2,1,0:T(8,128)(2,1)S(1)}, u32[]{:S(2)}, u32[]{:S(2)}) collective-permute-start(bf16[4,80,640]{2,1,0:T(8,128)(2,1)S(1)} %get-tuple-element.6), channel_id=1, source_target_pairs={{6,0},{0,2},{2,4},{4,6},{7,1},{1,3},{3,5},{5,7},{14,8},{8,10},{10,... | collective-permute-start | bytes 1228808 | tf_op jit(solution)/shard_map/ppermute | solution.py:20
  225.4 12.7 %collective-permute-start.20 = (bf16[4,80,640]{2,1,0:T(8,128)(2,1)S(1)}, bf16[4,80,640]{2,1,0:T(8,128)(2,1)S(1)}, u32[]{:S(2)}, u32[]{:S(2)}) collective-permute-start(bf16[4,80,640]{2,1,0:T(8,128)(2,1)S(1)} %get-tuple-element.6), channel_id=1, source_target_pairs={{2,0},{4,2},{6,4},{0,6},{3,1},{5,3},{7,5},{1,7},{10,8},{12,10},{14... | collective-permute-start | bytes 1228808 | tf_op jit(solution)/shard_map/ppermute | solution.py:20
  229.8 19.6 %collective-permute-start.12 = (bf16[80,2560]{1,0:T(8,128)(2,1)S(1)}, bf16[80,2560]{1,0:T(8,128)(2,1)S(1)}, u32[]{:S(2)}, u32[]{:S(2)}) collective-permute-start(bf16[80,2560]{1,0:T(8,128)(2,1)S(1)} %pad_maximum_fusion), channel_id=1, source_target_pairs={{128,0},{256,128},{384,256},{0,384},{129,1},{257,129},{385,257},{1... | collective-permute-start | bytes 1228808 | tf_op jit(solution)/shard_map/ppermute | solution.py:20
  234.2 20.7 %collective-permute-start.14 = (bf16[80,2560]{1,0:T(8,128)(2,1)S(1)}, bf16[80,2560]{1,0:T(8,128)(2,1)S(1)}, u32[]{:S(2)}, u32[]{:S(2)}) collective-permute-start(bf16[80,2560]{1,0:T(8,128)(2,1)S(1)} %pad_maximum_fusion), channel_id=1, source_target_pairs={{384,0},{0,128},{128,256},{256,384},{385,1},{1,129},{129,257},{257... | collective-permute-start | bytes 1228808 | tf_op jit(solution)/shard_map/ppermute | solution.py:20
  236.2 20.7 %collective-permute-start.23 = (bf16[2,80,640]{2,1,0:T(8,128)(2,1)S(1)}, bf16[2,80,640]{2,1,0:T(8,128)(2,1)S(1)}, u32[]{:S(2)}, u32[]{:S(2)}) collective-permute-start(bf16[2,80,640]{2,1,0:T(8,128)(2,1)S(1)} %slice.57), channel_id=1, source_target_pairs={{6,0},{0,2},{2,4},{4,6},{7,1},{1,3},{3,5},{5,7},{14,8},{8,10},{10,... | collective-permute-start | bytes 614408 | tf_op jit(solution)/shard_map/ppermute | solution.py:20
  238.2 18.7 %collective-permute-start.21 = (bf16[2,80,640]{2,1,0:T(8,128)(2,1)S(1)}, bf16[2,80,640]{2,1,0:T(8,128)(2,1)S(1)}, u32[]{:S(2)}, u32[]{:S(2)}) collective-permute-start(bf16[2,80,640]{2,1,0:T(8,128)(2,1)S(1)} %slice.56), channel_id=1, source_target_pairs={{2,0},{4,2},{6,4},{0,6},{3,1},{5,3},{7,5},{1,7},{10,8},{12,10},{14... | collective-permute-start | bytes 614408 | tf_op jit(solution)/shard_map/ppermute | solution.py:20
  249.4 13.3 %collective-permute-start.13 = (bf16[40,2560]{1,0:T(8,128)(2,1)S(1)}, bf16[40,2560]{1,0:T(8,128)(2,1)S(1)}, u32[]{:S(2)}, u32[]{:S(2)}) collective-permute-start(bf16[40,2560]{1,0:T(8,128)(2,1)S(1)} %slice.52), channel_id=1, source_target_pairs={{128,0},{256,128},{384,256},{0,384},{129,1},{257,129},{385,257},{1... | collective-permute-start | bytes 614408 | tf_op jit(solution)/shard_map/ppermute | solution.py:20
  254.9 13.3 %collective-permute-start.15 = (bf16[40,2560]{1,0:T(8,128)(2,1)S(1)}, bf16[40,2560]{1,0:T(8,128)(2,1)S(1)}, u32[]{:S(2)}, u32[]{:S(2)}) collective-permute-start(bf16[40,2560]{1,0:T(8,128)(2,1)S(1)} %slice.53), channel_id=1, source_target_pairs={{384,0},{0,128},{128,256},{256,384},{385,1},{1,129},{129,257},{257... | collective-permute-start | bytes 614408 | tf_op jit(solution)/shard_map/ppermute | solution.py:20
  269.6 12.6 %collective-permute-start.24 = (f32[160,320]{1,0:T(8,128)S(1)}, f32[160,320]{1,0:T(8,128)S(1)}, u32[]{:S(2)}, u32[]{:S(2)}) collective-permute-start(f32[160,320]{1,0:T(8,128)S(1)} %constant_dynamic-slice_fusion.2), channel_id=1, source_target_pairs={{1,0},{0,1},{3,2},{2,3},{5,4},{4,5},{7,6},{6,7},{9,8},{8,9},{11,10... | collective-permute-start | bytes 614408 | tf_op jit(solution)/shard_map/ppermute | solution.py:20
  300.8 14.1 %collective-permute-start.27 = (bf16[4,160,320]{2,1,0:T(8,128)(2,1)S(1)}, bf16[4,160,320]{2,1,0:T(8,128)(2,1)S(1)}, u32[]{:S(2)}, u32[]{:S(2)}) collective-permute-start(bf16[4,160,320]{2,1,0:T(8,128)(2,1)S(1)} %all_to_all.30), channel_id=1, source_target_pairs={{6,0},{0,2},{2,4},{4,6},{7,1},{1,3},{3,5},{5,7},{14,8},{8,10},{10,... | collective-permute-start | bytes 1228808 | tf_op jit(solution)/shard_map/ppermute | solution.py:20
  302.7 14.2 %collective-permute-start.25 = (bf16[4,160,320]{2,1,0:T(8,128)(2,1)S(1)}, bf16[4,160,320]{2,1,0:T(8,128)(2,1)S(1)}, u32[]{:S(2)}, u32[]{:S(2)}) collective-permute-start(bf16[4,160,320]{2,1,0:T(8,128)(2,1)S(1)} %all_to_all.30), channel_id=1, source_target_pairs={{2,0},{4,2},{6,4},{0,6},{3,1},{5,3},{7,5},{1,7},{10,8},{12,10},{14... | collective-permute-start | bytes 1228808 | tf_op jit(solution)/shard_map/ppermute | solution.py:20
  314.9 8.2 %collective-permute-start.28 = (bf16[2,160,320]{2,1,0:T(8,128)(2,1)S(1)}, bf16[2,160,320]{2,1,0:T(8,128)(2,1)S(1)}, u32[]{:S(2)}, u32[]{:S(2)}) collective-permute-start(bf16[2,160,320]{2,1,0:T(8,128)(2,1)S(1)} %slice.59), channel_id=1, source_target_pairs={{6,0},{0,2},{2,4},{4,6},{7,1},{1,3},{3,5},{5,7},{14,8},{8,10},{10,... | collective-permute-start | bytes 614408 | tf_op jit(solution)/shard_map/ppermute | solution.py:20
  316.9 7.7 %collective-permute-start.26 = (bf16[2,160,320]{2,1,0:T(8,128)(2,1)S(1)}, bf16[2,160,320]{2,1,0:T(8,128)(2,1)S(1)}, u32[]{:S(2)}, u32[]{:S(2)}) collective-permute-start(bf16[2,160,320]{2,1,0:T(8,128)(2,1)S(1)} %slice.58), channel_id=1, source_target_pairs={{2,0},{4,2},{6,4},{0,6},{3,1},{5,3},{7,5},{1,7},{10,8},{12,10},{14... | collective-permute-start | bytes 614408 | tf_op jit(solution)/shard_map/ppermute | solution.py:20
Sparse Core Ops, SparseCore 0:
  9.5 45.4 all-gather.5
  182.4 106.1 all-gather.9
  326.7 26.1 all-gather.7

commit v2 on v1

v2 whole, which is shorter than its diff:
```python
import math

import jax
import jax.numpy as jnp
from jax import lax
from jax.sharding import Mesh
from jax.sharding import PartitionSpec as P

QUINTIC_A = 3.4445
QUINTIC_B = -4.775
QUINTIC_C = 2.0315

SIZES = {"x": 4, "zh": 4, "zl": 4, "y": 4, "c": 2}
Z = ("zh", "zl")
F32 = jnp.float32
BF16 = jnp.bfloat16


def take(value, axis, distance):
    n = lax.axis_size(axis)
    return lax.ppermute(value, axis, [((i + distance) % n, i) for i in range(n)])


def home(a, b):
    a, b = a % 4, b % 4
    if (a - b) % 4 == 2:
        return (b - 1) % 4 * 4 + (b + 1) % 4
    return b * 4 + a


def fetch(piece, wanted):
    route = [(home(*wanted(p, q)), p * 4 + q) for p in range(4) for q in range(4)]
    return lax.ppermute(piece, Z, route)


def rolled(parts, start):
    stacked = jnp.concatenate([parts, parts[:-1]], axis=0)
    return lax.dynamic_slice_in_dim(stacked, start, 4, 0)


def gathered(value, axis):
    spread = jnp.broadcast_to(value[None], (4,) + value.shape)
    return lax.all_to_all(spread, axis, split_axis=0, concat_axis=0, tiled=True)


def exchanged_sum(value, axis):
    received = lax.all_to_all(value, axis, split_axis=0, concat_axis=0, tiled=True)
    return received.astype(F32).sum(0)


def local(iterate):
    rows, width = iterate.shape
    h, x, c = lax.axis_index("zh"), lax.axis_index("x"), lax.axis_index("c")
    slab = rows // 4
    pair = 2 * rows

    def columns(block):
        halves = block.reshape(2, pair, width)
        return halves[c], halves[1 - c]

    def tile(block, keep, give):
        sent = jnp.einsum("rn,sn->rs", block, give, preferred_element_type=F32).astype(BF16)
        other = take(sent, "c", 1)
        kept = jnp.einsum("rn,sn->rs", block, keep, preferred_element_type=F32)
        both = (kept + other.astype(F32)).astype(BF16)
        return exchanged_sum(both.reshape(4, -1, pair), "y").astype(BF16)

    upper, lower = take(iterate, "zh", 1), take(iterate, "zh", -1)
    mine = gathered(iterate, "x")
    keep, give = columns(mine)
    level = tile(iterate, keep, give)

    upper, lower, level = lax.optimization_barrier((upper, lower, level))
    cut = rows // 2
    opposite = (take(upper[:cut], "zh", 1), take(lower[cut:], "zh", -1))
    above = gathered(upper, "x")
    both = jnp.stack([upper, lower]).reshape(2, 4, slab, width)
    both = both.transpose(1, 0, 2, 3).reshape(pair, width)
    sides = tile(both, keep, give).reshape(2, slab, pair)
    below = lax.all_gather(lower, "x", axis=0, tiled=False)
    across = tile(lower, *columns(above))

    tiles = jnp.stack([level, sides[0], across, sides[1]])
    gram = exchanged_sum(rolled(tiles, (4 - h) % 4), "zl").astype(BF16)

    opposite, gram = lax.optimization_barrier((opposite, gram))
    opposite = lax.all_gather(jnp.concatenate(opposite, 0), "x", axis=0, tiled=False)

    left = fetch(gram, lambda p, q: (p, q))
    right = {t: fetch(gram, lambda p, q, t=t: (q, p + t)) for t in (1, -1, 0)}
    left = rolled(gathered(left, "zl"), h)
    left = jnp.concatenate([left[e] for e in range(4)], axis=1)
    left = gathered(left, "y").reshape(rows, 4 * pair)
    cut = slab // 32 * 16
    far = jnp.concatenate([take(right[1][:cut], "zh", 1), take(right[-1][cut:], "zh", -1)], 0)
    right = jnp.concatenate([right[0], right[1], far, right[-1]], axis=1)
    right = gathered(right, "x").reshape(rows, 4 * pair)
    square = jnp.einsum("jk,ik->ji", right, left, preferred_element_type=F32)
    own = jnp.where(x % 2 == 0, right[:, :rows], right[:, rows:pair]).astype(F32)
    own = jnp.where(x // 2 == c, own, 0.0)
    partial = (QUINTIC_B * own + QUINTIC_C * square).reshape(2, 2 * slab, rows)
    polynomial = (partial[c] + take(partial[1 - c], "c", 1)).astype(BF16)

    polynomial = rolled(gathered(polynomial, "zl"), h)
    polynomial = gathered(polynomial, "y").reshape(8 * rows, rows)
    swapped = take(polynomial, "c", 1)

    column = jnp.stack([mine.reshape(4, rows, width), above.reshape(4, rows, width), opposite, below])
    column = column.reshape(4, 2, 2, 4, slab, width).transpose(1, 3, 0, 2, 4, 5)
    column = column.reshape(2, 8 * rows, width)
    product = jnp.einsum("km,kn->mn", polynomial, column[c], preferred_element_type=F32)
    product += jnp.einsum("km,kn->mn", swapped, column[1 - c], preferred_element_type=F32)
    scale = 0.2 * math.sqrt(width * 32)
    return scale * (QUINTIC_A * iterate.astype(F32) + product)


def solution(mesh):
    fine = Mesh(mesh.devices.reshape(tuple(SIZES.values())), tuple(SIZES))
    spec = P(("x", "zh"), ("zl", "y", "c"))
    return jax.shard_map(local, mesh=fine, in_specs=(spec,), out_specs=spec, check_vma=False)
```

time: 370 us -> 436 us (1.18)
  blocking collectives: 18.4 us -> 58.6 us
  waiting for transfers between devices: 132 us -> 152 us
  starting transfers between devices: 151 us -> 132 us
  other arithmetic: 0.83 us -> 16.6 us
  local copies, waits for them, and re-layouts: 23.1 us -> 33.9 us
    all_to_all x0 -> x5, waiting for transfers between devices: none -> 78.7 us  [gathered(): return lax.all_to_all(spread, axis, split_axis=0, concat_axis=0, tiled=True)]
    ppermute x25 -> x11, starting transfers between devices: 109 us -> 60.1 us  [take(): lax.ppermute(value, axis, [((i + distance) % n, i) for i in range(n)])]
    all_to_all x0 -> x5, starting transfers between devices: none -> 48.9 us  [gathered(): return lax.all_to_all(spread, axis, split_axis=0, concat_axis=0, tiled=True)]
    all_to_all x1 -> x3, blocking collectives: 18.4 us -> 58.6 us  [the longest x2 46.7 us: gathered(): return lax.all_to_all(spread, axis, split_axis=0, concat_axis=0, tiled=True)]
    ppermute x25 -> x11, waiting for transfers between devices: 94.8 us -> 58.3 us  [take(): lax.ppermute(value, axis, [((i + distance) % n, i) for i in range(n)])]
    all_gather x3 -> x2, waiting for transfers between devices: 18.2 us -> 0.04 us  [the longest x1 0.02 us: local(): below = lax.all_gather(lower, 'x', axis=0, tiled=False)]
    all_to_all x5 -> x3, starting transfers between devices: 23.6 us -> 12.4 us  [exchanged_sum(): lax.all_to_all(value, axis, split_axis=0, concat_axis=0, tiled=True)]
    transpose x0 -> x1, other arithmetic: none -> 8.36 us  [local(): column = column.reshape(4, 2, 2, 4, slab, width).transpose(1, 3, 0, 2, 4, 5)]
  transfers between devices with their start and end apart: 37 -> 25, of which waited for: 16 -> 13; matrix products, arithmetic and copies ran while one was open for 11% -> 12% of each run, Pallas kernels for 0% -> 0%
where the time goes in v2:
time: 436 us; the launch traced here: 434 us
  waiting for transfers between devices  152 us (35%)
  starting transfers between devices  132 us (30%)
  blocking collectives  58.6 us (13%)
  local copies, waits for them, and re-layouts  33.9 us (8%)
  matrix products  27.4 us (6%)
  other arithmetic  16.6 us (4%)
  between operations  13.8 us (3%)
    all_to_all x5, waiting for transfers between devices, gathered(): return lax.all_to_all(spread, axis, split_axis=0, concat_axis=0, tiled=True)  78.7 us
    ppermute x11, starting transfers between devices, take(): lax.ppermute(value, axis, [((i + distance) % n, i) for i in range(n)])  60.1 us
    ppermute x11, waiting for transfers between devices, take(): lax.ppermute(value, axis, [((i + distance) % n, i) for i in range(n)])  58.3 us
    all_to_all x5, starting transfers between devices, gathered(): return lax.all_to_all(spread, axis, split_axis=0, concat_axis=0, tiled=True)  48.9 us
    all_to_all x2, blocking collectives, gathered(): return lax.all_to_all(spread, axis, split_axis=0, concat_axis=0, tiled=True)  46.7 us
    all_to_all x3, waiting for transfers between devices, exchanged_sum(): lax.all_to_all(value, axis, split_axis=0, concat_axis=0, tiled=True)  12.4 us
    all_to_all x3, starting transfers between devices, exchanged_sum(): lax.all_to_all(value, axis, split_axis=0, concat_axis=0, tiled=True)  12.4 us
    all_to_all x1, blocking collectives, exchanged_sum(): lax.all_to_all(value, axis, split_axis=0, concat_axis=0, tiled=True)  11.9 us
  transfers between devices with their start and end apart: 25, of which 13 were waited for; matrix products, arithmetic and copies ran while one was open for 12% of the time, Pallas kernels for 0%

profile of v2, /device:TPU:1, one launch (start us, length us, event | category | flops | bytes accessed | tf_op | source)
XLA Modules:
  0.0 434.0 jit_solution(4167005194264935934)
XLA Ops:
  6.5 2.6 broadcast_in_dim.17
  9.2 4.8 %all-to-all-start = ((bf16[4,320,800]{2,1,0:T(8,128)(2,1)}), bf16[4,320,800]{2,1,0:T(8,128)(2,1)S(1)}, u32[]{:S(2)}, u32[]{:S(2)}) async-start(bf16[4,320,800]{2,1,0:T(8,128)(2,1)} %broadcast_in_dim.17), calls=%async_computation | async-start | bytes 4587520 | tf_op jit(solution)/shard_map/all_to_all | solution.py:43
  14.0 22.5 %all-to-all-done = bf16[4,320,800]{2,1,0:T(8,128)(2,1)S(1)} async-done(((bf16[4,320,800]{2,1,0:T(8,128)(2,1)}), bf16[4,320,800]{2,1,0:T(8,128)(2,1)S(1)}, u32[]{:S(2)}, u32[]{:S(2)}) %all-to-all-start) | async-done | bytes 2048032 | tf_op jit(solution)/shard_map/all_to_all | solution.py:43
  36.6 2.5 fusion.17
  39.1 8.8 %collective-permute-start.2 = (bf16[320,640]{1,0:T(8,128)(2,1)}, bf16[320,640]{1,0:T(8,128)(2,1)}, u32[]{:S(2)}, u32[]{:S(2)}) collective-permute-start(bf16[320,640]{1,0:T(8,128)(2,1)} %fusion.17), channel_id=1, source_target_pairs={{1,0},{0,1},{3,2},{2,3},{5,4},{4,5},{7,6},{6,7},{9,8},{8,9},{11,10... | collective-permute-start | bytes 1228808 | tf_op jit(solution)/shard_map/ppermute | solution.py:21
  47.9 8.8 %collective-permute-start.1 = (bf16[320,800]{1,0:T(8,128)(2,1)}, bf16[320,800]{1,0:T(8,128)(2,1)S(1)}, u32[]{:S(2)}, u32[]{:S(2)}) collective-permute-start(bf16[320,800]{1,0:T(8,128)(2,1)} %param.1), channel_id=1, source_target_pairs={{96,0},{0,32},{32,64},{64,96},{97,1},{1,33},{33,65},{65,97},{98,2}... | collective-permute-start | bytes 1536008 | tf_op jit(solution)/shard_map/ppermute | solution.py:21
  56.7 5.6 %collective-permute-start = (bf16[320,800]{1,0:T(8,128)(2,1)}, bf16[320,800]{1,0:T(8,128)(2,1)S(1)}, u32[]{:S(2)}, u32[]{:S(2)}) collective-permute-start(bf16[320,800]{1,0:T(8,128)(2,1)} %param.1), channel_id=1, source_target_pairs={{32,0},{64,32},{96,64},{0,96},{33,1},{65,33},{97,65},{1,97},{34,2}... | collective-permute-start | bytes 1536008 | tf_op jit(solution)/shard_map/ppermute | solution.py:21
  64.1 11.9 %all_to_all.55 = bf16[4,80,640]{2,1,0:T(8,128)(2,1)} all-to-all(bf16[4,80,640]{2,1,0:T(8,128)(2,1)S(1)} %bitcast.122), channel_id=1, replica_groups=mesh['x'=4,'zh'=4,'zl'=4,'y'=4,'c'=2] {'y'}, dimensions={0} | all-to-all | bytes 819200 | tf_op jit(solution)/shard_map/all_to_all | solution.py:47
  77.1 5.8 %collective-permute-done.1 = bf16[320,800]{1,0:T(8,128)(2,1)S(1)} collective-permute-done((bf16[320,800]{1,0:T(8,128)(2,1)}, bf16[320,800]{1,0:T(8,128)(2,1)S(1)}, u32[]{:S(2)}, u32[]{:S(2)}) %collective-permute-start.1) | collective-permute-done | bytes 512032 | tf_op jit(solution)/shard_map/ppermute | solution.py:21
  82.9 32.9 %collective-permute-done = bf16[320,800]{1,0:T(8,128)(2,1)S(1)} collective-permute-done((bf16[320,800]{1,0:T(8,128)(2,1)}, bf16[320,800]{1,0:T(8,128)(2,1)S(1)}, u32[]{:S(2)}, u32[]{:S(2)}) %collective-permute-start) | collective-permute-done | bytes 512032 | tf_op jit(solution)/shard_map/ppermute | solution.py:21
  117.4 4.5 %all-to-all-start.3 = ((bf16[4,320,800]{2,1,0:T(8,128)(2,1)}), bf16[4,320,800]{2,1,0:T(8,128)(2,1)}, u32[]{:S(2)}, u32[]{:S(2)}) async-start(bf16[4,320,800]{2,1,0:T(8,128)(2,1)} %broadcast_in_dim.18), calls=%async_computation.3 | async-start | bytes 4587520 | tf_op jit(solution)/shard_map/all_to_all | solution.py:43
  122.0 2.1 convolution_convert_fusion
  124.1 2.7 collective-permute-start.5
  126.8 22.8 %all-to-all-done.3 = bf16[4,320,800]{2,1,0:T(8,128)(2,1)} async-done(((bf16[4,320,800]{2,1,0:T(8,128)(2,1)}), bf16[4,320,800]{2,1,0:T(8,128)(2,1)}, u32[]{:S(2)}, u32[]{:S(2)}) %all-to-all-start.3) | async-done | bytes 2048032 | tf_op jit(solution)/shard_map/all_to_all | solution.py:43
  149.7 2.8 convolution_convert_fusion.1
  152.5 3.6 collective-permute-start.6
  156.1 3.2 add_convert_fusion
  159.3 4.2 all-to-all-start.2
  163.6 2.8 fusion.15
  166.4 9.7 %all-to-all-done.2 = bf16[4,160,640]{2,1,0:T(8,128)(2,1)} async-done(((bf16[4,160,640]{2,1,0:T(8,128)(2,1)}), bf16[4,160,640]{2,1,0:T(8,128)(2,1)}, u32[]{:S(2)}, u32[]{:S(2)}) %all-to-all-start.2) | async-done | bytes 819232 | tf_op jit(solution)/shard_map/all_to_all | solution.py:47
  176.1 4.1 all-to-all-start.4
  180.9 2.0 reduce_sum.49
  184.4 2.8 all-to-all-done.4
  197.5 4.1 all-to-all-start.5
  203.1 7.0 %collective-permute-start.4 = (bf16[160,800]{1,0:T(8,128)(2,1)}, bf16[160,800]{1,0:T(8,128)(2,1)S(1)}, u32[]{:S(2)}, u32[]{:S(2)}) collective-permute-start(bf16[160,800]{1,0:T(8,128)(2,1)} %slice.51), channel_id=1, source_target_pairs={{96,0},{0,32},{32,64},{64,96},{97,1},{1,33},{33,65},{65,97},{98,2}... | collective-permute-start | bytes 768008 | tf_op jit(solution)/shard_map/ppermute | solution.py:21
  210.1 2.2 collective-permute-start.3
  213.4 3.5 collective-permute-done.4
  216.9 8.7 %collective-permute-done.3 = bf16[160,800]{1,0:T(8,128)(2,1)S(1)} collective-permute-done((bf16[160,800]{1,0:T(8,128)(2,1)}, bf16[160,800]{1,0:T(8,128)(2,1)S(1)}, u32[]{:S(2)}, u32[]{:S(2)}) %collective-permute-start.3) | collective-permute-done | bytes 256032 | tf_op jit(solution)/shard_map/ppermute | solution.py:21
  227.1 30.0 %all-to-all-start.7 = ((bf16[4,80,640]{2,1,0:T(8,128)(2,1)}), bf16[4,80,640]{2,1,0:T(8,128)(2,1)S(1)}, u32[]{:S(2)}, u32[]{:S(2)}) async-start(bf16[4,80,640]{2,1,0:T(8,128)(2,1)} %broadcast_in_dim.22), calls=%async_computation.7 | async-start | bytes 819200 | tf_op jit(solution)/shard_map/all_to_all | solution.py:43
  257.0 1.9 collective-permute-start.10
  259.0 7.3 %collective-permute-start.8 = (bf16[80,640]{1,0:T(8,128)(2,1)S(1)}, bf16[80,640]{1,0:T(8,128)(2,1)S(1)}, u32[]{:S(2)}, u32[]{:S(2)}) collective-permute-start(bf16[80,640]{1,0:T(8,128)(2,1)S(1)} %reduce_sum.51), channel_id=1, source_target_pairs={{32,0},{40,8},{48,16},{16,24},{56,32},{72,40},{80,48},{88,56},{96,... | collective-permute-start | bytes 307208 | tf_op jit(solution)/shard_map/ppermute | solution.py:33
  268.3 3.0 collective-permute-start.11
  271.3 6.2 %collective-permute-start.9 = (bf16[32,640]{1,0:T(8,128)(2,1)S(1)}, bf16[32,640]{1,0:T(8,128)(2,1)S(1)}, u32[]{:S(2)}, u32[]{:S(2)}) collective-permute-start(bf16[32,640]{1,0:T(8,128)(2,1)S(1)} %slice.68), channel_id=1, source_target_pairs={{32,0},{64,32},{96,64},{0,96},{33,1},{65,33},{97,65},{1,97},{34,2}... | collective-permute-start | bytes 122888 | tf_op jit(solution)/shard_map/ppermute | solution.py:21
  277.5 6.8 %collective-permute-done.9 = bf16[32,640]{1,0:T(8,128)(2,1)S(1)} collective-permute-done((bf16[32,640]{1,0:T(8,128)(2,1)S(1)}, bf16[32,640]{1,0:T(8,128)(2,1)S(1)}, u32[]{:S(2)}, u32[]{:S(2)}) %collective-permute-start.9) | collective-permute-done | bytes 40992 | tf_op jit(solution)/shard_map/ppermute | solution.py:21
  285.7 5.3 %all-to-all-start.6 = ((bf16[4,80,2560]{2,1,0:T(8,128)(2,1)}), bf16[4,80,2560]{2,1,0:T(8,128)(2,1)}, u32[]{:S(2)}, u32[]{:S(2)}) async-start(bf16[4,80,2560]{2,1,0:T(8,128)(2,1)} %broadcast_in_dim.19), calls=%async_computation.6 | async-start | bytes 3276800 | tf_op jit(solution)/shard_map/all_to_all | solution.py:43
  292.0 16.8 %all-to-all-done.6 = bf16[4,80,2560]{2,1,0:T(8,128)(2,1)} async-done(((bf16[4,80,2560]{2,1,0:T(8,128)(2,1)}), bf16[4,80,2560]{2,1,0:T(8,128)(2,1)}, u32[]{:S(2)}, u32[]{:S(2)}) %all-to-all-start.6) | async-done | bytes 1638432 | tf_op jit(solution)/shard_map/all_to_all | solution.py:43
  310.1 4.4 %all-to-all-start.8 = ((bf16[4,80,2560]{2,1,0:T(8,128)(2,1)}), bf16[4,80,2560]{2,1,0:T(8,128)(2,1)}, u32[]{:S(2)}, u32[]{:S(2)}) async-start(bf16[4,80,2560]{2,1,0:T(8,128)(2,1)} %broadcast_in_dim.23), calls=%async_computation.8 | async-start | bytes 3276800 | tf_op jit(solution)/shard_map/all_to_all | solution.py:43
  314.5 16.5 %all-to-all-done.8 = bf16[4,80,2560]{2,1,0:T(8,128)(2,1)} async-done(((bf16[4,80,2560]{2,1,0:T(8,128)(2,1)}), bf16[4,80,2560]{2,1,0:T(8,128)(2,1)}, u32[]{:S(2)}, u32[]{:S(2)}) %all-to-all-start.8) | async-done | bytes 1638432 | tf_op jit(solution)/shard_map/all_to_all | solution.py:43
  331.0 3.1 fusion.16
  334.9 7.7 %collective-permute-start.13 = (f32[160,320]{1,0:T(8,128)}, f32[160,320]{1,0:T(8,128)}, u32[]{:S(2)}, u32[]{:S(2)}) collective-permute-start(f32[160,320]{1,0:T(8,128)} %dynamic-slice_bitcast_fusion), channel_id=1, source_target_pairs={{1,0},{0,1},{3,2},{2,3},{5,4},{4,5},{7,6},{6,7},{9,8},{8,9},{11,10... | collective-permute-start | bytes 614408 | tf_op jit(solution)/shard_map/ppermute | solution.py:21
  345.1 20.3 %all_to_all.56 = bf16[4,160,320]{2,1,0:T(8,128)(2,1)S(1)} all-to-all(bf16[4,160,320]{2,1,0:T(8,128)(2,1)S(1)} %broadcast_in_dim.24), channel_id=1, replica_groups=mesh['x'=4,'zh'=4,'zl'=4,'y'=4,'c'=2] {'zl'}, dimensions={0} | all-to-all | bytes 819200 | tf_op jit(solution)/shard_map/all_to_all | solution.py:43
  365.9 26.5 %all_to_all.57 = bf16[4,4,160,320]{3,2,1,0:T(8,128)(2,1)} all-to-all(bf16[4,4,160,320]{3,2,1,0:T(8,128)(2,1)S(1)} %broadcast_in_dim.25), channel_id=1, replica_groups=mesh['x'=4,'zh'=4,'zl'=4,'y'=4,'c'=2] {'y'}, dimensions={0} | all-to-all | bytes 3276800 | tf_op jit(solution)/shard_map/all_to_all | solution.py:43
  392.3 4.0 copy.19
  396.3 4.7 %collective-permute-start.14 = (bf16[2560,320]{0,1:T(8,128)(2,1)}, bf16[2560,320]{0,1:T(8,128)(2,1)}, u32[]{:S(2)}, u32[]{:S(2)}) collective-permute-start(bf16[2560,320]{0,1:T(8,128)(2,1)} %copy.19), channel_id=1, source_target_pairs={{1,0},{0,1},{3,2},{2,3},{5,4},{4,5},{7,6},{6,7},{9,8},{8,9},{11,10... | collective-permute-start | bytes 4915208 | tf_op jit(solution)/shard_map/ppermute | solution.py:21
  401.1 8.4 %maximum_bitcast_fusion = bf16[2,4,4,2,80,800]{5,4,1,3,0,2:T(8,128)(2,1)} fusion(bf16[1,2,2,4,80,800]{5,4,3,2,1,0:T(8,128)(2,1)} %bitcast.114, bf16[1,2,2,4,80,800]{5,4,3,2,1,0:T(8,128)(2,1)} %bitcast.115, bf16[1,2,2,4,80,800]{5,4,3,2,1,0:T(8,128)(2,1)} %bitcast.33, bf16[1,2,2,4,80,800]{5,4,3,2,1,0:T(8,128)(2,1)S(1)} %bitcast.107), kind=kLoop, calls=%fused_computation | loop fusion | flops 12288000 | bytes 16384000 | tf_op jit(solution)/shard_map/transpose | solution.py:109
  409.4 8.3 %copy.18 = bf16[2,4,4,2,80,800]{5,4,3,2,1,0:T(8,128)(2,1)} copy(bf16[2,4,4,2,80,800]{5,4,1,3,0,2:T(8,128)(2,1)} %maximum_bitcast_fusion) | data formatting | bytes 16384000 | tf_op jit(solution)/shard_map/transpose | solution.py:109
  417.7 4.3 fusion.2
  422.7 4.5 %fusion.12 = f32[320,800]{1,0:T(8,128)} fusion(f32[320,800]{1,0:T(8,128)S(1)} %fusion.2, bf16[2560,320]{0,1:T(8,128)(2,1)} %collective-permute-done.14, bf16[2,2560,800]{2,1,0:T(8,128)(2,1)S(1)} %bitcast.109, s32[]{:T(128)S(6)} %select_n.55, bf16[320,800]{1,0:T(8,128)(2,1)} %param.1), kind=kOutput, calls=%fused_computation.11 | convolution fusion | flops 1312000000 | bytes 8908804 | tf_op jit(solution)/shard_map/km,kn->mn/dot_general | solution.py:112
  (67 shorter events, 31.3 us)
Async XLA Ops:
  9.2 27.4 %all-to-all-start = ((bf16[4,320,800]{2,1,0:T(8,128)(2,1)}), bf16[4,320,800]{2,1,0:T(8,128)(2,1)S(1)}, u32[]{:S(2)}, u32[]{:S(2)}) async-start(bf16[4,320,800]{2,1,0:T(8,128)(2,1)} %broadcast_in_dim.17), calls=%async_computation | async-start | bytes 4587520 | tf_op jit(solution)/shard_map/all_to_all | solution.py:43
  39.1 23.1 %collective-permute-start.2 = (bf16[320,640]{1,0:T(8,128)(2,1)}, bf16[320,640]{1,0:T(8,128)(2,1)}, u32[]{:S(2)}, u32[]{:S(2)}) collective-permute-start(bf16[320,640]{1,0:T(8,128)(2,1)} %fusion.17), channel_id=1, source_target_pairs={{1,0},{0,1},{3,2},{2,3},{5,4},{4,5},{7,6},{6,7},{9,8},{8,9},{11,10... | collective-permute-start | bytes 1228808 | tf_op jit(solution)/shard_map/ppermute | solution.py:21
  47.9 35.1 %collective-permute-start.1 = (bf16[320,800]{1,0:T(8,128)(2,1)}, bf16[320,800]{1,0:T(8,128)(2,1)S(1)}, u32[]{:S(2)}, u32[]{:S(2)}) collective-permute-start(bf16[320,800]{1,0:T(8,128)(2,1)} %param.1), channel_id=1, source_target_pairs={{96,0},{0,32},{32,64},{64,96},{97,1},{1,33},{33,65},{65,97},{98,2}... | collective-permute-start | bytes 1536008 | tf_op jit(solution)/shard_map/ppermute | solution.py:21
  56.7 59.1 %collective-permute-start = (bf16[320,800]{1,0:T(8,128)(2,1)}, bf16[320,800]{1,0:T(8,128)(2,1)S(1)}, u32[]{:S(2)}, u32[]{:S(2)}) collective-permute-start(bf16[320,800]{1,0:T(8,128)(2,1)} %param.1), channel_id=1, source_target_pairs={{32,0},{64,32},{96,64},{0,96},{33,1},{65,33},{97,65},{1,97},{34,2}... | collective-permute-start | bytes 1536008 | tf_op jit(solution)/shard_map/ppermute | solution.py:21
  82.9 119.4 %copy-start.2 = (bf16[320,800]{1,0:T(8,128)(2,1)}, bf16[320,800]{1,0:T(8,128)(2,1)S(1)}, u32[]{:S(2)}) copy-start(bf16[320,800]{1,0:T(8,128)(2,1)S(1)} %collective-permute-done.1) | copy-start | bytes 1536004
  117.4 32.3 %all-to-all-start.3 = ((bf16[4,320,800]{2,1,0:T(8,128)(2,1)}), bf16[4,320,800]{2,1,0:T(8,128)(2,1)}, u32[]{:S(2)}, u32[]{:S(2)}) async-start(bf16[4,320,800]{2,1,0:T(8,128)(2,1)} %broadcast_in_dim.18), calls=%async_computation.3 | async-start | bytes 4587520 | tf_op jit(solution)/shard_map/all_to_all | solution.py:43
  122.0 2.1 copy-start.3
  124.1 31.9 %collective-permute-start.5 = (bf16[640,640]{1,0:T(8,128)(2,1)}, bf16[640,640]{1,0:T(8,128)(2,1)}, u32[]{:S(2)}, u32[]{:S(2)}) collective-permute-start(bf16[640,640]{1,0:T(8,128)(2,1)} %convolution_convert_fusion), channel_id=1, source_target_pairs={{1,0},{0,1},{3,2},{2,3},{5,4},{4,5},{7,6},{6,7},{9,8},{8,9},{11,10... | collective-permute-start | bytes 2457608 | tf_op jit(solution)/shard_map/ppermute | solution.py:21
  149.7 6.4 %copy-start.4 = (bf16[2,4,80,800]{3,2,0,1:T(8,128)(2,1)S(1)}, bf16[2,4,80,800]{3,2,0,1:T(8,128)(2,1)}, u32[]{:S(2)}) copy-start(bf16[2,4,80,800]{3,2,0,1:T(8,128)(2,1)} %copy-done.3) | copy-start | bytes 3072004
  152.5 11.1 %collective-permute-start.6 = (bf16[320,640]{1,0:T(8,128)(2,1)}, bf16[320,640]{1,0:T(8,128)(2,1)}, u32[]{:S(2)}, u32[]{:S(2)}) collective-permute-start(bf16[320,640]{1,0:T(8,128)(2,1)} %convolution_convert_fusion.1), channel_id=1, source_target_pairs={{1,0},{0,1},{3,2},{2,3},{5,4},{4,5},{7,6},{6,7},{9,8},{8,9},{11,10... | collective-permute-start | bytes 1228808 | tf_op jit(solution)/shard_map/ppermute | solution.py:21
  159.3 16.8 %all-to-all-start.2 = ((bf16[4,160,640]{2,1,0:T(8,128)(2,1)}), bf16[4,160,640]{2,1,0:T(8,128)(2,1)}, u32[]{:S(2)}, u32[]{:S(2)}) async-start(bf16[4,160,640]{2,1,0:T(8,128)(2,1)} %bitcast.118), calls=%async_computation.2 | async-start | bytes 1638400 | tf_op jit(solution)/shard_map/all_to_all | solution.py:47
  176.1 11.1 %all-to-all-start.4 = ((bf16[4,80,640]{2,1,0:T(8,128)(2,1)}), bf16[4,80,640]{2,1,0:T(8,128)(2,1)}, u32[]{:S(2)}, u32[]{:S(2)}) async-start(bf16[4,80,640]{2,1,0:T(8,128)(2,1)} %bitcast.121), calls=%async_computation.4 | async-start | bytes 819200 | tf_op jit(solution)/shard_map/all_to_all | solution.py:47
  197.5 14.8 %all-to-all-start.5 = ((bf16[4,80,640]{2,1,0:T(8,128)(2,1)}), bf16[4,80,640]{2,1,0:T(8,128)(2,1)}, u32[]{:S(2)}, u32[]{:S(2)}) async-start(bf16[4,80,640]{2,1,0:T(8,128)(2,1)} %constant_dynamic-slice_fusion), calls=%async_computation.5 | async-start | bytes 819200 | tf_op jit(solution)/shard_map/all_to_all | solution.py:47
  203.1 13.8 %collective-permute-start.4 = (bf16[160,800]{1,0:T(8,128)(2,1)}, bf16[160,800]{1,0:T(8,128)(2,1)S(1)}, u32[]{:S(2)}, u32[]{:S(2)}) collective-permute-start(bf16[160,800]{1,0:T(8,128)(2,1)} %slice.51), channel_id=1, source_target_pairs={{96,0},{0,32},{32,64},{64,96},{97,1},{1,33},{33,65},{65,97},{98,2}... | collective-permute-start | bytes 768008 | tf_op jit(solution)/shard_map/ppermute | solution.py:21
  210.1 15.5 %collective-permute-start.3 = (bf16[160,800]{1,0:T(8,128)(2,1)}, bf16[160,800]{1,0:T(8,128)(2,1)S(1)}, u32[]{:S(2)}, u32[]{:S(2)}) collective-permute-start(bf16[160,800]{1,0:T(8,128)(2,1)} %slice.50), channel_id=1, source_target_pairs={{32,0},{64,32},{96,64},{0,96},{33,1},{65,33},{97,65},{1,97},{34,2}... | collective-permute-start | bytes 768008 | tf_op jit(solution)/shard_map/ppermute | solution.py:21
  225.6 1.5 copy-start.5
  225.6 0.7 collective-permute-start.12
  227.1 57.3 %all-to-all-start.7 = ((bf16[4,80,640]{2,1,0:T(8,128)(2,1)}), bf16[4,80,640]{2,1,0:T(8,128)(2,1)S(1)}, u32[]{:S(2)}, u32[]{:S(2)}) async-start(bf16[4,80,640]{2,1,0:T(8,128)(2,1)} %broadcast_in_dim.22), calls=%async_computation.7 | async-start | bytes 819200 | tf_op jit(solution)/shard_map/all_to_all | solution.py:43
  257.0 11.2 %collective-permute-start.10 = (bf16[80,640]{1,0:T(8,128)(2,1)S(1)}, bf16[80,640]{1,0:T(8,128)(2,1)S(1)}, u32[]{:S(2)}, u32[]{:S(2)}) collective-permute-start(bf16[80,640]{1,0:T(8,128)(2,1)S(1)} %reduce_sum.51), channel_id=1, source_target_pairs={{96,0},{64,8},{112,16},{120,24},{0,32},{8,40},{104,48},{24,56},{32... | collective-permute-start | bytes 307208 | tf_op jit(solution)/shard_map/ppermute | solution.py:33
  259.0 12.3 %collective-permute-start.8 = (bf16[80,640]{1,0:T(8,128)(2,1)S(1)}, bf16[80,640]{1,0:T(8,128)(2,1)S(1)}, u32[]{:S(2)}, u32[]{:S(2)}) collective-permute-start(bf16[80,640]{1,0:T(8,128)(2,1)S(1)} %reduce_sum.51), channel_id=1, source_target_pairs={{32,0},{40,8},{48,16},{16,24},{56,32},{72,40},{80,48},{88,56},{96,... | collective-permute-start | bytes 307208 | tf_op jit(solution)/shard_map/ppermute | solution.py:33
  266.2 11.3 %collective-permute-start.7 = (bf16[80,640]{1,0:T(8,128)(2,1)S(1)}, bf16[80,640]{1,0:T(8,128)(2,1)S(1)}, u32[]{:S(2)}, u32[]{:S(2)}) collective-permute-start(bf16[80,640]{1,0:T(8,128)(2,1)S(1)} %reduce_sum.51), channel_id=1, source_target_pairs={{0,0},{8,8},{104,16},{24,24},{32,32},{40,40},{48,48},{16,56},{56,6... | collective-permute-start | bytes 307208 | tf_op jit(solution)/shard_map/ppermute | solution.py:33
  268.3 16.1 %collective-permute-start.11 = (bf16[48,640]{1,0:T(8,128)(2,1)S(1)}, bf16[48,640]{1,0:T(8,128)(2,1)S(1)}, u32[]{:S(2)}, u32[]{:S(2)}) collective-permute-start(bf16[48,640]{1,0:T(8,128)(2,1)S(1)} %slice.69), channel_id=1, source_target_pairs={{96,0},{0,32},{32,64},{64,96},{97,1},{1,33},{33,65},{65,97},{98,2}... | collective-permute-start | bytes 184328 | tf_op jit(solution)/shard_map/ppermute | solution.py:21
  271.3 13.1 %collective-permute-start.9 = (bf16[32,640]{1,0:T(8,128)(2,1)S(1)}, bf16[32,640]{1,0:T(8,128)(2,1)S(1)}, u32[]{:S(2)}, u32[]{:S(2)}) collective-permute-start(bf16[32,640]{1,0:T(8,128)(2,1)S(1)} %slice.68), channel_id=1, source_target_pairs={{32,0},{64,32},{96,64},{0,96},{33,1},{65,33},{97,65},{1,97},{34,2}... | collective-permute-start | bytes 122888 | tf_op jit(solution)/shard_map/ppermute | solution.py:21
  285.7 23.1 %all-to-all-start.6 = ((bf16[4,80,2560]{2,1,0:T(8,128)(2,1)}), bf16[4,80,2560]{2,1,0:T(8,128)(2,1)}, u32[]{:S(2)}, u32[]{:S(2)}) async-start(bf16[4,80,2560]{2,1,0:T(8,128)(2,1)} %broadcast_in_dim.19), calls=%async_computation.6 | async-start | bytes 3276800 | tf_op jit(solution)/shard_map/all_to_all | solution.py:43
  291.0 110.1 %all-gather.7.cloned.1.call-start = ((), (), s32[]{:S(2)}) async-start(), calls=%async_computation.12 | async-start | bytes 2867200 | tf_op jit(solution)/shard_map/all_gather | solution.py:80
  310.1 20.9 %all-to-all-start.8 = ((bf16[4,80,2560]{2,1,0:T(8,128)(2,1)}), bf16[4,80,2560]{2,1,0:T(8,128)(2,1)}, u32[]{:S(2)}, u32[]{:S(2)}) async-start(bf16[4,80,2560]{2,1,0:T(8,128)(2,1)} %broadcast_in_dim.23), calls=%async_computation.8 | async-start | bytes 3276800 | tf_op jit(solution)/shard_map/all_to_all | solution.py:43
  314.5 86.6 %all-gather.5.cloned.1.call-start = ((), (), s32[]{:S(2)}) async-start(), calls=%async_computation.11 | async-start | bytes 2867200 | tf_op jit(solution)/shard_map/all_gather | solution.py:87
  331.0 11.6 %copy-start.6 = (bf16[160,800]{1,0:T(8,128)(2,1)S(1)}, bf16[160,800]{1,0:T(8,128)(2,1)}, u32[]{:S(2)}) copy-start(bf16[160,800]{1,0:T(8,128)(2,1)} %copy-done.5) | copy-start | bytes 768004
  334.9 9.2 %collective-permute-start.13 = (f32[160,320]{1,0:T(8,128)}, f32[160,320]{1,0:T(8,128)}, u32[]{:S(2)}, u32[]{:S(2)}) collective-permute-start(f32[160,320]{1,0:T(8,128)} %dynamic-slice_bitcast_fusion), channel_id=1, source_target_pairs={{1,0},{0,1},{3,2},{2,3},{5,4},{4,5},{7,6},{6,7},{9,8},{8,9},{11,10... | collective-permute-start | bytes 614408 | tf_op jit(solution)/shard_map/ppermute | solution.py:21
  396.3 25.7 %collective-permute-start.14 = (bf16[2560,320]{0,1:T(8,128)(2,1)}, bf16[2560,320]{0,1:T(8,128)(2,1)}, u32[]{:S(2)}, u32[]{:S(2)}) collective-permute-start(bf16[2560,320]{0,1:T(8,128)(2,1)} %copy.19), channel_id=1, source_target_pairs={{1,0},{0,1},{3,2},{2,3},{5,4},{4,5},{7,6},{6,7},{9,8},{8,9},{11,10... | collective-permute-start | bytes 4915208 | tf_op jit(solution)/shard_map/ppermute | solution.py:21
  409.4 8.3 %copy-start.1 = (bf16[4,4,160,320]{3,2,1,0:T(8,128)(2,1)S(1)}, bf16[4,4,160,320]{3,2,1,0:T(8,128)(2,1)}, u32[]{:S(2)}) copy-start(bf16[4,4,160,320]{3,2,1,0:T(8,128)(2,1)} %all_to_all.57) | copy-start | bytes 4915204
  417.7 5.0 %copy-start = (bf16[2,4,4,2,80,800]{5,4,3,2,1,0:T(8,128)(2,1)S(1)}, bf16[2,4,4,2,80,800]{5,4,3,2,1,0:T(8,128)(2,1)}, u32[]{:S(2)}) copy-start(bf16[2,4,4,2,80,800]{5,4,3,2,1,0:T(8,128)(2,1)} %copy.18) | copy-start | bytes 24576004
Sparse Core Ops, SparseCore 0:
  293.9 46.9 all-gather.6
  343.6 41.0 all-gather.4

commit v3 on v2

v3 whole, which is shorter than its diff:
```python
import math

import jax
import jax.numpy as jnp
from jax import lax
from jax.sharding import Mesh
from jax.sharding import PartitionSpec as P

QUINTIC_A = 3.4445
QUINTIC_B = -4.775
QUINTIC_C = 2.0315

SIZES = {"x": 4, "zh": 4, "zl": 4, "y": 4, "c": 2}
Z = ("zh", "zl")
F32 = jnp.float32
BF16 = jnp.bfloat16


def take(value, axis, distance):
    n = lax.axis_size(axis)
    return lax.ppermute(value, axis, [((i + distance) % n, i) for i in range(n)])


def home(a, b):
    if (a - b) % 4 == 2:
        return (b - 1) % 4 * 4 + (b + 1) % 4
    return b * 4 + a


def fetch(piece, wanted):
    route = [(home(*wanted(p, q)), p * 4 + q) for p in range(4) for q in range(4)]
    return lax.ppermute(piece, Z, route)


def rolled(parts, start):
    return [
        lax.select_n(start, *[parts[(s + i) % 4] for s in range(4)]) for i in range(4)
    ]


def gathered(value, axis):
    spread = jnp.broadcast_to(value[None], (lax.axis_size(axis),) + value.shape)
    return lax.all_to_all(spread, axis, split_axis=0, concat_axis=0, tiled=True)


def exchanged_sum(value, axis):
    received = lax.all_to_all(value, axis, split_axis=0, concat_axis=0, tiled=True)
    return received.astype(F32).sum(0)


def matmul_over_c(block, keep, give):
    sent = jnp.einsum("rn,sn->rs", block, give, preferred_element_type=F32).astype(BF16)
    other = take(sent, "c", 1)
    kept = jnp.einsum("rn,sn->rs", block, keep, preferred_element_type=F32)
    return (kept + other.astype(F32)).astype(BF16)


def local(iterate):
    rows, width = iterate.shape
    h, c = lax.axis_index("zh"), lax.axis_index("c")
    slab = rows // 4
    pair = 2 * rows

    def columns(block):
        halves = block.reshape(2, pair, -1)
        return halves[c], halves[1 - c]

    upper, lower = take(iterate, "zh", 1), take(iterate, "zh", -1)
    mine = lax.all_gather(iterate, "x", axis=0, tiled=True)
    above = lax.all_gather(upper, "x", axis=0, tiled=True)
    below = lax.all_gather(lower, "x", axis=0, tiled=True)
    cut = rows // 2
    odd = h % 2 == 1
    one = jnp.where(odd, upper, lower)[:cut]
    two = jnp.where(odd, lower, upper)[cut:]
    one = lax.all_gather(one, "zh", axis_index_groups=[[0, 1], [2, 3]])
    two = lax.all_gather(two, "zh", axis_index_groups=[[1, 2], [3, 0]])
    opposite = jnp.concatenate([one[1 - h % 2], two[h % 2]], axis=0)
    opposite = lax.all_gather(opposite, "x", axis=0, tiled=True)

    stacked = jnp.stack([iterate, upper, lower]).reshape(3, 4, slab, width)
    stacked = stacked.transpose(1, 0, 2, 3).reshape(3 * rows, width)
    tiles = matmul_over_c(stacked, *columns(mine))
    tiles = exchanged_sum(tiles.reshape(4, 3 * slab, pair), "y").astype(BF16)
    tiles = tiles.reshape(3, slab, pair)
    across = matmul_over_c(lower, *columns(above))
    across = exchanged_sum(across.reshape(4, slab, pair), "y").astype(BF16)
    by_l = jnp.stack(rolled([tiles[0], tiles[1], across, tiles[2]], (4 - h) % 4))
    gram = exchanged_sum(by_l, "zl").astype(BF16)

    turned = fetch(gram, lambda p, q: (p, q))
    gram = fetch(gram, lambda p, q: (q, p))
    left = gathered(gram, "zl").reshape(rows, pair)
    right = gathered(gram, ("x", "y")).reshape(2 * pair, pair)
    square = matmul_over_c(left, *columns(right))
    square = exchanged_sum(square.reshape(4, slab, pair), "zh")
    polynomial = (QUINTIC_B * turned.astype(F32) + QUINTIC_C * square).astype(BF16)

    polynomial = gathered(polynomial, "zl")
    polynomial = jnp.concatenate(rolled([polynomial[i] for i in range(4)], h), axis=1)
    polynomial = gathered(polynomial, "y").reshape(rows, 4 * pair)
    swapped = take(polynomial, "c", 1)

    blocks = [columns(block) for block in (mine, above, opposite, below)]
    own = jnp.concatenate([b[0] for b in blocks], axis=0)
    others = jnp.concatenate([b[1] for b in blocks], axis=0)
    product = jnp.einsum("mk,kn->mn", polynomial, own, preferred_element_type=F32)
    product += jnp.einsum("mk,kn->mn", swapped, others, preferred_element_type=F32)
    scale = 0.2 * math.sqrt(width * 32)
    return scale * (QUINTIC_A * iterate.astype(F32) + product)


def solution(mesh):
    fine = Mesh(mesh.devices.reshape(tuple(SIZES.values())), tuple(SIZES))
    spec = P(("x", "zh"), ("zl", "y", "c"))
    return jax.shard_map(local, mesh=fine, in_specs=(spec,), out_specs=spec, check_vma=False)
```

time: 436 us -> 391 us (0.90)
  blocking collectives: 58.6 us -> 119 us
  starting transfers between devices: 132 us -> 71.8 us
  local copies, waits for them, and re-layouts: 33.9 us -> 12 us
  other arithmetic: 16.6 us -> 3.23 us
  matrix products: 27.4 us -> 17.5 us
    all_to_all x5 -> x1, waiting for transfers between devices: 78.7 us -> 0.01 us  [gathered(): return lax.all_to_all(spread, axis, split_axis=0, concat_axis=0, tiled=True)]
    all_to_all x5 -> x1, starting transfers between devices: 48.9 us -> 7.42 us  [gathered(): return lax.all_to_all(spread, axis, split_axis=0, concat_axis=0, tiled=True)]
    all_gather x0 -> x2, blocking collectives: none -> 38.6 us  [the longest x1 27.1 us: local(): two = lax.all_gather(two, 'zh', axis_index_groups=[[1, 2], [3, 0]])]
    ppermute x11 -> x6, waiting for transfers between devices: 58.3 us -> 93 us  [take(): lax.ppermute(value, axis, [((i + distance) % n, i) for i in range(n)])]
    all_to_all x3, waiting for transfers between devices: 12.4 us -> 41.8 us  [exchanged_sum(): lax.all_to_all(value, axis, split_axis=0, concat_axis=0, tiled=True)]
    all_gather x2 -> x4, waiting for transfers between devices: 0.04 us -> 17.1 us  [the longest x1 17 us: local(): opposite = lax.all_gather(opposite, 'x', axis=0, tiled=True)]
    all_to_all x2 -> x3, blocking collectives: 46.7 us -> 61.9 us  [gathered(): return lax.all_to_all(spread, axis, split_axis=0, concat_axis=0, tiled=True)]
    dot_general x9 -> x8, matrix products: 27.4 us -> 17.5 us  [the longest x3 7.15 us: matmul_over_c(): kept = jnp.einsum('rn,sn->rs', block, keep, preferred_element_type=F32)]
  transfers between devices with their start and end apart: 25 -> 16, of which waited for: 13 -> 8; matrix products, arithmetic and copies ran while one was open for 12% -> 6% of each run, Pallas kernels for 0% -> 0%
where the time goes in v3:
time: 391 us; the launch traced here: 390 us
  waiting for transfers between devices  153 us (39%)
  blocking collectives  119 us (30%)
  starting transfers between devices  71.8 us (18%)
  matrix products  17.5 us (4%)
  between operations  13.5 us (3%)
  local copies, waits for them, and re-layouts  12 us (3%)
    ppermute x6, waiting for transfers between devices, take(): lax.ppermute(value, axis, [((i + distance) % n, i) for i in range(n)])  93 us
    all_to_all x3, blocking collectives, gathered(): return lax.all_to_all(spread, axis, split_axis=0, concat_axis=0, tiled=True)  61.9 us
    ppermute x6, starting transfers between devices, take(): lax.ppermute(value, axis, [((i + distance) % n, i) for i in range(n)])  51.7 us
    all_to_all x3, waiting for transfers between devices, exchanged_sum(): lax.all_to_all(value, axis, split_axis=0, concat_axis=0, tiled=True)  41.8 us
    all_gather x1, blocking collectives, local(): two = lax.all_gather(two, 'zh', axis_index_groups=[[1, 2], [3, 0]])  27.1 us
    all_to_all x1, blocking collectives, exchanged_sum(): lax.all_to_all(value, axis, split_axis=0, concat_axis=0, tiled=True)  18.8 us
    all_gather x1, waiting for transfers between devices, local(): opposite = lax.all_gather(opposite, 'x', axis=0, tiled=True)  17 us
    all_gather x1, blocking collectives, local(): one = lax.all_gather(one, 'zh', axis_index_groups=[[0, 1], [2, 3]])  11.5 us
  transfers between devices with their start and end apart: 16, of which 8 were waited for; matrix products, arithmetic and copies ran while one was open for 6% of the time, Pallas kernels for 0%

profile of v3, /device:TPU:1, one launch (start us, length us, event | category | flops | bytes accessed | tf_op | source)
XLA Modules:
  0.0 389.9 jit_solution(10581738242871691406)
XLA Ops:
  6.5 0.7 all-gather.7.cloned.1.call-update
  7.3 13.3 %collective-permute-start = (bf16[320,800]{1,0:T(8,128)(2,1)}, bf16[320,800]{1,0:T(8,128)(2,1)S(1)}, u32[]{:S(2)}, u32[]{:S(2)}) collective-permute-start(bf16[320,800]{1,0:T(8,128)(2,1)} %param.1), channel_id=1, source_target_pairs={{32,0},{64,32},{96,64},{0,96},{33,1},{65,33},{97,65},{1,97},{34,2}... | collective-permute-start | bytes 1536008 | tf_op jit(solution)/shard_map/ppermute | solution.py:21
  20.6 46.7 %collective-permute-done = bf16[320,800]{1,0:T(8,128)(2,1)S(1)} collective-permute-done((bf16[320,800]{1,0:T(8,128)(2,1)}, bf16[320,800]{1,0:T(8,128)(2,1)S(1)}, u32[]{:S(2)}, u32[]{:S(2)}) %collective-permute-start) | collective-permute-done | bytes 512032 | tf_op jit(solution)/shard_map/ppermute | solution.py:21
  67.3 0.8 copy-done.2
  68.1 8.6 %collective-permute-start.1 = (bf16[320,800]{1,0:T(8,128)(2,1)}, bf16[320,800]{1,0:T(8,128)(2,1)S(1)}, u32[]{:S(2)}, u32[]{:S(2)}) collective-permute-start(bf16[320,800]{1,0:T(8,128)(2,1)} %param.1), channel_id=1, source_target_pairs={{96,0},{0,32},{32,64},{64,96},{97,1},{1,33},{33,65},{65,97},{98,2}... | collective-permute-start | bytes 1536008 | tf_op jit(solution)/shard_map/ppermute | solution.py:21
  76.7 43.2 %collective-permute-done.1 = bf16[320,800]{1,0:T(8,128)(2,1)S(1)} collective-permute-done((bf16[320,800]{1,0:T(8,128)(2,1)}, bf16[320,800]{1,0:T(8,128)(2,1)S(1)}, u32[]{:S(2)}, u32[]{:S(2)}) %collective-permute-start.1) | collective-permute-done | bytes 512032 | tf_op jit(solution)/shard_map/ppermute | solution.py:21
  120.0 1.5 pad_maximum_fusion
  121.5 2.8 dynamic-slice_bitcast_fusion.7
  124.3 2.7 convolution_convert_fusion
  127.0 2.4 collective-permute-start.2
  129.5 1.8 dynamic-slice_bitcast_fusion.4
  131.3 0.7 fusion.28
  132.0 1.9 collective-permute-start.3
  133.9 1.7 collective-permute-done.3
  135.7 1.5 fusion.27
  137.1 4.2 %all-to-all-start.1 = ((bf16[4,80,640]{2,1,0:T(8,128)(2,1)}), bf16[4,80,640]{2,1,0:T(8,128)(2,1)S(1)}, u32[]{:S(2)}, u32[]{:S(2)}) async-start(bf16[4,80,640]{2,1,0:T(8,128)(2,1)} %bitcast.18), calls=%async_computation.1 | async-start | bytes 819200 | tf_op jit(solution)/shard_map/all_to_all | solution.py:47
  141.3 4.4 %add_convert_fusion = bf16[960,640]{1,0:T(8,128)(2,1)} fusion(bf16[960,640]{1,0:T(8,128)(2,1)} %collective-permute-done.2, bf16[960,800]{1,0:T(8,128)(2,1)S(1)} %bitcast.98, bf16[640,800]{1,0:T(8,128)(2,1)} %get-tuple-element.9), kind=kOutput, calls=%fused_computation.16 | convolution fusion | flops 984883200 | bytes 5017600 | tf_op jit(solution)/shard_map/rn,sn->rs/dot_general | solution.py:54
  145.7 3.6 all-to-all-done.1
  149.3 3.5 all-to-all-start
  152.9 15.6 %all-to-all-done = bf16[4,240,640]{2,1,0:T(8,128)(2,1)S(1)} async-done(((bf16[4,240,640]{2,1,0:T(8,128)(2,1)}), bf16[4,240,640]{2,1,0:T(8,128)(2,1)S(1)}, u32[]{:S(2)}, u32[]{:S(2)}) %all-to-all-start) | async-done | bytes 1228832 | tf_op jit(solution)/shard_map/all_to_all | solution.py:47
  168.6 0.3 reduce_sum.45
  169.0 18.8 %all_to_all.40 = bf16[4,80,640]{2,1,0:T(8,128)(2,1)S(1)} all-to-all(bf16[4,80,640]{2,1,0:T(8,128)(2,1)S(1)} %pad_maximum_fusion.2), channel_id=1, replica_groups=mesh['x'=4,'zh'=4,'zl'=4,'y'=4,'c'=2] {'zl'}, dimensions={0} | all-to-all | bytes 819200 | tf_op jit(solution)/shard_map/all_to_all | solution.py:47
  187.9 0.7 collective-permute-start.5
  188.7 22.2 %all_to_all.41 = bf16[4,80,640]{2,1,0:T(8,128)(2,1)S(1)} all-to-all(bf16[4,80,640]{2,1,0:T(8,128)(2,1)S(1)} %broadcast_in_dim.8), channel_id=1, replica_groups=mesh['x'=4,'zh'=4,'zl'=4,'y'=4,'c'=2] {'zl'}, dimensions={0} | all-to-all | bytes 819200 | tf_op jit(solution)/shard_map/all_to_all | solution.py:43
  210.9 0.1 broadcast_in_dim.9
  211.0 24.3 %all_to_all.42 = bf16[16,80,640]{2,1,0:T(8,128)(2,1)S(1)} all-to-all(bf16[16,80,640]{2,1,0:T(8,128)(2,1)S(1)} %broadcast_in_dim.9), channel_id=1, replica_groups=mesh['x'=4,'zh'=4,'zl'=4,'y'=4,'c'=2] {'x','y'}, dimensions={0} | all-to-all | bytes 3276800 | tf_op jit(solution)/shard_map/all_to_all | solution.py:43
  235.3 0.5 convolution_convert_fusion.2
  235.9 6.6 %collective-permute-start.6 = (bf16[320,640]{1,0:T(8,128)(2,1)S(1)}, bf16[320,640]{1,0:T(8,128)(2,1)S(1)}, u32[]{:S(2)}, u32[]{:S(2)}) collective-permute-start(bf16[320,640]{1,0:T(8,128)(2,1)S(1)} %convolution_convert_fusion.2), channel_id=1, source_target_pairs={{1,0},{0,1},{3,2},{2,3},{5,4},{4,5},{7,6},{6,7},{9,8},{8,9},{11,10... | collective-permute-start | bytes 1228808 | tf_op jit(solution)/shard_map/ppermute | solution.py:21
  242.5 1.3 collective-permute-done.6
  243.8 1.3 fusion.26
  245.1 3.5 all-to-all-start.5
  248.6 0.8 collective-permute-start.4
  249.4 22.6 %all-to-all-done.5 = bf16[4,80,640]{2,1,0:T(8,128)(2,1)S(1)} async-done(((bf16[4,80,640]{2,1,0:T(8,128)(2,1)}), bf16[4,80,640]{2,1,0:T(8,128)(2,1)S(1)}, u32[]{:S(2)}, u32[]{:S(2)}) %all-to-all-start.5) | async-done | bytes 409632 | tf_op jit(solution)/shard_map/all_to_all | solution.py:47
  272.2 0.8 broadcast_in_dim.10
  273.0 7.4 %all-to-all-start.6 = ((bf16[4,80,640]{2,1,0:T(8,128)(2,1)}), bf16[4,80,640]{2,1,0:T(8,128)(2,1)S(1)}, u32[]{:S(2)}, u32[]{:S(2)}) async-start(bf16[4,80,640]{2,1,0:T(8,128)(2,1)} %broadcast_in_dim.10), calls=%async_computation.6 | async-start | bytes 819200 | tf_op jit(solution)/shard_map/all_to_all | solution.py:43
  280.5 11.5 %all-gather = bf16[320,800]{1,0:T(8,128)(2,1)S(1)} all-gather(bf16[160,800]{1,0:T(8,128)(2,1)S(1)} %get-tuple-element.13), channel_id=2, replica_groups={{0,32},{64,96},{1,33},{65,97},{2,34},{66,98},{3,35},{67,99},{4,36},{68,..., dimensions={0}, use_global_device_ids=true | all-gather | bytes 768000 | tf_op jit(solution)/shard_map/all_gather | solution.py:76
  292.0 27.1 %all-gather.1 = bf16[320,800]{1,0:T(8,128)(2,1)S(1)} all-gather(bf16[160,800]{1,0:T(8,128)(2,1)S(1)} %get-tuple-element.14), channel_id=3, replica_groups={{32,64},{96,0},{33,65},{97,1},{34,66},{98,2},{35,67},{99,3},{36,68},{10..., dimensions={0}, use_global_device_ids=true | all-gather | bytes 768000 | tf_op jit(solution)/shard_map/all_gather | solution.py:77
  319.1 0.9 pad_maximum_fusion.1
  320.1 0.1 broadcast_in_dim.11
  320.2 15.3 %all_to_all.43 = bf16[4,80,2560]{2,1,0:T(8,128)(2,1)S(1)} all-to-all(bf16[4,80,2560]{2,1,0:T(8,128)(2,1)S(1)} %broadcast_in_dim.11), channel_id=1, replica_groups=mesh['x'=4,'zh'=4,'zl'=4,'y'=4,'c'=2] {'y'}, dimensions={0} | all-to-all | bytes 3276800 | tf_op jit(solution)/shard_map/all_to_all | solution.py:43
  335.6 18.9 %collective-permute-start.7 = (bf16[320,2560]{1,0:T(8,128)(2,1)S(1)}, bf16[320,2560]{1,0:T(8,128)(2,1)}, u32[]{:S(2)}, u32[]{:S(2)}) collective-permute-start(bf16[320,2560]{1,0:T(8,128)(2,1)S(1)} %bitcast.99), channel_id=1, source_target_pairs={{1,0},{0,1},{3,2},{2,3},{5,4},{4,5},{7,6},{6,7},{9,8},{8,9},{11,10... | collective-permute-start | bytes 4915208 | tf_op jit(solution)/shard_map/ppermute | solution.py:21
  354.5 2.8 dynamic-slice_bitcast_fusion.2
  357.3 17.0 %all-gather.11.cloned.1.call-done = bf16[1280,800]{1,0:T(8,128)(2,1)} async-done(((bf16[320,800]{1,0:T(8,128)(2,1)}), bf16[1280,800]{1,0:T(8,128)(2,1)}) %all-gather.11.cloned.1.call-update) | async-done | bytes 2048016 | tf_op jit(solution)/shard_map/all_gather | solution.py:79
  374.3 1.9 dynamic-slice_bitcast_fusion.3
  376.3 0.3 copy-done.11
  376.6 0.3 copy-done.12
  376.9 3.5 fusion.8
  380.5 3.0 fusion.22
  (50 shorter events, 0.9 us)
Async XLA Ops:
  6.5 113.4 %copy-start.4 = (bf16[320,800]{1,0:T(8,128)(2,1)S(1)}, bf16[320,800]{1,0:T(8,128)(2,1)}, u32[]{:S(2)}) copy-start(bf16[320,800]{1,0:T(8,128)(2,1)} %param.1) | copy-start | bytes 1536004
  6.5 115.0 %all-gather.7.cloned.1.call-start = ((), (), s32[]{:S(2)}) async-start(), calls=%async_computation.8 | async-start | bytes 2867200 | tf_op jit(solution)/shard_map/all_gather | solution.py:69
  7.3 122.2 %all-gather.9.cloned.1.call-start = ((), (), s32[]{:S(2)}) async-start(), calls=%async_computation.9 | async-start | bytes 2867200 | tf_op jit(solution)/shard_map/all_gather | solution.py:70
  7.3 60.0 %collective-permute-start = (bf16[320,800]{1,0:T(8,128)(2,1)}, bf16[320,800]{1,0:T(8,128)(2,1)S(1)}, u32[]{:S(2)}, u32[]{:S(2)}) collective-permute-start(bf16[320,800]{1,0:T(8,128)(2,1)} %param.1), channel_id=1, source_target_pairs={{32,0},{64,32},{96,64},{0,96},{33,1},{65,33},{97,65},{1,97},{34,2}... | collective-permute-start | bytes 1536008 | tf_op jit(solution)/shard_map/ppermute | solution.py:21
  67.3 0.8 copy-start.2
  68.1 51.8 %collective-permute-start.1 = (bf16[320,800]{1,0:T(8,128)(2,1)}, bf16[320,800]{1,0:T(8,128)(2,1)S(1)}, u32[]{:S(2)}, u32[]{:S(2)}) collective-permute-start(bf16[320,800]{1,0:T(8,128)(2,1)} %param.1), channel_id=1, source_target_pairs={{96,0},{0,32},{32,64},{64,96},{97,1},{1,33},{33,65},{65,97},{98,2}... | collective-permute-start | bytes 1536008 | tf_op jit(solution)/shard_map/ppermute | solution.py:21
  120.0 15.7 %copy-start = (bf16[320,800]{1,0:T(8,128)(2,1)}, bf16[320,800]{1,0:T(8,128)(2,1)S(1)}, u32[]{:S(2)}) copy-start(bf16[320,800]{1,0:T(8,128)(2,1)S(1)} %collective-permute-done.1) | copy-start | bytes 1536004
  124.3 2.7 copy-start.6
  127.0 14.3 %collective-permute-start.2 = (bf16[960,640]{1,0:T(8,128)(2,1)}, bf16[960,640]{1,0:T(8,128)(2,1)}, u32[]{:S(2)}, u32[]{:S(2)}) collective-permute-start(bf16[960,640]{1,0:T(8,128)(2,1)} %convolution_convert_fusion), channel_id=1, source_target_pairs={{1,0},{0,1},{3,2},{2,3},{5,4},{4,5},{7,6},{6,7},{9,8},{8,9},{11,10... | collective-permute-start | bytes 3686408 | tf_op jit(solution)/shard_map/ppermute | solution.py:21
  131.3 5.9 %copy-start.8 = (bf16[640,800]{1,0:T(8,128)(2,1)}, bf16[640,800]{1,0:T(8,128)(2,1)S(1)}, u32[]{:S(2)}) copy-start(bf16[640,800]{1,0:T(8,128)(2,1)S(1)} %get-tuple-element.12) | copy-start | bytes 3072004
  131.3 5.9 %copy-start.10 = (bf16[640,800]{1,0:T(8,128)(2,1)}, bf16[640,800]{1,0:T(8,128)(2,1)S(1)}, u32[]{:S(2)}) copy-start(bf16[640,800]{1,0:T(8,128)(2,1)S(1)} %get-tuple-element.11) | copy-start | bytes 3072004
  132.0 3.6 collective-permute-start.3
  137.1 12.1 %all-to-all-start.1 = ((bf16[4,80,640]{2,1,0:T(8,128)(2,1)}), bf16[4,80,640]{2,1,0:T(8,128)(2,1)S(1)}, u32[]{:S(2)}, u32[]{:S(2)}) async-start(bf16[4,80,640]{2,1,0:T(8,128)(2,1)} %bitcast.18), calls=%async_computation.1 | async-start | bytes 819200 | tf_op jit(solution)/shard_map/all_to_all | solution.py:47
  149.3 19.3 %all-to-all-start = ((bf16[4,240,640]{2,1,0:T(8,128)(2,1)}), bf16[4,240,640]{2,1,0:T(8,128)(2,1)S(1)}, u32[]{:S(2)}, u32[]{:S(2)}) async-start(bf16[4,240,640]{2,1,0:T(8,128)(2,1)} %bitcast.103), calls=%async_computation | async-start | bytes 2457600 | tf_op jit(solution)/shard_map/all_to_all | solution.py:47
  152.8 201.7 %all-gather.13.cloned.1.call-start = ((), (), s32[]{:S(2)}) async-start(), calls=%async_computation.11 | async-start | bytes 2867200 | tf_op jit(solution)/shard_map/all_gather | solution.py:71
  187.9 0.7 collective-permute-start.5
  235.9 8.0 %collective-permute-start.6 = (bf16[320,640]{1,0:T(8,128)(2,1)S(1)}, bf16[320,640]{1,0:T(8,128)(2,1)S(1)}, u32[]{:S(2)}, u32[]{:S(2)}) collective-permute-start(bf16[320,640]{1,0:T(8,128)(2,1)S(1)} %convolution_convert_fusion.2), channel_id=1, source_target_pairs={{1,0},{0,1},{3,2},{2,3},{5,4},{4,5},{7,6},{6,7},{9,8},{8,9},{11,10... | collective-permute-start | bytes 1228808 | tf_op jit(solution)/shard_map/ppermute | solution.py:21
  245.1 26.9 %all-to-all-start.5 = ((bf16[4,80,640]{2,1,0:T(8,128)(2,1)}), bf16[4,80,640]{2,1,0:T(8,128)(2,1)S(1)}, u32[]{:S(2)}, u32[]{:S(2)}) async-start(bf16[4,80,640]{2,1,0:T(8,128)(2,1)} %bitcast.27), calls=%async_computation.5 | async-start | bytes 819200 | tf_op jit(solution)/shard_map/all_to_all | solution.py:47
  248.6 31.8 %copy-start.1 = (bf16[320,800]{1,0:T(8,128)(2,1)S(1)}, bf16[320,800]{1,0:T(8,128)(2,1)}, u32[]{:S(2)}) copy-start(bf16[320,800]{1,0:T(8,128)(2,1)} %copy-done) | copy-start | bytes 1536004
  248.6 31.8 %copy-start.3 = (bf16[320,800]{1,0:T(8,128)(2,1)S(1)}, bf16[320,800]{1,0:T(8,128)(2,1)}, u32[]{:S(2)}) copy-start(bf16[320,800]{1,0:T(8,128)(2,1)} %copy-done.2) | copy-start | bytes 1536004
  248.6 23.5 %collective-permute-start.4 = (bf16[80,640]{1,0:T(8,128)(2,1)S(1)}, bf16[80,640]{1,0:T(8,128)(2,1)S(1)}, u32[]{:S(2)}, u32[]{:S(2)}) collective-permute-start(bf16[80,640]{1,0:T(8,128)(2,1)S(1)} %reduce_sum.47), channel_id=1, source_target_pairs={{0,0},{32,8},{56,16},{96,24},{8,32},{40,40},{72,48},{64,56},{104,6... | collective-permute-start | bytes 307208 | tf_op jit(solution)/shard_map/ppermute | solution.py:32
  273.0 47.0 %all-to-all-start.6 = ((bf16[4,80,640]{2,1,0:T(8,128)(2,1)}), bf16[4,80,640]{2,1,0:T(8,128)(2,1)S(1)}, u32[]{:S(2)}, u32[]{:S(2)}) async-start(bf16[4,80,640]{2,1,0:T(8,128)(2,1)} %broadcast_in_dim.10), calls=%async_computation.6 | async-start | bytes 819200 | tf_op jit(solution)/shard_map/all_to_all | solution.py:43
  280.4 93.9 %all-gather.11.cloned.1.call-start = ((), (), s32[]{:S(2)}) async-start(), calls=%async_computation.10 | async-start | bytes 2867200 | tf_op jit(solution)/shard_map/all_gather | solution.py:79
  335.6 40.7 %collective-permute-start.7 = (bf16[320,2560]{1,0:T(8,128)(2,1)S(1)}, bf16[320,2560]{1,0:T(8,128)(2,1)}, u32[]{:S(2)}, u32[]{:S(2)}) collective-permute-start(bf16[320,2560]{1,0:T(8,128)(2,1)S(1)} %bitcast.99), channel_id=1, source_target_pairs={{1,0},{0,1},{3,2},{2,3},{5,4},{4,5},{7,6},{6,7},{9,8},{8,9},{11,10... | collective-permute-start | bytes 4915208 | tf_op jit(solution)/shard_map/ppermute | solution.py:21
  374.3 2.0 copy-start.7
  374.3 2.3 copy-start.11
  374.3 2.6 copy-start.12
  376.9 3.5 copy-start.5
  376.9 3.5 copy-start.9
Sparse Core Ops, SparseCore 0:
  9.5 45.4 all-gather.6
  68.3 43.1 all-gather.8
  242.6 29.5 all-gather.12
  320.1 54.1 all-gather.10

commit v4 on v3

--- a/solution.py
+++ b/solution.py
@@ -43,6 +43,10 @@
     return lax.all_to_all(spread, axis, split_axis=0, concat_axis=0, tiled=True)
 
 
+def around(value, axis):
+    return [value] + [take(value, axis, distance) for distance in (1, 2, 3)]
+
+
 def exchanged_sum(value, axis):
     received = lax.all_to_all(value, axis, split_axis=0, concat_axis=0, tiled=True)
     return received.astype(F32).sum(0)
@@ -57,7 +61,7 @@
 
 def local(iterate):
     rows, width = iterate.shape
-    h, c = lax.axis_index("zh"), lax.axis_index("c")
+    h, l, c = lax.axis_index("zh"), lax.axis_index("zl"), lax.axis_index("c")
     slab = rows // 4
     pair = 2 * rows
 
@@ -65,39 +69,37 @@
         halves = block.reshape(2, pair, -1)
         return halves[c], halves[1 - c]
 
+    def tiles(block, others):
+        part = jnp.einsum(
+            "rn,csn->crs", block, others.reshape(2, pair, width), preferred_element_type=F32
+        )
+        part = part.astype(BF16).reshape(8, -1, pair)
+        return exchanged_sum(part, ("c", "y")).astype(BF16).reshape(-1, slab, pair)
+
     upper, lower = take(iterate, "zh", 1), take(iterate, "zh", -1)
+    upper, lower = lax.optimization_barrier((upper, lower))
     mine = lax.all_gather(iterate, "x", axis=0, tiled=True)
     above = lax.all_gather(upper, "x", axis=0, tiled=True)
     below = lax.all_gather(lower, "x", axis=0, tiled=True)
     cut = rows // 2
-    odd = h % 2 == 1
-    one = jnp.where(odd, upper, lower)[:cut]
-    two = jnp.where(odd, lower, upper)[cut:]
-    one = lax.all_gather(one, "zh", axis_index_groups=[[0, 1], [2, 3]])
-    two = lax.all_gather(two, "zh", axis_index_groups=[[1, 2], [3, 0]])
-    opposite = jnp.concatenate([one[1 - h % 2], two[h % 2]], axis=0)
-    opposite = lax.all_gather(opposite, "x", axis=0, tiled=True)
+    opposite = [take(upper[:cut], "zh", 1), take(lower[cut:], "zh", -1)]
+    opposite = lax.all_gather(jnp.concatenate(opposite, axis=0), "x", axis=0, tiled=True)
 
     stacked = jnp.stack([iterate, upper, lower]).reshape(3, 4, slab, width)
-    stacked = stacked.transpose(1, 0, 2, 3).reshape(3 * rows, width)
-    tiles = matmul_over_c(stacked, *columns(mine))
-    tiles = exchanged_sum(tiles.reshape(4, 3 * slab, pair), "y").astype(BF16)
-    tiles = tiles.reshape(3, slab, pair)
-    across = matmul_over_c(lower, *columns(above))
-    across = exchanged_sum(across.reshape(4, slab, pair), "y").astype(BF16)
-    by_l = jnp.stack(rolled([tiles[0], tiles[1], across, tiles[2]], (4 - h) % 4))
+    near = tiles(stacked.transpose(1, 0, 2, 3).reshape(3 * rows, width), mine)
+    across = tiles(lower, above)[0]
+    by_l = jnp.stack(rolled([near[0], near[1], across, near[2]], (4 - h) % 4))
     gram = exchanged_sum(by_l, "zl").astype(BF16)
 
     turned = fetch(gram, lambda p, q: (p, q))
     gram = fetch(gram, lambda p, q: (q, p))
-    left = gathered(gram, "zl").reshape(rows, pair)
+    left = jnp.concatenate(rolled(around(gram, "zl"), (4 - l) % 4), axis=0)
     right = gathered(gram, ("x", "y")).reshape(2 * pair, pair)
     square = matmul_over_c(left, *columns(right))
     square = exchanged_sum(square.reshape(4, slab, pair), "zh")
     polynomial = (QUINTIC_B * turned.astype(F32) + QUINTIC_C * square).astype(BF16)
 
-    polynomial = gathered(polynomial, "zl")
-    polynomial = jnp.concatenate(rolled([polynomial[i] for i in range(4)], h), axis=1)
+    polynomial = jnp.concatenate(rolled(around(polynomial, "zl"), (h - l) % 4), axis=1)
     polynomial = gathered(polynomial, "y").reshape(rows, 4 * pair)
     swapped = take(polynomial, "c", 1)
 

time: 391 us -> 404 us (1.033)
  blocking collectives: 119 us -> 38.7 us
  waiting for transfers between devices: 153 us -> 196 us
  starting transfers between devices: 71.8 us -> 107 us
  local copies, waits for them, and re-layouts: 12 us -> 22.3 us
  matrix products: 17.5 us -> 22 us
    all_gather x1, waiting for transfers between devices: 0.02 us -> 43.2 us  [local(): above = lax.all_gather(upper, 'x', axis=0, tiled=True)]
    all_to_all x3 -> x1, blocking collectives: 61.9 us -> 22.8 us  [gathered(): return lax.all_to_all(spread, axis, split_axis=0, concat_axis=0, tiled=True)]
    all_gather x2 -> x0, blocking collectives: 38.6 us -> none  [the longest x1 27.1 us: local(): two = lax.all_gather(two, 'zh', axis_index_groups=[[1, 2], [3, 0]])]
    all_gather x1, waiting for transfers between devices: 0.02 us -> 32.2 us  [local(): mine = lax.all_gather(iterate, 'x', axis=0, tiled=True)]
    ppermute x6 -> x12, starting transfers between devices: 51.7 us -> 76.1 us  [take(): lax.ppermute(value, axis, [((i + distance) % n, i) for i in range(n)])]
    all_gather x1, waiting for transfers between devices: 17 us -> 0.01 us  [local(): lax.all_gather(jnp.concatenate(opposite, axis=0), 'x', axis=0, tiled=True)]
    all_to_all x3, starting transfers between devices: 11.2 us -> 25.8 us  [exchanged_sum(): lax.all_to_all(value, axis, split_axis=0, concat_axis=0, tiled=True)]
    unnamed x26 -> x36, local copies, waits for them, and re-layouts: 1.55 us -> 15.1 us
  transfers between devices with their start and end apart: 16 -> 22, of which waited for: 8 -> 8; matrix products, arithmetic and copies ran while one was open for 6% -> 10% of each run, Pallas kernels for 0% -> 0%
where the time goes in v4:
time: 404 us; the launch traced here: 403 us
  waiting for transfers between devices  196 us (49%)
  starting transfers between devices  107 us (26%)
  blocking collectives  38.7 us (10%)
  local copies, waits for them, and re-layouts  22.3 us (6%)
  matrix products  22 us (5%)
  between operations  13.6 us (3%)
    ppermute x12, waiting for transfers between devices, take(): lax.ppermute(value, axis, [((i + distance) % n, i) for i in range(n)])  89.3 us
    ppermute x12, starting transfers between devices, take(): lax.ppermute(value, axis, [((i + distance) % n, i) for i in range(n)])  76.1 us
    all_gather x1, waiting for transfers between devices, local(): above = lax.all_gather(upper, 'x', axis=0, tiled=True)  43.2 us
    all_gather x1, waiting for transfers between devices, local(): mine = lax.all_gather(iterate, 'x', axis=0, tiled=True)  32.2 us
    all_to_all x3, waiting for transfers between devices, exchanged_sum(): lax.all_to_all(value, axis, split_axis=0, concat_axis=0, tiled=True)  30 us
    all_to_all x3, starting transfers between devices, exchanged_sum(): lax.all_to_all(value, axis, split_axis=0, concat_axis=0, tiled=True)  25.8 us
    all_to_all x1, blocking collectives, gathered(): return lax.all_to_all(spread, axis, split_axis=0, concat_axis=0, tiled=True)  22.8 us
    all_to_all x1, blocking collectives, exchanged_sum(): lax.all_to_all(value, axis, split_axis=0, concat_axis=0, tiled=True)  15.9 us
  transfers between devices with their start and end apart: 22, of which 8 were waited for; matrix products, arithmetic and copies ran while one was open for 10% of the time, Pallas kernels for 0%

profile of v4, /device:TPU:1, one launch (start us, length us, event | category | flops | bytes accessed | tf_op | source)
XLA Modules:
  0.0 403.0 jit_solution(13495029932135527498)
XLA Ops:
  6.5 13.3 %collective-permute-start = (bf16[320,800]{1,0:T(8,128)(2,1)}, bf16[320,800]{1,0:T(8,128)(2,1)S(1)}, u32[]{:S(2)}, u32[]{:S(2)}) collective-permute-start(bf16[320,800]{1,0:T(8,128)(2,1)} %param.1), channel_id=1, source_target_pairs={{32,0},{64,32},{96,64},{0,96},{33,1},{65,33},{97,65},{1,97},{34,2}... | collective-permute-start | bytes 1536008 | tf_op jit(solution)/shard_map/ppermute | solution.py:21
  19.8 1.9 collective-permute-start.1
  21.8 44.7 %collective-permute-done = bf16[320,800]{1,0:T(8,128)(2,1)S(1)} collective-permute-done((bf16[320,800]{1,0:T(8,128)(2,1)}, bf16[320,800]{1,0:T(8,128)(2,1)S(1)}, u32[]{:S(2)}, u32[]{:S(2)}) %collective-permute-start) | collective-permute-done | bytes 512032 | tf_op jit(solution)/shard_map/ppermute | solution.py:21
  66.5 0.8 copy-done.2
  67.4 0.7 all-gather.5.cloned.1.call-update
  68.1 43.2 %all-gather.7.cloned.1.call-done = bf16[1280,800]{1,0:T(8,128)(2,1)} async-done(((bf16[320,800]{1,0:T(8,128)(2,1)}), bf16[1280,800]{1,0:T(8,128)(2,1)}) %all-gather.7.cloned.1.call-update) | async-done | bytes 2048016 | tf_op jit(solution)/shard_map/all_gather | solution.py:82
  111.3 3.6 convolution_convert_fusion.1
  114.9 5.1 %all-to-all-start.1 = ((bf16[8,80,640]{2,1,0:T(8,128)(2,1)}), bf16[8,80,640]{2,1,0:T(8,128)(2,1)S(1)}, u32[]{:S(2)}, u32[]{:S(2)}) async-start(bf16[8,80,640]{2,1,0:T(8,128)(2,1)} %bitcast.15), calls=%async_computation.1 | async-start | bytes 1638400 | tf_op jit(solution)/shard_map/all_to_all | solution.py:51
  120.0 1.5 pad_maximum_fusion
  121.5 32.2 %all-gather.5.cloned.1.call-done = bf16[1280,800]{1,0:T(8,128)(2,1)} async-done(((bf16[320,800]{1,0:T(8,128)(2,1)}), bf16[1280,800]{1,0:T(8,128)(2,1)}) %all-gather.5.cloned.1.call-update) | async-done | bytes 2048016 | tf_op jit(solution)/shard_map/all_gather | solution.py:81
  153.7 6.4 %convolution_convert_fusion = bf16[960,2,640]{2,0,1:T(8,128)(2,1)} fusion(bf16[960,800,1]{1,0,2:T(8,128)(2,1)} %bitcast.71, bf16[2,640,800]{2,1,0:T(8,128)(2,1)} %bitcast.66), kind=kOutput, calls=%fused_computation.16 | convolution fusion | flops 1967308800 | bytes 6041600 | tf_op jit(solution)/shard_map/rn,csn->crs/dot_general | solution.py:73
  160.1 5.0 %all-to-all-start = ((bf16[8,240,640]{2,1,0:T(8,128)(2,1)}), bf16[8,240,640]{2,1,0:T(8,128)(2,1)S(1)}, u32[]{:S(2)}, u32[]{:S(2)}) async-start(bf16[8,240,640]{2,1,0:T(8,128)(2,1)} %bitcast.63), calls=%async_computation | async-start | bytes 4915200 | tf_op jit(solution)/shard_map/all_to_all | solution.py:51
  165.1 30.0 %all-to-all-done = bf16[8,240,640]{2,1,0:T(8,128)(2,1)S(1)} async-done(((bf16[8,240,640]{2,1,0:T(8,128)(2,1)}), bf16[8,240,640]{2,1,0:T(8,128)(2,1)S(1)}, u32[]{:S(2)}, u32[]{:S(2)}) %all-to-all-start) | async-done | bytes 2457632 | tf_op jit(solution)/shard_map/all_to_all | solution.py:51
  195.7 15.9 %all_to_all.30 = bf16[4,80,640]{2,1,0:T(8,128)(2,1)S(1)} all-to-all(bf16[4,80,640]{2,1,0:T(8,128)(2,1)S(1)} %pad_maximum_fusion.2), channel_id=1, replica_groups=mesh['x'=4,'zh'=4,'zl'=4,'y'=4,'c'=2] {'zl'}, dimensions={0} | all-to-all | bytes 819200 | tf_op jit(solution)/shard_map/all_to_all | solution.py:51
  212.4 1.4 broadcast_in_dim.4
  213.8 3.7 all-to-all-start.3
  217.5 0.7 all-gather.11.cloned.1.call-update
  218.2 1.9 collective-permute-start.6
  220.2 12.2 %collective-permute-start.5 = (bf16[80,640]{1,0:T(8,128)(2,1)S(1)}, bf16[80,640]{1,0:T(8,128)(2,1)S(1)}, u32[]{:S(2)}, u32[]{:S(2)}) collective-permute-start(bf16[80,640]{1,0:T(8,128)(2,1)S(1)} %collective-permute-done.3), channel_id=1, source_target_pairs={{16,0},{24,8},{0,16},{8,24},{17,1},{25,9},{1,17},{9,25},{18,2},{26... | collective-permute-start | bytes 307208 | tf_op jit(solution)/shard_map/ppermute | solution.py:21
  232.4 4.3 %collective-permute-start.4 = (bf16[80,640]{1,0:T(8,128)(2,1)S(1)}, bf16[80,640]{1,0:T(8,128)(2,1)S(1)}, u32[]{:S(2)}, u32[]{:S(2)}) collective-permute-start(bf16[80,640]{1,0:T(8,128)(2,1)S(1)} %collective-permute-done.3), channel_id=1, source_target_pairs={{8,0},{16,8},{24,16},{0,24},{9,1},{17,9},{25,17},{1,25},{10,2},{18... | collective-permute-start | bytes 307208 | tf_op jit(solution)/shard_map/ppermute | solution.py:21
  236.7 2.3 collective-permute-done.4
  239.1 1.3 convolution_convert_fusion.2
  240.4 5.7 %collective-permute-start.7 = (bf16[320,640]{1,0:T(8,128)(2,1)}, bf16[320,640]{1,0:T(8,128)(2,1)}, u32[]{:S(2)}, u32[]{:S(2)}) collective-permute-start(bf16[320,640]{1,0:T(8,128)(2,1)} %convolution_convert_fusion.2), channel_id=1, source_target_pairs={{1,0},{0,1},{3,2},{2,3},{5,4},{4,5},{7,6},{6,7},{9,8},{8,9},{11,10... | collective-permute-start | bytes 1228808 | tf_op jit(solution)/shard_map/ppermute | solution.py:21
  246.1 1.7 collective-permute-done.7
  247.8 2.3 fusion.25
  250.2 15.7 %all-to-all-start.4 = ((bf16[4,80,640]{2,1,0:T(8,128)(2,1)}), bf16[4,80,640]{2,1,0:T(8,128)(2,1)S(1)}, u32[]{:S(2)}, u32[]{:S(2)}) async-start(bf16[4,80,640]{2,1,0:T(8,128)(2,1)} %bitcast.23), calls=%async_computation.4 | async-start | bytes 819200 | tf_op jit(solution)/shard_map/all_to_all | solution.py:51
  265.9 7.3 %collective-permute-start.12 = (bf16[160,800]{1,0:T(8,128)(2,1)S(1)}, bf16[160,800]{1,0:T(8,128)(2,1)S(1)}, u32[]{:S(2)}, u32[]{:S(2)}) collective-permute-start(bf16[160,800]{1,0:T(8,128)(2,1)S(1)} %slice.22), channel_id=1, source_target_pairs={{96,0},{0,32},{32,64},{64,96},{97,1},{1,33},{33,65},{65,97},{98,2}... | collective-permute-start | bytes 768008 | tf_op jit(solution)/shard_map/ppermute | solution.py:21
  273.2 1.9 collective-permute-start.11
  275.2 38.9 %collective-permute-done.12 = bf16[160,800]{1,0:T(8,128)(2,1)S(1)} collective-permute-done((bf16[160,800]{1,0:T(8,128)(2,1)S(1)}, bf16[160,800]{1,0:T(8,128)(2,1)S(1)}, u32[]{:S(2)}, u32[]{:S(2)}) %collective-permute-start.12) | collective-permute-done | bytes 256032 | tf_op jit(solution)/shard_map/ppermute | solution.py:21
  314.1 0.9 pad_maximum_fusion.1
  315.8 5.4 %collective-permute-start.10 = (bf16[80,640]{1,0:T(8,128)(2,1)S(1)}, bf16[80,640]{1,0:T(8,128)(2,1)S(1)}, u32[]{:S(2)}, u32[]{:S(2)}) collective-permute-start(bf16[80,640]{1,0:T(8,128)(2,1)S(1)} %add_convert_fusion), channel_id=1, source_target_pairs={{24,0},{0,8},{8,16},{16,24},{25,1},{1,9},{9,17},{17,25},{26,2},{2,... | collective-permute-start | bytes 307208 | tf_op jit(solution)/shard_map/ppermute | solution.py:21
  321.2 12.9 %collective-permute-start.9 = (bf16[80,640]{1,0:T(8,128)(2,1)S(1)}, bf16[80,640]{1,0:T(8,128)(2,1)S(1)}, u32[]{:S(2)}, u32[]{:S(2)}) collective-permute-start(bf16[80,640]{1,0:T(8,128)(2,1)S(1)} %add_convert_fusion), channel_id=1, source_target_pairs={{16,0},{24,8},{0,16},{8,24},{17,1},{25,9},{1,17},{9,25},{18,2},{26... | collective-permute-start | bytes 307208 | tf_op jit(solution)/shard_map/ppermute | solution.py:21
  334.1 4.3 %collective-permute-start.8 = (bf16[80,640]{1,0:T(8,128)(2,1)S(1)}, bf16[80,640]{1,0:T(8,128)(2,1)S(1)}, u32[]{:S(2)}, u32[]{:S(2)}) collective-permute-start(bf16[80,640]{1,0:T(8,128)(2,1)S(1)} %add_convert_fusion), channel_id=1, source_target_pairs={{8,0},{16,8},{24,16},{0,24},{9,1},{17,9},{25,17},{1,25},{10,2},{18... | collective-permute-start | bytes 307208 | tf_op jit(solution)/shard_map/ppermute | solution.py:21
  338.4 1.6 collective-permute-done.8
  340.3 22.8 %all_to_all.31 = bf16[4,80,2560]{2,1,0:T(8,128)(2,1)} all-to-all(bf16[4,80,2560]{2,1,0:T(8,128)(2,1)S(1)} %broadcast_in_dim.5), channel_id=1, replica_groups=mesh['x'=4,'zh'=4,'zl'=4,'y'=4,'c'=2] {'y'}, dimensions={0} | all-to-all | bytes 3276800 | tf_op jit(solution)/shard_map/all_to_all | solution.py:43
  363.1 5.0 %collective-permute-start.13 = (bf16[320,2560]{1,0:T(8,128)(2,1)}, bf16[320,2560]{1,0:T(8,128)(2,1)}, u32[]{:S(2)}, u32[]{:S(2)}) collective-permute-start(bf16[320,2560]{1,0:T(8,128)(2,1)} %bitcast.24), channel_id=1, source_target_pairs={{1,0},{0,1},{3,2},{2,3},{5,4},{4,5},{7,6},{6,7},{9,8},{8,9},{11,10... | collective-permute-start | bytes 4915208 | tf_op jit(solution)/shard_map/ppermute | solution.py:21
  368.3 1.7 copy.53
  370.0 1.7 copy.51
  371.7 1.8 constant_dynamic-slice_fusion.2
  373.5 1.7 copy.54
  375.2 1.7 copy.52
  376.9 3.7 constant_dynamic-slice_fusion
  380.5 2.4 copy.62
  382.9 1.7 copy.60
  384.6 1.7 copy.59
  386.3 1.7 copy.61
  388.0 4.0 %fusion = f32[320,800]{1,0:T(8,128)S(1)} fusion(bf16[320,2560]{1,0:T(8,128)(2,1)} %bitcast.24, bf16[640,800]{0,1:T(8,128)(2,1)} %bitcast.80, bf16[640,800]{0,1:T(8,128)(2,1)} %bitcast.81, bf16[640,800]{0,1:T(8,128)(2,1)S(1)} %bitcast.77, bf16[640,800]{0,1:T(8,128)(2,1)S(1)} %bitcast.76), kind=kOutput, calls=%fused_computation | convolution fusion | flops 1327104000 | bytes 6758400 | tf_op jit(solution)/shard_map/mk,kn->mn/dot_general | solution.py:109
  392.1 4.4 %fusion.22 = f32[320,800]{1,0:T(8,128)} fusion(f32[320,800]{1,0:T(8,128)S(1)} %fusion, bf16[320,2560]{1,0:T(8,128)(2,1)} %collective-permute-done.13, bf16[640,800]{0,1:T(8,128)(2,1)S(1)} %bitcast.78, bf16[640,800]{0,1:T(8,128)(2,1)S(1)} %bitcast.79, bf16[640,800]{0,1:T(8,128)(2,1)S(1)} %bitcast.75, bf16[640,800]{0,1:T(8,128)(2,1)S(1)} %bitcast.74, ...), kind=kOutput, calls=%fused_computation.22 | convolution fusion | flops 1328384000 | bytes 8294400 | tf_op jit(solution)/shard_map/mk,kn->mn/dot_general | solution.py:110
  (63 shorter events, 2.9 us)
Async XLA Ops:
  6.5 104.7 %all-gather.7.cloned.1.call-start = ((), (), s32[]{:S(2)}) async-start(), calls=%async_computation.7 | async-start | bytes 2867200 | tf_op jit(solution)/shard_map/all_gather | solution.py:82
  6.5 60.0 %collective-permute-start = (bf16[320,800]{1,0:T(8,128)(2,1)}, bf16[320,800]{1,0:T(8,128)(2,1)S(1)}, u32[]{:S(2)}, u32[]{:S(2)}) collective-permute-start(bf16[320,800]{1,0:T(8,128)(2,1)} %param.1), channel_id=1, source_target_pairs={{32,0},{64,32},{96,64},{0,96},{33,1},{65,33},{97,65},{1,97},{34,2}... | collective-permute-start | bytes 1536008 | tf_op jit(solution)/shard_map/ppermute | solution.py:21
  19.8 46.7 %collective-permute-start.1 = (bf16[320,800]{1,0:T(8,128)(2,1)}, bf16[320,800]{1,0:T(8,128)(2,1)S(1)}, u32[]{:S(2)}, u32[]{:S(2)}) collective-permute-start(bf16[320,800]{1,0:T(8,128)(2,1)} %param.1), channel_id=1, source_target_pairs={{96,0},{0,32},{32,64},{64,96},{97,1},{1,33},{33,65},{65,97},{98,2}... | collective-permute-start | bytes 1536008 | tf_op jit(solution)/shard_map/ppermute | solution.py:21
  66.5 0.8 copy-start.2
  66.5 53.5 %copy-start = (bf16[320,800]{1,0:T(8,128)(2,1)}, bf16[320,800]{1,0:T(8,128)(2,1)S(1)}, u32[]{:S(2)}) copy-start(bf16[320,800]{1,0:T(8,128)(2,1)S(1)} %collective-permute-done.1) | copy-start | bytes 1536004
  67.4 86.3 %all-gather.5.cloned.1.call-start = ((), (), s32[]{:S(2)}) async-start(), calls=%async_computation.6 | async-start | bytes 2867200 | tf_op jit(solution)/shard_map/all_gather | solution.py:81
  114.9 5.1 %copy-start.3 = (bf16[320,800]{1,0:T(8,128)(2,1)S(1)}, bf16[320,800]{1,0:T(8,128)(2,1)}, u32[]{:S(2)}) copy-start(bf16[320,800]{1,0:T(8,128)(2,1)} %copy-done.2) | copy-start | bytes 1536004
  114.9 5.1 %copy-start.6 = (bf16[320,800]{1,0:T(8,128)(2,1)S(1)}, bf16[320,800]{1,0:T(8,128)(2,1)}, u32[]{:S(2)}) copy-start(bf16[320,800]{1,0:T(8,128)(2,1)} %param.1) | copy-start | bytes 1536004
  114.9 45.2 %all-to-all-start.1 = ((bf16[8,80,640]{2,1,0:T(8,128)(2,1)}), bf16[8,80,640]{2,1,0:T(8,128)(2,1)S(1)}, u32[]{:S(2)}, u32[]{:S(2)}) async-start(bf16[8,80,640]{2,1,0:T(8,128)(2,1)} %bitcast.15), calls=%async_computation.1 | async-start | bytes 1638400 | tf_op jit(solution)/shard_map/all_to_all | solution.py:51
  160.1 35.0 %all-to-all-start = ((bf16[8,240,640]{2,1,0:T(8,128)(2,1)}), bf16[8,240,640]{2,1,0:T(8,128)(2,1)S(1)}, u32[]{:S(2)}, u32[]{:S(2)}) async-start(bf16[8,240,640]{2,1,0:T(8,128)(2,1)} %bitcast.63), calls=%async_computation | async-start | bytes 4915200 | tf_op jit(solution)/shard_map/all_to_all | solution.py:51
  211.7 0.7 collective-permute-start.3
  213.8 25.3 %all-to-all-start.3 = ((bf16[16,80,640]{2,1,0:T(8,128)(2,1)}), bf16[16,80,640]{2,1,0:T(8,128)(2,1)S(1)}, u32[]{:S(2)}, u32[]{:S(2)}) async-start(bf16[16,80,640]{2,1,0:T(8,128)(2,1)} %broadcast_in_dim.4), calls=%async_computation.3 | async-start | bytes 3276800 | tf_op jit(solution)/shard_map/all_to_all | solution.py:43
  217.5 159.4 %all-gather.11.cloned.1.call-start = ((), (), s32[]{:S(2)}) async-start(), calls=%async_computation.9 | async-start | bytes 2867200 | tf_op jit(solution)/shard_map/all_gather | solution.py:83
  218.2 18.5 %collective-permute-start.6 = (bf16[80,640]{1,0:T(8,128)(2,1)S(1)}, bf16[80,640]{1,0:T(8,128)(2,1)S(1)}, u32[]{:S(2)}, u32[]{:S(2)}) collective-permute-start(bf16[80,640]{1,0:T(8,128)(2,1)S(1)} %collective-permute-done.3), channel_id=1, source_target_pairs={{24,0},{0,8},{8,16},{16,24},{25,1},{1,9},{9,17},{17,25},{26,2},{2,... | collective-permute-start | bytes 307208 | tf_op jit(solution)/shard_map/ppermute | solution.py:21
  220.2 16.5 %collective-permute-start.5 = (bf16[80,640]{1,0:T(8,128)(2,1)S(1)}, bf16[80,640]{1,0:T(8,128)(2,1)S(1)}, u32[]{:S(2)}, u32[]{:S(2)}) collective-permute-start(bf16[80,640]{1,0:T(8,128)(2,1)S(1)} %collective-permute-done.3), channel_id=1, source_target_pairs={{16,0},{24,8},{0,16},{8,24},{17,1},{25,9},{1,17},{9,25},{18,2},{26... | collective-permute-start | bytes 307208 | tf_op jit(solution)/shard_map/ppermute | solution.py:21
  232.4 6.6 %collective-permute-start.4 = (bf16[80,640]{1,0:T(8,128)(2,1)S(1)}, bf16[80,640]{1,0:T(8,128)(2,1)S(1)}, u32[]{:S(2)}, u32[]{:S(2)}) collective-permute-start(bf16[80,640]{1,0:T(8,128)(2,1)S(1)} %collective-permute-done.3), channel_id=1, source_target_pairs={{8,0},{16,8},{24,16},{0,24},{9,1},{17,9},{25,17},{1,25},{10,2},{18... | collective-permute-start | bytes 307208 | tf_op jit(solution)/shard_map/ppermute | solution.py:21
  240.4 7.4 %collective-permute-start.7 = (bf16[320,640]{1,0:T(8,128)(2,1)}, bf16[320,640]{1,0:T(8,128)(2,1)}, u32[]{:S(2)}, u32[]{:S(2)}) collective-permute-start(bf16[320,640]{1,0:T(8,128)(2,1)} %convolution_convert_fusion.2), channel_id=1, source_target_pairs={{1,0},{0,1},{3,2},{2,3},{5,4},{4,5},{7,6},{6,7},{9,8},{8,9},{11,10... | collective-permute-start | bytes 1228808 | tf_op jit(solution)/shard_map/ppermute | solution.py:21
  246.1 19.8 %copy-start.4 = (bf16[320,800]{1,0:T(8,128)(2,1)S(1)}, bf16[320,800]{1,0:T(8,128)(2,1)}, u32[]{:S(2)}) copy-start(bf16[320,800]{1,0:T(8,128)(2,1)} %copy-done.2) | copy-start | bytes 1536004
  246.1 19.8 %copy-start.1 = (bf16[320,800]{1,0:T(8,128)(2,1)S(1)}, bf16[320,800]{1,0:T(8,128)(2,1)}, u32[]{:S(2)}) copy-start(bf16[320,800]{1,0:T(8,128)(2,1)} %copy-done) | copy-start | bytes 1536004
  250.2 65.5 %all-to-all-start.4 = ((bf16[4,80,640]{2,1,0:T(8,128)(2,1)}), bf16[4,80,640]{2,1,0:T(8,128)(2,1)S(1)}, u32[]{:S(2)}, u32[]{:S(2)}) async-start(bf16[4,80,640]{2,1,0:T(8,128)(2,1)} %bitcast.23), calls=%async_computation.4 | async-start | bytes 819200 | tf_op jit(solution)/shard_map/all_to_all | solution.py:51
  265.9 111.0 %all-gather.9.cloned.1.call-start = ((), (), s32[]{:S(2)}) async-start(), calls=%async_computation.8 | async-start | bytes 2867200 | tf_op jit(solution)/shard_map/all_gather | solution.py:86
  265.9 48.1 %collective-permute-start.12 = (bf16[160,800]{1,0:T(8,128)(2,1)S(1)}, bf16[160,800]{1,0:T(8,128)(2,1)S(1)}, u32[]{:S(2)}, u32[]{:S(2)}) collective-permute-start(bf16[160,800]{1,0:T(8,128)(2,1)S(1)} %slice.22), channel_id=1, source_target_pairs={{96,0},{0,32},{32,64},{64,96},{97,1},{1,33},{33,65},{65,97},{98,2}... | collective-permute-start | bytes 768008 | tf_op jit(solution)/shard_map/ppermute | solution.py:21
  273.2 40.9 %collective-permute-start.11 = (bf16[160,800]{1,0:T(8,128)(2,1)S(1)}, bf16[160,800]{1,0:T(8,128)(2,1)S(1)}, u32[]{:S(2)}, u32[]{:S(2)}) collective-permute-start(bf16[160,800]{1,0:T(8,128)(2,1)S(1)} %slice.21), channel_id=1, source_target_pairs={{32,0},{64,32},{96,64},{0,96},{33,1},{65,33},{97,65},{1,97},{34,2}... | collective-permute-start | bytes 768008 | tf_op jit(solution)/shard_map/ppermute | solution.py:21
  315.0 0.7 collective-permute-start.2
  315.8 22.6 %collective-permute-start.10 = (bf16[80,640]{1,0:T(8,128)(2,1)S(1)}, bf16[80,640]{1,0:T(8,128)(2,1)S(1)}, u32[]{:S(2)}, u32[]{:S(2)}) collective-permute-start(bf16[80,640]{1,0:T(8,128)(2,1)S(1)} %add_convert_fusion), channel_id=1, source_target_pairs={{24,0},{0,8},{8,16},{16,24},{25,1},{1,9},{9,17},{17,25},{26,2},{2,... | collective-permute-start | bytes 307208 | tf_op jit(solution)/shard_map/ppermute | solution.py:21
  321.2 17.2 %collective-permute-start.9 = (bf16[80,640]{1,0:T(8,128)(2,1)S(1)}, bf16[80,640]{1,0:T(8,128)(2,1)S(1)}, u32[]{:S(2)}, u32[]{:S(2)}) collective-permute-start(bf16[80,640]{1,0:T(8,128)(2,1)S(1)} %add_convert_fusion), channel_id=1, source_target_pairs={{16,0},{24,8},{0,16},{8,24},{17,1},{25,9},{1,17},{9,25},{18,2},{26... | collective-permute-start | bytes 307208 | tf_op jit(solution)/shard_map/ppermute | solution.py:21
  334.1 5.9 %collective-permute-start.8 = (bf16[80,640]{1,0:T(8,128)(2,1)S(1)}, bf16[80,640]{1,0:T(8,128)(2,1)S(1)}, u32[]{:S(2)}, u32[]{:S(2)}) collective-permute-start(bf16[80,640]{1,0:T(8,128)(2,1)S(1)} %add_convert_fusion), channel_id=1, source_target_pairs={{8,0},{16,8},{24,16},{0,24},{9,1},{17,9},{25,17},{1,25},{10,2},{18... | collective-permute-start | bytes 307208 | tf_op jit(solution)/shard_map/ppermute | solution.py:21
  340.3 27.8 %copy-start.5 = (bf16[1280,800]{1,0:T(8,128)(2,1)S(1)}, bf16[1280,800]{1,0:T(8,128)(2,1)}, u32[]{:S(2)}) copy-start(bf16[1280,800]{1,0:T(8,128)(2,1)} %all-gather.5.cloned.1.call-done) | copy-start | bytes 6144004
  363.1 29.0 %collective-permute-start.13 = (bf16[320,2560]{1,0:T(8,128)(2,1)}, bf16[320,2560]{1,0:T(8,128)(2,1)}, u32[]{:S(2)}, u32[]{:S(2)}) collective-permute-start(bf16[320,2560]{1,0:T(8,128)(2,1)} %bitcast.24), channel_id=1, source_target_pairs={{1,0},{0,1},{3,2},{2,3},{5,4},{4,5},{7,6},{6,7},{9,8},{8,9},{11,10... | collective-permute-start | bytes 4915208 | tf_op jit(solution)/shard_map/ppermute | solution.py:21
  384.6 3.4 copy-start.10
  386.3 1.7 copy-start.11
  388.0 4.1 %copy-start.7 = (bf16[320,800]{1,0:T(8,128)(2,1)S(1)}, bf16[320,800]{1,0:T(8,128)(2,1)}, u32[]{:S(2)}) copy-start(bf16[320,800]{1,0:T(8,128)(2,1)} %param.1) | copy-start | bytes 1536004
  388.0 4.1 %copy-start.8 = (bf16[1,640,800]{1,2,0:T(8,128)(2,1)S(1)}, bf16[1,640,800]{1,2,0:T(8,128)(2,1)}, u32[]{:S(2)}) copy-start(bf16[1,640,800]{1,2,0:T(8,128)(2,1)} %copy.53) | copy-start | bytes 3072004
  388.0 4.1 %copy-start.9 = (bf16[1,640,800]{1,2,0:T(8,128)(2,1)S(1)}, bf16[1,640,800]{1,2,0:T(8,128)(2,1)}, u32[]{:S(2)}) copy-start(bf16[1,640,800]{1,2,0:T(8,128)(2,1)} %copy.54) | copy-start | bytes 3072004
  388.0 4.1 %copy-start.12 = (bf16[1,640,800]{1,2,0:T(8,128)(2,1)S(1)}, bf16[1,640,800]{1,2,0:T(8,128)(2,1)}, u32[]{:S(2)}) copy-start(bf16[1,640,800]{1,2,0:T(8,128)(2,1)} %copy.62) | copy-start | bytes 3072004
  388.0 4.1 %copy-start.13 = (bf16[1,640,800]{1,2,0:T(8,128)(2,1)S(1)}, bf16[1,640,800]{1,2,0:T(8,128)(2,1)}, u32[]{:S(2)}) copy-start(bf16[1,640,800]{1,2,0:T(8,128)(2,1)} %copy.61) | copy-start | bytes 3072004
Sparse Core Ops, SparseCore 0:
  67.5 43.7 all-gather.6
  113.4 40.2 all-gather.4
  220.4 49.1 all-gather.10
  315.1 30.3 all-gather.8

commit v5 on v4

--- a/solution.py
+++ b/solution.py
@@ -1,8 +1,11 @@
+import functools
 import math
 
 import jax
 import jax.numpy as jnp
 from jax import lax
+from jax.experimental import pallas as pl
+from jax.experimental.pallas import tpu as pltpu
 from jax.sharding import Mesh
 from jax.sharding import PartitionSpec as P
 
@@ -59,6 +62,48 @@
     return (kept + other.astype(F32)).astype(BF16)
 
 
+def product_kernel(other, scale, *refs):
+    total, left, *blocks, out, held, arrived = refs
+    pair = left.shape[1] // 4
+    c = lax.axis_index("c")
+    start = pl.multiple_of((1 - c if other else c) * pair, pair)
+    copies = [
+        pltpu.make_async_copy(block.at[pl.ds(start, pair), :], held.at[e], arrived.at[e])
+        for e, block in enumerate(blocks)
+    ]
+    for copy in copies:
+        copy.start()
+    value = total[...]
+    for e, copy in enumerate(copies):
+        copy.wait()
+        value += jnp.dot(
+            left[:, e * pair : (e + 1) * pair], held[e], preferred_element_type=F32
+        )
+    out[...] = scale * value
+
+
+def add_product(other, scale, total, left, blocks):
+    rows, width = total.shape
+    pair = left.shape[1] // 4
+    vmem = pl.BlockSpec(memory_space=pltpu.VMEM)
+    return pl.pallas_call(
+        functools.partial(product_kernel, other, scale),
+        out_shape=jax.ShapeDtypeStruct(total.shape, F32),
+        in_specs=[vmem, vmem] + [pl.BlockSpec(memory_space=pl.ANY)] * 4,
+        out_specs=vmem,
+        scratch_shapes=[
+            pltpu.VMEM((4, pair, width), BF16),
+            pltpu.SemaphoreType.DMA((4,)),
+        ],
+        cost_estimate=pl.CostEstimate(
+            flops=2 * left.size * width,
+            bytes_accessed=2 * left.size + 8 * pair * width + 8 * total.size,
+            transcendentals=0,
+        ),
+        compiler_params=pltpu.CompilerParams(vmem_limit_bytes=32 * 2**20),
+    )(total, left, *blocks)
+
+
 def local(iterate):
     rows, width = iterate.shape
     h, l, c = lax.axis_index("zh"), lax.axis_index("zl"), lax.axis_index("c")
@@ -69,25 +114,31 @@
         halves = block.reshape(2, pair, -1)
         return halves[c], halves[1 - c]
 
-    def tiles(block, others):
+    def partial_tiles(block, others):
         part = jnp.einsum(
             "rn,csn->crs", block, others.reshape(2, pair, width), preferred_element_type=F32
         )
-        part = part.astype(BF16).reshape(8, -1, pair)
+        return part.astype(BF16).reshape(8, -1, pair)
+
+    def summed_tiles(part):
         return exchanged_sum(part, ("c", "y")).astype(BF16).reshape(-1, slab, pair)
 
     upper, lower = take(iterate, "zh", 1), take(iterate, "zh", -1)
-    upper, lower = lax.optimization_barrier((upper, lower))
     mine = lax.all_gather(iterate, "x", axis=0, tiled=True)
+    upper, lower, mine = lax.optimization_barrier((upper, lower, mine))
     above = lax.all_gather(upper, "x", axis=0, tiled=True)
     below = lax.all_gather(lower, "x", axis=0, tiled=True)
     cut = rows // 2
     opposite = [take(upper[:cut], "zh", 1), take(lower[cut:], "zh", -1)]
+
+    stacked = jnp.stack([iterate, upper, lower]).reshape(3, 4, slab, width)
+    near = partial_tiles(stacked.transpose(1, 0, 2, 3).reshape(3 * rows, width), mine)
+    near = summed_tiles(near)
+    across = partial_tiles(lower, above)
+    across, opposite = lax.optimization_barrier((across, opposite))
+    across = summed_tiles(across)[0]
     opposite = lax.all_gather(jnp.concatenate(opposite, axis=0), "x", axis=0, tiled=True)
 
-    stacked = jnp.stack([iterate, upper, lower]).reshape(3, 4, slab, width)
-    near = tiles(stacked.transpose(1, 0, 2, 3).reshape(3 * rows, width), mine)
-    across = tiles(lower, above)[0]
     by_l = jnp.stack(rolled([near[0], near[1], across, near[2]], (4 - h) % 4))
     gram = exchanged_sum(by_l, "zl").astype(BF16)
 
@@ -99,17 +150,16 @@
     square = exchanged_sum(square.reshape(4, slab, pair), "zh")
     polynomial = (QUINTIC_B * turned.astype(F32) + QUINTIC_C * square).astype(BF16)
 
-    polynomial = jnp.concatenate(rolled(around(polynomial, "zl"), (h - l) % 4), axis=1)
+    polynomial = gathered(polynomial, "zl")
+    polynomial = jnp.concatenate(rolled([polynomial[i] for i in range(4)], h), axis=1)
     polynomial = gathered(polynomial, "y").reshape(rows, 4 * pair)
     swapped = take(polynomial, "c", 1)
 
-    blocks = [columns(block) for block in (mine, above, opposite, below)]
-    own = jnp.concatenate([b[0] for b in blocks], axis=0)
-    others = jnp.concatenate([b[1] for b in blocks], axis=0)
-    product = jnp.einsum("mk,kn->mn", polynomial, own, preferred_element_type=F32)
-    product += jnp.einsum("mk,kn->mn", swapped, others, preferred_element_type=F32)
     scale = 0.2 * math.sqrt(width * 32)
-    return scale * (QUINTIC_A * iterate.astype(F32) + product)
+    blocks = (mine, above, opposite, below)
+    total = QUINTIC_A * iterate.astype(F32)
+    total = add_product(False, 1.0, total, polynomial, blocks)
+    return add_product(True, scale, total, swapped, blocks)
 
 
 def solution(mesh):

time: 404 us -> 303 us (0.75)
  waiting for transfers between devices: 196 us -> 112 us
  local copies, waits for them, and re-layouts: 22.3 us -> 10.5 us
  starting transfers between devices: 107 us -> 95.7 us
  Pallas kernels: 0 us -> 10.9 us
  matrix products: 22 us -> 12.5 us
    ppermute x12 -> x9, waiting for transfers between devices: 89.3 us -> 50.8 us  [take(): lax.ppermute(value, axis, [((i + distance) % n, i) for i in range(n)])]
    all_gather x1, waiting for transfers between devices: 32.2 us -> 0.01 us  [local(): mine = lax.all_gather(iterate, 'x', axis=0, tiled=True)]
    all_gather x1, waiting for transfers between devices: 43.2 us -> 18.3 us  [local(): above = lax.all_gather(upper, 'x', axis=0, tiled=True)]
    ppermute x12 -> x9, starting transfers between devices: 76.1 us -> 56.1 us  [take(): lax.ppermute(value, axis, [((i + distance) % n, i) for i in range(n)])]
    pallas_call x0 -> x2, Pallas kernels: none -> 10.9 us  [add_product(): pl.pallas_call(functools.partial(product_kernel, other, scale), out_shape...]
    dot_general x4 -> x2, matrix products: 18.4 us -> 7.59 us  [partial_tiles(): jnp.einsum('rn,csn->crs', block, others.reshape(2, pair, width), preferre...]
    all_to_all x1 -> x2, starting transfers between devices: 3.71 us -> 12.1 us  [gathered(): return lax.all_to_all(spread, axis, split_axis=0, concat_axis=0, tiled=True)]
    unnamed x36 -> x24, local copies, waits for them, and re-layouts: 15.1 us -> 6.79 us
  transfers between devices with their start and end apart: 22 -> 20, of which waited for: 8 -> 8; matrix products, arithmetic and copies ran while one was open for 10% -> 6% of each run, Pallas kernels for 0% -> 2%
where the time goes in v5:
time: 303 us; the launch traced here: 302 us
  waiting for transfers between devices  112 us (37%)
  starting transfers between devices  95.7 us (32%)
  blocking collectives  41.1 us (14%)
  between operations  13.5 us (4%)
  matrix products  12.5 us (4%)
  Pallas kernels  10.9 us (4%)
  local copies, waits for them, and re-layouts  10.5 us (3%)
  other arithmetic  5.3 us (2%)
    ppermute x9, starting transfers between devices, take(): lax.ppermute(value, axis, [((i + distance) % n, i) for i in range(n)])  56.1 us
    ppermute x9, waiting for transfers between devices, take(): lax.ppermute(value, axis, [((i + distance) % n, i) for i in range(n)])  50.8 us
    all_to_all x3, waiting for transfers between devices, exchanged_sum(): lax.all_to_all(value, axis, split_axis=0, concat_axis=0, tiled=True)  31.9 us
    all_to_all x3, starting transfers between devices, exchanged_sum(): lax.all_to_all(value, axis, split_axis=0, concat_axis=0, tiled=True)  26.1 us
    all_to_all x1, blocking collectives, exchanged_sum(): lax.all_to_all(value, axis, split_axis=0, concat_axis=0, tiled=True)  21.6 us
    all_to_all x1, blocking collectives, gathered(): return lax.all_to_all(spread, axis, split_axis=0, concat_axis=0, tiled=True)  19.5 us
    all_gather x1, waiting for transfers between devices, local(): above = lax.all_gather(upper, 'x', axis=0, tiled=True)  18.3 us
    all_to_all x2, starting transfers between devices, gathered(): return lax.all_to_all(spread, axis, split_axis=0, concat_axis=0, tiled=True)  12.1 us
  transfers between devices with their start and end apart: 20, of which 8 were waited for; matrix products, arithmetic and copies ran while one was open for 6% of the time, Pallas kernels for 2%

profile of v5, /device:TPU:1, one launch (start us, length us, event | category | flops | bytes accessed | tf_op | source)
XLA Modules:
  0.0 301.9 jit_solution(5007548828157570236)
XLA Ops:
  6.5 0.7 all-gather.5.cloned.1.call-update
  7.3 13.3 %collective-permute-start = (bf16[320,800]{1,0:T(8,128)(2,1)}, bf16[320,800]{1,0:T(8,128)(2,1)S(1)}, u32[]{:S(2)}, u32[]{:S(2)}) collective-permute-start(bf16[320,800]{1,0:T(8,128)(2,1)} %param.1), channel_id=1, source_target_pairs={{32,0},{64,32},{96,64},{0,96},{33,1},{65,33},{97,65},{1,97},{34,2}... | collective-permute-start | bytes 1536008 | tf_op jit(solution)/shard_map/ppermute | solution.py:24
  20.6 1.9 collective-permute-start.1
  22.5 44.7 %collective-permute-done = bf16[320,800]{1,0:T(8,128)(2,1)S(1)} collective-permute-done((bf16[320,800]{1,0:T(8,128)(2,1)}, bf16[320,800]{1,0:T(8,128)(2,1)S(1)}, u32[]{:S(2)}, u32[]{:S(2)}) %collective-permute-start) | collective-permute-done | bytes 512032 | tf_op jit(solution)/shard_map/ppermute | solution.py:24
  67.3 0.8 copy-done.6
  68.1 1.6 pad_maximum_fusion
  69.8 0.3 copy-done
  70.1 4.0 %convolution_convert_fusion = bf16[2,640,960]{1,2,0:T(8,128)(2,1)} fusion(bf16[2,640,800]{2,1,0:T(8,128)(2,1)S(1)} %bitcast.53, bf16[960,800,1]{1,0,2:T(8,128)(2,1)S(1)} %bitcast.59), kind=kOutput, calls=%fused_computation | convolution fusion | flops 1967308800 | bytes 6041600 | tf_op jit(solution)/shard_map/rn,csn->crs/dot_general | solution.py:118
  74.1 8.3 %all-to-all-start = ((bf16[8,240,640]{2,1,0:T(8,128)(2,1)}), bf16[8,240,640]{2,1,0:T(8,128)(2,1)}, u32[]{:S(2)}, u32[]{:S(2)}) async-start(bf16[8,240,640]{2,1,0:T(8,128)(2,1)} %bitcast.58), calls=%async_computation | async-start | bytes 4915200 | tf_op jit(solution)/shard_map/all_to_all | solution.py:54
  82.5 0.7 slice.33
  83.2 0.7 slice.32
  83.9 5.7 %collective-permute-start.3 = (bf16[160,800]{1,0:T(8,128)(2,1)}, bf16[160,800]{1,0:T(8,128)(2,1)S(1)}, u32[]{:S(2)}, u32[]{:S(2)}) collective-permute-start(bf16[160,800]{1,0:T(8,128)(2,1)} %slice.33), channel_id=1, source_target_pairs={{96,0},{0,32},{32,64},{64,96},{97,1},{1,33},{33,65},{65,97},{98,2}... | collective-permute-start | bytes 768008 | tf_op jit(solution)/shard_map/ppermute | solution.py:24
  89.7 4.0 %collective-permute-start.2 = (bf16[160,800]{1,0:T(8,128)(2,1)}, bf16[160,800]{1,0:T(8,128)(2,1)S(1)}, u32[]{:S(2)}, u32[]{:S(2)}) collective-permute-start(bf16[160,800]{1,0:T(8,128)(2,1)} %slice.32), channel_id=1, source_target_pairs={{32,0},{64,32},{96,64},{0,96},{33,1},{65,33},{97,65},{1,97},{34,2}... | collective-permute-start | bytes 768008 | tf_op jit(solution)/shard_map/ppermute | solution.py:24
  93.7 18.3 %all-gather.7.cloned.1.call-done.refs_3_ = bf16[1280,800]{1,0:T(8,128)(2,1)} async-done(((bf16[320,800]{1,0:T(8,128)(2,1)}), bf16[1280,800]{1,0:T(8,128)(2,1)}) %all-gather.7.cloned.1.call-update) | async-done | bytes 2048016 | tf_op jit(solution)/shard_map/all_gather | solution.py:129
  112.1 3.6 %convolution_convert_fusion.1 = bf16[2,640,320]{1,2,0:T(8,128)(2,1)} fusion(bf16[2,640,800]{2,1,0:T(8,128)(2,1)} %bitcast.54, bf16[320,800]{1,0:T(8,128)(2,1)S(1)} %collective-permute-done.1), kind=kOutput, calls=%fused_computation.2 | convolution fusion | flops 655769600 | bytes 3379200 | tf_op jit(solution)/shard_map/rn,csn->crs/dot_general | solution.py:118
  115.7 0.7 copy-done.8
  116.4 5.0 %all-to-all-start.1 = ((bf16[8,80,640]{2,1,0:T(8,128)(2,1)}), bf16[8,80,640]{2,1,0:T(8,128)(2,1)S(1)}, u32[]{:S(2)}, u32[]{:S(2)}) async-start(bf16[8,80,640]{2,1,0:T(8,128)(2,1)} %bitcast.60), calls=%async_computation.1 | async-start | bytes 1638400 | tf_op jit(solution)/shard_map/all_to_all | solution.py:54
  121.3 2.1 reduce_sum.45
  123.4 10.4 %all-to-all-done.1 = bf16[8,80,640]{2,1,0:T(8,128)(2,1)S(1)} async-done(((bf16[8,80,640]{2,1,0:T(8,128)(2,1)}), bf16[8,80,640]{2,1,0:T(8,128)(2,1)S(1)}, u32[]{:S(2)}, u32[]{:S(2)}) %all-to-all-start.1) | async-done | bytes 819232 | tf_op jit(solution)/shard_map/all_to_all | solution.py:54
  133.9 0.1 reduce_sum.46
  134.1 21.6 %all_to_all.35 = bf16[4,80,640]{2,1,0:T(8,128)(2,1)S(1)} all-to-all(bf16[4,80,640]{2,1,0:T(8,128)(2,1)S(1)} %pad_maximum_fusion.2), channel_id=1, replica_groups=mesh['x'=4,'zh'=4,'zl'=4,'y'=4,'c'=2] {'zl'}, dimensions={0} | all-to-all | bytes 819200 | tf_op jit(solution)/shard_map/all_to_all | solution.py:54
  155.8 0.7 collective-permute-start.5
  156.5 1.3 broadcast_in_dim.6
  157.9 4.5 %all-to-all-start.3 = ((bf16[16,80,640]{2,1,0:T(8,128)(2,1)}), bf16[16,80,640]{2,1,0:T(8,128)(2,1)}, u32[]{:S(2)}, u32[]{:S(2)}) async-start(bf16[16,80,640]{2,1,0:T(8,128)(2,1)} %broadcast_in_dim.6), calls=%async_computation.3 | async-start | bytes 3276800 | tf_op jit(solution)/shard_map/all_to_all | solution.py:46
  162.4 3.7 %collective-permute-start.6 = (bf16[80,640]{1,0:T(8,128)(2,1)S(1)}, bf16[80,640]{1,0:T(8,128)(2,1)S(1)}, u32[]{:S(2)}, u32[]{:S(2)}) collective-permute-start(bf16[80,640]{1,0:T(8,128)(2,1)S(1)} %collective-permute-done.5), channel_id=1, source_target_pairs={{8,0},{16,8},{24,16},{0,24},{9,1},{17,9},{25,17},{1,25},{10,2},{18... | collective-permute-start | bytes 307208 | tf_op jit(solution)/shard_map/ppermute | solution.py:24
  166.1 10.4 %collective-permute-start.7 = (bf16[80,640]{1,0:T(8,128)(2,1)S(1)}, bf16[80,640]{1,0:T(8,128)(2,1)S(1)}, u32[]{:S(2)}, u32[]{:S(2)}) collective-permute-start(bf16[80,640]{1,0:T(8,128)(2,1)S(1)} %collective-permute-done.5), channel_id=1, source_target_pairs={{16,0},{24,8},{0,16},{8,24},{17,1},{25,9},{1,17},{9,25},{18,2},{26... | collective-permute-start | bytes 307208 | tf_op jit(solution)/shard_map/ppermute | solution.py:24
  176.5 3.4 %collective-permute-start.8 = (bf16[80,640]{1,0:T(8,128)(2,1)S(1)}, bf16[80,640]{1,0:T(8,128)(2,1)S(1)}, u32[]{:S(2)}, u32[]{:S(2)}) collective-permute-start(bf16[80,640]{1,0:T(8,128)(2,1)S(1)} %collective-permute-done.5), channel_id=1, source_target_pairs={{24,0},{0,8},{8,16},{16,24},{25,1},{1,9},{9,17},{17,25},{26,2},{2,... | collective-permute-start | bytes 307208 | tf_op jit(solution)/shard_map/ppermute | solution.py:24
  179.9 4.5 %collective-permute-done.8 = bf16[80,640]{1,0:T(8,128)(2,1)S(1)} collective-permute-done((bf16[80,640]{1,0:T(8,128)(2,1)S(1)}, bf16[80,640]{1,0:T(8,128)(2,1)S(1)}, u32[]{:S(2)}, u32[]{:S(2)}) %collective-permute-start.8) | collective-permute-done | bytes 102432 | tf_op jit(solution)/shard_map/ppermute | solution.py:24
  184.5 2.4 convolution_convert_fusion.2
  186.9 5.4 %collective-permute-start.9 = (bf16[320,640]{1,0:T(8,128)(2,1)}, bf16[320,640]{1,0:T(8,128)(2,1)S(1)}, u32[]{:S(2)}, u32[]{:S(2)}) collective-permute-start(bf16[320,640]{1,0:T(8,128)(2,1)} %convolution_convert_fusion.2), channel_id=1, source_target_pairs={{1,0},{0,1},{3,2},{2,3},{5,4},{4,5},{7,6},{6,7},{9,8},{8,9},{11,10... | collective-permute-start | bytes 1228808 | tf_op jit(solution)/shard_map/ppermute | solution.py:24
  192.3 1.5 collective-permute-done.9
  193.9 2.4 fusion
  196.3 12.8 %all-to-all-start.4 = ((bf16[4,80,640]{2,1,0:T(8,128)(2,1)}), bf16[4,80,640]{2,1,0:T(8,128)(2,1)S(1)}, u32[]{:S(2)}, u32[]{:S(2)}) async-start(bf16[4,80,640]{2,1,0:T(8,128)(2,1)} %bitcast.23), calls=%async_computation.4 | async-start | bytes 819200 | tf_op jit(solution)/shard_map/all_to_all | solution.py:54
  209.1 0.7 collective-permute-start.4
  209.8 21.5 %all-to-all-done.4 = bf16[4,80,640]{2,1,0:T(8,128)(2,1)S(1)} async-done(((bf16[4,80,640]{2,1,0:T(8,128)(2,1)}), bf16[4,80,640]{2,1,0:T(8,128)(2,1)S(1)}, u32[]{:S(2)}, u32[]{:S(2)}) %all-to-all-start.4) | async-done | bytes 409632 | tf_op jit(solution)/shard_map/all_to_all | solution.py:54
  231.4 0.8 broadcast_in_dim.7
  232.2 7.6 %all-to-all-start.5 = ((bf16[4,80,640]{2,1,0:T(8,128)(2,1)}), bf16[4,80,640]{2,1,0:T(8,128)(2,1)S(1)}, u32[]{:S(2)}, u32[]{:S(2)}) async-start(bf16[4,80,640]{2,1,0:T(8,128)(2,1)} %broadcast_in_dim.7), calls=%async_computation.5 | async-start | bytes 819200 | tf_op jit(solution)/shard_map/all_to_all | solution.py:46
  239.8 0.9 pad_maximum_fusion.1
  240.7 7.1 %all-to-all-done.5 = bf16[4,80,640]{2,1,0:T(8,128)(2,1)S(1)} async-done(((bf16[4,80,640]{2,1,0:T(8,128)(2,1)}), bf16[4,80,640]{2,1,0:T(8,128)(2,1)S(1)}, u32[]{:S(2)}, u32[]{:S(2)}) %all-to-all-start.5) | async-done | bytes 409632 | tf_op jit(solution)/shard_map/all_to_all | solution.py:46
  247.9 0.1 broadcast_in_dim.8
  248.1 19.5 %all_to_all.36 = bf16[4,80,2560]{2,1,0:T(8,128)(2,1)} all-to-all(bf16[4,80,2560]{2,1,0:T(8,128)(2,1)S(1)} %broadcast_in_dim.8), channel_id=1, replica_groups=mesh['x'=4,'zh'=4,'zl'=4,'y'=4,'c'=2] {'y'}, dimensions={0} | all-to-all | bytes 3276800 | tf_op jit(solution)/shard_map/all_to_all | solution.py:46
  267.5 8.3 %collective-permute-start.10 = (bf16[320,2560]{1,0:T(8,128)(2,1)}, bf16[320,2560]{1,0:T(8,128)(2,1)}, u32[]{:S(2)}, u32[]{:S(2)}) collective-permute-start(bf16[320,2560]{1,0:T(8,128)(2,1)} %bitcast.28.refs_1_), channel_id=1, source_target_pairs={{1,0},{0,1},{3,2},{2,3},{5,4},{4,5},{7,6},{6,7},{9,8},{8,9},{11,10... | collective-permute-start | bytes 4915208 | tf_op jit(solution)/shard_map/ppermute | solution.py:24
  276.0 3.5 %all-gather.9.cloned.1.call-done.refs_4_ = bf16[1280,800]{1,0:T(8,128)(2,1)} async-done(((bf16[320,800]{1,0:T(8,128)(2,1)}), bf16[1280,800]{1,0:T(8,128)(2,1)}) %all-gather.9.cloned.1.call-update) | async-done | bytes 2048016 | tf_op jit(solution)/shard_map/all_gather | solution.py:140
  279.4 1.6 copy-done.1
  281.1 1.6 copy-done.2
  282.7 1.6 copy-done.3
  284.4 4.9 %shard_map.17.refs_0_ = f32[320,800]{1,0:T(8,128)S(1)} custom-call(f32[320,800]{1,0:T(8,128)S(1)} %convert_multiply_fusion.refs_0_, bf16[320,2560]{1,0:T(8,128)(2,1)} %bitcast.28.refs_1_, bf16[1280,800]{1,0:T(8,128)(2,1)S(1)} %copy-done, bf16[1280,800]{1,0:T(8,128)(2,1)S(1)} %copy-done.1, bf16[1280,800]{1,0:T(8,128)(2,1)S(1)} %copy-done.3, ...), custom_call_target="tpu_custom_call" | custom-call | flops 1310720000 | bytes 7782400 | tf_op jit(solution)/shard_map/pallas_call | solution.py:89
  289.3 6.0 %shard_map.18 = f32[320,800]{1,0:T(8,128)} custom-call(f32[320,800]{1,0:T(8,128)S(1)} %shard_map.17.refs_0_, bf16[320,2560]{1,0:T(8,128)(2,1)} %collective-permute-done.10.refs_1_, bf16[1280,800]{1,0:T(8,128)(2,1)S(1)} %copy-done, bf16[1280,800]{1,0:T(8,128)(2,1)S(1)} %copy-done.1, bf16[1280,800]{1,0:T(8,128)(2,1)S(1)} %copy-done.3, ...), custom_call_target="tpu_custom_call" | custom-call | flops 1310720000 | bytes 7782400 | tf_op jit(solution)/shard_map/pallas_call | solution.py:89
  (46 shorter events, 0.8 us)
Async XLA Ops:
  6.5 60.8 %all-gather.5.cloned.1.call-start = ((), (), s32[]{:S(2)}) async-start(), calls=%async_computation.7 | async-start | bytes 2867200 | tf_op jit(solution)/shard_map/all_gather | solution.py:127
  7.3 104.8 %all-gather.7.cloned.1.call-start = ((), (), s32[]{:S(2)}) async-start(), calls=%async_computation.8 | async-start | bytes 2867200 | tf_op jit(solution)/shard_map/all_gather | solution.py:129
  7.3 60.0 %collective-permute-start = (bf16[320,800]{1,0:T(8,128)(2,1)}, bf16[320,800]{1,0:T(8,128)(2,1)S(1)}, u32[]{:S(2)}, u32[]{:S(2)}) collective-permute-start(bf16[320,800]{1,0:T(8,128)(2,1)} %param.1), channel_id=1, source_target_pairs={{32,0},{64,32},{96,64},{0,96},{33,1},{65,33},{97,65},{1,97},{34,2}... | collective-permute-start | bytes 1536008 | tf_op jit(solution)/shard_map/ppermute | solution.py:24
  20.6 46.7 %collective-permute-start.1 = (bf16[320,800]{1,0:T(8,128)(2,1)}, bf16[320,800]{1,0:T(8,128)(2,1)S(1)}, u32[]{:S(2)}, u32[]{:S(2)}) collective-permute-start(bf16[320,800]{1,0:T(8,128)(2,1)} %param.1), channel_id=1, source_target_pairs={{96,0},{0,32},{32,64},{64,96},{97,1},{1,33},{33,65},{65,97},{98,2}... | collective-permute-start | bytes 1536008 | tf_op jit(solution)/shard_map/ppermute | solution.py:24
  67.3 0.8 copy-start.6
  67.3 44.8 %copy-start.5 = (bf16[320,800]{1,0:T(8,128)(2,1)}, bf16[320,800]{1,0:T(8,128)(2,1)S(1)}, u32[]{:S(2)}) copy-start(bf16[320,800]{1,0:T(8,128)(2,1)S(1)} %collective-permute-done.1) | copy-start | bytes 1536004
  68.1 2.0 copy-start
  74.1 9.1 %copy-start.7 = (bf16[320,800]{1,0:T(8,128)(2,1)S(1)}, bf16[320,800]{1,0:T(8,128)(2,1)}, u32[]{:S(2)}) copy-start(bf16[320,800]{1,0:T(8,128)(2,1)} %copy-done.6) | copy-start | bytes 1536004
  74.1 41.5 %all-to-all-start = ((bf16[8,240,640]{2,1,0:T(8,128)(2,1)}), bf16[8,240,640]{2,1,0:T(8,128)(2,1)}, u32[]{:S(2)}, u32[]{:S(2)}) async-start(bf16[8,240,640]{2,1,0:T(8,128)(2,1)} %bitcast.58), calls=%async_computation | async-start | bytes 4915200 | tf_op jit(solution)/shard_map/all_to_all | solution.py:54
  83.9 31.7 %collective-permute-start.3 = (bf16[160,800]{1,0:T(8,128)(2,1)}, bf16[160,800]{1,0:T(8,128)(2,1)S(1)}, u32[]{:S(2)}, u32[]{:S(2)}) collective-permute-start(bf16[160,800]{1,0:T(8,128)(2,1)} %slice.33), channel_id=1, source_target_pairs={{96,0},{0,32},{32,64},{64,96},{97,1},{1,33},{33,65},{65,97},{98,2}... | collective-permute-start | bytes 768008 | tf_op jit(solution)/shard_map/ppermute | solution.py:24
  89.7 26.0 %collective-permute-start.2 = (bf16[160,800]{1,0:T(8,128)(2,1)}, bf16[160,800]{1,0:T(8,128)(2,1)S(1)}, u32[]{:S(2)}, u32[]{:S(2)}) collective-permute-start(bf16[160,800]{1,0:T(8,128)(2,1)} %slice.32), channel_id=1, source_target_pairs={{32,0},{64,32},{96,64},{0,96},{33,1},{65,33},{97,65},{1,97},{34,2}... | collective-permute-start | bytes 768008 | tf_op jit(solution)/shard_map/ppermute | solution.py:24
  115.6 0.7 copy-start.8
  115.6 5.7 %copy-start.10 = (bf16[160,800]{1,0:T(8,128)(2,1)}, bf16[160,800]{1,0:T(8,128)(2,1)S(1)}, u32[]{:S(2)}) copy-start(bf16[160,800]{1,0:T(8,128)(2,1)S(1)} %collective-permute-done.2) | copy-start | bytes 768004
  116.4 17.5 %all-to-all-start.1 = ((bf16[8,80,640]{2,1,0:T(8,128)(2,1)}), bf16[8,80,640]{2,1,0:T(8,128)(2,1)S(1)}, u32[]{:S(2)}, u32[]{:S(2)}) async-start(bf16[8,80,640]{2,1,0:T(8,128)(2,1)} %bitcast.60), calls=%async_computation.1 | async-start | bytes 1638400 | tf_op jit(solution)/shard_map/all_to_all | solution.py:54
  155.8 0.7 collective-permute-start.5
  157.9 26.6 %all-to-all-start.3 = ((bf16[16,80,640]{2,1,0:T(8,128)(2,1)}), bf16[16,80,640]{2,1,0:T(8,128)(2,1)}, u32[]{:S(2)}, u32[]{:S(2)}) async-start(bf16[16,80,640]{2,1,0:T(8,128)(2,1)} %broadcast_in_dim.6), calls=%async_computation.3 | async-start | bytes 3276800 | tf_op jit(solution)/shard_map/all_to_all | solution.py:46
  162.4 113.6 %all-gather.11.cloned.1.call-start = ((), (), s32[]{:S(2)}) async-start(), calls=%async_computation.10 | async-start | bytes 2867200 | tf_op jit(solution)/shard_map/all_gather | solution.py:130
  162.4 17.5 %collective-permute-start.6 = (bf16[80,640]{1,0:T(8,128)(2,1)S(1)}, bf16[80,640]{1,0:T(8,128)(2,1)S(1)}, u32[]{:S(2)}, u32[]{:S(2)}) collective-permute-start(bf16[80,640]{1,0:T(8,128)(2,1)S(1)} %collective-permute-done.5), channel_id=1, source_target_pairs={{8,0},{16,8},{24,16},{0,24},{9,1},{17,9},{25,17},{1,25},{10,2},{18... | collective-permute-start | bytes 307208 | tf_op jit(solution)/shard_map/ppermute | solution.py:24
  166.1 13.8 %collective-permute-start.7 = (bf16[80,640]{1,0:T(8,128)(2,1)S(1)}, bf16[80,640]{1,0:T(8,128)(2,1)S(1)}, u32[]{:S(2)}, u32[]{:S(2)}) collective-permute-start(bf16[80,640]{1,0:T(8,128)(2,1)S(1)} %collective-permute-done.5), channel_id=1, source_target_pairs={{16,0},{24,8},{0,16},{8,24},{17,1},{25,9},{1,17},{9,25},{18,2},{26... | collective-permute-start | bytes 307208 | tf_op jit(solution)/shard_map/ppermute | solution.py:24
  176.5 7.9 %collective-permute-start.8 = (bf16[80,640]{1,0:T(8,128)(2,1)S(1)}, bf16[80,640]{1,0:T(8,128)(2,1)S(1)}, u32[]{:S(2)}, u32[]{:S(2)}) collective-permute-start(bf16[80,640]{1,0:T(8,128)(2,1)S(1)} %collective-permute-done.5), channel_id=1, source_target_pairs={{24,0},{0,8},{8,16},{16,24},{25,1},{1,9},{9,17},{17,25},{26,2},{2,... | collective-permute-start | bytes 307208 | tf_op jit(solution)/shard_map/ppermute | solution.py:24
  186.9 6.9 %collective-permute-start.9 = (bf16[320,640]{1,0:T(8,128)(2,1)}, bf16[320,640]{1,0:T(8,128)(2,1)S(1)}, u32[]{:S(2)}, u32[]{:S(2)}) collective-permute-start(bf16[320,640]{1,0:T(8,128)(2,1)} %convolution_convert_fusion.2), channel_id=1, source_target_pairs={{1,0},{0,1},{3,2},{2,3},{5,4},{4,5},{7,6},{6,7},{9,8},{8,9},{11,10... | collective-permute-start | bytes 1228808 | tf_op jit(solution)/shard_map/ppermute | solution.py:24
  196.3 43.5 %copy-start.9 = (bf16[160,800]{1,0:T(8,128)(2,1)S(1)}, bf16[160,800]{1,0:T(8,128)(2,1)}, u32[]{:S(2)}) copy-start(bf16[160,800]{1,0:T(8,128)(2,1)} %copy-done.8) | copy-start | bytes 768004
  196.3 43.5 %copy-start.11 = (bf16[160,800]{1,0:T(8,128)(2,1)S(1)}, bf16[160,800]{1,0:T(8,128)(2,1)}, u32[]{:S(2)}) copy-start(bf16[160,800]{1,0:T(8,128)(2,1)} %copy-done.10) | copy-start | bytes 768004
  196.3 35.0 %all-to-all-start.4 = ((bf16[4,80,640]{2,1,0:T(8,128)(2,1)}), bf16[4,80,640]{2,1,0:T(8,128)(2,1)S(1)}, u32[]{:S(2)}, u32[]{:S(2)}) async-start(bf16[4,80,640]{2,1,0:T(8,128)(2,1)} %bitcast.23), calls=%async_computation.4 | async-start | bytes 819200 | tf_op jit(solution)/shard_map/all_to_all | solution.py:54
  209.1 22.3 %collective-permute-start.4 = (bf16[80,640]{1,0:T(8,128)(2,1)S(1)}, bf16[80,640]{1,0:T(8,128)(2,1)S(1)}, u32[]{:S(2)}, u32[]{:S(2)}) collective-permute-start(bf16[80,640]{1,0:T(8,128)(2,1)S(1)} %reduce_sum.47), channel_id=1, source_target_pairs={{0,0},{32,8},{56,16},{96,24},{8,32},{40,40},{72,48},{64,56},{104,6... | collective-permute-start | bytes 307208 | tf_op jit(solution)/shard_map/ppermute | solution.py:35
  232.2 15.6 %all-to-all-start.5 = ((bf16[4,80,640]{2,1,0:T(8,128)(2,1)}), bf16[4,80,640]{2,1,0:T(8,128)(2,1)S(1)}, u32[]{:S(2)}, u32[]{:S(2)}) async-start(bf16[4,80,640]{2,1,0:T(8,128)(2,1)} %broadcast_in_dim.7), calls=%async_computation.5 | async-start | bytes 819200 | tf_op jit(solution)/shard_map/all_to_all | solution.py:46
  239.8 39.6 %all-gather.9.cloned.1.call-start = ((), (), s32[]{:S(2)}) async-start(), calls=%async_computation.9 | async-start | bytes 2867200 | tf_op jit(solution)/shard_map/all_gather | solution.py:140
  248.0 27.8 %copy-start.4 = (bf16[320,800]{1,0:T(8,128)(2,1)S(1)}, bf16[320,800]{1,0:T(8,128)(2,1)}, u32[]{:S(2)}) copy-start(bf16[320,800]{1,0:T(8,128)(2,1)} %param.1) | copy-start | bytes 1536004
  267.5 21.8 %collective-permute-start.10 = (bf16[320,2560]{1,0:T(8,128)(2,1)}, bf16[320,2560]{1,0:T(8,128)(2,1)}, u32[]{:S(2)}, u32[]{:S(2)}) collective-permute-start(bf16[320,2560]{1,0:T(8,128)(2,1)} %bitcast.28.refs_1_), channel_id=1, source_target_pairs={{1,0},{0,1},{3,2},{2,3},{5,4},{4,5},{7,6},{6,7},{9,8},{8,9},{11,10... | collective-permute-start | bytes 4915208 | tf_op jit(solution)/shard_map/ppermute | solution.py:24
  279.4 1.6 copy-start.1
  281.1 1.6 copy-start.2
  282.7 1.6 copy-start.3
Sparse Core Ops, SparseCore 0:
  9.5 45.4 all-gather.4
  68.2 43.7 all-gather.6
  192.4 41.8 all-gather.10
  242.4 36.9 all-gather.8

commit v6 on v5

--- a/solution.py
+++ b/solution.py
@@ -62,45 +62,37 @@
     return (kept + other.astype(F32)).astype(BF16)
 
 
-def product_kernel(other, scale, *refs):
-    total, left, *blocks, out, held, arrived = refs
+def product_kernel(other, total, left, *refs):
+    *blocks, out = refs
     pair = left.shape[1] // 4
     c = lax.axis_index("c")
     start = pl.multiple_of((1 - c if other else c) * pair, pair)
-    copies = [
-        pltpu.make_async_copy(block.at[pl.ds(start, pair), :], held.at[e], arrived.at[e])
-        for e, block in enumerate(blocks)
-    ]
-    for copy in copies:
-        copy.start()
-    value = total[...]
-    for e, copy in enumerate(copies):
-        copy.wait()
-        value += jnp.dot(
-            left[:, e * pair : (e + 1) * pair], held[e], preferred_element_type=F32
+    value = None
+    for e, block in enumerate(blocks):
+        part = jnp.dot(
+            left[:, e * pair : (e + 1) * pair],
+            block[pl.ds(start, pair), :],
+            preferred_element_type=F32,
         )
-    out[...] = scale * value
+        value = part if value is None else value + part
+    if other:
+        out[...] = 0.2 * math.sqrt(out.shape[1] * 32) * (total[...] + value)
+    else:
+        out[...] = QUINTIC_A * total[...].astype(F32) + value
 
 
-def add_product(other, scale, total, left, blocks):
-    rows, width = total.shape
-    pair = left.shape[1] // 4
-    vmem = pl.BlockSpec(memory_space=pltpu.VMEM)
+def add_product(other, total, left, blocks):
     return pl.pallas_call(
-        functools.partial(product_kernel, other, scale),
+        functools.partial(product_kernel, other),
         out_shape=jax.ShapeDtypeStruct(total.shape, F32),
-        in_specs=[vmem, vmem] + [pl.BlockSpec(memory_space=pl.ANY)] * 4,
-        out_specs=vmem,
-        scratch_shapes=[
-            pltpu.VMEM((4, pair, width), BF16),
-            pltpu.SemaphoreType.DMA((4,)),
-        ],
+        in_specs=[pl.BlockSpec(memory_space=pltpu.VMEM)] * 6,
+        out_specs=pl.BlockSpec(memory_space=pltpu.VMEM),
         cost_estimate=pl.CostEstimate(
-            flops=2 * left.size * width,
-            bytes_accessed=2 * left.size + 8 * pair * width + 8 * total.size,
+            flops=2 * left.size * total.shape[1],
+            bytes_accessed=2 * left.size + 8 * total.size,
             transcendentals=0,
         ),
-        compiler_params=pltpu.CompilerParams(vmem_limit_bytes=32 * 2**20),
+        compiler_params=pltpu.CompilerParams(vmem_limit_bytes=24 * 2**20),
     )(total, left, *blocks)
 
 
@@ -146,8 +138,10 @@
     gram = fetch(gram, lambda p, q: (q, p))
     left = jnp.concatenate(rolled(around(gram, "zl"), (4 - l) % 4), axis=0)
     right = gathered(gram, ("x", "y")).reshape(2 * pair, pair)
+    right, below = lax.optimization_barrier((right, below))
     square = matmul_over_c(left, *columns(right))
     square = exchanged_sum(square.reshape(4, slab, pair), "zh")
+    square, opposite = lax.optimization_barrier((square, opposite))
     polynomial = (QUINTIC_B * turned.astype(F32) + QUINTIC_C * square).astype(BF16)
 
     polynomial = gathered(polynomial, "zl")
@@ -155,11 +149,9 @@
     polynomial = gathered(polynomial, "y").reshape(rows, 4 * pair)
     swapped = take(polynomial, "c", 1)
 
-    scale = 0.2 * math.sqrt(width * 32)
     blocks = (mine, above, opposite, below)
-    total = QUINTIC_A * iterate.astype(F32)
-    total = add_product(False, 1.0, total, polynomial, blocks)
-    return add_product(True, scale, total, swapped, blocks)
+    total = add_product(False, iterate, polynomial, blocks)
+    return add_product(True, total, swapped, blocks)
 
 
 def solution(mesh):

time: 303 us -> 292 us (0.964)
  Pallas kernels: 10.9 us -> 5.26 us
  local copies, waits for them, and re-layouts: 10.5 us -> 5.63 us
    pallas_call x2, Pallas kernels: 10.9 us -> 5.26 us  [add_product(): pl.pallas_call(functools.partial(product_kernel, other), out_shape=jax.Sh...]
    unnamed x24, local copies, waits for them, and re-layouts: 6.79 us -> 1.95 us
    all_gather x1, waiting for transfers between devices: 3.46 us -> 0.02 us  [local(): lax.all_gather(jnp.concatenate(opposite, axis=0), 'x', axis=0, tiled=True)]
  transfers between devices with their start and end apart: 20 -> 20, of which waited for: 8 -> 9; matrix products, arithmetic and copies ran while one was open for 6% -> 7% of each run, Pallas kernels for 2% -> 1%
where the time goes in v6:
time: 292 us; the launch traced here: 289 us
  waiting for transfers between devices  109 us (37%)
  starting transfers between devices  97.1 us (33%)
  blocking collectives  40.7 us (14%)
  between operations  13.5 us (5%)
  matrix products  12.6 us (4%)
  local copies, waits for them, and re-layouts  5.63 us (2%)
  Pallas kernels  5.26 us (2%)
  other arithmetic  5.2 us (2%)
    ppermute x9, starting transfers between devices, take(): lax.ppermute(value, axis, [((i + distance) % n, i) for i in range(n)])  56.8 us
    ppermute x9, waiting for transfers between devices, take(): lax.ppermute(value, axis, [((i + distance) % n, i) for i in range(n)])  51.5 us
    all_to_all x3, waiting for transfers between devices, exchanged_sum(): lax.all_to_all(value, axis, split_axis=0, concat_axis=0, tiled=True)  30.9 us
    all_to_all x3, starting transfers between devices, exchanged_sum(): lax.all_to_all(value, axis, split_axis=0, concat_axis=0, tiled=True)  26.5 us
    all_to_all x1, blocking collectives, exchanged_sum(): lax.all_to_all(value, axis, split_axis=0, concat_axis=0, tiled=True)  22.7 us
    all_gather x1, waiting for transfers between devices, local(): above = lax.all_gather(upper, 'x', axis=0, tiled=True)  18.3 us
    all_to_all x1, blocking collectives, gathered(): return lax.all_to_all(spread, axis, split_axis=0, concat_axis=0, tiled=True)  18 us
    all_to_all x2, starting transfers between devices, gathered(): return lax.all_to_all(spread, axis, split_axis=0, concat_axis=0, tiled=True)  12.3 us
  transfers between devices with their start and end apart: 20, of which 9 were waited for; matrix products, arithmetic and copies ran while one was open for 7% of the time, Pallas kernels for 1%

profile of v6, /device:TPU:1, one launch (start us, length us, event | category | flops | bytes accessed | tf_op | source)
XLA Modules:
  0.0 289.2 jit_solution(4125434530904993261)
XLA Ops:
  6.5 0.7 all-gather.5.cloned.1.call-update
  7.3 13.3 %collective-permute-start = (bf16[320,800]{1,0:T(8,128)(2,1)}, bf16[320,800]{1,0:T(8,128)(2,1)S(1)}, u32[]{:S(2)}, u32[]{:S(2)}) collective-permute-start(bf16[320,800]{1,0:T(8,128)(2,1)} %total.1), channel_id=1, source_target_pairs={{32,0},{64,32},{96,64},{0,96},{33,1},{65,33},{97,65},{1,97},{34,2}... | collective-permute-start | bytes 1536008 | tf_op jit(solution)/shard_map/ppermute | solution.py:24
  20.6 1.9 collective-permute-start.1
  22.5 44.7 %collective-permute-done = bf16[320,800]{1,0:T(8,128)(2,1)S(1)} collective-permute-done((bf16[320,800]{1,0:T(8,128)(2,1)}, bf16[320,800]{1,0:T(8,128)(2,1)S(1)}, u32[]{:S(2)}, u32[]{:S(2)}) %collective-permute-start) | collective-permute-done | bytes 512032 | tf_op jit(solution)/shard_map/ppermute | solution.py:24
  67.3 0.8 copy-done.6
  68.1 1.6 pad_maximum_fusion
  69.8 0.3 copy-done
  70.1 4.0 %convolution_convert_fusion = bf16[2,640,960]{1,2,0:T(8,128)(2,1)} fusion(bf16[2,640,800]{2,1,0:T(8,128)(2,1)S(1)} %bitcast.54, bf16[960,800,1]{1,0,2:T(8,128)(2,1)S(1)} %bitcast.62), kind=kOutput, calls=%fused_computation | convolution fusion | flops 1967308800 | bytes 6041600 | tf_op jit(solution)/shard_map/rn,csn->crs/dot_general | solution.py:110
  74.1 8.3 %all-to-all-start = ((bf16[8,240,640]{2,1,0:T(8,128)(2,1)}), bf16[8,240,640]{2,1,0:T(8,128)(2,1)}, u32[]{:S(2)}, u32[]{:S(2)}) async-start(bf16[8,240,640]{2,1,0:T(8,128)(2,1)} %bitcast.61), calls=%async_computation | async-start | bytes 4915200 | tf_op jit(solution)/shard_map/all_to_all | solution.py:54
  82.5 0.7 slice.33
  83.2 0.7 slice.32
  84.0 5.7 %collective-permute-start.3 = (bf16[160,800]{1,0:T(8,128)(2,1)}, bf16[160,800]{1,0:T(8,128)(2,1)S(1)}, u32[]{:S(2)}, u32[]{:S(2)}) collective-permute-start(bf16[160,800]{1,0:T(8,128)(2,1)} %slice.33), channel_id=1, source_target_pairs={{96,0},{0,32},{32,64},{64,96},{97,1},{1,33},{33,65},{65,97},{98,2}... | collective-permute-start | bytes 768008 | tf_op jit(solution)/shard_map/ppermute | solution.py:24
  89.7 4.0 %collective-permute-start.2 = (bf16[160,800]{1,0:T(8,128)(2,1)}, bf16[160,800]{1,0:T(8,128)(2,1)S(1)}, u32[]{:S(2)}, u32[]{:S(2)}) collective-permute-start(bf16[160,800]{1,0:T(8,128)(2,1)} %slice.32), channel_id=1, source_target_pairs={{32,0},{64,32},{96,64},{0,96},{33,1},{65,33},{97,65},{1,97},{34,2}... | collective-permute-start | bytes 768008 | tf_op jit(solution)/shard_map/ppermute | solution.py:24
  93.8 18.3 %all-gather.7.cloned.1.call-done.refs_1_ = bf16[1280,800]{1,0:T(8,128)(2,1)} async-done(((bf16[320,800]{1,0:T(8,128)(2,1)}), bf16[1280,800]{1,0:T(8,128)(2,1)}) %all-gather.7.cloned.1.call-update) | async-done | bytes 2048016 | tf_op jit(solution)/shard_map/all_gather | solution.py:121
  112.1 3.7 %convolution_convert_fusion.1 = bf16[2,640,320]{1,2,0:T(8,128)(2,1)} fusion(bf16[2,640,800]{2,1,0:T(8,128)(2,1)} %bitcast.55, bf16[320,800]{1,0:T(8,128)(2,1)} %copy-done.5), kind=kOutput, calls=%fused_computation.2 | convolution fusion | flops 655769600 | bytes 3379200 | tf_op jit(solution)/shard_map/rn,csn->crs/dot_general | solution.py:110
  115.8 0.7 copy-done.8
  116.5 0.1 copy-done.10
  116.6 5.0 %all-to-all-start.1 = ((bf16[8,80,640]{2,1,0:T(8,128)(2,1)}), bf16[8,80,640]{2,1,0:T(8,128)(2,1)S(1)}, u32[]{:S(2)}, u32[]{:S(2)}) async-start(bf16[8,80,640]{2,1,0:T(8,128)(2,1)} %bitcast.63), calls=%async_computation.1 | async-start | bytes 1638400 | tf_op jit(solution)/shard_map/all_to_all | solution.py:54
  121.5 2.1 reduce_sum.45
  123.6 10.4 %all-to-all-done.1 = bf16[8,80,640]{2,1,0:T(8,128)(2,1)S(1)} async-done(((bf16[8,80,640]{2,1,0:T(8,128)(2,1)}), bf16[8,80,640]{2,1,0:T(8,128)(2,1)S(1)}, u32[]{:S(2)}, u32[]{:S(2)}) %all-to-all-start.1) | async-done | bytes 819232 | tf_op jit(solution)/shard_map/all_to_all | solution.py:54
  134.1 0.1 reduce_sum.46
  134.2 0.1 select_bitcast_fusion.7
  134.3 22.7 %all_to_all.35 = bf16[4,80,640]{2,1,0:T(8,128)(2,1)S(1)} all-to-all(bf16[4,80,640]{2,1,0:T(8,128)(2,1)S(1)} %pad_maximum_fusion.2), channel_id=1, replica_groups=mesh['x'=4,'zh'=4,'zl'=4,'y'=4,'c'=2] {'zl'}, dimensions={0} | all-to-all | bytes 819200 | tf_op jit(solution)/shard_map/all_to_all | solution.py:54
  157.1 0.7 collective-permute-start.5
  157.8 1.3 broadcast_in_dim.6
  159.1 4.5 %all-to-all-start.3 = ((bf16[16,80,640]{2,1,0:T(8,128)(2,1)}), bf16[16,80,640]{2,1,0:T(8,128)(2,1)}, u32[]{:S(2)}, u32[]{:S(2)}) async-start(bf16[16,80,640]{2,1,0:T(8,128)(2,1)} %broadcast_in_dim.6), calls=%async_computation.3 | async-start | bytes 3276800 | tf_op jit(solution)/shard_map/all_to_all | solution.py:46
  163.7 0.9 pad_maximum_fusion.1
  164.6 3.7 %collective-permute-start.6 = (bf16[80,640]{1,0:T(8,128)(2,1)S(1)}, bf16[80,640]{1,0:T(8,128)(2,1)S(1)}, u32[]{:S(2)}, u32[]{:S(2)}) collective-permute-start(bf16[80,640]{1,0:T(8,128)(2,1)S(1)} %collective-permute-done.5), channel_id=1, source_target_pairs={{8,0},{16,8},{24,16},{0,24},{9,1},{17,9},{25,17},{1,25},{10,2},{18... | collective-permute-start | bytes 307208 | tf_op jit(solution)/shard_map/ppermute | solution.py:24
  168.2 10.4 %collective-permute-start.7 = (bf16[80,640]{1,0:T(8,128)(2,1)S(1)}, bf16[80,640]{1,0:T(8,128)(2,1)S(1)}, u32[]{:S(2)}, u32[]{:S(2)}) collective-permute-start(bf16[80,640]{1,0:T(8,128)(2,1)S(1)} %collective-permute-done.5), channel_id=1, source_target_pairs={{16,0},{24,8},{0,16},{8,24},{17,1},{25,9},{1,17},{9,25},{18,2},{26... | collective-permute-start | bytes 307208 | tf_op jit(solution)/shard_map/ppermute | solution.py:24
  178.6 3.4 %collective-permute-start.8 = (bf16[80,640]{1,0:T(8,128)(2,1)S(1)}, bf16[80,640]{1,0:T(8,128)(2,1)S(1)}, u32[]{:S(2)}, u32[]{:S(2)}) collective-permute-start(bf16[80,640]{1,0:T(8,128)(2,1)S(1)} %collective-permute-done.5), channel_id=1, source_target_pairs={{24,0},{0,8},{8,16},{16,24},{25,1},{1,9},{9,17},{17,25},{26,2},{2,... | collective-permute-start | bytes 307208 | tf_op jit(solution)/shard_map/ppermute | solution.py:24
  182.0 0.3 collective-permute-done.7
  182.3 3.9 %collective-permute-done.8 = bf16[80,640]{1,0:T(8,128)(2,1)S(1)} collective-permute-done((bf16[80,640]{1,0:T(8,128)(2,1)S(1)}, bf16[80,640]{1,0:T(8,128)(2,1)S(1)}, u32[]{:S(2)}, u32[]{:S(2)}) %collective-permute-start.8) | collective-permute-done | bytes 102432 | tf_op jit(solution)/shard_map/ppermute | solution.py:24
  186.3 2.4 convolution_convert_fusion.2
  188.8 5.3 %collective-permute-start.9 = (bf16[320,640]{1,0:T(8,128)(2,1)}, bf16[320,640]{1,0:T(8,128)(2,1)S(1)}, u32[]{:S(2)}, u32[]{:S(2)}) collective-permute-start(bf16[320,640]{1,0:T(8,128)(2,1)} %convolution_convert_fusion.2), channel_id=1, source_target_pairs={{1,0},{0,1},{3,2},{2,3},{5,4},{4,5},{7,6},{6,7},{9,8},{8,9},{11,10... | collective-permute-start | bytes 1228808 | tf_op jit(solution)/shard_map/ppermute | solution.py:24
  194.1 1.6 collective-permute-done.9
  195.6 2.4 fusion
  198.1 13.2 %all-to-all-start.4 = ((bf16[4,80,640]{2,1,0:T(8,128)(2,1)}), bf16[4,80,640]{2,1,0:T(8,128)(2,1)S(1)}, u32[]{:S(2)}, u32[]{:S(2)}) async-start(bf16[4,80,640]{2,1,0:T(8,128)(2,1)} %bitcast.24), calls=%async_computation.4 | async-start | bytes 819200 | tf_op jit(solution)/shard_map/all_to_all | solution.py:54
  211.3 0.7 collective-permute-start.4
  211.9 20.5 %all-to-all-done.4 = bf16[4,80,640]{2,1,0:T(8,128)(2,1)S(1)} async-done(((bf16[4,80,640]{2,1,0:T(8,128)(2,1)}), bf16[4,80,640]{2,1,0:T(8,128)(2,1)S(1)}, u32[]{:S(2)}, u32[]{:S(2)}) %all-to-all-start.4) | async-done | bytes 409632 | tf_op jit(solution)/shard_map/all_to_all | solution.py:54
  232.6 0.8 broadcast_in_dim.7
  233.4 7.8 %all-to-all-start.5 = ((bf16[4,80,640]{2,1,0:T(8,128)(2,1)}), bf16[4,80,640]{2,1,0:T(8,128)(2,1)S(1)}, u32[]{:S(2)}, u32[]{:S(2)}) async-start(bf16[4,80,640]{2,1,0:T(8,128)(2,1)} %broadcast_in_dim.7), calls=%async_computation.5 | async-start | bytes 819200 | tf_op jit(solution)/shard_map/all_to_all | solution.py:46
  241.2 7.9 %all-to-all-done.5 = bf16[4,80,640]{2,1,0:T(8,128)(2,1)S(1)} async-done(((bf16[4,80,640]{2,1,0:T(8,128)(2,1)}), bf16[4,80,640]{2,1,0:T(8,128)(2,1)S(1)}, u32[]{:S(2)}, u32[]{:S(2)}) %all-to-all-start.5) | async-done | bytes 409632 | tf_op jit(solution)/shard_map/all_to_all | solution.py:46
  249.2 0.1 broadcast_in_dim.8
  249.3 18.0 %all_to_all.36 = bf16[4,80,2560]{2,1,0:T(8,128)(2,1)S(1)} all-to-all(bf16[4,80,2560]{2,1,0:T(8,128)(2,1)S(1)} %broadcast_in_dim.8), channel_id=1, replica_groups=mesh['x'=4,'zh'=4,'zl'=4,'y'=4,'c'=2] {'y'}, dimensions={0} | all-to-all | bytes 3276800 | tf_op jit(solution)/shard_map/all_to_all | solution.py:46
  267.3 9.1 %collective-permute-start.10 = (bf16[320,2560]{1,0:T(8,128)(2,1)S(1)}, bf16[320,2560]{1,0:T(8,128)(2,1)S(1)}, u32[]{:S(2)}, u32[]{:S(2)}) collective-permute-start(bf16[320,2560]{1,0:T(8,128)(2,1)S(1)} %bitcast.56), channel_id=1, source_target_pairs={{1,0},{0,1},{3,2},{2,3},{5,4},{4,5},{7,6},{6,7},{9,8},{8,9},{11,10... | collective-permute-start | bytes 4915208 | tf_op jit(solution)/shard_map/ppermute | solution.py:24
  276.5 2.1 shard_map.17.total
  278.6 0.9 collective-permute-done.10.left
  279.6 3.1 %shard_map.18 = f32[320,800]{1,0:T(8,128)} custom-call(f32[320,800]{1,0:T(8,128)S(1)} %shard_map.17.total, bf16[320,2560]{1,0:T(8,128)(2,1)S(1)} %collective-permute-done.10.left, bf16[1280,800]{1,0:T(8,128)(2,1)S(1)} %copy-done, bf16[1280,800]{1,0:T(8,128)(2,1)S(1)} %copy-done.1, bf16[1280,800]{1,0:T(8,128)(2,1)S(1)} %copy-done.3, ...), custom_call_target="tpu_custom_call" | custom-call | flops 1310720000 | bytes 3686400 | tf_op jit(solution)/shard_map/pallas_call | solution.py:85
  (45 shorter events, 0.6 us)
Async XLA Ops:
  6.5 60.8 %all-gather.5.cloned.1.call-start = ((), (), s32[]{:S(2)}) async-start(), calls=%async_computation.7 | async-start | bytes 2867200 | tf_op jit(solution)/shard_map/all_gather | solution.py:119
  7.3 104.8 %all-gather.7.cloned.1.call-start = ((), (), s32[]{:S(2)}) async-start(), calls=%async_computation.8 | async-start | bytes 2867200 | tf_op jit(solution)/shard_map/all_gather | solution.py:121
  7.3 60.0 %collective-permute-start = (bf16[320,800]{1,0:T(8,128)(2,1)}, bf16[320,800]{1,0:T(8,128)(2,1)S(1)}, u32[]{:S(2)}, u32[]{:S(2)}) collective-permute-start(bf16[320,800]{1,0:T(8,128)(2,1)} %total.1), channel_id=1, source_target_pairs={{32,0},{64,32},{96,64},{0,96},{33,1},{65,33},{97,65},{1,97},{34,2}... | collective-permute-start | bytes 1536008 | tf_op jit(solution)/shard_map/ppermute | solution.py:24
  20.6 46.7 %collective-permute-start.1 = (bf16[320,800]{1,0:T(8,128)(2,1)}, bf16[320,800]{1,0:T(8,128)(2,1)S(1)}, u32[]{:S(2)}, u32[]{:S(2)}) collective-permute-start(bf16[320,800]{1,0:T(8,128)(2,1)} %total.1), channel_id=1, source_target_pairs={{96,0},{0,32},{32,64},{64,96},{97,1},{1,33},{33,65},{65,97},{98,2}... | collective-permute-start | bytes 1536008 | tf_op jit(solution)/shard_map/ppermute | solution.py:24
  67.3 0.8 copy-start.6
  67.3 15.2 %copy-start.5 = (bf16[320,800]{1,0:T(8,128)(2,1)}, bf16[320,800]{1,0:T(8,128)(2,1)S(1)}, u32[]{:S(2)}) copy-start(bf16[320,800]{1,0:T(8,128)(2,1)S(1)} %collective-permute-done.1) | copy-start | bytes 1536004
  68.1 2.0 copy-start
  74.1 9.1 %copy-start.7 = (bf16[320,800]{1,0:T(8,128)(2,1)S(1)}, bf16[320,800]{1,0:T(8,128)(2,1)}, u32[]{:S(2)}) copy-start(bf16[320,800]{1,0:T(8,128)(2,1)} %copy-done.6) | copy-start | bytes 1536004
  74.1 41.6 %all-to-all-start = ((bf16[8,240,640]{2,1,0:T(8,128)(2,1)}), bf16[8,240,640]{2,1,0:T(8,128)(2,1)}, u32[]{:S(2)}, u32[]{:S(2)}) async-start(bf16[8,240,640]{2,1,0:T(8,128)(2,1)} %bitcast.61), calls=%async_computation | async-start | bytes 4915200 | tf_op jit(solution)/shard_map/all_to_all | solution.py:54
  82.5 103.8 %all-gather.9.cloned.1.call-start = ((), (), s32[]{:S(2)}) async-start(), calls=%async_computation.9 | async-start | bytes 2867200 | tf_op jit(solution)/shard_map/all_gather | solution.py:122
  84.0 31.8 %collective-permute-start.3 = (bf16[160,800]{1,0:T(8,128)(2,1)}, bf16[160,800]{1,0:T(8,128)(2,1)S(1)}, u32[]{:S(2)}, u32[]{:S(2)}) collective-permute-start(bf16[160,800]{1,0:T(8,128)(2,1)} %slice.33), channel_id=1, source_target_pairs={{96,0},{0,32},{32,64},{64,96},{97,1},{1,33},{33,65},{65,97},{98,2}... | collective-permute-start | bytes 768008 | tf_op jit(solution)/shard_map/ppermute | solution.py:24
  89.7 26.0 %collective-permute-start.2 = (bf16[160,800]{1,0:T(8,128)(2,1)}, bf16[160,800]{1,0:T(8,128)(2,1)S(1)}, u32[]{:S(2)}, u32[]{:S(2)}) collective-permute-start(bf16[160,800]{1,0:T(8,128)(2,1)} %slice.32), channel_id=1, source_target_pairs={{32,0},{64,32},{96,64},{0,96},{33,1},{65,33},{97,65},{1,97},{34,2}... | collective-permute-start | bytes 768008 | tf_op jit(solution)/shard_map/ppermute | solution.py:24
  115.7 0.7 copy-start.8
  115.8 0.8 copy-start.10
  116.6 17.5 %all-to-all-start.1 = ((bf16[8,80,640]{2,1,0:T(8,128)(2,1)}), bf16[8,80,640]{2,1,0:T(8,128)(2,1)S(1)}, u32[]{:S(2)}, u32[]{:S(2)}) async-start(bf16[8,80,640]{2,1,0:T(8,128)(2,1)} %bitcast.63), calls=%async_computation.1 | async-start | bytes 1638400 | tf_op jit(solution)/shard_map/all_to_all | solution.py:54
  157.1 0.7 collective-permute-start.5
  159.1 4.6 %copy-start.9 = (bf16[160,800]{1,0:T(8,128)(2,1)S(1)}, bf16[160,800]{1,0:T(8,128)(2,1)}, u32[]{:S(2)}) copy-start(bf16[160,800]{1,0:T(8,128)(2,1)} %copy-done.8) | copy-start | bytes 768004
  159.1 4.6 %copy-start.11 = (bf16[160,800]{1,0:T(8,128)(2,1)S(1)}, bf16[160,800]{1,0:T(8,128)(2,1)}, u32[]{:S(2)}) copy-start(bf16[160,800]{1,0:T(8,128)(2,1)} %copy-done.10) | copy-start | bytes 768004
  159.1 27.3 %all-to-all-start.3 = ((bf16[16,80,640]{2,1,0:T(8,128)(2,1)}), bf16[16,80,640]{2,1,0:T(8,128)(2,1)}, u32[]{:S(2)}, u32[]{:S(2)}) async-start(bf16[16,80,640]{2,1,0:T(8,128)(2,1)} %broadcast_in_dim.6), calls=%async_computation.3 | async-start | bytes 3276800 | tf_op jit(solution)/shard_map/all_to_all | solution.py:46
  163.6 68.9 %all-gather.11.cloned.1.call-start = ((), (), s32[]{:S(2)}) async-start(), calls=%async_computation.10 | async-start | bytes 2867200 | tf_op jit(solution)/shard_map/all_gather | solution.py:132
  164.6 17.4 %collective-permute-start.6 = (bf16[80,640]{1,0:T(8,128)(2,1)S(1)}, bf16[80,640]{1,0:T(8,128)(2,1)S(1)}, u32[]{:S(2)}, u32[]{:S(2)}) collective-permute-start(bf16[80,640]{1,0:T(8,128)(2,1)S(1)} %collective-permute-done.5), channel_id=1, source_target_pairs={{8,0},{16,8},{24,16},{0,24},{9,1},{17,9},{25,17},{1,25},{10,2},{18... | collective-permute-start | bytes 307208 | tf_op jit(solution)/shard_map/ppermute | solution.py:24
  168.2 14.1 %collective-permute-start.7 = (bf16[80,640]{1,0:T(8,128)(2,1)S(1)}, bf16[80,640]{1,0:T(8,128)(2,1)S(1)}, u32[]{:S(2)}, u32[]{:S(2)}) collective-permute-start(bf16[80,640]{1,0:T(8,128)(2,1)S(1)} %collective-permute-done.5), channel_id=1, source_target_pairs={{16,0},{24,8},{0,16},{8,24},{17,1},{25,9},{1,17},{9,25},{18,2},{26... | collective-permute-start | bytes 307208 | tf_op jit(solution)/shard_map/ppermute | solution.py:24
  178.6 7.6 %collective-permute-start.8 = (bf16[80,640]{1,0:T(8,128)(2,1)S(1)}, bf16[80,640]{1,0:T(8,128)(2,1)S(1)}, u32[]{:S(2)}, u32[]{:S(2)}) collective-permute-start(bf16[80,640]{1,0:T(8,128)(2,1)S(1)} %collective-permute-done.5), channel_id=1, source_target_pairs={{24,0},{0,8},{8,16},{16,24},{25,1},{1,9},{9,17},{17,25},{26,2},{2,... | collective-permute-start | bytes 307208 | tf_op jit(solution)/shard_map/ppermute | solution.py:24
  188.8 6.9 %collective-permute-start.9 = (bf16[320,640]{1,0:T(8,128)(2,1)}, bf16[320,640]{1,0:T(8,128)(2,1)S(1)}, u32[]{:S(2)}, u32[]{:S(2)}) collective-permute-start(bf16[320,640]{1,0:T(8,128)(2,1)} %convolution_convert_fusion.2), channel_id=1, source_target_pairs={{1,0},{0,1},{3,2},{2,3},{5,4},{4,5},{7,6},{6,7},{9,8},{8,9},{11,10... | collective-permute-start | bytes 1228808 | tf_op jit(solution)/shard_map/ppermute | solution.py:24
  198.1 34.4 %all-to-all-start.4 = ((bf16[4,80,640]{2,1,0:T(8,128)(2,1)}), bf16[4,80,640]{2,1,0:T(8,128)(2,1)S(1)}, u32[]{:S(2)}, u32[]{:S(2)}) async-start(bf16[4,80,640]{2,1,0:T(8,128)(2,1)} %bitcast.24), calls=%async_computation.4 | async-start | bytes 819200 | tf_op jit(solution)/shard_map/all_to_all | solution.py:54
  211.3 21.2 %collective-permute-start.4 = (bf16[80,640]{1,0:T(8,128)(2,1)S(1)}, bf16[80,640]{1,0:T(8,128)(2,1)S(1)}, u32[]{:S(2)}, u32[]{:S(2)}) collective-permute-start(bf16[80,640]{1,0:T(8,128)(2,1)S(1)} %reduce_sum.47), channel_id=1, source_target_pairs={{0,0},{32,8},{56,16},{96,24},{8,32},{40,40},{72,48},{64,56},{104,6... | collective-permute-start | bytes 307208 | tf_op jit(solution)/shard_map/ppermute | solution.py:35
  233.4 43.1 %copy-start.4 = (bf16[320,800]{1,0:T(8,128)(2,1)S(1)}, bf16[320,800]{1,0:T(8,128)(2,1)}, u32[]{:S(2)}) copy-start(bf16[320,800]{1,0:T(8,128)(2,1)} %total.1) | copy-start | bytes 1536004
  233.4 15.7 %all-to-all-start.5 = ((bf16[4,80,640]{2,1,0:T(8,128)(2,1)}), bf16[4,80,640]{2,1,0:T(8,128)(2,1)S(1)}, u32[]{:S(2)}, u32[]{:S(2)}) async-start(bf16[4,80,640]{2,1,0:T(8,128)(2,1)} %broadcast_in_dim.7), calls=%async_computation.5 | async-start | bytes 819200 | tf_op jit(solution)/shard_map/all_to_all | solution.py:46
  249.1 27.4 %copy-start.3 = (bf16[1280,800]{1,0:T(8,128)(2,1)S(1)}, bf16[1280,800]{1,0:T(8,128)(2,1)}, u32[]{:S(2)}) copy-start(bf16[1280,800]{1,0:T(8,128)(2,1)} %all-gather.11.cloned.1.call-done.refs_2_) | copy-start | bytes 6144004
  249.2 27.3 %copy-start.2 = (bf16[1280,800]{1,0:T(8,128)(2,1)S(1)}, bf16[1280,800]{1,0:T(8,128)(2,1)}, u32[]{:S(2)}) copy-start(bf16[1280,800]{1,0:T(8,128)(2,1)} %all-gather.9.cloned.1.call-done.refs_3_) | copy-start | bytes 6144004
  249.3 27.1 %copy-start.1 = (bf16[1280,800]{1,0:T(8,128)(2,1)S(1)}, bf16[1280,800]{1,0:T(8,128)(2,1)}, u32[]{:S(2)}) copy-start(bf16[1280,800]{1,0:T(8,128)(2,1)} %all-gather.7.cloned.1.call-done.refs_1_) | copy-start | bytes 6144004
  267.3 12.2 %collective-permute-start.10 = (bf16[320,2560]{1,0:T(8,128)(2,1)S(1)}, bf16[320,2560]{1,0:T(8,128)(2,1)S(1)}, u32[]{:S(2)}, u32[]{:S(2)}) collective-permute-start(bf16[320,2560]{1,0:T(8,128)(2,1)S(1)} %bitcast.56), channel_id=1, source_target_pairs={{1,0},{0,1},{3,2},{2,3},{5,4},{4,5},{7,6},{6,7},{9,8},{8,9},{11,10... | collective-permute-start | bytes 4915208 | tf_op jit(solution)/shard_map/ppermute | solution.py:24
Sparse Core Ops, SparseCore 0:
  9.5 45.4 all-gather.4
  68.2 43.7 all-gather.6
  114.2 40.2 all-gather.8
  166.2 47.5 all-gather.10

commit v7 on v6

--- a/solution.py
+++ b/solution.py
@@ -57,7 +57,7 @@
 
 def matmul_over_c(block, keep, give):
     sent = jnp.einsum("rn,sn->rs", block, give, preferred_element_type=F32).astype(BF16)
-    other = take(sent, "c", 1)
+    other = lax.all_gather(sent, "c", axis=0, tiled=False)[1 - lax.axis_index("c")]
     kept = jnp.einsum("rn,sn->rs", block, keep, preferred_element_type=F32)
     return (kept + other.astype(F32)).astype(BF16)
 
@@ -138,13 +138,13 @@
     gram = fetch(gram, lambda p, q: (q, p))
     left = jnp.concatenate(rolled(around(gram, "zl"), (4 - l) % 4), axis=0)
     right = gathered(gram, ("x", "y")).reshape(2 * pair, pair)
-    right, below = lax.optimization_barrier((right, below))
+    left, right, below, turned = lax.optimization_barrier((left, right, below, turned))
     square = matmul_over_c(left, *columns(right))
     square = exchanged_sum(square.reshape(4, slab, pair), "zh")
     square, opposite = lax.optimization_barrier((square, opposite))
     polynomial = (QUINTIC_B * turned.astype(F32) + QUINTIC_C * square).astype(BF16)
 
-    polynomial = gathered(polynomial, "zl")
+    polynomial = lax.all_gather(polynomial, "zl", axis=0, tiled=False)
     polynomial = jnp.concatenate(rolled([polynomial[i] for i in range(4)], h), axis=1)
     polynomial = gathered(polynomial, "y").reshape(rows, 4 * pair)
     swapped = take(polynomial, "c", 1)

time: 292 us -> 286 us (0.979)
  blocking collectives: 40.7 us -> 57.2 us
  starting transfers between devices: 97.1 us -> 86.5 us
  waiting for transfers between devices: 109 us -> 101 us
    all_gather x0 -> x2, blocking collectives: none -> 18.3 us  [the longest x1 12.8 us: local(): polynomial = lax.all_gather(polynomial, 'zl', axis=0, tiled=False)]
    all_to_all x2 -> x1, waiting for transfers between devices: 7.91 us -> 0.01 us  [gathered(): return lax.all_to_all(spread, axis, split_axis=0, concat_axis=0, tiled=True)]
    all_to_all x2 -> x1, starting transfers between devices: 12.3 us -> 4.53 us  [gathered(): return lax.all_to_all(spread, axis, split_axis=0, concat_axis=0, tiled=True)]
    ppermute x9 -> x8, starting transfers between devices: 56.8 us -> 53.8 us  [take(): lax.ppermute(value, axis, [((i + distance) % n, i) for i in range(n)])]
    ppermute x9 -> x8, waiting for transfers between devices: 51.5 us -> 49.2 us  [take(): lax.ppermute(value, axis, [((i + distance) % n, i) for i in range(n)])]
  transfers between devices with their start and end apart: 20 -> 18, of which waited for: 9 -> 6; matrix products, arithmetic and copies ran while one was open for 7% -> 7% of each run, Pallas kernels for 1% -> 1%
where the time goes in v7:
time: 286 us; the launch traced here: 285 us
  waiting for transfers between devices  101 us (35%)
  starting transfers between devices  86.5 us (30%)
  blocking collectives  57.2 us (20%)
  between operations  13.5 us (5%)
  matrix products  11.8 us (4%)
  Pallas kernels  5.26 us (2%)
  other arithmetic  5.25 us (2%)
  local copies, waits for them, and re-layouts  4.82 us (2%)
    ppermute x8, starting transfers between devices, take(): lax.ppermute(value, axis, [((i + distance) % n, i) for i in range(n)])  53.8 us
    ppermute x8, waiting for transfers between devices, take(): lax.ppermute(value, axis, [((i + distance) % n, i) for i in range(n)])  49.2 us
    all_to_all x3, waiting for transfers between devices, exchanged_sum(): lax.all_to_all(value, axis, split_axis=0, concat_axis=0, tiled=True)  32.4 us
    all_to_all x3, starting transfers between devices, exchanged_sum(): lax.all_to_all(value, axis, split_axis=0, concat_axis=0, tiled=True)  26.8 us
    all_to_all x1, blocking collectives, exchanged_sum(): lax.all_to_all(value, axis, split_axis=0, concat_axis=0, tiled=True)  22.7 us
    all_gather x1, waiting for transfers between devices, local(): above = lax.all_gather(upper, 'x', axis=0, tiled=True)  18.3 us
    all_to_all x1, blocking collectives, gathered(): return lax.all_to_all(spread, axis, split_axis=0, concat_axis=0, tiled=True)  16.3 us
    all_gather x1, blocking collectives, local(): polynomial = lax.all_gather(polynomial, 'zl', axis=0, tiled=False)  12.8 us
  transfers between devices with their start and end apart: 18, of which 6 were waited for; matrix products, arithmetic and copies ran while one was open for 7% of the time, Pallas kernels for 1%

profile of v7, /device:TPU:1, one launch (start us, length us, event | category | flops | bytes accessed | tf_op | source)
XLA Modules:
  0.0 285.0 jit_solution(17172742771019442628)
XLA Ops:
  6.5 0.7 all-gather.7.cloned.1.call-update
  7.3 13.3 %collective-permute-start = (bf16[320,800]{1,0:T(8,128)(2,1)}, bf16[320,800]{1,0:T(8,128)(2,1)S(1)}, u32[]{:S(2)}, u32[]{:S(2)}) collective-permute-start(bf16[320,800]{1,0:T(8,128)(2,1)} %total.1), channel_id=1, source_target_pairs={{32,0},{64,32},{96,64},{0,96},{33,1},{65,33},{97,65},{1,97},{34,2}... | collective-permute-start | bytes 1536008 | tf_op jit(solution)/shard_map/ppermute | solution.py:24
  20.6 1.9 collective-permute-start.1
  22.5 44.7 %collective-permute-done = bf16[320,800]{1,0:T(8,128)(2,1)S(1)} collective-permute-done((bf16[320,800]{1,0:T(8,128)(2,1)}, bf16[320,800]{1,0:T(8,128)(2,1)S(1)}, u32[]{:S(2)}, u32[]{:S(2)}) %collective-permute-start) | collective-permute-done | bytes 512032 | tf_op jit(solution)/shard_map/ppermute | solution.py:24
  67.3 0.8 copy-done.6
  68.1 1.6 pad_maximum_fusion
  69.8 0.3 copy-done
  70.1 4.0 %convolution_convert_fusion = bf16[2,640,960]{1,2,0:T(8,128)(2,1)} fusion(bf16[2,640,800]{2,1,0:T(8,128)(2,1)S(1)} %bitcast.52, bf16[960,800,1]{1,0,2:T(8,128)(2,1)S(1)} %bitcast.61), kind=kOutput, calls=%fused_computation | convolution fusion | flops 1967308800 | bytes 6041600 | tf_op jit(solution)/shard_map/rn,csn->crs/dot_general | solution.py:110
  74.1 8.3 %all-to-all-start = ((bf16[8,240,640]{2,1,0:T(8,128)(2,1)}), bf16[8,240,640]{2,1,0:T(8,128)(2,1)}, u32[]{:S(2)}, u32[]{:S(2)}) async-start(bf16[8,240,640]{2,1,0:T(8,128)(2,1)} %bitcast.59), calls=%async_computation | async-start | bytes 4915200 | tf_op jit(solution)/shard_map/all_to_all | solution.py:54
  82.5 0.7 slice.33
  83.2 0.7 slice.32
  84.0 5.7 %collective-permute-start.3 = (bf16[160,800]{1,0:T(8,128)(2,1)}, bf16[160,800]{1,0:T(8,128)(2,1)S(1)}, u32[]{:S(2)}, u32[]{:S(2)}) collective-permute-start(bf16[160,800]{1,0:T(8,128)(2,1)} %slice.33), channel_id=1, source_target_pairs={{96,0},{0,32},{32,64},{64,96},{97,1},{1,33},{33,65},{65,97},{98,2}... | collective-permute-start | bytes 768008 | tf_op jit(solution)/shard_map/ppermute | solution.py:24
  89.7 4.0 %collective-permute-start.2 = (bf16[160,800]{1,0:T(8,128)(2,1)}, bf16[160,800]{1,0:T(8,128)(2,1)S(1)}, u32[]{:S(2)}, u32[]{:S(2)}) collective-permute-start(bf16[160,800]{1,0:T(8,128)(2,1)} %slice.32), channel_id=1, source_target_pairs={{32,0},{64,32},{96,64},{0,96},{33,1},{65,33},{97,65},{1,97},{34,2}... | collective-permute-start | bytes 768008 | tf_op jit(solution)/shard_map/ppermute | solution.py:24
  93.8 18.3 %all-gather.9.cloned.1.call-done.refs_1_ = bf16[1280,800]{1,0:T(8,128)(2,1)} async-done(((bf16[320,800]{1,0:T(8,128)(2,1)}), bf16[1280,800]{1,0:T(8,128)(2,1)}) %all-gather.9.cloned.1.call-update) | async-done | bytes 2048016 | tf_op jit(solution)/shard_map/all_gather | solution.py:121
  112.1 3.7 %convolution_convert_fusion.1 = bf16[2,640,320]{1,2,0:T(8,128)(2,1)} fusion(bf16[2,640,800]{2,1,0:T(8,128)(2,1)} %bitcast.53, bf16[320,800]{1,0:T(8,128)(2,1)} %copy-done.5), kind=kOutput, calls=%fused_computation.2 | convolution fusion | flops 655769600 | bytes 3379200 | tf_op jit(solution)/shard_map/rn,csn->crs/dot_general | solution.py:110
  115.8 0.7 copy-done.8
  116.5 0.1 copy-done.10
  116.6 5.0 %all-to-all-start.1 = ((bf16[8,80,640]{2,1,0:T(8,128)(2,1)}), bf16[8,80,640]{2,1,0:T(8,128)(2,1)S(1)}, u32[]{:S(2)}, u32[]{:S(2)}) async-start(bf16[8,80,640]{2,1,0:T(8,128)(2,1)} %bitcast.62), calls=%async_computation.1 | async-start | bytes 1638400 | tf_op jit(solution)/shard_map/all_to_all | solution.py:54
  121.5 2.1 reduce_sum.45
  123.6 10.4 %all-to-all-done.1 = bf16[8,80,640]{2,1,0:T(8,128)(2,1)S(1)} async-done(((bf16[8,80,640]{2,1,0:T(8,128)(2,1)}), bf16[8,80,640]{2,1,0:T(8,128)(2,1)S(1)}, u32[]{:S(2)}, u32[]{:S(2)}) %all-to-all-start.1) | async-done | bytes 819232 | tf_op jit(solution)/shard_map/all_to_all | solution.py:54
  134.1 0.1 reduce_sum.46
  134.2 0.1 select_bitcast_fusion.3
  134.3 0.1 pad_maximum_fusion.2
  134.3 22.7 %all_to_all.30 = bf16[4,80,640]{2,1,0:T(8,128)(2,1)S(1)} all-to-all(bf16[4,80,640]{2,1,0:T(8,128)(2,1)S(1)} %pad_maximum_fusion.2), channel_id=1, replica_groups=mesh['x'=4,'zh'=4,'zl'=4,'y'=4,'c'=2] {'zl'}, dimensions={0} | all-to-all | bytes 819200 | tf_op jit(solution)/shard_map/all_to_all | solution.py:54
  157.0 0.1 reduce_sum.47
  157.0 0.7 collective-permute-start.4
  157.7 1.3 broadcast_in_dim.4
  159.0 4.5 %all-to-all-start.3 = ((bf16[16,80,640]{2,1,0:T(8,128)(2,1)}), bf16[16,80,640]{2,1,0:T(8,128)(2,1)}, u32[]{:S(2)}, u32[]{:S(2)}) async-start(bf16[16,80,640]{2,1,0:T(8,128)(2,1)} %broadcast_in_dim.4), calls=%async_computation.3 | async-start | bytes 3276800 | tf_op jit(solution)/shard_map/all_to_all | solution.py:46
  163.6 0.9 pad_maximum_fusion.1
  164.5 3.7 %collective-permute-start.5 = (bf16[80,640]{1,0:T(8,128)(2,1)S(1)}, bf16[80,640]{1,0:T(8,128)(2,1)S(1)}, u32[]{:S(2)}, u32[]{:S(2)}) collective-permute-start(bf16[80,640]{1,0:T(8,128)(2,1)S(1)} %collective-permute-done.4), channel_id=1, source_target_pairs={{8,0},{16,8},{24,16},{0,24},{9,1},{17,9},{25,17},{1,25},{10,2},{18... | collective-permute-start | bytes 307208 | tf_op jit(solution)/shard_map/ppermute | solution.py:24
  168.2 10.4 %collective-permute-start.6 = (bf16[80,640]{1,0:T(8,128)(2,1)S(1)}, bf16[80,640]{1,0:T(8,128)(2,1)S(1)}, u32[]{:S(2)}, u32[]{:S(2)}) collective-permute-start(bf16[80,640]{1,0:T(8,128)(2,1)S(1)} %collective-permute-done.4), channel_id=1, source_target_pairs={{16,0},{24,8},{0,16},{8,24},{17,1},{25,9},{1,17},{9,25},{18,2},{26... | collective-permute-start | bytes 307208 | tf_op jit(solution)/shard_map/ppermute | solution.py:24
  178.6 3.4 %collective-permute-start.7 = (bf16[80,640]{1,0:T(8,128)(2,1)S(1)}, bf16[80,640]{1,0:T(8,128)(2,1)S(1)}, u32[]{:S(2)}, u32[]{:S(2)}) collective-permute-start(bf16[80,640]{1,0:T(8,128)(2,1)S(1)} %collective-permute-done.4), channel_id=1, source_target_pairs={{24,0},{0,8},{8,16},{16,24},{25,1},{1,9},{9,17},{17,25},{26,2},{2,... | collective-permute-start | bytes 307208 | tf_op jit(solution)/shard_map/ppermute | solution.py:24
  181.9 0.7 collective-permute-start.8
  182.6 3.5 %collective-permute-done.7 = bf16[80,640]{1,0:T(8,128)(2,1)S(1)} collective-permute-done((bf16[80,640]{1,0:T(8,128)(2,1)S(1)}, bf16[80,640]{1,0:T(8,128)(2,1)S(1)}, u32[]{:S(2)}, u32[]{:S(2)}) %collective-permute-start.7) | collective-permute-done | bytes 102432 | tf_op jit(solution)/shard_map/ppermute | solution.py:24
  186.2 0.1 select_select_fusion.7
  186.3 1.7 convolution_convert_fusion.2
  188.0 5.5 %all-gather = bf16[640,640]{1,0:T(8,128)(2,1)S(1)} all-gather(bf16[320,640]{1,0:T(8,128)(2,1)S(1)} %convolution_convert_fusion.2), channel_id=2, replica_groups=mesh['x'=4,'zh'=4,'zl'=4,'y'=4,'c'=2] {'c'}, dimensions={0}, use_global_device_ids=true | all-gather | bytes 1228800 | tf_op jit(solution)/shard_map/all_gather | solution.py:60
  193.5 2.4 fusion
  196.0 13.5 %all-to-all-start.4 = ((bf16[4,80,640]{2,1,0:T(8,128)(2,1)}), bf16[4,80,640]{2,1,0:T(8,128)(2,1)S(1)}, u32[]{:S(2)}, u32[]{:S(2)}) async-start(bf16[4,80,640]{2,1,0:T(8,128)(2,1)} %bitcast.26), calls=%async_computation.4 | async-start | bytes 819200 | tf_op jit(solution)/shard_map/all_to_all | solution.py:54
  209.4 22.0 %all-to-all-done.4 = bf16[4,80,640]{2,1,0:T(8,128)(2,1)S(1)} async-done(((bf16[4,80,640]{2,1,0:T(8,128)(2,1)}), bf16[4,80,640]{2,1,0:T(8,128)(2,1)S(1)}, u32[]{:S(2)}, u32[]{:S(2)}) %all-to-all-start.4) | async-done | bytes 409632 | tf_op jit(solution)/shard_map/all_to_all | solution.py:54
  231.6 12.8 %all-gather.1 = bf16[320,640]{1,0:T(8,128)(2,1)S(1)} all-gather(bf16[80,640]{1,0:T(8,128)(2,1)S(1)} %add_convert_fusion), channel_id=3, replica_groups=mesh['x'=4,'zh'=4,'zl'=4,'y'=4,'c'=2] {'zl'}, dimensions={0}, use_global_device_ids=true | all-gather | bytes 512000 | tf_op jit(solution)/shard_map/all_gather | solution.py:147
  244.3 0.1 select_select_fusion.3
  244.5 0.1 broadcast_in_dim.5
  244.6 16.3 %all_to_all.31 = bf16[4,80,2560]{2,1,0:T(8,128)(2,1)S(1)} all-to-all(bf16[4,80,2560]{2,1,0:T(8,128)(2,1)S(1)} %broadcast_in_dim.5), channel_id=1, replica_groups=mesh['x'=4,'zh'=4,'zl'=4,'y'=4,'c'=2] {'y'}, dimensions={0} | all-to-all | bytes 3276800 | tf_op jit(solution)/shard_map/all_to_all | solution.py:46
  260.9 11.4 %collective-permute-start.9 = (bf16[320,2560]{1,0:T(8,128)(2,1)S(1)}, bf16[320,2560]{1,0:T(8,128)(2,1)S(1)}, u32[]{:S(2)}, u32[]{:S(2)}) collective-permute-start(bf16[320,2560]{1,0:T(8,128)(2,1)S(1)} %bitcast.54), channel_id=1, source_target_pairs={{1,0},{0,1},{3,2},{2,3},{5,4},{4,5},{7,6},{6,7},{9,8},{8,9},{11,10... | collective-permute-start | bytes 4915208 | tf_op jit(solution)/shard_map/ppermute | solution.py:24
  272.3 2.1 shard_map.17.total
  274.5 0.9 collective-permute-done.9.left
  275.4 3.1 %shard_map.18 = f32[320,800]{1,0:T(8,128)} custom-call(f32[320,800]{1,0:T(8,128)S(1)} %shard_map.17.total, bf16[320,2560]{1,0:T(8,128)(2,1)S(1)} %collective-permute-done.9.left, bf16[1280,800]{1,0:T(8,128)(2,1)S(1)} %copy-done, bf16[1280,800]{1,0:T(8,128)(2,1)S(1)} %copy-done.1, bf16[1280,800]{1,0:T(8,128)(2,1)S(1)} %copy-done.3, ...), custom_call_target="tpu_custom_call" | custom-call | flops 1310720000 | bytes 3686400 | tf_op jit(solution)/shard_map/pallas_call | solution.py:85
  (43 shorter events, 0.4 us)
Async XLA Ops:
  6.5 60.8 %all-gather.7.cloned.1.call-start = ((), (), s32[]{:S(2)}) async-start(), calls=%async_computation.6 | async-start | bytes 2867200 | tf_op jit(solution)/shard_map/all_gather | solution.py:119
  7.3 104.8 %all-gather.9.cloned.1.call-start = ((), (), s32[]{:S(2)}) async-start(), calls=%async_computation.7 | async-start | bytes 2867200 | tf_op jit(solution)/shard_map/all_gather | solution.py:121
  7.3 60.0 %collective-permute-start = (bf16[320,800]{1,0:T(8,128)(2,1)}, bf16[320,800]{1,0:T(8,128)(2,1)S(1)}, u32[]{:S(2)}, u32[]{:S(2)}) collective-permute-start(bf16[320,800]{1,0:T(8,128)(2,1)} %total.1), channel_id=1, source_target_pairs={{32,0},{64,32},{96,64},{0,96},{33,1},{65,33},{97,65},{1,97},{34,2}... | collective-permute-start | bytes 1536008 | tf_op jit(solution)/shard_map/ppermute | solution.py:24
  20.6 46.7 %collective-permute-start.1 = (bf16[320,800]{1,0:T(8,128)(2,1)}, bf16[320,800]{1,0:T(8,128)(2,1)S(1)}, u32[]{:S(2)}, u32[]{:S(2)}) collective-permute-start(bf16[320,800]{1,0:T(8,128)(2,1)} %total.1), channel_id=1, source_target_pairs={{96,0},{0,32},{32,64},{64,96},{97,1},{1,33},{33,65},{65,97},{98,2}... | collective-permute-start | bytes 1536008 | tf_op jit(solution)/shard_map/ppermute | solution.py:24
  67.3 0.8 copy-start.6
  67.3 15.2 %copy-start.5 = (bf16[320,800]{1,0:T(8,128)(2,1)}, bf16[320,800]{1,0:T(8,128)(2,1)S(1)}, u32[]{:S(2)}) copy-start(bf16[320,800]{1,0:T(8,128)(2,1)S(1)} %collective-permute-done.1) | copy-start | bytes 1536004
  68.1 2.0 copy-start
  74.1 9.1 %copy-start.7 = (bf16[320,800]{1,0:T(8,128)(2,1)S(1)}, bf16[320,800]{1,0:T(8,128)(2,1)}, u32[]{:S(2)}) copy-start(bf16[320,800]{1,0:T(8,128)(2,1)} %copy-done.6) | copy-start | bytes 1536004
  74.1 41.6 %all-to-all-start = ((bf16[8,240,640]{2,1,0:T(8,128)(2,1)}), bf16[8,240,640]{2,1,0:T(8,128)(2,1)}, u32[]{:S(2)}, u32[]{:S(2)}) async-start(bf16[8,240,640]{2,1,0:T(8,128)(2,1)} %bitcast.59), calls=%async_computation | async-start | bytes 4915200 | tf_op jit(solution)/shard_map/all_to_all | solution.py:54
  82.5 103.8 %all-gather.11.cloned.1.call-start = ((), (), s32[]{:S(2)}) async-start(), calls=%async_computation.8 | async-start | bytes 2867200 | tf_op jit(solution)/shard_map/all_gather | solution.py:122
  84.0 31.8 %collective-permute-start.3 = (bf16[160,800]{1,0:T(8,128)(2,1)}, bf16[160,800]{1,0:T(8,128)(2,1)S(1)}, u32[]{:S(2)}, u32[]{:S(2)}) collective-permute-start(bf16[160,800]{1,0:T(8,128)(2,1)} %slice.33), channel_id=1, source_target_pairs={{96,0},{0,32},{32,64},{64,96},{97,1},{1,33},{33,65},{65,97},{98,2}... | collective-permute-start | bytes 768008 | tf_op jit(solution)/shard_map/ppermute | solution.py:24
  89.7 26.0 %collective-permute-start.2 = (bf16[160,800]{1,0:T(8,128)(2,1)}, bf16[160,800]{1,0:T(8,128)(2,1)S(1)}, u32[]{:S(2)}, u32[]{:S(2)}) collective-permute-start(bf16[160,800]{1,0:T(8,128)(2,1)} %slice.32), channel_id=1, source_target_pairs={{32,0},{64,32},{96,64},{0,96},{33,1},{65,33},{97,65},{1,97},{34,2}... | collective-permute-start | bytes 768008 | tf_op jit(solution)/shard_map/ppermute | solution.py:24
  115.7 0.7 copy-start.8
  115.8 0.8 copy-start.10
  116.6 17.5 %all-to-all-start.1 = ((bf16[8,80,640]{2,1,0:T(8,128)(2,1)}), bf16[8,80,640]{2,1,0:T(8,128)(2,1)S(1)}, u32[]{:S(2)}, u32[]{:S(2)}) async-start(bf16[8,80,640]{2,1,0:T(8,128)(2,1)} %bitcast.62), calls=%async_computation.1 | async-start | bytes 1638400 | tf_op jit(solution)/shard_map/all_to_all | solution.py:54
  157.0 0.7 collective-permute-start.4
  159.0 4.6 %copy-start.9 = (bf16[160,800]{1,0:T(8,128)(2,1)S(1)}, bf16[160,800]{1,0:T(8,128)(2,1)}, u32[]{:S(2)}) copy-start(bf16[160,800]{1,0:T(8,128)(2,1)} %copy-done.8) | copy-start | bytes 768004
  159.0 4.6 %copy-start.11 = (bf16[160,800]{1,0:T(8,128)(2,1)S(1)}, bf16[160,800]{1,0:T(8,128)(2,1)}, u32[]{:S(2)}) copy-start(bf16[160,800]{1,0:T(8,128)(2,1)} %copy-done.10) | copy-start | bytes 768004
  159.0 27.3 %all-to-all-start.3 = ((bf16[16,80,640]{2,1,0:T(8,128)(2,1)}), bf16[16,80,640]{2,1,0:T(8,128)(2,1)}, u32[]{:S(2)}, u32[]{:S(2)}) async-start(bf16[16,80,640]{2,1,0:T(8,128)(2,1)} %broadcast_in_dim.4), calls=%async_computation.3 | async-start | bytes 3276800 | tf_op jit(solution)/shard_map/all_to_all | solution.py:46
  163.6 67.9 %all-gather.13.cloned.1.call-start = ((), (), s32[]{:S(2)}) async-start(), calls=%async_computation.9 | async-start | bytes 2867200 | tf_op jit(solution)/shard_map/all_gather | solution.py:132
  164.5 18.1 %collective-permute-start.5 = (bf16[80,640]{1,0:T(8,128)(2,1)S(1)}, bf16[80,640]{1,0:T(8,128)(2,1)S(1)}, u32[]{:S(2)}, u32[]{:S(2)}) collective-permute-start(bf16[80,640]{1,0:T(8,128)(2,1)S(1)} %collective-permute-done.4), channel_id=1, source_target_pairs={{8,0},{16,8},{24,16},{0,24},{9,1},{17,9},{25,17},{1,25},{10,2},{18... | collective-permute-start | bytes 307208 | tf_op jit(solution)/shard_map/ppermute | solution.py:24
  168.2 14.5 %collective-permute-start.6 = (bf16[80,640]{1,0:T(8,128)(2,1)S(1)}, bf16[80,640]{1,0:T(8,128)(2,1)S(1)}, u32[]{:S(2)}, u32[]{:S(2)}) collective-permute-start(bf16[80,640]{1,0:T(8,128)(2,1)S(1)} %collective-permute-done.4), channel_id=1, source_target_pairs={{16,0},{24,8},{0,16},{8,24},{17,1},{25,9},{1,17},{9,25},{18,2},{26... | collective-permute-start | bytes 307208 | tf_op jit(solution)/shard_map/ppermute | solution.py:24
  178.6 7.6 %collective-permute-start.7 = (bf16[80,640]{1,0:T(8,128)(2,1)S(1)}, bf16[80,640]{1,0:T(8,128)(2,1)S(1)}, u32[]{:S(2)}, u32[]{:S(2)}) collective-permute-start(bf16[80,640]{1,0:T(8,128)(2,1)S(1)} %collective-permute-done.4), channel_id=1, source_target_pairs={{24,0},{0,8},{8,16},{16,24},{25,1},{1,9},{9,17},{17,25},{26,2},{2,... | collective-permute-start | bytes 307208 | tf_op jit(solution)/shard_map/ppermute | solution.py:24
  181.9 4.4 %collective-permute-start.8 = (bf16[80,640]{1,0:T(8,128)(2,1)S(1)}, bf16[80,640]{1,0:T(8,128)(2,1)S(1)}, u32[]{:S(2)}, u32[]{:S(2)}) collective-permute-start(bf16[80,640]{1,0:T(8,128)(2,1)S(1)} %reduce_sum.47), channel_id=1, source_target_pairs={{0,0},{32,8},{56,16},{96,24},{8,32},{40,40},{72,48},{64,56},{104,6... | collective-permute-start | bytes 307208 | tf_op jit(solution)/shard_map/ppermute | solution.py:35
  196.0 35.4 %all-to-all-start.4 = ((bf16[4,80,640]{2,1,0:T(8,128)(2,1)}), bf16[4,80,640]{2,1,0:T(8,128)(2,1)S(1)}, u32[]{:S(2)}, u32[]{:S(2)}) async-start(bf16[4,80,640]{2,1,0:T(8,128)(2,1)} %bitcast.26), calls=%async_computation.4 | async-start | bytes 819200 | tf_op jit(solution)/shard_map/all_to_all | solution.py:54
  231.5 40.8 %copy-start.4 = (bf16[320,800]{1,0:T(8,128)(2,1)S(1)}, bf16[320,800]{1,0:T(8,128)(2,1)}, u32[]{:S(2)}) copy-start(bf16[320,800]{1,0:T(8,128)(2,1)} %total.1) | copy-start | bytes 1536004
  244.3 28.0 %copy-start.3 = (bf16[1280,800]{1,0:T(8,128)(2,1)S(1)}, bf16[1280,800]{1,0:T(8,128)(2,1)}, u32[]{:S(2)}) copy-start(bf16[1280,800]{1,0:T(8,128)(2,1)} %all-gather.13.cloned.1.call-done.refs_2_) | copy-start | bytes 6144004
  244.5 27.8 %copy-start.2 = (bf16[1280,800]{1,0:T(8,128)(2,1)S(1)}, bf16[1280,800]{1,0:T(8,128)(2,1)}, u32[]{:S(2)}) copy-start(bf16[1280,800]{1,0:T(8,128)(2,1)} %all-gather.11.cloned.1.call-done.refs_3_) | copy-start | bytes 6144004
  244.6 27.7 %copy-start.1 = (bf16[1280,800]{1,0:T(8,128)(2,1)S(1)}, bf16[1280,800]{1,0:T(8,128)(2,1)}, u32[]{:S(2)}) copy-start(bf16[1280,800]{1,0:T(8,128)(2,1)} %all-gather.9.cloned.1.call-done.refs_1_) | copy-start | bytes 6144004
  260.9 14.5 %collective-permute-start.9 = (bf16[320,2560]{1,0:T(8,128)(2,1)S(1)}, bf16[320,2560]{1,0:T(8,128)(2,1)S(1)}, u32[]{:S(2)}, u32[]{:S(2)}) collective-permute-start(bf16[320,2560]{1,0:T(8,128)(2,1)S(1)} %bitcast.54), channel_id=1, source_target_pairs={{1,0},{0,1},{3,2},{2,3},{5,4},{4,5},{7,6},{6,7},{9,8},{8,9},{11,10... | collective-permute-start | bytes 4915208 | tf_op jit(solution)/shard_map/ppermute | solution.py:24
Sparse Core Ops, SparseCore 0:
  9.5 45.4 all-gather.6
  68.2 43.7 all-gather.8
  114.2 40.2 all-gather.10
  166.2 47.5 all-gather.12

commit v8 on v7

--- a/solution.py
+++ b/solution.py
@@ -14,7 +14,6 @@
 QUINTIC_C = 2.0315
 
 SIZES = {"x": 4, "zh": 4, "zl": 4, "y": 4, "c": 2}
-Z = ("zh", "zl")
 F32 = jnp.float32
 BF16 = jnp.bfloat16
 
@@ -22,17 +21,6 @@
 def take(value, axis, distance):
     n = lax.axis_size(axis)
     return lax.ppermute(value, axis, [((i + distance) % n, i) for i in range(n)])
-
-
-def home(a, b):
-    if (a - b) % 4 == 2:
-        return (b - 1) % 4 * 4 + (b + 1) % 4
-    return b * 4 + a
-
-
-def fetch(piece, wanted):
-    route = [(home(*wanted(p, q)), p * 4 + q) for p in range(4) for q in range(4)]
-    return lax.ppermute(piece, Z, route)
 
 
 def rolled(parts, start):
@@ -121,24 +109,28 @@
     above = lax.all_gather(upper, "x", axis=0, tiled=True)
     below = lax.all_gather(lower, "x", axis=0, tiled=True)
     cut = rows // 2
-    opposite = [take(upper[:cut], "zh", 1), take(lower[cut:], "zh", -1)]
+    opposite = lax.optimization_barrier((upper[:cut], lower[cut:]))
+    opposite = (take(opposite[0], "zh", 1), take(opposite[1], "zh", -1))
+    opposite = jnp.concatenate(lax.optimization_barrier(opposite), axis=0)
 
-    stacked = jnp.stack([iterate, upper, lower]).reshape(3, 4, slab, width)
-    near = partial_tiles(stacked.transpose(1, 0, 2, 3).reshape(3 * rows, width), mine)
-    near = summed_tiles(near)
-    across = partial_tiles(lower, above)
-    across, opposite = lax.optimization_barrier((across, opposite))
-    across = summed_tiles(across)[0]
-    opposite = lax.all_gather(jnp.concatenate(opposite, axis=0), "x", axis=0, tiled=True)
+    sides = jnp.stack([iterate, upper, lower]).reshape(3, 4, slab, width)
+    sides = partial_tiles(sides.transpose(1, 0, 2, 3).reshape(3 * rows, width), mine)
+    sides = summed_tiles(sides)
+    across = partial_tiles(opposite, mine)
+    sides, across = lax.optimization_barrier((sides, across))
+    across = summed_tiles(across)
+    opposite = lax.all_gather(opposite, "x", axis=0, tiled=True)
 
-    by_l = jnp.stack(rolled([near[0], near[1], across, near[2]], (4 - h) % 4))
+    by_l = jnp.stack(rolled([sides[0], sides[1], across[0], sides[2]], (4 - h) % 4))
     gram = exchanged_sum(by_l, "zl").astype(BF16)
 
-    turned = fetch(gram, lambda p, q: (p, q))
-    gram = fetch(gram, lambda p, q: (q, p))
-    left = jnp.concatenate(rolled(around(gram, "zl"), (4 - l) % 4), axis=0)
+    turned = [(q * 4 + p, p * 4 + q) for p in range(4) for q in range(4)]
+    turned = lax.ppermute(gram, ("zh", "zl"), turned)
+    left = lax.all_gather(gram, "zl", axis=0, tiled=True)
     right = gathered(gram, ("x", "y")).reshape(2 * pair, pair)
-    left, right, below, turned = lax.optimization_barrier((left, right, below, turned))
+    left, right, above, below, turned = lax.optimization_barrier(
+        (left, right, above, below, turned)
+    )
     square = matmul_over_c(left, *columns(right))
     square = exchanged_sum(square.reshape(4, slab, pair), "zh")
     square, opposite = lax.optimization_barrier((square, opposite))

time: 286 us -> 281 us (0.983)
  blocking collectives: 57.2 us -> 89.7 us
  starting transfers between devices: 86.5 us -> 55.3 us
    all_gather x0 -> x1, blocking collectives: none -> 20.7 us  [local(): left = lax.all_gather(gram, 'zl', axis=0, tiled=True)]
    ppermute x8 -> x5, starting transfers between devices: 53.8 us -> 33.4 us  [take(): lax.ppermute(value, axis, [((i + distance) % n, i) for i in range(n)])]
    all_gather x1, waiting for transfers between devices: 18.3 us -> 0.01 us  [local(): above = lax.all_gather(upper, 'x', axis=0, tiled=True)]
    ppermute x8 -> x5, waiting for transfers between devices: 49.2 us -> 60.1 us  [take(): lax.ppermute(value, axis, [((i + distance) % n, i) for i in range(n)])]
    all_to_all x3, starting transfers between devices: 26.8 us -> 16.8 us  [exchanged_sum(): lax.all_to_all(value, axis, split_axis=0, concat_axis=0, tiled=True)]
    all_to_all x1, blocking collectives: 16.3 us -> 21.9 us  [gathered(): return lax.all_to_all(spread, axis, split_axis=0, concat_axis=0, tiled=True)]
    all_to_all x1, blocking collectives: 22.7 us -> 28.1 us  [exchanged_sum(): lax.all_to_all(value, axis, split_axis=0, concat_axis=0, tiled=True)]
    all_to_all x3, waiting for transfers between devices: 32.4 us -> 37.7 us  [exchanged_sum(): lax.all_to_all(value, axis, split_axis=0, concat_axis=0, tiled=True)]
  transfers between devices with their start and end apart: 18 -> 14, of which waited for: 6 -> 6; matrix products, arithmetic and copies ran while one was open for 7% -> 6% of each run, Pallas kernels for 1% -> 1%
where the time goes in v8:
time: 281 us
  waiting for transfers between devices  99.1 us (35%)
  blocking collectives  89.7 us (32%)
  starting transfers between devices  55.3 us (20%)
  between operations  13.4 us (5%)
  matrix products  10.1 us (4%)
  Pallas kernels  5.26 us (2%)
  other arithmetic  4.27 us (2%)
  local copies, waits for them, and re-layouts  3.43 us (1%)
    ppermute x5, waiting for transfers between devices, take(): lax.ppermute(value, axis, [((i + distance) % n, i) for i in range(n)])  60.1 us
    all_to_all x3, waiting for transfers between devices, exchanged_sum(): lax.all_to_all(value, axis, split_axis=0, concat_axis=0, tiled=True)  37.7 us
    ppermute x5, starting transfers between devices, take(): lax.ppermute(value, axis, [((i + distance) % n, i) for i in range(n)])  33.4 us
    all_to_all x1, blocking collectives, exchanged_sum(): lax.all_to_all(value, axis, split_axis=0, concat_axis=0, tiled=True)  28.1 us
    all_to_all x1, blocking collectives, gathered(): return lax.all_to_all(spread, axis, split_axis=0, concat_axis=0, tiled=True)  21.9 us
    all_gather x1, blocking collectives, local(): left = lax.all_gather(gram, 'zl', axis=0, tiled=True)  20.7 us
    all_to_all x3, starting transfers between devices, exchanged_sum(): lax.all_to_all(value, axis, split_axis=0, concat_axis=0, tiled=True)  16.8 us
    all_gather x1, blocking collectives, local(): polynomial = lax.all_gather(polynomial, 'zl', axis=0, tiled=False)  12.9 us
  transfers between devices with their start and end apart: 14, of which 6 were waited for; matrix products, arithmetic and copies ran while one was open for 6% of the time, Pallas kernels for 1%

profile of v8, /device:TPU:1, one launch (start us, length us, event | category | flops | bytes accessed | tf_op | source)
XLA Modules:
  0.0 280.6 jit_solution(17554723984576622258)
XLA Ops:
  6.5 0.7 all-gather.7.cloned.1.call-update
  7.3 0.0 all-gather.11.cloned.1.call-start
  7.3 13.3 %collective-permute-start = (bf16[320,800]{1,0:T(8,128)(2,1)}, bf16[320,800]{1,0:T(8,128)(2,1)S(1)}, u32[]{:S(2)}, u32[]{:S(2)}) collective-permute-start(bf16[320,800]{1,0:T(8,128)(2,1)} %total.1), channel_id=1, source_target_pairs={{32,0},{64,32},{96,64},{0,96},{33,1},{65,33},{97,65},{1,97},{34,2}... | collective-permute-start | bytes 1536008 | tf_op jit(solution)/shard_map/ppermute | solution.py:23
  20.6 1.9 collective-permute-start.1
  22.5 44.7 %collective-permute-done = bf16[320,800]{1,0:T(8,128)(2,1)S(1)} collective-permute-done((bf16[320,800]{1,0:T(8,128)(2,1)}, bf16[320,800]{1,0:T(8,128)(2,1)S(1)}, u32[]{:S(2)}, u32[]{:S(2)}) %collective-permute-start) | collective-permute-done | bytes 512032 | tf_op jit(solution)/shard_map/ppermute | solution.py:23
  67.3 0.8 copy-done.6
  68.1 0.0 all-gather.11.cloned.1.call-update
  68.2 1.6 pad_maximum_fusion
  69.8 0.3 copy-done
  70.2 4.0 %convolution_convert_fusion = bf16[2,640,960]{1,2,0:T(8,128)(2,1)} fusion(bf16[2,640,800]{2,1,0:T(8,128)(2,1)S(1)} %bitcast.57, bf16[960,800,1]{1,0,2:T(8,128)(2,1)S(1)} %bitcast.66), kind=kOutput, calls=%fused_computation | convolution fusion | flops 1967308800 | bytes 6041600 | tf_op jit(solution)/shard_map/rn,csn->crs/dot_general | solution.py:98
  74.2 8.3 %all-to-all-start = ((bf16[8,240,640]{2,1,0:T(8,128)(2,1)}), bf16[8,240,640]{2,1,0:T(8,128)(2,1)}, u32[]{:S(2)}, u32[]{:S(2)}) async-start(bf16[8,240,640]{2,1,0:T(8,128)(2,1)} %bitcast.64), calls=%async_computation | async-start | bytes 4915200 | tf_op jit(solution)/shard_map/all_to_all | solution.py:42
  82.5 0.7 slice.27
  83.3 7.9 %collective-permute-start.2 = (bf16[160,800]{1,0:T(8,128)(2,1)}, bf16[160,800]{1,0:T(8,128)(2,1)S(1)}, u32[]{:S(2)}, u32[]{:S(2)}) collective-permute-start(bf16[160,800]{1,0:T(8,128)(2,1)} %slice.27), channel_id=1, source_target_pairs={{32,0},{64,32},{96,64},{0,96},{33,1},{65,33},{97,65},{1,97},{34,2}... | collective-permute-start | bytes 768008 | tf_op jit(solution)/shard_map/ppermute | solution.py:23
  91.2 1.9 collective-permute-start.3
  93.1 0.0 all-gather.9.cloned.1.call-update
  93.1 14.4 %collective-permute-done.2 = bf16[160,800]{1,0:T(8,128)(2,1)S(1)} collective-permute-done((bf16[160,800]{1,0:T(8,128)(2,1)}, bf16[160,800]{1,0:T(8,128)(2,1)S(1)}, u32[]{:S(2)}, u32[]{:S(2)}) %collective-permute-start.2) | collective-permute-done | bytes 256032 | tf_op jit(solution)/shard_map/ppermute | solution.py:23
  107.6 0.0 collective-permute-done.3
  107.7 1.9 convolution_convert_fusion.1
  109.6 3.3 %all-to-all-done = bf16[8,240,640]{2,1,0:T(8,128)(2,1)} async-done(((bf16[8,240,640]{2,1,0:T(8,128)(2,1)}), bf16[8,240,640]{2,1,0:T(8,128)(2,1)}, u32[]{:S(2)}, u32[]{:S(2)}) %all-to-all-start) | async-done | bytes 2457632 | tf_op jit(solution)/shard_map/all_to_all | solution.py:42
  113.0 2.1 reduce_sum.47
  115.1 4.5 %all-to-all-start.1 = ((bf16[8,80,640]{2,1,0:T(8,128)(2,1)}), bf16[8,80,640]{2,1,0:T(8,128)(2,1)S(1)}, u32[]{:S(2)}, u32[]{:S(2)}) async-start(bf16[8,80,640]{2,1,0:T(8,128)(2,1)} %bitcast.68), calls=%async_computation.1 | async-start | bytes 1638400 | tf_op jit(solution)/shard_map/all_to_all | solution.py:42
  119.6 12.5 %all-to-all-done.1 = bf16[8,80,640]{2,1,0:T(8,128)(2,1)S(1)} async-done(((bf16[8,80,640]{2,1,0:T(8,128)(2,1)}), bf16[8,80,640]{2,1,0:T(8,128)(2,1)S(1)}, u32[]{:S(2)}, u32[]{:S(2)}) %all-to-all-start.1) | async-done | bytes 819232 | tf_op jit(solution)/shard_map/all_to_all | solution.py:42
  132.1 0.1 reduce_sum.48
  132.2 0.1 fusion.6
  132.3 0.1 pad_maximum_fusion.1
  132.4 28.1 %all_to_all.30 = bf16[4,80,640]{2,1,0:T(8,128)(2,1)S(1)} all-to-all(bf16[4,80,640]{2,1,0:T(8,128)(2,1)S(1)} %pad_maximum_fusion.1), channel_id=1, replica_groups=mesh['x'=4,'zh'=4,'zl'=4,'y'=4,'c'=2] {'zl'}, dimensions={0} | all-to-all | bytes 819200 | tf_op jit(solution)/shard_map/all_to_all | solution.py:42
  160.4 0.1 reduce_sum.50
  160.5 1.3 broadcast_in_dim.4
  161.8 4.4 %all-to-all-start.3 = ((bf16[16,80,640]{2,1,0:T(8,128)(2,1)}), bf16[16,80,640]{2,1,0:T(8,128)(2,1)}, u32[]{:S(2)}, u32[]{:S(2)}) async-start(bf16[16,80,640]{2,1,0:T(8,128)(2,1)} %broadcast_in_dim.4), calls=%async_computation.3 | async-start | bytes 3276800 | tf_op jit(solution)/shard_map/all_to_all | solution.py:34
  166.2 0.0 all-gather.13.cloned.1.call-start
  166.3 0.5 all-gather.13.cloned.1.call-update
  166.8 0.7 collective-permute-start.4
  167.5 20.7 %all_gather.28 = bf16[320,640]{1,0:T(8,128)(2,1)S(1)} all-gather(bf16[80,640]{1,0:T(8,128)(2,1)S(1)} %reduce_sum.50), channel_id=1, replica_groups=mesh['x'=4,'zh'=4,'zl'=4,'y'=4,'c'=2] {'zl'}, dimensions={0}, use_global_device_ids=true | all-gather | bytes 512000 | tf_op jit(solution)/shard_map/all_gather | solution.py:129
  188.2 1.7 convolution_convert_fusion.2
  189.9 6.1 %all-gather = bf16[640,640]{1,0:T(8,128)(2,1)S(1)} all-gather(bf16[320,640]{1,0:T(8,128)(2,1)S(1)} %convolution_convert_fusion.2), channel_id=2, replica_groups=mesh['x'=4,'zh'=4,'zl'=4,'y'=4,'c'=2] {'c'}, dimensions={0}, use_global_device_ids=true | all-gather | bytes 1228800 | tf_op jit(solution)/shard_map/all_gather | solution.py:48
  196.0 2.4 fusion
  198.4 3.9 %all-to-all-start.4 = ((bf16[4,80,640]{2,1,0:T(8,128)(2,1)}), bf16[4,80,640]{2,1,0:T(8,128)(2,1)S(1)}, u32[]{:S(2)}, u32[]{:S(2)}) async-start(bf16[4,80,640]{2,1,0:T(8,128)(2,1)} %bitcast.23), calls=%async_computation.4 | async-start | bytes 819200 | tf_op jit(solution)/shard_map/all_to_all | solution.py:42
  202.3 21.8 %all-to-all-done.4 = bf16[4,80,640]{2,1,0:T(8,128)(2,1)S(1)} async-done(((bf16[4,80,640]{2,1,0:T(8,128)(2,1)}), bf16[4,80,640]{2,1,0:T(8,128)(2,1)S(1)}, u32[]{:S(2)}, u32[]{:S(2)}) %all-to-all-start.4) | async-done | bytes 409632 | tf_op jit(solution)/shard_map/all_to_all | solution.py:42
  224.2 0.1 convert_reduce_fusion
  224.2 0.0 all-gather.13.cloned.1.call-done.refs_2_
  224.3 12.9 %all-gather.1 = bf16[320,640]{1,0:T(8,128)(2,1)S(1)} all-gather(bf16[80,640]{1,0:T(8,128)(2,1)S(1)} %add_convert_fusion), channel_id=3, replica_groups=mesh['x'=4,'zh'=4,'zl'=4,'y'=4,'c'=2] {'zl'}, dimensions={0}, use_global_device_ids=true | all-gather | bytes 512000 | tf_op jit(solution)/shard_map/all_gather | solution.py:139
  237.2 0.1 select_select_fusion.3
  237.3 0.1 broadcast_in_dim.5
  237.5 21.9 %all_to_all.31 = bf16[4,80,2560]{2,1,0:T(8,128)(2,1)S(1)} all-to-all(bf16[4,80,2560]{2,1,0:T(8,128)(2,1)S(1)} %broadcast_in_dim.5), channel_id=1, replica_groups=mesh['x'=4,'zh'=4,'zl'=4,'y'=4,'c'=2] {'y'}, dimensions={0} | all-to-all | bytes 3276800 | tf_op jit(solution)/shard_map/all_to_all | solution.py:34
  259.4 8.4 %collective-permute-start.5 = (bf16[320,2560]{1,0:T(8,128)(2,1)S(1)}, bf16[320,2560]{1,0:T(8,128)(2,1)S(1)}, u32[]{:S(2)}, u32[]{:S(2)}) collective-permute-start(bf16[320,2560]{1,0:T(8,128)(2,1)S(1)} %bitcast.59), channel_id=1, source_target_pairs={{1,0},{0,1},{3,2},{2,3},{5,4},{4,5},{7,6},{6,7},{9,8},{8,9},{11,10... | collective-permute-start | bytes 4915208 | tf_op jit(solution)/shard_map/ppermute | solution.py:23
  267.8 2.1 shard_map.17.total
  270.0 0.9 collective-permute-done.5.left
  270.9 3.1 %shard_map.18 = f32[320,800]{1,0:T(8,128)} custom-call(f32[320,800]{1,0:T(8,128)S(1)} %shard_map.17.total, bf16[320,2560]{1,0:T(8,128)(2,1)S(1)} %collective-permute-done.5.left, bf16[1280,800]{1,0:T(8,128)(2,1)S(1)} %copy-done, bf16[1280,800]{1,0:T(8,128)(2,1)S(1)} %copy-done.2, bf16[1280,800]{1,0:T(8,128)(2,1)S(1)} %copy-done.3, ...), custom_call_target="tpu_custom_call" | custom-call | flops 1310720000 | bytes 3686400 | tf_op jit(solution)/shard_map/pallas_call | solution.py:73
  (29 shorter events, 0.2 us)
Async XLA Ops:
  6.5 60.8 %all-gather.7.cloned.1.call-start = ((), (), s32[]{:S(2)}) async-start(), calls=%async_computation.6 | async-start | bytes 2867200 | tf_op jit(solution)/shard_map/all_gather | solution.py:107
  7.3 180.9 %all-gather.11.cloned.1.call-start = ((), (), s32[]{:S(2)}) async-start(), calls=%async_computation.8 | async-start | bytes 2867200 | tf_op jit(solution)/shard_map/all_gather | solution.py:110
  7.3 60.0 %collective-permute-start = (bf16[320,800]{1,0:T(8,128)(2,1)}, bf16[320,800]{1,0:T(8,128)(2,1)S(1)}, u32[]{:S(2)}, u32[]{:S(2)}) collective-permute-start(bf16[320,800]{1,0:T(8,128)(2,1)} %total.1), channel_id=1, source_target_pairs={{32,0},{64,32},{96,64},{0,96},{33,1},{65,33},{97,65},{1,97},{34,2}... | collective-permute-start | bytes 1536008 | tf_op jit(solution)/shard_map/ppermute | solution.py:23
  20.6 46.7 %collective-permute-start.1 = (bf16[320,800]{1,0:T(8,128)(2,1)}, bf16[320,800]{1,0:T(8,128)(2,1)S(1)}, u32[]{:S(2)}, u32[]{:S(2)}) collective-permute-start(bf16[320,800]{1,0:T(8,128)(2,1)} %total.1), channel_id=1, source_target_pairs={{96,0},{0,32},{32,64},{64,96},{97,1},{1,33},{33,65},{65,97},{98,2}... | collective-permute-start | bytes 1536008 | tf_op jit(solution)/shard_map/ppermute | solution.py:23
  67.3 15.2 %copy-start.5 = (bf16[320,800]{1,0:T(8,128)(2,1)}, bf16[320,800]{1,0:T(8,128)(2,1)S(1)}, u32[]{:S(2)}) copy-start(bf16[320,800]{1,0:T(8,128)(2,1)S(1)} %collective-permute-done) | copy-start | bytes 1536004
  67.3 0.9 copy-start.6
  68.2 2.0 copy-start
  74.2 9.1 %copy-start.7 = (bf16[320,800]{1,0:T(8,128)(2,1)S(1)}, bf16[320,800]{1,0:T(8,128)(2,1)}, u32[]{:S(2)}) copy-start(bf16[320,800]{1,0:T(8,128)(2,1)} %copy-done.6) | copy-start | bytes 1536004
  74.2 38.8 %all-to-all-start = ((bf16[8,240,640]{2,1,0:T(8,128)(2,1)}), bf16[8,240,640]{2,1,0:T(8,128)(2,1)}, u32[]{:S(2)}, u32[]{:S(2)}) async-start(bf16[8,240,640]{2,1,0:T(8,128)(2,1)} %bitcast.64), calls=%async_computation | async-start | bytes 4915200 | tf_op jit(solution)/shard_map/all_to_all | solution.py:42
  82.5 105.7 %all-gather.9.cloned.1.call-start = ((), (), s32[]{:S(2)}) async-start(), calls=%async_computation.7 | async-start | bytes 2867200 | tf_op jit(solution)/shard_map/all_gather | solution.py:109
  83.3 24.3 %collective-permute-start.2 = (bf16[160,800]{1,0:T(8,128)(2,1)}, bf16[160,800]{1,0:T(8,128)(2,1)S(1)}, u32[]{:S(2)}, u32[]{:S(2)}) collective-permute-start(bf16[160,800]{1,0:T(8,128)(2,1)} %slice.27), channel_id=1, source_target_pairs={{32,0},{64,32},{96,64},{0,96},{33,1},{65,33},{97,65},{1,97},{34,2}... | collective-permute-start | bytes 768008 | tf_op jit(solution)/shard_map/ppermute | solution.py:23
  91.2 16.4 %collective-permute-start.3 = (bf16[160,800]{1,0:T(8,128)(2,1)S(1)}, bf16[160,800]{1,0:T(8,128)(2,1)S(1)}, u32[]{:S(2)}, u32[]{:S(2)}) collective-permute-start(bf16[160,800]{1,0:T(8,128)(2,1)S(1)} %slice.28), channel_id=1, source_target_pairs={{96,0},{0,32},{32,64},{64,96},{97,1},{1,33},{33,65},{65,97},{98,2}... | collective-permute-start | bytes 768008 | tf_op jit(solution)/shard_map/ppermute | solution.py:23
  107.7 1.9 copy-start.8
  115.1 17.0 %all-to-all-start.1 = ((bf16[8,80,640]{2,1,0:T(8,128)(2,1)}), bf16[8,80,640]{2,1,0:T(8,128)(2,1)S(1)}, u32[]{:S(2)}, u32[]{:S(2)}) async-start(bf16[8,80,640]{2,1,0:T(8,128)(2,1)} %bitcast.68), calls=%async_computation.1 | async-start | bytes 1638400 | tf_op jit(solution)/shard_map/all_to_all | solution.py:42
  161.8 26.4 %all-to-all-start.3 = ((bf16[16,80,640]{2,1,0:T(8,128)(2,1)}), bf16[16,80,640]{2,1,0:T(8,128)(2,1)}, u32[]{:S(2)}, u32[]{:S(2)}) async-start(bf16[16,80,640]{2,1,0:T(8,128)(2,1)} %broadcast_in_dim.4), calls=%async_computation.3 | async-start | bytes 3276800 | tf_op jit(solution)/shard_map/all_to_all | solution.py:34
  166.2 58.0 %all-gather.13.cloned.1.call-start = ((), (), s32[]{:S(2)}) async-start(), calls=%async_computation.9 | async-start | bytes 2867200 | tf_op jit(solution)/shard_map/all_gather | solution.py:122
  166.8 21.4 %collective-permute-start.4 = (bf16[80,640]{1,0:T(8,128)(2,1)S(1)}, bf16[80,640]{1,0:T(8,128)(2,1)S(1)}, u32[]{:S(2)}, u32[]{:S(2)}) collective-permute-start(bf16[80,640]{1,0:T(8,128)(2,1)S(1)} %reduce_sum.50), channel_id=1, source_target_pairs={{0,0},{32,8},{64,16},{96,24},{8,32},{40,40},{72,48},{104,56},{16,6... | collective-permute-start | bytes 307208 | tf_op jit(solution)/shard_map/ppermute | solution.py:128
  198.4 25.7 %all-to-all-start.4 = ((bf16[4,80,640]{2,1,0:T(8,128)(2,1)}), bf16[4,80,640]{2,1,0:T(8,128)(2,1)S(1)}, u32[]{:S(2)}, u32[]{:S(2)}) async-start(bf16[4,80,640]{2,1,0:T(8,128)(2,1)} %bitcast.23), calls=%async_computation.4 | async-start | bytes 819200 | tf_op jit(solution)/shard_map/all_to_all | solution.py:42
  224.2 43.5 %copy-start.4 = (bf16[320,800]{1,0:T(8,128)(2,1)S(1)}, bf16[320,800]{1,0:T(8,128)(2,1)}, u32[]{:S(2)}) copy-start(bf16[320,800]{1,0:T(8,128)(2,1)} %total.1) | copy-start | bytes 1536004
  237.2 30.6 %copy-start.3 = (bf16[1280,800]{1,0:T(8,128)(2,1)S(1)}, bf16[1280,800]{1,0:T(8,128)(2,1)}, u32[]{:S(2)}) copy-start(bf16[1280,800]{1,0:T(8,128)(2,1)} %all-gather.13.cloned.1.call-done.refs_2_) | copy-start | bytes 6144004
  237.3 30.5 %copy-start.2 = (bf16[1280,800]{1,0:T(8,128)(2,1)S(1)}, bf16[1280,800]{1,0:T(8,128)(2,1)}, u32[]{:S(2)}) copy-start(bf16[1280,800]{1,0:T(8,128)(2,1)} %all-gather.9.cloned.1.call-done.refs_1_) | copy-start | bytes 6144004
  237.5 30.4 %copy-start.1 = (bf16[1280,800]{1,0:T(8,128)(2,1)S(1)}, bf16[1280,800]{1,0:T(8,128)(2,1)}, u32[]{:S(2)}) copy-start(bf16[1280,800]{1,0:T(8,128)(2,1)} %all-gather.11.cloned.1.call-done.refs_3_) | copy-start | bytes 6144004
  259.4 11.5 %collective-permute-start.5 = (bf16[320,2560]{1,0:T(8,128)(2,1)S(1)}, bf16[320,2560]{1,0:T(8,128)(2,1)S(1)}, u32[]{:S(2)}, u32[]{:S(2)}) collective-permute-start(bf16[320,2560]{1,0:T(8,128)(2,1)S(1)} %bitcast.59), channel_id=1, source_target_pairs={{1,0},{0,1},{3,2},{2,3},{5,4},{4,5},{7,6},{6,7},{9,8},{8,9},{11,10... | collective-permute-start | bytes 4915208 | tf_op jit(solution)/shard_map/ppermute | solution.py:23
Sparse Core Ops, SparseCore 0:
  9.5 45.4 all-gather.6
  68.3 44.5 all-gather.10
  115.0 40.2 all-gather.8
  168.8 38.0 all-gather.12

commit v9 on v8

--- a/solution.py
+++ b/solution.py
@@ -38,9 +38,12 @@
     return [value] + [take(value, axis, distance) for distance in (1, 2, 3)]
 
 
+def exchanged(value, axis):
+    return lax.all_to_all(value, axis, split_axis=0, concat_axis=0, tiled=True)
+
+
 def exchanged_sum(value, axis):
-    received = lax.all_to_all(value, axis, split_axis=0, concat_axis=0, tiled=True)
-    return received.astype(F32).sum(0)
+    return exchanged(value, axis).astype(F32).sum(0)
 
 
 def matmul_over_c(block, keep, give):
@@ -100,8 +103,8 @@
         )
         return part.astype(BF16).reshape(8, -1, pair)
 
-    def summed_tiles(part):
-        return exchanged_sum(part, ("c", "y")).astype(BF16).reshape(-1, slab, pair)
+    def summed_tiles(parts):
+        return parts.astype(F32).sum(0).astype(BF16).reshape(-1, slab, pair)
 
     upper, lower = take(iterate, "zh", 1), take(iterate, "zh", -1)
     mine = lax.all_gather(iterate, "x", axis=0, tiled=True)
@@ -115,10 +118,10 @@
 
     sides = jnp.stack([iterate, upper, lower]).reshape(3, 4, slab, width)
     sides = partial_tiles(sides.transpose(1, 0, 2, 3).reshape(3 * rows, width), mine)
-    sides = summed_tiles(sides)
-    across = partial_tiles(opposite, mine)
+    sides = exchanged(sides, ("c", "y"))
+    across = matmul_over_c(opposite, *columns(mine)).reshape(4, slab, pair)
     sides, across = lax.optimization_barrier((sides, across))
-    across = summed_tiles(across)
+    sides, across = summed_tiles(sides), summed_tiles(exchanged(across, "y"))
     opposite = lax.all_gather(opposite, "x", axis=0, tiled=True)
 
     by_l = jnp.stack(rolled([sides[0], sides[1], across[0], sides[2]], (4 - h) % 4))

time: 281 us -> 275 us (0.979)
  waiting for transfers between devices: 99.1 us -> 93.9 us
  blocking collectives: 89.7 us -> 86.8 us
    all_to_all x3, waiting for transfers between devices: 37.7 us -> 29.3 us  [exchanged(): return lax.all_to_all(value, axis, split_axis=0, concat_axis=0, tiled=True)]
    all_gather x1 -> x2, blocking collectives: 6.1 us -> 12 us  [matmul_over_c(): lax.all_gather(sent, 'c', axis=0, tiled=False)[1 - lax.axis_index('c')]]
    all_to_all x1, blocking collectives: 28.1 us -> 23.5 us  [exchanged(): return lax.all_to_all(value, axis, split_axis=0, concat_axis=0, tiled=True)]
    ppermute x5, waiting for transfers between devices: 60.1 us -> 63.3 us  [take(): lax.ppermute(value, axis, [((i + distance) % n, i) for i in range(n)])]
    dot_general x2 -> x1, matrix products: 5.95 us -> 4.01 us  [partial_tiles(): jnp.einsum('rn,csn->crs', block, others.reshape(2, pair, width), preferre...]
where the time goes in v9:
time: 275 us; the launch traced here: 274 us
  waiting for transfers between devices  93.9 us (34%)
  blocking collectives  86.8 us (32%)
  starting transfers between devices  56.2 us (20%)
  between operations  13.4 us (5%)
  matrix products  10.3 us (4%)
  Pallas kernels  5.26 us (2%)
  local copies, waits for them, and re-layouts  4.33 us (2%)
  other arithmetic  4.22 us (2%)
    ppermute x5, waiting for transfers between devices, take(): lax.ppermute(value, axis, [((i + distance) % n, i) for i in range(n)])  63.3 us
    ppermute x5, starting transfers between devices, take(): lax.ppermute(value, axis, [((i + distance) % n, i) for i in range(n)])  33.9 us
    all_to_all x3, waiting for transfers between devices, exchanged(): return lax.all_to_all(value, axis, split_axis=0, concat_axis=0, tiled=True)  29.3 us
    all_to_all x1, blocking collectives, exchanged(): return lax.all_to_all(value, axis, split_axis=0, concat_axis=0, tiled=True)  23.5 us
    all_gather x1, blocking collectives, local(): left = lax.all_gather(gram, 'zl', axis=0, tiled=True)  20.1 us
    all_to_all x1, blocking collectives, gathered(): return lax.all_to_all(spread, axis, split_axis=0, concat_axis=0, tiled=True)  19.4 us
    all_to_all x3, starting transfers between devices, exchanged(): return lax.all_to_all(value, axis, split_axis=0, concat_axis=0, tiled=True)  16.4 us
    all_gather x2, blocking collectives, matmul_over_c(): lax.all_gather(sent, 'c', axis=0, tiled=False)[1 - lax.axis_index('c')]  12 us
  transfers between devices with their start and end apart: 14, of which 6 were waited for; matrix products, arithmetic and copies ran while one was open for 6% of the time, Pallas kernels for 1%

profile of v9, /device:TPU:1, one launch (start us, length us, event | category | flops | bytes accessed | tf_op | source)
XLA Modules:
  0.0 274.4 jit_solution(1258859921473633442)
XLA Ops:
  6.5 0.7 all-gather.8.cloned.1.call-update
  7.3 0.0 all-gather.10.cloned.1.call-start
  7.3 13.3 %collective-permute-start = (bf16[320,800]{1,0:T(8,128)(2,1)}, bf16[320,800]{1,0:T(8,128)(2,1)S(1)}, u32[]{:S(2)}, u32[]{:S(2)}) collective-permute-start(bf16[320,800]{1,0:T(8,128)(2,1)} %total.1), channel_id=1, source_target_pairs={{32,0},{64,32},{96,64},{0,96},{33,1},{65,33},{97,65},{1,97},{34,2}... | collective-permute-start | bytes 1536008 | tf_op jit(solution)/shard_map/ppermute | solution.py:23
  20.6 1.9 collective-permute-start.1
  22.5 44.7 %collective-permute-done = bf16[320,800]{1,0:T(8,128)(2,1)S(1)} collective-permute-done((bf16[320,800]{1,0:T(8,128)(2,1)}, bf16[320,800]{1,0:T(8,128)(2,1)S(1)}, u32[]{:S(2)}, u32[]{:S(2)}) %collective-permute-start) | collective-permute-done | bytes 512032 | tf_op jit(solution)/shard_map/ppermute | solution.py:23
  67.3 0.8 copy-done.5
  68.1 1.6 pad_maximum_fusion
  69.8 0.3 copy-done
  70.1 4.0 %convolution_convert_fusion = bf16[2,640,960]{1,2,0:T(8,128)(2,1)} fusion(bf16[2,640,800]{2,1,0:T(8,128)(2,1)S(1)} %bitcast.57, bf16[960,800,1]{1,0,2:T(8,128)(2,1)S(1)} %bitcast.67), kind=kOutput, calls=%fused_computation | convolution fusion | flops 1967308800 | bytes 6041600 | tf_op jit(solution)/shard_map/rn,csn->crs/dot_general | solution.py:101
  74.1 8.3 %all-to-all-start = ((bf16[8,240,640]{2,1,0:T(8,128)(2,1)}), bf16[8,240,640]{2,1,0:T(8,128)(2,1)}, u32[]{:S(2)}, u32[]{:S(2)}) async-start(bf16[8,240,640]{2,1,0:T(8,128)(2,1)} %bitcast.65), calls=%async_computation | async-start | bytes 4915200 | tf_op jit(solution)/shard_map/all_to_all | solution.py:42
  82.5 0.7 slice.30
  83.2 7.9 %collective-permute-start.2 = (bf16[160,800]{1,0:T(8,128)(2,1)}, bf16[160,800]{1,0:T(8,128)(2,1)S(1)}, u32[]{:S(2)}, u32[]{:S(2)}) collective-permute-start(bf16[160,800]{1,0:T(8,128)(2,1)} %slice.30), channel_id=1, source_target_pairs={{32,0},{64,32},{96,64},{0,96},{33,1},{65,33},{97,65},{1,97},{34,2}... | collective-permute-start | bytes 768008 | tf_op jit(solution)/shard_map/ppermute | solution.py:23
  91.1 1.9 collective-permute-start.3
  93.1 14.5 %collective-permute-done.2 = bf16[160,800]{1,0:T(8,128)(2,1)S(1)} collective-permute-done((bf16[160,800]{1,0:T(8,128)(2,1)}, bf16[160,800]{1,0:T(8,128)(2,1)S(1)}, u32[]{:S(2)}, u32[]{:S(2)}) %collective-permute-start.2) | collective-permute-done | bytes 256032 | tf_op jit(solution)/shard_map/ppermute | solution.py:23
  107.6 3.1 %collective-permute-done.3 = bf16[160,800]{1,0:T(8,128)(2,1)} collective-permute-done((bf16[160,800]{1,0:T(8,128)(2,1)S(1)}, bf16[160,800]{1,0:T(8,128)(2,1)}, u32[]{:S(2)}, u32[]{:S(2)}) %collective-permute-start.3) | collective-permute-done | bytes 256032 | tf_op jit(solution)/shard_map/ppermute | solution.py:23
  110.7 1.0 constant_dynamic-update-slice_fusion
  111.7 0.7 convolution_convert_fusion.1
  112.4 5.6 %all-gather = bf16[640,640]{1,0:T(8,128)(2,1)S(1)} all-gather(bf16[320,640]{1,0:T(8,128)(2,1)S(1)} %convolution_convert_fusion.1), channel_id=2, replica_groups=mesh['x'=4,'zh'=4,'zl'=4,'y'=4,'c'=2] {'c'}, dimensions={0}, use_global_device_ids=true | all-gather | bytes 1228800 | tf_op jit(solution)/shard_map/all_gather | solution.py:51
  118.0 1.5 fusion
  119.5 4.2 %all-to-all-start.1 = ((bf16[4,80,640]{2,1,0:T(8,128)(2,1)}), bf16[4,80,640]{2,1,0:T(8,128)(2,1)S(1)}, u32[]{:S(2)}, u32[]{:S(2)}) async-start(bf16[4,80,640]{2,1,0:T(8,128)(2,1)} %bitcast.69), calls=%async_computation.1 | async-start | bytes 819200 | tf_op jit(solution)/shard_map/all_to_all | solution.py:42
  123.7 2.1 reduce_sum.45
  125.8 5.3 %all-to-all-done.1 = bf16[4,80,640]{2,1,0:T(8,128)(2,1)S(1)} async-done(((bf16[4,80,640]{2,1,0:T(8,128)(2,1)}), bf16[4,80,640]{2,1,0:T(8,128)(2,1)S(1)}, u32[]{:S(2)}, u32[]{:S(2)}) %all-to-all-start.1) | async-done | bytes 409632 | tf_op jit(solution)/shard_map/all_to_all | solution.py:42
  131.1 0.1 reduce_sum.46
  131.1 0.1 select_bitcast_fusion.3
  131.2 0.1 pad_maximum_fusion.1
  131.3 23.5 %all_to_all.30 = bf16[4,80,640]{2,1,0:T(8,128)(2,1)S(1)} all-to-all(bf16[4,80,640]{2,1,0:T(8,128)(2,1)S(1)} %pad_maximum_fusion.1), channel_id=1, replica_groups=mesh['x'=4,'zh'=4,'zl'=4,'y'=4,'c'=2] {'zl'}, dimensions={0} | all-to-all | bytes 819200 | tf_op jit(solution)/shard_map/all_to_all | solution.py:42
  154.8 0.1 reduce_sum.47
  154.8 1.3 broadcast_in_dim.4
  156.1 5.0 %all-to-all-start.3 = ((bf16[16,80,640]{2,1,0:T(8,128)(2,1)}), bf16[16,80,640]{2,1,0:T(8,128)(2,1)}, u32[]{:S(2)}, u32[]{:S(2)}) async-start(bf16[16,80,640]{2,1,0:T(8,128)(2,1)} %broadcast_in_dim.4), calls=%async_computation.3 | async-start | bytes 3276800 | tf_op jit(solution)/shard_map/all_to_all | solution.py:34
  161.2 0.0 all-gather.14.cloned.1.call-start
  161.2 0.5 all-gather.14.cloned.1.call-update
  161.7 0.7 collective-permute-start.4
  162.4 20.1 %all_gather.36 = bf16[320,640]{1,0:T(8,128)(2,1)S(1)} all-gather(bf16[80,640]{1,0:T(8,128)(2,1)S(1)} %reduce_sum.47), channel_id=1, replica_groups=mesh['x'=4,'zh'=4,'zl'=4,'y'=4,'c'=2] {'zl'}, dimensions={0}, use_global_device_ids=true | all-gather | bytes 512000 | tf_op jit(solution)/shard_map/all_gather | solution.py:132
  182.6 1.7 convolution_convert_fusion.2
  184.2 6.4 %all-gather.1 = bf16[640,640]{1,0:T(8,128)(2,1)S(1)} all-gather(bf16[320,640]{1,0:T(8,128)(2,1)S(1)} %convolution_convert_fusion.2), channel_id=3, replica_groups=mesh['x'=4,'zh'=4,'zl'=4,'y'=4,'c'=2] {'c'}, dimensions={0}, use_global_device_ids=true | all-gather | bytes 1228800 | tf_op jit(solution)/shard_map/all_gather | solution.py:51
  190.7 2.4 fusion.1
  193.1 4.0 %all-to-all-start.4 = ((bf16[4,80,640]{2,1,0:T(8,128)(2,1)}), bf16[4,80,640]{2,1,0:T(8,128)(2,1)S(1)}, u32[]{:S(2)}, u32[]{:S(2)}) async-start(bf16[4,80,640]{2,1,0:T(8,128)(2,1)} %bitcast.27), calls=%async_computation.4 | async-start | bytes 819200 | tf_op jit(solution)/shard_map/all_to_all | solution.py:42
  197.1 24.0 %all-to-all-done.4 = bf16[4,80,640]{2,1,0:T(8,128)(2,1)S(1)} async-done(((bf16[4,80,640]{2,1,0:T(8,128)(2,1)}), bf16[4,80,640]{2,1,0:T(8,128)(2,1)S(1)}, u32[]{:S(2)}, u32[]{:S(2)}) %all-to-all-start.4) | async-done | bytes 409632 | tf_op jit(solution)/shard_map/all_to_all | solution.py:42
  221.1 0.1 convert_reduce_fusion
  221.2 0.0 all-gather.14.cloned.1.call-done.refs_2_
  221.3 11.8 %all-gather.2 = bf16[320,640]{1,0:T(8,128)(2,1)S(1)} all-gather(bf16[80,640]{1,0:T(8,128)(2,1)S(1)} %add_convert_fusion), channel_id=4, replica_groups=mesh['x'=4,'zh'=4,'zl'=4,'y'=4,'c'=2] {'zl'}, dimensions={0}, use_global_device_ids=true | all-gather | bytes 512000 | tf_op jit(solution)/shard_map/all_gather | solution.py:142
  233.1 0.1 select_select_fusion.3
  233.2 0.1 broadcast_in_dim.5
  233.3 19.4 %all_to_all.31 = bf16[4,80,2560]{2,1,0:T(8,128)(2,1)S(1)} all-to-all(bf16[4,80,2560]{2,1,0:T(8,128)(2,1)S(1)} %broadcast_in_dim.5), channel_id=1, replica_groups=mesh['x'=4,'zh'=4,'zl'=4,'y'=4,'c'=2] {'y'}, dimensions={0} | all-to-all | bytes 3276800 | tf_op jit(solution)/shard_map/all_to_all | solution.py:34
  252.7 8.9 %collective-permute-start.5 = (bf16[320,2560]{1,0:T(8,128)(2,1)S(1)}, bf16[320,2560]{1,0:T(8,128)(2,1)S(1)}, u32[]{:S(2)}, u32[]{:S(2)}) collective-permute-start(bf16[320,2560]{1,0:T(8,128)(2,1)S(1)} %bitcast.60), channel_id=1, source_target_pairs={{1,0},{0,1},{3,2},{2,3},{5,4},{4,5},{7,6},{6,7},{9,8},{8,9},{11,10... | collective-permute-start | bytes 4915208 | tf_op jit(solution)/shard_map/ppermute | solution.py:23
  261.7 2.1 shard_map.17.total
  263.9 0.9 collective-permute-done.5.left
  264.8 3.1 %shard_map.18 = f32[320,800]{1,0:T(8,128)} custom-call(f32[320,800]{1,0:T(8,128)S(1)} %shard_map.17.total, bf16[320,2560]{1,0:T(8,128)(2,1)S(1)} %collective-permute-done.5.left, bf16[1280,800]{1,0:T(8,128)(2,1)S(1)} %copy-done, bf16[1280,800]{1,0:T(8,128)(2,1)S(1)} %copy-done.1, bf16[1280,800]{1,0:T(8,128)(2,1)S(1)} %copy-done.3, ...), custom_call_target="tpu_custom_call" | custom-call | flops 1310720000 | bytes 3686400 | tf_op jit(solution)/shard_map/pallas_call | solution.py:76
  (31 shorter events, 0.2 us)
Async XLA Ops:
  6.5 60.8 %all-gather.8.cloned.1.call-start = ((), (), s32[]{:S(2)}) async-start(), calls=%async_computation.6 | async-start | bytes 2867200 | tf_op jit(solution)/shard_map/all_gather | solution.py:110
  7.3 175.3 %all-gather.10.cloned.1.call-start = ((), (), s32[]{:S(2)}) async-start(), calls=%async_computation.7 | async-start | bytes 2867200 | tf_op jit(solution)/shard_map/all_gather | solution.py:112
  7.3 60.0 %collective-permute-start = (bf16[320,800]{1,0:T(8,128)(2,1)}, bf16[320,800]{1,0:T(8,128)(2,1)S(1)}, u32[]{:S(2)}, u32[]{:S(2)}) collective-permute-start(bf16[320,800]{1,0:T(8,128)(2,1)} %total.1), channel_id=1, source_target_pairs={{32,0},{64,32},{96,64},{0,96},{33,1},{65,33},{97,65},{1,97},{34,2}... | collective-permute-start | bytes 1536008 | tf_op jit(solution)/shard_map/ppermute | solution.py:23
  20.6 46.7 %collective-permute-start.1 = (bf16[320,800]{1,0:T(8,128)(2,1)}, bf16[320,800]{1,0:T(8,128)(2,1)S(1)}, u32[]{:S(2)}, u32[]{:S(2)}) collective-permute-start(bf16[320,800]{1,0:T(8,128)(2,1)} %total.1), channel_id=1, source_target_pairs={{96,0},{0,32},{32,64},{64,96},{97,1},{1,33},{33,65},{65,97},{98,2}... | collective-permute-start | bytes 1536008 | tf_op jit(solution)/shard_map/ppermute | solution.py:23
  67.3 0.8 copy-start.5
  67.3 15.9 %copy-start.7 = (bf16[320,800]{1,0:T(8,128)(2,1)}, bf16[320,800]{1,0:T(8,128)(2,1)S(1)}, u32[]{:S(2)}) copy-start(bf16[320,800]{1,0:T(8,128)(2,1)S(1)} %collective-permute-done.1) | copy-start | bytes 1536004
  68.1 2.0 copy-start
  74.1 8.3 %copy-start.6 = (bf16[320,800]{1,0:T(8,128)(2,1)S(1)}, bf16[320,800]{1,0:T(8,128)(2,1)}, u32[]{:S(2)}) copy-start(bf16[320,800]{1,0:T(8,128)(2,1)} %copy-done.5) | copy-start | bytes 1536004
  74.1 45.4 %all-to-all-start = ((bf16[8,240,640]{2,1,0:T(8,128)(2,1)}), bf16[8,240,640]{2,1,0:T(8,128)(2,1)}, u32[]{:S(2)}, u32[]{:S(2)}) async-start(bf16[8,240,640]{2,1,0:T(8,128)(2,1)} %bitcast.65), calls=%async_computation | async-start | bytes 4915200 | tf_op jit(solution)/shard_map/all_to_all | solution.py:42
  82.5 100.1 %all-gather.12.cloned.1.call-start = ((), (), s32[]{:S(2)}) async-start(), calls=%async_computation.8 | async-start | bytes 2867200 | tf_op jit(solution)/shard_map/all_gather | solution.py:113
  83.2 24.4 %collective-permute-start.2 = (bf16[160,800]{1,0:T(8,128)(2,1)}, bf16[160,800]{1,0:T(8,128)(2,1)S(1)}, u32[]{:S(2)}, u32[]{:S(2)}) collective-permute-start(bf16[160,800]{1,0:T(8,128)(2,1)} %slice.30), channel_id=1, source_target_pairs={{32,0},{64,32},{96,64},{0,96},{33,1},{65,33},{97,65},{1,97},{34,2}... | collective-permute-start | bytes 768008 | tf_op jit(solution)/shard_map/ppermute | solution.py:23
  91.1 19.6 %collective-permute-start.3 = (bf16[160,800]{1,0:T(8,128)(2,1)S(1)}, bf16[160,800]{1,0:T(8,128)(2,1)}, u32[]{:S(2)}, u32[]{:S(2)}) collective-permute-start(bf16[160,800]{1,0:T(8,128)(2,1)S(1)} %slice.31), channel_id=1, source_target_pairs={{96,0},{0,32},{32,64},{64,96},{97,1},{1,33},{33,65},{65,97},{98,2}... | collective-permute-start | bytes 768008 | tf_op jit(solution)/shard_map/ppermute | solution.py:23
  111.7 6.3 %copy-start.8 = (bf16[320,800]{1,0:T(8,128)(2,1)}, bf16[320,800]{1,0:T(8,128)(2,1)S(1)}, u32[]{:S(2)}) copy-start(bf16[320,800]{1,0:T(8,128)(2,1)S(1)} %constant_dynamic-update-slice_fusion) | copy-start | bytes 1536004
  119.5 11.5 %all-to-all-start.1 = ((bf16[4,80,640]{2,1,0:T(8,128)(2,1)}), bf16[4,80,640]{2,1,0:T(8,128)(2,1)S(1)}, u32[]{:S(2)}, u32[]{:S(2)}) async-start(bf16[4,80,640]{2,1,0:T(8,128)(2,1)} %bitcast.69), calls=%async_computation.1 | async-start | bytes 819200 | tf_op jit(solution)/shard_map/all_to_all | solution.py:42
  156.1 26.4 %all-to-all-start.3 = ((bf16[16,80,640]{2,1,0:T(8,128)(2,1)}), bf16[16,80,640]{2,1,0:T(8,128)(2,1)}, u32[]{:S(2)}, u32[]{:S(2)}) async-start(bf16[16,80,640]{2,1,0:T(8,128)(2,1)} %broadcast_in_dim.4), calls=%async_computation.3 | async-start | bytes 3276800 | tf_op jit(solution)/shard_map/all_to_all | solution.py:34
  161.2 60.0 %all-gather.14.cloned.1.call-start = ((), (), s32[]{:S(2)}) async-start(), calls=%async_computation.9 | async-start | bytes 2867200 | tf_op jit(solution)/shard_map/all_gather | solution.py:125
  161.7 20.8 %collective-permute-start.4 = (bf16[80,640]{1,0:T(8,128)(2,1)S(1)}, bf16[80,640]{1,0:T(8,128)(2,1)S(1)}, u32[]{:S(2)}, u32[]{:S(2)}) collective-permute-start(bf16[80,640]{1,0:T(8,128)(2,1)S(1)} %reduce_sum.47), channel_id=1, source_target_pairs={{0,0},{32,8},{64,16},{96,24},{8,32},{40,40},{72,48},{104,56},{16,6... | collective-permute-start | bytes 307208 | tf_op jit(solution)/shard_map/ppermute | solution.py:131
  193.1 28.0 %all-to-all-start.4 = ((bf16[4,80,640]{2,1,0:T(8,128)(2,1)}), bf16[4,80,640]{2,1,0:T(8,128)(2,1)S(1)}, u32[]{:S(2)}, u32[]{:S(2)}) async-start(bf16[4,80,640]{2,1,0:T(8,128)(2,1)} %bitcast.27), calls=%async_computation.4 | async-start | bytes 819200 | tf_op jit(solution)/shard_map/all_to_all | solution.py:42
  221.2 40.5 %copy-start.4 = (bf16[320,800]{1,0:T(8,128)(2,1)S(1)}, bf16[320,800]{1,0:T(8,128)(2,1)}, u32[]{:S(2)}) copy-start(bf16[320,800]{1,0:T(8,128)(2,1)} %total.1) | copy-start | bytes 1536004
  233.1 28.6 %copy-start.3 = (bf16[1280,800]{1,0:T(8,128)(2,1)S(1)}, bf16[1280,800]{1,0:T(8,128)(2,1)}, u32[]{:S(2)}) copy-start(bf16[1280,800]{1,0:T(8,128)(2,1)} %all-gather.14.cloned.1.call-done.refs_2_) | copy-start | bytes 6144004
  233.2 28.5 %copy-start.2 = (bf16[1280,800]{1,0:T(8,128)(2,1)S(1)}, bf16[1280,800]{1,0:T(8,128)(2,1)}, u32[]{:S(2)}) copy-start(bf16[1280,800]{1,0:T(8,128)(2,1)} %all-gather.12.cloned.1.call-done.refs_3_) | copy-start | bytes 6144004
  233.3 28.4 %copy-start.1 = (bf16[1280,800]{1,0:T(8,128)(2,1)S(1)}, bf16[1280,800]{1,0:T(8,128)(2,1)}, u32[]{:S(2)}) copy-start(bf16[1280,800]{1,0:T(8,128)(2,1)} %all-gather.10.cloned.1.call-done.refs_1_) | copy-start | bytes 6144004
  252.7 12.1 %collective-permute-start.5 = (bf16[320,2560]{1,0:T(8,128)(2,1)S(1)}, bf16[320,2560]{1,0:T(8,128)(2,1)S(1)}, u32[]{:S(2)}, u32[]{:S(2)}) collective-permute-start(bf16[320,2560]{1,0:T(8,128)(2,1)S(1)} %bitcast.60), channel_id=1, source_target_pairs={{1,0},{0,1},{3,2},{2,3},{5,4},{4,5},{7,6},{6,7},{9,8},{8,9},{11,10... | collective-permute-start | bytes 4915208 | tf_op jit(solution)/shard_map/ppermute | solution.py:23
Sparse Core Ops, SparseCore 0:
  9.5 45.4 all-gather.7
  68.2 43.7 all-gather.9
  114.2 40.2 all-gather.11
  163.8 38.4 all-gather.13

commit v10 on v9

--- a/solution.py
+++ b/solution.py
@@ -21,6 +21,15 @@
 def take(value, axis, distance):
     n = lax.axis_size(axis)
     return lax.ppermute(value, axis, [((i + distance) % n, i) for i in range(n)])
+
+
+def shifted(value, step):
+    route = [
+        (h * 2 + c, (h + (step if c == 0 else -step)) % 4 * 2 + c)
+        for h in range(4)
+        for c in range(2)
+    ]
+    return lax.ppermute(value, ("zh", "c"), route)
 
 
 def rolled(parts, start):
@@ -59,12 +68,9 @@
     c = lax.axis_index("c")
     start = pl.multiple_of((1 - c if other else c) * pair, pair)
     value = None
-    for e, block in enumerate(blocks):
-        part = jnp.dot(
-            left[:, e * pair : (e + 1) * pair],
-            block[pl.ds(start, pair), :],
-            preferred_element_type=F32,
-        )
+    for e, block in zip((0, 3 - 2 * c, 2, 1 + 2 * c), blocks):
+        part = left[:, pl.ds(pl.multiple_of(e * pair, 128), pair)]
+        part = jnp.dot(part, block[pl.ds(start, pair), :], preferred_element_type=F32)
         value = part if value is None else value + part
     if other:
         out[...] = 0.2 * math.sqrt(out.shape[1] * 32) * (total[...] + value)
@@ -106,14 +112,15 @@
     def summed_tiles(parts):
         return parts.astype(F32).sum(0).astype(BF16).reshape(-1, slab, pair)
 
-    upper, lower = take(iterate, "zh", 1), take(iterate, "zh", -1)
+    first, second = shifted(iterate, 1), shifted(iterate, -1)
     mine = lax.all_gather(iterate, "x", axis=0, tiled=True)
-    upper, lower, mine = lax.optimization_barrier((upper, lower, mine))
-    above = lax.all_gather(upper, "x", axis=0, tiled=True)
-    below = lax.all_gather(lower, "x", axis=0, tiled=True)
+    first, second, mine = lax.optimization_barrier((first, second, mine))
+    firsts = lax.all_gather(first, "x", axis=0, tiled=True)
+    seconds = lax.all_gather(second, "x", axis=0, tiled=True)
+    upper, lower = jnp.where(c == 0, second, first), jnp.where(c == 0, first, second)
     cut = rows // 2
-    opposite = lax.optimization_barrier((upper[:cut], lower[cut:]))
-    opposite = (take(opposite[0], "zh", 1), take(opposite[1], "zh", -1))
+    opposite = lax.optimization_barrier((first[:cut], second[cut:]))
+    opposite = (shifted(opposite[0], 1), shifted(opposite[1], -1))
     opposite = jnp.concatenate(lax.optimization_barrier(opposite), axis=0)
 
     sides = jnp.stack([iterate, upper, lower]).reshape(3, 4, slab, width)
@@ -131,8 +138,8 @@
     turned = lax.ppermute(gram, ("zh", "zl"), turned)
     left = lax.all_gather(gram, "zl", axis=0, tiled=True)
     right = gathered(gram, ("x", "y")).reshape(2 * pair, pair)
-    left, right, above, below, turned = lax.optimization_barrier(
-        (left, right, above, below, turned)
+    left, right, firsts, seconds, turned = lax.optimization_barrier(
+        (left, right, firsts, seconds, turned)
     )
     square = matmul_over_c(left, *columns(right))
     square = exchanged_sum(square.reshape(4, slab, pair), "zh")
@@ -144,7 +151,7 @@
     polynomial = gathered(polynomial, "y").reshape(rows, 4 * pair)
     swapped = take(polynomial, "c", 1)
 
-    blocks = (mine, above, opposite, below)
+    blocks = (mine, firsts, opposite, seconds)
     total = add_product(False, iterate, polynomial, blocks)
     return add_product(True, total, swapped, blocks)
 

time: 275 us -> 275 us (level)
  blocking collectives: 86.8 us -> 77 us
  local copies, waits for them, and re-layouts: 4.33 us -> 8.02 us
  starting transfers between devices: 56.2 us -> 59.5 us
    ppermute x0 -> x4, waiting for transfers between devices: none -> 64.2 us  [shifted(): return lax.ppermute(value, ('zh', 'c'), route)]
    ppermute x5 -> x1, waiting for transfers between devices: 63.3 us -> 0.92 us  [take(): lax.ppermute(value, axis, [((i + distance) % n, i) for i in range(n)])]
    ppermute x0 -> x4, starting transfers between devices: none -> 25 us  [shifted(): return lax.ppermute(value, ('zh', 'c'), route)]
    ppermute x5 -> x1, starting transfers between devices: 33.9 us -> 8.97 us  [take(): lax.ppermute(value, axis, [((i + distance) % n, i) for i in range(n)])]
    all_to_all x1, blocking collectives: 23.5 us -> 15 us  [exchanged(): return lax.all_to_all(value, axis, split_axis=0, concat_axis=0, tiled=True)]
    all_gather x2, blocking collectives: 12 us -> 8.51 us  [matmul_over_c(): lax.all_gather(sent, 'c', axis=0, tiled=False)[1 - lax.axis_index('c')]]
    all_to_all x3, starting transfers between devices: 16.4 us -> 19.8 us  [exchanged(): return lax.all_to_all(value, axis, split_axis=0, concat_axis=0, tiled=True)]
    all_gather x1, blocking collectives: 20.1 us -> 23 us  [local(): left = lax.all_gather(gram, 'zl', axis=0, tiled=True)]
  transfers between devices with their start and end apart: 14 -> 14, of which waited for: 6 -> 6; matrix products, arithmetic and copies ran while one was open for 6% -> 8% of each run, Pallas kernels for 1% -> 1%
where the time goes in v10:
time: 275 us; the launch traced here: 274 us
  waiting for transfers between devices  93.5 us (34%)
  blocking collectives  77 us (28%)
  starting transfers between devices  59.5 us (22%)
  between operations  13.4 us (5%)
  matrix products  10.4 us (4%)
  local copies, waits for them, and re-layouts  8.02 us (3%)
  other arithmetic  6.65 us (2%)
  Pallas kernels  5.28 us (2%)
    ppermute x4, waiting for transfers between devices, shifted(): return lax.ppermute(value, ('zh', 'c'), route)  64.2 us
    all_to_all x3, waiting for transfers between devices, exchanged(): return lax.all_to_all(value, axis, split_axis=0, concat_axis=0, tiled=True)  27.1 us
    ppermute x4, starting transfers between devices, shifted(): return lax.ppermute(value, ('zh', 'c'), route)  25 us
    all_gather x1, blocking collectives, local(): left = lax.all_gather(gram, 'zl', axis=0, tiled=True)  23 us
    all_to_all x3, starting transfers between devices, exchanged(): return lax.all_to_all(value, axis, split_axis=0, concat_axis=0, tiled=True)  19.8 us
    all_to_all x1, blocking collectives, gathered(): return lax.all_to_all(spread, axis, split_axis=0, concat_axis=0, tiled=True)  18.1 us
    all_to_all x1, blocking collectives, exchanged(): return lax.all_to_all(value, axis, split_axis=0, concat_axis=0, tiled=True)  15 us
    all_gather x1, blocking collectives, local(): polynomial = lax.all_gather(polynomial, 'zl', axis=0, tiled=False)  12.4 us
  transfers between devices with their start and end apart: 14, of which 6 were waited for; matrix products, arithmetic and copies ran while one was open for 8% of the time, Pallas kernels for 1%

profile of v10, /device:TPU:1, one launch (start us, length us, event | category | flops | bytes accessed | tf_op | source)
XLA Modules:
  0.0 273.8 jit_solution(16619245144972588020)
XLA Ops:
  6.5 0.7 all-gather.8.cloned.1.call-update
  7.3 13.3 %collective-permute-start = (bf16[320,800]{1,0:T(8,128)(2,1)}, bf16[320,800]{1,0:T(8,128)(2,1)S(1)}, u32[]{:S(2)}, u32[]{:S(2)}) collective-permute-start(bf16[320,800]{1,0:T(8,128)(2,1)} %total.1), channel_id=1, source_target_pairs={{0,32},{1,97},{32,64},{33,1},{64,96},{65,33},{96,0},{97,65},{2,34}... | collective-permute-start | bytes 1536008 | tf_op jit(solution)/shard_map/ppermute | solution.py:32
  20.6 1.9 collective-permute-start.1
  22.5 44.7 %collective-permute-done = bf16[320,800]{1,0:T(8,128)(2,1)S(1)} collective-permute-done((bf16[320,800]{1,0:T(8,128)(2,1)}, bf16[320,800]{1,0:T(8,128)(2,1)S(1)}, u32[]{:S(2)}, u32[]{:S(2)}) %collective-permute-start) | collective-permute-done | bytes 512032 | tf_op jit(solution)/shard_map/ppermute | solution.py:32
  67.2 0.8 copy-done.5
  68.0 1.2 broadcast_select_fusion.1
  69.2 0.3 pad_maximum_fusion
  69.5 1.4 copy-done
  70.9 4.0 %convolution_convert_fusion = bf16[2,640,960]{1,2,0:T(8,128)(2,1)} fusion(bf16[2,640,800]{2,1,0:T(8,128)(2,1)S(1)} %bitcast.57, bf16[960,800,1]{1,0,2:T(8,128)(2,1)S(1)} %bitcast.67), kind=kOutput, calls=%fused_computation | convolution fusion | flops 1967308800 | bytes 6041600 | tf_op jit(solution)/shard_map/rn,csn->crs/dot_general | solution.py:107
  74.9 7.8 %all-to-all-start = ((bf16[8,240,640]{2,1,0:T(8,128)(2,1)}), bf16[8,240,640]{2,1,0:T(8,128)(2,1)}, u32[]{:S(2)}, u32[]{:S(2)}) async-start(bf16[8,240,640]{2,1,0:T(8,128)(2,1)} %bitcast.63), calls=%async_computation | async-start | bytes 4915200 | tf_op jit(solution)/shard_map/all_to_all | solution.py:51
  82.7 0.7 slice.30
  83.5 1.0 slice.31
  84.4 7.9 %collective-permute-start.2 = (bf16[160,800]{1,0:T(8,128)(2,1)}, bf16[160,800]{1,0:T(8,128)(2,1)S(1)}, u32[]{:S(2)}, u32[]{:S(2)}) collective-permute-start(bf16[160,800]{1,0:T(8,128)(2,1)} %slice.30), channel_id=1, source_target_pairs={{0,32},{1,97},{32,64},{33,1},{64,96},{65,33},{96,0},{97,65},{2,34}... | collective-permute-start | bytes 768008 | tf_op jit(solution)/shard_map/ppermute | solution.py:32
  92.3 1.9 collective-permute-start.3
  94.3 19.3 %collective-permute-done.2 = bf16[160,800]{1,0:T(8,128)(2,1)S(1)} collective-permute-done((bf16[160,800]{1,0:T(8,128)(2,1)}, bf16[160,800]{1,0:T(8,128)(2,1)S(1)}, u32[]{:S(2)}, u32[]{:S(2)}) %collective-permute-start.2) | collective-permute-done | bytes 256032 | tf_op jit(solution)/shard_map/ppermute | solution.py:32
  113.6 0.7 copy-done.9
  114.3 0.2 collective-permute-done.3
  114.5 1.0 constant_dynamic-update-slice_fusion.1
  115.5 1.0 constant_dynamic-update-slice_fusion
  116.5 0.7 convolution_convert_fusion.1
  117.2 2.6 all-gather
  119.8 1.5 fusion
  121.3 4.2 %all-to-all-start.1 = ((bf16[4,80,640]{2,1,0:T(8,128)(2,1)}), bf16[4,80,640]{2,1,0:T(8,128)(2,1)S(1)}, u32[]{:S(2)}, u32[]{:S(2)}) async-start(bf16[4,80,640]{2,1,0:T(8,128)(2,1)} %bitcast.70), calls=%async_computation.1 | async-start | bytes 819200 | tf_op jit(solution)/shard_map/all_to_all | solution.py:51
  125.5 2.8 %reduce_sum.45 = bf16[240,640]{1,0:T(8,128)(2,1)} reduce(bf16[8,240,640]{2,1,0:T(8,128)(2,1)} %all-to-all-done, bf16[]{:T(256)} %constant.36.clone.1), dimensions={0}, to_apply=%region_0.1 | reduce | flops 1075200 | bytes 2764802 | tf_op jit(solution)/shard_map/reduce_sum | solution.py:113
  128.3 4.6 %all-to-all-done.1 = bf16[4,80,640]{2,1,0:T(8,128)(2,1)S(1)} async-done(((bf16[4,80,640]{2,1,0:T(8,128)(2,1)}), bf16[4,80,640]{2,1,0:T(8,128)(2,1)S(1)}, u32[]{:S(2)}, u32[]{:S(2)}) %all-to-all-start.1) | async-done | bytes 409632 | tf_op jit(solution)/shard_map/all_to_all | solution.py:51
  132.9 0.1 reduce_sum.46
  132.9 1.1 select_bitcast_fusion.3
  134.0 0.1 pad_maximum_fusion.1
  134.1 15.0 %all_to_all.30 = bf16[4,80,640]{2,1,0:T(8,128)(2,1)S(1)} all-to-all(bf16[4,80,640]{2,1,0:T(8,128)(2,1)S(1)} %pad_maximum_fusion.1), channel_id=1, replica_groups=mesh['x'=4,'zh'=4,'zl'=4,'y'=4,'c'=2] {'zl'}, dimensions={0} | all-to-all | bytes 819200 | tf_op jit(solution)/shard_map/all_to_all | solution.py:51
  149.1 1.3 broadcast_in_dim.4
  150.4 4.9 %all-to-all-start.3 = ((bf16[16,80,640]{2,1,0:T(8,128)(2,1)}), bf16[16,80,640]{2,1,0:T(8,128)(2,1)}, u32[]{:S(2)}, u32[]{:S(2)}) async-start(bf16[16,80,640]{2,1,0:T(8,128)(2,1)} %broadcast_in_dim.4), calls=%async_computation.3 | async-start | bytes 3276800 | tf_op jit(solution)/shard_map/all_to_all | solution.py:43
  155.4 0.5 all-gather.14.cloned.1.call-update
  155.9 0.7 collective-permute-start.4
  156.6 23.0 %all_gather.36 = bf16[320,640]{1,0:T(8,128)(2,1)S(1)} all-gather(bf16[80,640]{1,0:T(8,128)(2,1)S(1)} %reduce_sum.47), channel_id=1, replica_groups=mesh['x'=4,'zh'=4,'zl'=4,'y'=4,'c'=2] {'zl'}, dimensions={0}, use_global_device_ids=true | all-gather | bytes 512000 | tf_op jit(solution)/shard_map/all_gather | solution.py:139
  179.7 1.7 convolution_convert_fusion.2
  181.4 6.0 %all-gather.1 = bf16[640,640]{1,0:T(8,128)(2,1)S(1)} all-gather(bf16[320,640]{1,0:T(8,128)(2,1)S(1)} %convolution_convert_fusion.2), channel_id=3, replica_groups=mesh['x'=4,'zh'=4,'zl'=4,'y'=4,'c'=2] {'c'}, dimensions={0}, use_global_device_ids=true | all-gather | bytes 1228800 | tf_op jit(solution)/shard_map/all_gather | solution.py:60
  187.3 2.4 fusion.1
  189.8 7.9 %all-to-all-start.4 = ((bf16[4,80,640]{2,1,0:T(8,128)(2,1)}), bf16[4,80,640]{2,1,0:T(8,128)(2,1)S(1)}, u32[]{:S(2)}, u32[]{:S(2)}) async-start(bf16[4,80,640]{2,1,0:T(8,128)(2,1)} %bitcast.68), calls=%async_computation.4 | async-start | bytes 819200 | tf_op jit(solution)/shard_map/all_to_all | solution.py:51
  197.6 22.6 %all-to-all-done.4 = bf16[4,80,640]{2,1,0:T(8,128)(2,1)S(1)} async-done(((bf16[4,80,640]{2,1,0:T(8,128)(2,1)}), bf16[4,80,640]{2,1,0:T(8,128)(2,1)S(1)}, u32[]{:S(2)}, u32[]{:S(2)}) %all-to-all-start.4) | async-done | bytes 409632 | tf_op jit(solution)/shard_map/all_to_all | solution.py:51
  220.3 0.9 add_convert_fusion
  221.2 12.4 %all-gather.2 = bf16[320,640]{1,0:T(8,128)(2,1)S(1)} all-gather(bf16[80,640]{1,0:T(8,128)(2,1)S(1)} %add_convert_fusion), channel_id=4, replica_groups=mesh['x'=4,'zh'=4,'zl'=4,'y'=4,'c'=2] {'zl'}, dimensions={0}, use_global_device_ids=true | all-gather | bytes 512000 | tf_op jit(solution)/shard_map/all_gather | solution.py:149
  233.6 0.1 select_select_fusion.3
  233.8 0.1 broadcast_in_dim.5
  233.9 18.1 %all_to_all.31 = bf16[4,80,2560]{2,1,0:T(8,128)(2,1)S(1)} all-to-all(bf16[4,80,2560]{2,1,0:T(8,128)(2,1)S(1)} %broadcast_in_dim.5), channel_id=1, replica_groups=mesh['x'=4,'zh'=4,'zl'=4,'y'=4,'c'=2] {'y'}, dimensions={0} | all-to-all | bytes 3276800 | tf_op jit(solution)/shard_map/all_to_all | solution.py:43
  252.0 9.0 %collective-permute-start.5 = (bf16[320,2560]{1,0:T(8,128)(2,1)S(1)}, bf16[320,2560]{1,0:T(8,128)(2,1)S(1)}, u32[]{:S(2)}, u32[]{:S(2)}) collective-permute-start(bf16[320,2560]{1,0:T(8,128)(2,1)S(1)} %bitcast.60), channel_id=1, source_target_pairs={{1,0},{0,1},{3,2},{2,3},{5,4},{4,5},{7,6},{6,7},{9,8},{8,9},{11,10... | collective-permute-start | bytes 4915208 | tf_op jit(solution)/shard_map/ppermute | solution.py:23
  261.0 2.1 shard_map.17.total
  263.2 0.9 collective-permute-done.5.left
  264.1 3.1 %shard_map.18 = f32[320,800]{1,0:T(8,128)} custom-call(f32[320,800]{1,0:T(8,128)S(1)} %shard_map.17.total, bf16[320,2560]{1,0:T(8,128)(2,1)S(1)} %collective-permute-done.5.left, bf16[1280,800]{1,0:T(8,128)(2,1)S(1)} %copy-done, bf16[1280,800]{1,0:T(8,128)(2,1)S(1)} %copy-done.1, bf16[1280,800]{1,0:T(8,128)(2,1)S(1)} %copy-done.3, ...), custom_call_target="tpu_custom_call" | custom-call | flops 1310720000 | bytes 3686400 | tf_op jit(solution)/shard_map/pallas_call | solution.py:82
  (36 shorter events, 0.4 us)
Async XLA Ops:
  6.5 60.7 %all-gather.8.cloned.1.call-start = ((), (), s32[]{:S(2)}) async-start(), calls=%async_computation.6 | async-start | bytes 2867200 | tf_op jit(solution)/shard_map/all_gather | solution.py:116
  6.5 62.7 %copy-start.4 = (bf16[320,800]{1,0:T(8,128)(2,1)S(1)}, bf16[320,800]{1,0:T(8,128)(2,1)}, u32[]{:S(2)}) copy-start(bf16[320,800]{1,0:T(8,128)(2,1)} %total.1) | copy-start | bytes 1536004
  7.3 172.4 %all-gather.10.cloned.1.call-start = ((), (), s32[]{:S(2)}) async-start(), calls=%async_computation.7 | async-start | bytes 2867200 | tf_op jit(solution)/shard_map/all_gather | solution.py:118
  7.3 59.9 %collective-permute-start = (bf16[320,800]{1,0:T(8,128)(2,1)}, bf16[320,800]{1,0:T(8,128)(2,1)S(1)}, u32[]{:S(2)}, u32[]{:S(2)}) collective-permute-start(bf16[320,800]{1,0:T(8,128)(2,1)} %total.1), channel_id=1, source_target_pairs={{0,32},{1,97},{32,64},{33,1},{64,96},{65,33},{96,0},{97,65},{2,34}... | collective-permute-start | bytes 1536008 | tf_op jit(solution)/shard_map/ppermute | solution.py:32
  20.6 46.6 %collective-permute-start.1 = (bf16[320,800]{1,0:T(8,128)(2,1)}, bf16[320,800]{1,0:T(8,128)(2,1)S(1)}, u32[]{:S(2)}, u32[]{:S(2)}) collective-permute-start(bf16[320,800]{1,0:T(8,128)(2,1)} %total.1), channel_id=1, source_target_pairs={{0,96},{1,33},{32,0},{33,65},{64,32},{65,97},{96,64},{97,1},{2,98}... | collective-permute-start | bytes 1536008 | tf_op jit(solution)/shard_map/ppermute | solution.py:32
  67.2 0.8 copy-start.5
  67.2 2.0 copy-start.7
  69.2 1.6 copy-start
  74.9 7.8 %copy-start.6 = (bf16[320,800]{1,0:T(8,128)(2,1)S(1)}, bf16[320,800]{1,0:T(8,128)(2,1)}, u32[]{:S(2)}) copy-start(bf16[320,800]{1,0:T(8,128)(2,1)} %copy-done.5) | copy-start | bytes 1536004
  74.9 46.4 %all-to-all-start = ((bf16[8,240,640]{2,1,0:T(8,128)(2,1)}), bf16[8,240,640]{2,1,0:T(8,128)(2,1)}, u32[]{:S(2)}, u32[]{:S(2)}) async-start(bf16[8,240,640]{2,1,0:T(8,128)(2,1)} %bitcast.63), calls=%async_computation | async-start | bytes 4915200 | tf_op jit(solution)/shard_map/all_to_all | solution.py:51
  82.7 96.9 %all-gather.12.cloned.1.call-start = ((), (), s32[]{:S(2)}) async-start(), calls=%async_computation.8 | async-start | bytes 2867200 | tf_op jit(solution)/shard_map/all_gather | solution.py:119
  84.4 29.1 %collective-permute-start.2 = (bf16[160,800]{1,0:T(8,128)(2,1)}, bf16[160,800]{1,0:T(8,128)(2,1)S(1)}, u32[]{:S(2)}, u32[]{:S(2)}) collective-permute-start(bf16[160,800]{1,0:T(8,128)(2,1)} %slice.30), channel_id=1, source_target_pairs={{0,32},{1,97},{32,64},{33,1},{64,96},{65,33},{96,0},{97,65},{2,34}... | collective-permute-start | bytes 768008 | tf_op jit(solution)/shard_map/ppermute | solution.py:32
  92.3 22.2 %collective-permute-start.3 = (bf16[160,800]{1,0:T(8,128)(2,1)S(1)}, bf16[160,800]{1,0:T(8,128)(2,1)}, u32[]{:S(2)}, u32[]{:S(2)}) collective-permute-start(bf16[160,800]{1,0:T(8,128)(2,1)S(1)} %slice.31), channel_id=1, source_target_pairs={{0,96},{1,33},{32,0},{33,65},{64,32},{65,97},{96,64},{97,1},{2,98}... | collective-permute-start | bytes 768008 | tf_op jit(solution)/shard_map/ppermute | solution.py:32
  113.6 0.7 copy-start.9
  116.5 3.3 %copy-start.8 = (bf16[320,800]{1,0:T(8,128)(2,1)}, bf16[320,800]{1,0:T(8,128)(2,1)S(1)}, u32[]{:S(2)}) copy-start(bf16[320,800]{1,0:T(8,128)(2,1)S(1)} %constant_dynamic-update-slice_fusion) | copy-start | bytes 1536004
  121.3 11.5 %all-to-all-start.1 = ((bf16[4,80,640]{2,1,0:T(8,128)(2,1)}), bf16[4,80,640]{2,1,0:T(8,128)(2,1)S(1)}, u32[]{:S(2)}, u32[]{:S(2)}) async-start(bf16[4,80,640]{2,1,0:T(8,128)(2,1)} %bitcast.70), calls=%async_computation.1 | async-start | bytes 819200 | tf_op jit(solution)/shard_map/all_to_all | solution.py:51
  150.4 29.3 %all-to-all-start.3 = ((bf16[16,80,640]{2,1,0:T(8,128)(2,1)}), bf16[16,80,640]{2,1,0:T(8,128)(2,1)}, u32[]{:S(2)}, u32[]{:S(2)}) async-start(bf16[16,80,640]{2,1,0:T(8,128)(2,1)} %broadcast_in_dim.4), calls=%async_computation.3 | async-start | bytes 3276800 | tf_op jit(solution)/shard_map/all_to_all | solution.py:43
  155.4 64.9 %all-gather.14.cloned.1.call-start = ((), (), s32[]{:S(2)}) async-start(), calls=%async_computation.9 | async-start | bytes 2867200 | tf_op jit(solution)/shard_map/all_gather | solution.py:132
  155.9 23.7 %collective-permute-start.4 = (bf16[80,640]{1,0:T(8,128)(2,1)S(1)}, bf16[80,640]{1,0:T(8,128)(2,1)S(1)}, u32[]{:S(2)}, u32[]{:S(2)}) collective-permute-start(bf16[80,640]{1,0:T(8,128)(2,1)S(1)} %reduce_sum.47), channel_id=1, source_target_pairs={{0,0},{32,8},{64,16},{96,24},{8,32},{40,40},{72,48},{104,56},{16,6... | collective-permute-start | bytes 307208 | tf_op jit(solution)/shard_map/ppermute | solution.py:138
  179.7 10.1 %copy-start.10 = (bf16[80,640]{1,0:T(8,128)(2,1)}, bf16[80,640]{1,0:T(8,128)(2,1)S(1)}, u32[]{:S(2)}) copy-start(bf16[80,640]{1,0:T(8,128)(2,1)S(1)} %collective-permute-done.4) | copy-start | bytes 307204
  189.8 30.4 %all-to-all-start.4 = ((bf16[4,80,640]{2,1,0:T(8,128)(2,1)}), bf16[4,80,640]{2,1,0:T(8,128)(2,1)S(1)}, u32[]{:S(2)}, u32[]{:S(2)}) async-start(bf16[4,80,640]{2,1,0:T(8,128)(2,1)} %bitcast.68), calls=%async_computation.4 | async-start | bytes 819200 | tf_op jit(solution)/shard_map/all_to_all | solution.py:51
  233.6 27.4 %copy-start.3 = (bf16[1280,800]{1,0:T(8,128)(2,1)S(1)}, bf16[1280,800]{1,0:T(8,128)(2,1)}, u32[]{:S(2)}) copy-start(bf16[1280,800]{1,0:T(8,128)(2,1)} %all-gather.14.cloned.1.call-done.refs_2_) | copy-start | bytes 6144004
  233.8 27.3 %copy-start.2 = (bf16[1280,800]{1,0:T(8,128)(2,1)S(1)}, bf16[1280,800]{1,0:T(8,128)(2,1)}, u32[]{:S(2)}) copy-start(bf16[1280,800]{1,0:T(8,128)(2,1)} %all-gather.12.cloned.1.call-done.refs_3_) | copy-start | bytes 6144004
  233.9 27.1 %copy-start.1 = (bf16[1280,800]{1,0:T(8,128)(2,1)S(1)}, bf16[1280,800]{1,0:T(8,128)(2,1)}, u32[]{:S(2)}) copy-start(bf16[1280,800]{1,0:T(8,128)(2,1)} %all-gather.10.cloned.1.call-done.refs_1_) | copy-start | bytes 6144004
  252.0 12.1 %collective-permute-start.5 = (bf16[320,2560]{1,0:T(8,128)(2,1)S(1)}, bf16[320,2560]{1,0:T(8,128)(2,1)S(1)}, u32[]{:S(2)}, u32[]{:S(2)}) collective-permute-start(bf16[320,2560]{1,0:T(8,128)(2,1)S(1)} %bitcast.60), channel_id=1, source_target_pairs={{1,0},{0,1},{3,2},{2,3},{5,4},{4,5},{7,6},{6,7},{9,8},{8,9},{11,10... | collective-permute-start | bytes 4915208 | tf_op jit(solution)/shard_map/ppermute | solution.py:23
Sparse Core Ops, SparseCore 0:
  9.5 45.4 all-gather.7
  68.1 43.8 all-gather.9
  114.1 40.2 all-gather.11
  158.0 42.3 all-gather.13

commit v11 on v9

--- a/solution.py
+++ b/solution.py
@@ -21,6 +21,15 @@
 def take(value, axis, distance):
     n = lax.axis_size(axis)
     return lax.ppermute(value, axis, [((i + distance) % n, i) for i in range(n)])
+
+
+def shifted(value, step):
+    route = [
+        (h * 2 + c, (h + (step if c == 0 else -step)) % 4 * 2 + c)
+        for h in range(4)
+        for c in range(2)
+    ]
+    return lax.ppermute(value, ("zh", "c"), route)
 
 
 def rolled(parts, start):
@@ -112,8 +121,11 @@
     above = lax.all_gather(upper, "x", axis=0, tiled=True)
     below = lax.all_gather(lower, "x", axis=0, tiled=True)
     cut = rows // 2
-    opposite = lax.optimization_barrier((upper[:cut], lower[cut:]))
-    opposite = (take(opposite[0], "zh", 1), take(opposite[1], "zh", -1))
+    opposite = lax.optimization_barrier((
+        jnp.where(c == 0, lower[:cut], upper[:cut]),
+        jnp.where(c == 0, upper[cut:], lower[cut:]),
+    ))
+    opposite = (shifted(opposite[0], 1), shifted(opposite[1], -1))
     opposite = jnp.concatenate(lax.optimization_barrier(opposite), axis=0)
 
     sides = jnp.stack([iterate, upper, lower]).reshape(3, 4, slab, width)

time: 275 us -> 270 us (0.982)
  blocking collectives: 86.8 us -> 79.8 us
  starting transfers between devices: 56.2 us -> 60.5 us
    ppermute x0 -> x2, waiting for transfers between devices: none -> 17.8 us  [shifted(): return lax.ppermute(value, ('zh', 'c'), route)]
    ppermute x5 -> x3, waiting for transfers between devices: 63.3 us -> 45.7 us  [take(): lax.ppermute(value, axis, [((i + distance) % n, i) for i in range(n)])]
    ppermute x0 -> x2, starting transfers between devices: none -> 9.79 us  [shifted(): return lax.ppermute(value, ('zh', 'c'), route)]
    ppermute x5 -> x3, starting transfers between devices: 33.9 us -> 26.4 us  [take(): lax.ppermute(value, axis, [((i + distance) % n, i) for i in range(n)])]
    all_gather x2, blocking collectives: 12 us -> 8.54 us  [matmul_over_c(): lax.all_gather(sent, 'c', axis=0, tiled=False)[1 - lax.axis_index('c')]]
    all_to_all x1, blocking collectives: 19.4 us -> 16.1 us  [gathered(): return lax.all_to_all(spread, axis, split_axis=0, concat_axis=0, tiled=True)]
    all_to_all x1, blocking collectives: 23.5 us -> 20.3 us  [exchanged(): return lax.all_to_all(value, axis, split_axis=0, concat_axis=0, tiled=True)]
  transfers between devices with their start and end apart: 14 -> 14, of which waited for: 6 -> 5; matrix products, arithmetic and copies ran while one was open for 6% -> 6% of each run, Pallas kernels for 1% -> 1%
where the time goes in v11:
time: 270 us; the launch traced here: 269 us
  waiting for transfers between devices  92 us (34%)
  blocking collectives  79.8 us (30%)
  starting transfers between devices  60.5 us (22%)
  between operations  13.4 us (5%)
  matrix products  10.4 us (4%)
  Pallas kernels  5.26 us (2%)
  other arithmetic  5.1 us (2%)
    ppermute x3, waiting for transfers between devices, take(): lax.ppermute(value, axis, [((i + distance) % n, i) for i in range(n)])  45.7 us
    all_to_all x3, waiting for transfers between devices, exchanged(): return lax.all_to_all(value, axis, split_axis=0, concat_axis=0, tiled=True)  27.3 us
    ppermute x3, starting transfers between devices, take(): lax.ppermute(value, axis, [((i + distance) % n, i) for i in range(n)])  26.4 us
    all_gather x1, blocking collectives, local(): left = lax.all_gather(gram, 'zl', axis=0, tiled=True)  22.2 us
    all_to_all x1, blocking collectives, exchanged(): return lax.all_to_all(value, axis, split_axis=0, concat_axis=0, tiled=True)  20.3 us
    all_to_all x3, starting transfers between devices, exchanged(): return lax.all_to_all(value, axis, split_axis=0, concat_axis=0, tiled=True)  18.6 us
    ppermute x2, waiting for transfers between devices, shifted(): return lax.ppermute(value, ('zh', 'c'), route)  17.8 us
    all_to_all x1, blocking collectives, gathered(): return lax.all_to_all(spread, axis, split_axis=0, concat_axis=0, tiled=True)  16.1 us
  transfers between devices with their start and end apart: 14, of which 5 were waited for; matrix products, arithmetic and copies ran while one was open for 6% of the time, Pallas kernels for 1%

profile of v11, /device:TPU:1, one launch (start us, length us, event | category | flops | bytes accessed | tf_op | source)
XLA Modules:
  0.0 269.1 jit_solution(477217146704329913)
XLA Ops:
  6.5 0.7 all-gather.8.cloned.1.call-update
  7.3 0.0 all-gather.10.cloned.1.call-start
  7.3 13.3 %collective-permute-start = (bf16[320,800]{1,0:T(8,128)(2,1)}, bf16[320,800]{1,0:T(8,128)(2,1)S(1)}, u32[]{:S(2)}, u32[]{:S(2)}) collective-permute-start(bf16[320,800]{1,0:T(8,128)(2,1)} %total.1), channel_id=1, source_target_pairs={{32,0},{64,32},{96,64},{0,96},{33,1},{65,33},{97,65},{1,97},{34,2}... | collective-permute-start | bytes 1536008 | tf_op jit(solution)/shard_map/ppermute | solution.py:23
  20.6 1.9 collective-permute-start.1
  22.5 44.7 %collective-permute-done = bf16[320,800]{1,0:T(8,128)(2,1)S(1)} collective-permute-done((bf16[320,800]{1,0:T(8,128)(2,1)}, bf16[320,800]{1,0:T(8,128)(2,1)S(1)}, u32[]{:S(2)}, u32[]{:S(2)}) %collective-permute-start) | collective-permute-done | bytes 512032 | tf_op jit(solution)/shard_map/ppermute | solution.py:23
  67.3 0.8 copy-done.5
  68.1 0.0 all-gather.10.cloned.1.call-update
  68.1 1.6 pad_maximum_fusion
  69.8 0.3 copy-done
  70.1 4.0 %convolution_convert_fusion = bf16[2,640,960]{1,2,0:T(8,128)(2,1)} fusion(bf16[2,640,800]{2,1,0:T(8,128)(2,1)S(1)} %bitcast.57, bf16[960,800,1]{1,0,2:T(8,128)(2,1)S(1)} %bitcast.67), kind=kOutput, calls=%fused_computation | convolution fusion | flops 1967308800 | bytes 6041600 | tf_op jit(solution)/shard_map/rn,csn->crs/dot_general | solution.py:110
  74.1 8.3 %all-to-all-start = ((bf16[8,240,640]{2,1,0:T(8,128)(2,1)}), bf16[8,240,640]{2,1,0:T(8,128)(2,1)}, u32[]{:S(2)}, u32[]{:S(2)}) async-start(bf16[8,240,640]{2,1,0:T(8,128)(2,1)} %bitcast.65), calls=%async_computation | async-start | bytes 4915200 | tf_op jit(solution)/shard_map/all_to_all | solution.py:51
  82.5 0.9 slice_select_fusion
  83.4 7.9 %collective-permute-start.2 = (bf16[160,800]{1,0:T(8,128)(2,1)}, bf16[160,800]{1,0:T(8,128)(2,1)S(1)}, u32[]{:S(2)}, u32[]{:S(2)}) collective-permute-start(bf16[160,800]{1,0:T(8,128)(2,1)} %get-tuple-element.24), channel_id=1, source_target_pairs={{0,32},{1,97},{32,64},{33,1},{64,96},{65,33},{96,0},{97,65},{2,34}... | collective-permute-start | bytes 768008 | tf_op jit(solution)/shard_map/ppermute | solution.py:32
  91.2 1.9 collective-permute-start.3
  93.2 0.0 all-gather.12.cloned.1.call-update
  93.2 17.8 %collective-permute-done.2 = bf16[160,800]{1,0:T(8,128)(2,1)S(1)} collective-permute-done((bf16[160,800]{1,0:T(8,128)(2,1)}, bf16[160,800]{1,0:T(8,128)(2,1)S(1)}, u32[]{:S(2)}, u32[]{:S(2)}) %collective-permute-start.2) | collective-permute-done | bytes 256032 | tf_op jit(solution)/shard_map/ppermute | solution.py:32
  111.0 0.7 convolution_convert_fusion.1
  111.8 2.7 %all-gather = bf16[640,640]{1,0:T(8,128)(2,1)S(1)} all-gather(bf16[320,640]{1,0:T(8,128)(2,1)S(1)} %convolution_convert_fusion.1), channel_id=2, replica_groups=mesh['x'=4,'zh'=4,'zl'=4,'y'=4,'c'=2] {'c'}, dimensions={0}, use_global_device_ids=true | all-gather | bytes 1228800 | tf_op jit(solution)/shard_map/all_gather | solution.py:60
  114.5 1.5 fusion
  116.0 4.5 %all-to-all-start.1 = ((bf16[4,80,640]{2,1,0:T(8,128)(2,1)}), bf16[4,80,640]{2,1,0:T(8,128)(2,1)S(1)}, u32[]{:S(2)}, u32[]{:S(2)}) async-start(bf16[4,80,640]{2,1,0:T(8,128)(2,1)} %bitcast.16), calls=%async_computation.1 | async-start | bytes 819200 | tf_op jit(solution)/shard_map/all_to_all | solution.py:51
  120.5 2.1 reduce_sum.45
  122.6 5.3 %all-to-all-done.1 = bf16[4,80,640]{2,1,0:T(8,128)(2,1)S(1)} async-done(((bf16[4,80,640]{2,1,0:T(8,128)(2,1)}), bf16[4,80,640]{2,1,0:T(8,128)(2,1)S(1)}, u32[]{:S(2)}, u32[]{:S(2)}) %all-to-all-start.1) | async-done | bytes 409632 | tf_op jit(solution)/shard_map/all_to_all | solution.py:51
  127.9 0.1 reduce_sum.46
  128.0 0.1 select_bitcast_fusion.3
  128.1 0.1 pad_maximum_fusion.1
  128.1 20.3 %all_to_all.30 = bf16[4,80,640]{2,1,0:T(8,128)(2,1)S(1)} all-to-all(bf16[4,80,640]{2,1,0:T(8,128)(2,1)S(1)} %pad_maximum_fusion.1), channel_id=1, replica_groups=mesh['x'=4,'zh'=4,'zl'=4,'y'=4,'c'=2] {'zl'}, dimensions={0} | all-to-all | bytes 819200 | tf_op jit(solution)/shard_map/all_to_all | solution.py:51
  148.4 0.1 reduce_sum.47
  148.5 1.3 broadcast_in_dim.4
  149.8 5.0 %all-to-all-start.3 = ((bf16[16,80,640]{2,1,0:T(8,128)(2,1)}), bf16[16,80,640]{2,1,0:T(8,128)(2,1)}, u32[]{:S(2)}, u32[]{:S(2)}) async-start(bf16[16,80,640]{2,1,0:T(8,128)(2,1)} %broadcast_in_dim.4), calls=%async_computation.3 | async-start | bytes 3276800 | tf_op jit(solution)/shard_map/all_to_all | solution.py:43
  154.8 0.0 all-gather.14.cloned.1.call-start
  154.9 0.5 all-gather.14.cloned.1.call-update
  155.4 0.7 collective-permute-start.4
  156.1 22.2 %all_gather.36 = bf16[320,640]{1,0:T(8,128)(2,1)S(1)} all-gather(bf16[80,640]{1,0:T(8,128)(2,1)S(1)} %reduce_sum.47), channel_id=1, replica_groups=mesh['x'=4,'zh'=4,'zl'=4,'y'=4,'c'=2] {'zl'}, dimensions={0}, use_global_device_ids=true | all-gather | bytes 512000 | tf_op jit(solution)/shard_map/all_gather | solution.py:144
  178.3 1.7 convolution_convert_fusion.2
  180.0 5.8 %all-gather.1 = bf16[640,640]{1,0:T(8,128)(2,1)S(1)} all-gather(bf16[320,640]{1,0:T(8,128)(2,1)S(1)} %convolution_convert_fusion.2), channel_id=3, replica_groups=mesh['x'=4,'zh'=4,'zl'=4,'y'=4,'c'=2] {'c'}, dimensions={0}, use_global_device_ids=true | all-gather | bytes 1228800 | tf_op jit(solution)/shard_map/all_gather | solution.py:60
  185.9 2.4 fusion.1
  188.3 5.7 %all-to-all-start.4 = ((bf16[4,80,640]{2,1,0:T(8,128)(2,1)}), bf16[4,80,640]{2,1,0:T(8,128)(2,1)S(1)}, u32[]{:S(2)}, u32[]{:S(2)}) async-start(bf16[4,80,640]{2,1,0:T(8,128)(2,1)} %bitcast.27), calls=%async_computation.4 | async-start | bytes 819200 | tf_op jit(solution)/shard_map/all_to_all | solution.py:51
  194.0 22.0 %all-to-all-done.4 = bf16[4,80,640]{2,1,0:T(8,128)(2,1)S(1)} async-done(((bf16[4,80,640]{2,1,0:T(8,128)(2,1)}), bf16[4,80,640]{2,1,0:T(8,128)(2,1)S(1)}, u32[]{:S(2)}, u32[]{:S(2)}) %all-to-all-start.4) | async-done | bytes 409632 | tf_op jit(solution)/shard_map/all_to_all | solution.py:51
  216.0 0.1 convert_reduce_fusion
  216.1 0.0 all-gather.14.cloned.1.call-done.refs_2_
  216.2 12.7 %all-gather.2 = bf16[320,640]{1,0:T(8,128)(2,1)S(1)} all-gather(bf16[80,640]{1,0:T(8,128)(2,1)S(1)} %add_convert_fusion), channel_id=4, replica_groups=mesh['x'=4,'zh'=4,'zl'=4,'y'=4,'c'=2] {'zl'}, dimensions={0}, use_global_device_ids=true | all-gather | bytes 512000 | tf_op jit(solution)/shard_map/all_gather | solution.py:154
  228.9 0.1 select_select_fusion.3
  229.0 0.1 broadcast_in_dim.5
  229.1 16.1 %all_to_all.31 = bf16[4,80,2560]{2,1,0:T(8,128)(2,1)S(1)} all-to-all(bf16[4,80,2560]{2,1,0:T(8,128)(2,1)S(1)} %broadcast_in_dim.5), channel_id=1, replica_groups=mesh['x'=4,'zh'=4,'zl'=4,'y'=4,'c'=2] {'y'}, dimensions={0} | all-to-all | bytes 3276800 | tf_op jit(solution)/shard_map/all_to_all | solution.py:43
  245.2 11.2 %collective-permute-start.5 = (bf16[320,2560]{1,0:T(8,128)(2,1)S(1)}, bf16[320,2560]{1,0:T(8,128)(2,1)S(1)}, u32[]{:S(2)}, u32[]{:S(2)}) collective-permute-start(bf16[320,2560]{1,0:T(8,128)(2,1)S(1)} %bitcast.60), channel_id=1, source_target_pairs={{1,0},{0,1},{3,2},{2,3},{5,4},{4,5},{7,6},{6,7},{9,8},{8,9},{11,10... | collective-permute-start | bytes 4915208 | tf_op jit(solution)/shard_map/ppermute | solution.py:23
  256.4 2.1 shard_map.17.total
  258.5 0.9 collective-permute-done.5.left
  259.5 3.1 %shard_map.18 = f32[320,800]{1,0:T(8,128)} custom-call(f32[320,800]{1,0:T(8,128)S(1)} %shard_map.17.total, bf16[320,2560]{1,0:T(8,128)(2,1)S(1)} %collective-permute-done.5.left, bf16[1280,800]{1,0:T(8,128)(2,1)S(1)} %copy-done, bf16[1280,800]{1,0:T(8,128)(2,1)S(1)} %copy-done.1, bf16[1280,800]{1,0:T(8,128)(2,1)S(1)} %copy-done.3, ...), custom_call_target="tpu_custom_call" | custom-call | flops 1310720000 | bytes 3686400 | tf_op jit(solution)/shard_map/pallas_call | solution.py:85
  (30 shorter events, 0.2 us)
Async XLA Ops:
  6.5 60.8 %all-gather.8.cloned.1.call-start = ((), (), s32[]{:S(2)}) async-start(), calls=%async_computation.6 | async-start | bytes 2867200 | tf_op jit(solution)/shard_map/all_gather | solution.py:119
  7.3 171.1 %all-gather.10.cloned.1.call-start = ((), (), s32[]{:S(2)}) async-start(), calls=%async_computation.7 | async-start | bytes 2867200 | tf_op jit(solution)/shard_map/all_gather | solution.py:121
  7.3 60.0 %collective-permute-start = (bf16[320,800]{1,0:T(8,128)(2,1)}, bf16[320,800]{1,0:T(8,128)(2,1)S(1)}, u32[]{:S(2)}, u32[]{:S(2)}) collective-permute-start(bf16[320,800]{1,0:T(8,128)(2,1)} %total.1), channel_id=1, source_target_pairs={{32,0},{64,32},{96,64},{0,96},{33,1},{65,33},{97,65},{1,97},{34,2}... | collective-permute-start | bytes 1536008 | tf_op jit(solution)/shard_map/ppermute | solution.py:23
  20.6 46.7 %collective-permute-start.1 = (bf16[320,800]{1,0:T(8,128)(2,1)}, bf16[320,800]{1,0:T(8,128)(2,1)S(1)}, u32[]{:S(2)}, u32[]{:S(2)}) collective-permute-start(bf16[320,800]{1,0:T(8,128)(2,1)} %total.1), channel_id=1, source_target_pairs={{96,0},{0,32},{32,64},{64,96},{97,1},{1,33},{33,65},{65,97},{98,2}... | collective-permute-start | bytes 1536008 | tf_op jit(solution)/shard_map/ppermute | solution.py:23
  67.3 0.8 copy-start.5
  67.3 15.2 %copy-start.7 = (bf16[320,800]{1,0:T(8,128)(2,1)}, bf16[320,800]{1,0:T(8,128)(2,1)S(1)}, u32[]{:S(2)}) copy-start(bf16[320,800]{1,0:T(8,128)(2,1)S(1)} %collective-permute-done.1) | copy-start | bytes 1536004
  68.1 2.0 copy-start
  74.1 8.4 %copy-start.6 = (bf16[320,800]{1,0:T(8,128)(2,1)S(1)}, bf16[320,800]{1,0:T(8,128)(2,1)}, u32[]{:S(2)}) copy-start(bf16[320,800]{1,0:T(8,128)(2,1)} %copy-done.5) | copy-start | bytes 1536004
  74.1 41.9 %all-to-all-start = ((bf16[8,240,640]{2,1,0:T(8,128)(2,1)}), bf16[8,240,640]{2,1,0:T(8,128)(2,1)}, u32[]{:S(2)}, u32[]{:S(2)}) async-start(bf16[8,240,640]{2,1,0:T(8,128)(2,1)} %bitcast.65), calls=%async_computation | async-start | bytes 4915200 | tf_op jit(solution)/shard_map/all_to_all | solution.py:51
  82.5 95.9 %all-gather.12.cloned.1.call-start = ((), (), s32[]{:S(2)}) async-start(), calls=%async_computation.8 | async-start | bytes 2867200 | tf_op jit(solution)/shard_map/all_gather | solution.py:122
  83.4 27.6 %collective-permute-start.2 = (bf16[160,800]{1,0:T(8,128)(2,1)}, bf16[160,800]{1,0:T(8,128)(2,1)S(1)}, u32[]{:S(2)}, u32[]{:S(2)}) collective-permute-start(bf16[160,800]{1,0:T(8,128)(2,1)} %get-tuple-element.24), channel_id=1, source_target_pairs={{0,32},{1,97},{32,64},{33,1},{64,96},{65,33},{96,0},{97,65},{2,34}... | collective-permute-start | bytes 768008 | tf_op jit(solution)/shard_map/ppermute | solution.py:32
  91.2 19.7 %collective-permute-start.3 = (bf16[160,800]{1,0:T(8,128)(2,1)}, bf16[160,800]{1,0:T(8,128)(2,1)S(1)}, u32[]{:S(2)}, u32[]{:S(2)}) collective-permute-start(bf16[160,800]{1,0:T(8,128)(2,1)} %get-tuple-element.25), channel_id=1, source_target_pairs={{0,96},{1,33},{32,0},{33,65},{64,32},{65,97},{96,64},{97,1},{2,98}... | collective-permute-start | bytes 768008 | tf_op jit(solution)/shard_map/ppermute | solution.py:32
  111.0 3.5 %copy-start.8 = (bf16[320,800]{1,0:T(8,128)(2,1)}, bf16[320,800]{1,0:T(8,128)(2,1)S(1)}, u32[]{:S(2)}) copy-start(bf16[320,800]{1,0:T(8,128)(2,1)S(1)} %constant_dynamic-update-slice_fusion) | copy-start | bytes 1536004
  116.0 11.9 %all-to-all-start.1 = ((bf16[4,80,640]{2,1,0:T(8,128)(2,1)}), bf16[4,80,640]{2,1,0:T(8,128)(2,1)S(1)}, u32[]{:S(2)}, u32[]{:S(2)}) async-start(bf16[4,80,640]{2,1,0:T(8,128)(2,1)} %bitcast.16), calls=%async_computation.1 | async-start | bytes 819200 | tf_op jit(solution)/shard_map/all_to_all | solution.py:51
  149.8 28.5 %all-to-all-start.3 = ((bf16[16,80,640]{2,1,0:T(8,128)(2,1)}), bf16[16,80,640]{2,1,0:T(8,128)(2,1)}, u32[]{:S(2)}, u32[]{:S(2)}) async-start(bf16[16,80,640]{2,1,0:T(8,128)(2,1)} %broadcast_in_dim.4), calls=%async_computation.3 | async-start | bytes 3276800 | tf_op jit(solution)/shard_map/all_to_all | solution.py:43
  154.8 61.3 %all-gather.14.cloned.1.call-start = ((), (), s32[]{:S(2)}) async-start(), calls=%async_computation.9 | async-start | bytes 2867200 | tf_op jit(solution)/shard_map/all_gather | solution.py:137
  155.4 22.9 %collective-permute-start.4 = (bf16[80,640]{1,0:T(8,128)(2,1)S(1)}, bf16[80,640]{1,0:T(8,128)(2,1)S(1)}, u32[]{:S(2)}, u32[]{:S(2)}) collective-permute-start(bf16[80,640]{1,0:T(8,128)(2,1)S(1)} %reduce_sum.47), channel_id=1, source_target_pairs={{0,0},{32,8},{64,16},{96,24},{8,32},{40,40},{72,48},{104,56},{16,6... | collective-permute-start | bytes 307208 | tf_op jit(solution)/shard_map/ppermute | solution.py:143
  188.3 27.7 %all-to-all-start.4 = ((bf16[4,80,640]{2,1,0:T(8,128)(2,1)}), bf16[4,80,640]{2,1,0:T(8,128)(2,1)S(1)}, u32[]{:S(2)}, u32[]{:S(2)}) async-start(bf16[4,80,640]{2,1,0:T(8,128)(2,1)} %bitcast.27), calls=%async_computation.4 | async-start | bytes 819200 | tf_op jit(solution)/shard_map/all_to_all | solution.py:51
  216.1 40.2 %copy-start.4 = (bf16[320,800]{1,0:T(8,128)(2,1)S(1)}, bf16[320,800]{1,0:T(8,128)(2,1)}, u32[]{:S(2)}) copy-start(bf16[320,800]{1,0:T(8,128)(2,1)} %total.1) | copy-start | bytes 1536004
  228.9 27.5 %copy-start.3 = (bf16[1280,800]{1,0:T(8,128)(2,1)S(1)}, bf16[1280,800]{1,0:T(8,128)(2,1)}, u32[]{:S(2)}) copy-start(bf16[1280,800]{1,0:T(8,128)(2,1)} %all-gather.14.cloned.1.call-done.refs_2_) | copy-start | bytes 6144004
  229.0 27.4 %copy-start.2 = (bf16[1280,800]{1,0:T(8,128)(2,1)S(1)}, bf16[1280,800]{1,0:T(8,128)(2,1)}, u32[]{:S(2)}) copy-start(bf16[1280,800]{1,0:T(8,128)(2,1)} %all-gather.12.cloned.1.call-done.refs_3_) | copy-start | bytes 6144004
  229.1 27.3 %copy-start.1 = (bf16[1280,800]{1,0:T(8,128)(2,1)S(1)}, bf16[1280,800]{1,0:T(8,128)(2,1)}, u32[]{:S(2)}) copy-start(bf16[1280,800]{1,0:T(8,128)(2,1)} %all-gather.10.cloned.1.call-done.refs_1_) | copy-start | bytes 6144004
  245.2 14.3 %collective-permute-start.5 = (bf16[320,2560]{1,0:T(8,128)(2,1)S(1)}, bf16[320,2560]{1,0:T(8,128)(2,1)S(1)}, u32[]{:S(2)}, u32[]{:S(2)}) collective-permute-start(bf16[320,2560]{1,0:T(8,128)(2,1)S(1)} %bitcast.60), channel_id=1, source_target_pairs={{1,0},{0,1},{3,2},{2,3},{5,4},{4,5},{7,6},{6,7},{9,8},{8,9},{11,10... | collective-permute-start | bytes 4915208 | tf_op jit(solution)/shard_map/ppermute | solution.py:23
Sparse Core Ops, SparseCore 0:
  9.5 45.4 all-gather.7
  68.2 43.7 all-gather.9
  114.2 40.2 all-gather.11
  157.5 41.5 all-gather.13

commit v12 on v11

--- a/solution.py
+++ b/solution.py
@@ -146,7 +146,9 @@
     left, right, above, below, turned = lax.optimization_barrier(
         (left, right, above, below, turned)
     )
-    square = matmul_over_c(left, *columns(right))
+    square = jnp.einsum("rn,csn->crs", left, right.reshape(2, pair, pair), preferred_element_type=F32)
+    other = lax.all_gather(square[1 - c].astype(BF16), "c", axis=0, tiled=False)[1 - c]
+    square = (square[c] + other.astype(F32)).astype(BF16)
     square = exchanged_sum(square.reshape(4, slab, pair), "zh")
     square, opposite = lax.optimization_barrier((square, opposite))
     polynomial = (QUINTIC_B * turned.astype(F32) + QUINTIC_C * square).astype(BF16)

time: 270 us -> 270 us (level)
    all_gather x0 -> x1, blocking collectives: none -> 6.71 us  [local(): lax.all_gather(square[1 - c].astype(BF16), 'c', axis=0, tiled=False)[1 - c]]
    all_gather x2 -> x1, blocking collectives: 8.54 us -> 2.75 us  [matmul_over_c(): lax.all_gather(sent, 'c', axis=0, tiled=False)[1 - lax.axis_index('c')]]
where the time goes in v12:
time: 270 us; the launch traced here: 269 us
  waiting for transfers between devices  91.4 us (34%)
  blocking collectives  81.4 us (30%)
  starting transfers between devices  60.7 us (22%)
  between operations  13.4 us (5%)
  matrix products  8.58 us (3%)
  other arithmetic  5.93 us (2%)
  Pallas kernels  5.26 us (2%)
  local copies, waits for them, and re-layouts  2.71 us (1%)
    ppermute x3, waiting for transfers between devices, take(): lax.ppermute(value, axis, [((i + distance) % n, i) for i in range(n)])  45.7 us
    all_to_all x3, waiting for transfers between devices, exchanged(): return lax.all_to_all(value, axis, split_axis=0, concat_axis=0, tiled=True)  27.2 us
    ppermute x3, starting transfers between devices, take(): lax.ppermute(value, axis, [((i + distance) % n, i) for i in range(n)])  25.8 us
    all_gather x1, blocking collectives, local(): left = lax.all_gather(gram, 'zl', axis=0, tiled=True)  21.2 us
    all_to_all x1, blocking collectives, exchanged(): return lax.all_to_all(value, axis, split_axis=0, concat_axis=0, tiled=True)  20.9 us
    all_to_all x3, starting transfers between devices, exchanged(): return lax.all_to_all(value, axis, split_axis=0, concat_axis=0, tiled=True)  19.4 us
    all_to_all x1, blocking collectives, gathered(): return lax.all_to_all(spread, axis, split_axis=0, concat_axis=0, tiled=True)  17.3 us
    ppermute x2, waiting for transfers between devices, shifted(): return lax.ppermute(value, ('zh', 'c'), route)  17.2 us
  transfers between devices with their start and end apart: 14, of which 5 were waited for; matrix products, arithmetic and copies ran while one was open for 6% of the time, Pallas kernels for 1%

profile of v12, /device:TPU:1, one launch (start us, length us, event | category | flops | bytes accessed | tf_op | source)
XLA Modules:
  0.0 269.5 jit_solution(8729244289672470911)
XLA Ops:
  6.5 0.7 all-gather.7.cloned.1.call-update
  7.3 0.0 all-gather.11.cloned.1.call-start
  7.3 13.3 %collective-permute-start = (bf16[320,800]{1,0:T(8,128)(2,1)}, bf16[320,800]{1,0:T(8,128)(2,1)S(1)}, u32[]{:S(2)}, u32[]{:S(2)}) collective-permute-start(bf16[320,800]{1,0:T(8,128)(2,1)} %total.1), channel_id=1, source_target_pairs={{32,0},{64,32},{96,64},{0,96},{33,1},{65,33},{97,65},{1,97},{34,2}... | collective-permute-start | bytes 1536008 | tf_op jit(solution)/shard_map/ppermute | solution.py:23
  20.6 1.9 collective-permute-start.1
  22.5 44.7 %collective-permute-done = bf16[320,800]{1,0:T(8,128)(2,1)S(1)} collective-permute-done((bf16[320,800]{1,0:T(8,128)(2,1)}, bf16[320,800]{1,0:T(8,128)(2,1)S(1)}, u32[]{:S(2)}, u32[]{:S(2)}) %collective-permute-start) | collective-permute-done | bytes 512032 | tf_op jit(solution)/shard_map/ppermute | solution.py:23
  67.3 0.8 copy-done.6
  68.1 1.6 pad_maximum_fusion
  69.8 0.3 copy-done
  70.1 4.0 %convolution_convert_fusion = bf16[2,640,960]{1,2,0:T(8,128)(2,1)} fusion(bf16[2,640,800]{2,1,0:T(8,128)(2,1)S(1)} %bitcast.55, bf16[960,800,1]{1,0,2:T(8,128)(2,1)S(1)} %bitcast.64), kind=kOutput, calls=%fused_computation | convolution fusion | flops 1967308800 | bytes 6041600 | tf_op jit(solution)/shard_map/rn,csn->crs/dot_general | solution.py:110
  74.1 8.3 %all-to-all-start = ((bf16[8,240,640]{2,1,0:T(8,128)(2,1)}), bf16[8,240,640]{2,1,0:T(8,128)(2,1)}, u32[]{:S(2)}, u32[]{:S(2)}) async-start(bf16[8,240,640]{2,1,0:T(8,128)(2,1)} %bitcast.63), calls=%async_computation | async-start | bytes 4915200 | tf_op jit(solution)/shard_map/all_to_all | solution.py:51
  82.5 0.9 slice_select_fusion
  83.4 7.9 %collective-permute-start.2 = (bf16[160,800]{1,0:T(8,128)(2,1)}, bf16[160,800]{1,0:T(8,128)(2,1)S(1)}, u32[]{:S(2)}, u32[]{:S(2)}) collective-permute-start(bf16[160,800]{1,0:T(8,128)(2,1)} %get-tuple-element.24), channel_id=1, source_target_pairs={{0,32},{1,97},{32,64},{33,1},{64,96},{65,33},{96,0},{97,65},{2,34}... | collective-permute-start | bytes 768008 | tf_op jit(solution)/shard_map/ppermute | solution.py:32
  91.3 1.9 collective-permute-start.3
  93.2 0.0 all-gather.9.cloned.1.call-update
  93.2 17.2 %collective-permute-done.2 = bf16[160,800]{1,0:T(8,128)(2,1)S(1)} collective-permute-done((bf16[160,800]{1,0:T(8,128)(2,1)}, bf16[160,800]{1,0:T(8,128)(2,1)S(1)}, u32[]{:S(2)}, u32[]{:S(2)}) %collective-permute-start.2) | collective-permute-done | bytes 256032 | tf_op jit(solution)/shard_map/ppermute | solution.py:32
  110.5 0.7 convolution_convert_fusion.1
  111.3 2.7 %all-gather = bf16[640,640]{1,0:T(8,128)(2,1)S(1)} all-gather(bf16[320,640]{1,0:T(8,128)(2,1)S(1)} %convolution_convert_fusion.1), channel_id=2, replica_groups=mesh['x'=4,'zh'=4,'zl'=4,'y'=4,'c'=2] {'c'}, dimensions={0}, use_global_device_ids=true | all-gather | bytes 1228800 | tf_op jit(solution)/shard_map/all_gather | solution.py:60
  114.0 1.5 fusion
  115.5 4.0 %all-to-all-start.1 = ((bf16[4,80,640]{2,1,0:T(8,128)(2,1)}), bf16[4,80,640]{2,1,0:T(8,128)(2,1)S(1)}, u32[]{:S(2)}, u32[]{:S(2)}) async-start(bf16[4,80,640]{2,1,0:T(8,128)(2,1)} %bitcast.16), calls=%async_computation.1 | async-start | bytes 819200 | tf_op jit(solution)/shard_map/all_to_all | solution.py:51
  119.5 2.1 reduce_sum.45
  121.6 5.3 %all-to-all-done.1 = bf16[4,80,640]{2,1,0:T(8,128)(2,1)S(1)} async-done(((bf16[4,80,640]{2,1,0:T(8,128)(2,1)}), bf16[4,80,640]{2,1,0:T(8,128)(2,1)S(1)}, u32[]{:S(2)}, u32[]{:S(2)}) %all-to-all-start.1) | async-done | bytes 409632 | tf_op jit(solution)/shard_map/all_to_all | solution.py:51
  126.9 0.1 reduce_sum.46
  127.0 0.1 select_bitcast_fusion.3
  127.1 0.1 pad_maximum_fusion.1
  127.1 20.9 %all_to_all.30 = bf16[4,80,640]{2,1,0:T(8,128)(2,1)S(1)} all-to-all(bf16[4,80,640]{2,1,0:T(8,128)(2,1)S(1)} %pad_maximum_fusion.1), channel_id=1, replica_groups=mesh['x'=4,'zh'=4,'zl'=4,'y'=4,'c'=2] {'zl'}, dimensions={0} | all-to-all | bytes 819200 | tf_op jit(solution)/shard_map/all_to_all | solution.py:51
  148.1 0.1 reduce_sum.47
  148.2 1.3 broadcast_in_dim.4
  149.5 5.0 %all-to-all-start.3 = ((bf16[16,80,640]{2,1,0:T(8,128)(2,1)}), bf16[16,80,640]{2,1,0:T(8,128)(2,1)}, u32[]{:S(2)}, u32[]{:S(2)}) async-start(bf16[16,80,640]{2,1,0:T(8,128)(2,1)} %broadcast_in_dim.4), calls=%async_computation.3 | async-start | bytes 3276800 | tf_op jit(solution)/shard_map/all_to_all | solution.py:43
  154.5 0.0 all-gather.13.cloned.1.call-start
  154.5 0.5 all-gather.13.cloned.1.call-update
  155.1 0.7 collective-permute-start.4
  155.7 21.2 %all_gather.34 = bf16[320,640]{1,0:T(8,128)(2,1)S(1)} all-gather(bf16[80,640]{1,0:T(8,128)(2,1)S(1)} %reduce_sum.47), channel_id=1, replica_groups=mesh['x'=4,'zh'=4,'zl'=4,'y'=4,'c'=2] {'zl'}, dimensions={0}, use_global_device_ids=true | all-gather | bytes 512000 | tf_op jit(solution)/shard_map/all_gather | solution.py:144
  176.9 2.3 fusion.7
  179.3 0.1 fusion.6
  179.4 6.7 %all_gather.37 = bf16[2,320,640]{2,1,0:T(8,128)(2,1)S(1)} all-gather(bf16[1,320,640]{2,1,0:T(8,128)(2,1)S(1)} %fusion.6), channel_id=1, replica_groups=mesh['x'=4,'zh'=4,'zl'=4,'y'=4,'c'=2] {'c'}, dimensions={0}, use_global_device_ids=true | all-gather | bytes 1228800 | tf_op jit(solution)/shard_map/all_gather | solution.py:150
  186.1 0.8 fusion.5
  186.9 7.1 %all-to-all-start.4 = ((bf16[4,80,640]{2,1,0:T(8,128)(2,1)}), bf16[4,80,640]{2,1,0:T(8,128)(2,1)S(1)}, u32[]{:S(2)}, u32[]{:S(2)}) async-start(bf16[4,80,640]{2,1,0:T(8,128)(2,1)} %bitcast.26), calls=%async_computation.4 | async-start | bytes 819200 | tf_op jit(solution)/shard_map/all_to_all | solution.py:51
  194.0 21.9 %all-to-all-done.4 = bf16[4,80,640]{2,1,0:T(8,128)(2,1)S(1)} async-done(((bf16[4,80,640]{2,1,0:T(8,128)(2,1)}), bf16[4,80,640]{2,1,0:T(8,128)(2,1)S(1)}, u32[]{:S(2)}, u32[]{:S(2)}) %all-to-all-start.4) | async-done | bytes 409632 | tf_op jit(solution)/shard_map/all_to_all | solution.py:51
  215.9 0.1 convert_reduce_fusion
  216.0 0.0 all-gather.13.cloned.1.call-done.refs_2_
  216.1 12.5 %all-gather.1 = bf16[320,640]{1,0:T(8,128)(2,1)S(1)} all-gather(bf16[80,640]{1,0:T(8,128)(2,1)S(1)} %add_convert_fusion), channel_id=3, replica_groups=mesh['x'=4,'zh'=4,'zl'=4,'y'=4,'c'=2] {'zl'}, dimensions={0}, use_global_device_ids=true | all-gather | bytes 512000 | tf_op jit(solution)/shard_map/all_gather | solution.py:156
  228.5 0.1 select_select_fusion.3
  228.7 0.1 broadcast_in_dim.5
  228.8 17.3 %all_to_all.31 = bf16[4,80,2560]{2,1,0:T(8,128)(2,1)S(1)} all-to-all(bf16[4,80,2560]{2,1,0:T(8,128)(2,1)S(1)} %broadcast_in_dim.5), channel_id=1, replica_groups=mesh['x'=4,'zh'=4,'zl'=4,'y'=4,'c'=2] {'y'}, dimensions={0} | all-to-all | bytes 3276800 | tf_op jit(solution)/shard_map/all_to_all | solution.py:43
  246.1 10.5 %collective-permute-start.5 = (bf16[320,2560]{1,0:T(8,128)(2,1)S(1)}, bf16[320,2560]{1,0:T(8,128)(2,1)S(1)}, u32[]{:S(2)}, u32[]{:S(2)}) collective-permute-start(bf16[320,2560]{1,0:T(8,128)(2,1)S(1)} %bitcast.58), channel_id=1, source_target_pairs={{1,0},{0,1},{3,2},{2,3},{5,4},{4,5},{7,6},{6,7},{9,8},{8,9},{11,10... | collective-permute-start | bytes 4915208 | tf_op jit(solution)/shard_map/ppermute | solution.py:23
  256.7 2.1 shard_map.17.total
  258.9 0.9 collective-permute-done.5.left
  259.8 3.1 %shard_map.18 = f32[320,800]{1,0:T(8,128)} custom-call(f32[320,800]{1,0:T(8,128)S(1)} %shard_map.17.total, bf16[320,2560]{1,0:T(8,128)(2,1)S(1)} %collective-permute-done.5.left, bf16[1280,800]{1,0:T(8,128)(2,1)S(1)} %copy-done, bf16[1280,800]{1,0:T(8,128)(2,1)S(1)} %copy-done.2, bf16[1280,800]{1,0:T(8,128)(2,1)S(1)} %copy-done.3, ...), custom_call_target="tpu_custom_call" | custom-call | flops 1310720000 | bytes 3686400 | tf_op jit(solution)/shard_map/pallas_call | solution.py:85
  (31 shorter events, 0.2 us)
Async XLA Ops:
  6.5 60.8 %all-gather.7.cloned.1.call-start = ((), (), s32[]{:S(2)}) async-start(), calls=%async_computation.6 | async-start | bytes 2867200 | tf_op jit(solution)/shard_map/all_gather | solution.py:119
  7.3 169.7 %all-gather.11.cloned.1.call-start = ((), (), s32[]{:S(2)}) async-start(), calls=%async_computation.8 | async-start | bytes 2867200 | tf_op jit(solution)/shard_map/all_gather | solution.py:122
  7.3 60.0 %collective-permute-start = (bf16[320,800]{1,0:T(8,128)(2,1)}, bf16[320,800]{1,0:T(8,128)(2,1)S(1)}, u32[]{:S(2)}, u32[]{:S(2)}) collective-permute-start(bf16[320,800]{1,0:T(8,128)(2,1)} %total.1), channel_id=1, source_target_pairs={{32,0},{64,32},{96,64},{0,96},{33,1},{65,33},{97,65},{1,97},{34,2}... | collective-permute-start | bytes 1536008 | tf_op jit(solution)/shard_map/ppermute | solution.py:23
  20.6 46.7 %collective-permute-start.1 = (bf16[320,800]{1,0:T(8,128)(2,1)}, bf16[320,800]{1,0:T(8,128)(2,1)S(1)}, u32[]{:S(2)}, u32[]{:S(2)}) collective-permute-start(bf16[320,800]{1,0:T(8,128)(2,1)} %total.1), channel_id=1, source_target_pairs={{96,0},{0,32},{32,64},{64,96},{97,1},{1,33},{33,65},{65,97},{98,2}... | collective-permute-start | bytes 1536008 | tf_op jit(solution)/shard_map/ppermute | solution.py:23
  67.3 15.2 %copy-start.5 = (bf16[320,800]{1,0:T(8,128)(2,1)}, bf16[320,800]{1,0:T(8,128)(2,1)S(1)}, u32[]{:S(2)}) copy-start(bf16[320,800]{1,0:T(8,128)(2,1)S(1)} %collective-permute-done) | copy-start | bytes 1536004
  67.3 0.8 copy-start.6
  68.1 2.0 copy-start
  74.1 8.3 %copy-start.7 = (bf16[320,800]{1,0:T(8,128)(2,1)S(1)}, bf16[320,800]{1,0:T(8,128)(2,1)}, u32[]{:S(2)}) copy-start(bf16[320,800]{1,0:T(8,128)(2,1)} %copy-done.6) | copy-start | bytes 1536004
  74.1 41.4 %all-to-all-start = ((bf16[8,240,640]{2,1,0:T(8,128)(2,1)}), bf16[8,240,640]{2,1,0:T(8,128)(2,1)}, u32[]{:S(2)}, u32[]{:S(2)}) async-start(bf16[8,240,640]{2,1,0:T(8,128)(2,1)} %bitcast.63), calls=%async_computation | async-start | bytes 4915200 | tf_op jit(solution)/shard_map/all_to_all | solution.py:51
  82.5 94.5 %all-gather.9.cloned.1.call-start = ((), (), s32[]{:S(2)}) async-start(), calls=%async_computation.7 | async-start | bytes 2867200 | tf_op jit(solution)/shard_map/all_gather | solution.py:121
  83.4 27.1 %collective-permute-start.2 = (bf16[160,800]{1,0:T(8,128)(2,1)}, bf16[160,800]{1,0:T(8,128)(2,1)S(1)}, u32[]{:S(2)}, u32[]{:S(2)}) collective-permute-start(bf16[160,800]{1,0:T(8,128)(2,1)} %get-tuple-element.24), channel_id=1, source_target_pairs={{0,32},{1,97},{32,64},{33,1},{64,96},{65,33},{96,0},{97,65},{2,34}... | collective-permute-start | bytes 768008 | tf_op jit(solution)/shard_map/ppermute | solution.py:32
  91.3 19.2 %collective-permute-start.3 = (bf16[160,800]{1,0:T(8,128)(2,1)}, bf16[160,800]{1,0:T(8,128)(2,1)S(1)}, u32[]{:S(2)}, u32[]{:S(2)}) collective-permute-start(bf16[160,800]{1,0:T(8,128)(2,1)} %get-tuple-element.25), channel_id=1, source_target_pairs={{0,96},{1,33},{32,0},{33,65},{64,32},{65,97},{96,64},{97,1},{2,98}... | collective-permute-start | bytes 768008 | tf_op jit(solution)/shard_map/ppermute | solution.py:32
  110.5 3.5 %copy-start.8 = (bf16[320,800]{1,0:T(8,128)(2,1)}, bf16[320,800]{1,0:T(8,128)(2,1)S(1)}, u32[]{:S(2)}) copy-start(bf16[320,800]{1,0:T(8,128)(2,1)S(1)} %constant_dynamic-update-slice_fusion) | copy-start | bytes 1536004
  115.5 11.4 %all-to-all-start.1 = ((bf16[4,80,640]{2,1,0:T(8,128)(2,1)}), bf16[4,80,640]{2,1,0:T(8,128)(2,1)S(1)}, u32[]{:S(2)}, u32[]{:S(2)}) async-start(bf16[4,80,640]{2,1,0:T(8,128)(2,1)} %bitcast.16), calls=%async_computation.1 | async-start | bytes 819200 | tf_op jit(solution)/shard_map/all_to_all | solution.py:51
  149.5 27.5 %all-to-all-start.3 = ((bf16[16,80,640]{2,1,0:T(8,128)(2,1)}), bf16[16,80,640]{2,1,0:T(8,128)(2,1)}, u32[]{:S(2)}, u32[]{:S(2)}) async-start(bf16[16,80,640]{2,1,0:T(8,128)(2,1)} %broadcast_in_dim.4), calls=%async_computation.3 | async-start | bytes 3276800 | tf_op jit(solution)/shard_map/all_to_all | solution.py:43
  154.5 61.5 %all-gather.13.cloned.1.call-start = ((), (), s32[]{:S(2)}) async-start(), calls=%async_computation.9 | async-start | bytes 2867200 | tf_op jit(solution)/shard_map/all_gather | solution.py:137
  155.1 21.9 %collective-permute-start.4 = (bf16[80,640]{1,0:T(8,128)(2,1)S(1)}, bf16[80,640]{1,0:T(8,128)(2,1)S(1)}, u32[]{:S(2)}, u32[]{:S(2)}) collective-permute-start(bf16[80,640]{1,0:T(8,128)(2,1)S(1)} %reduce_sum.47), channel_id=1, source_target_pairs={{0,0},{32,8},{64,16},{96,24},{8,32},{40,40},{72,48},{104,56},{16,6... | collective-permute-start | bytes 307208 | tf_op jit(solution)/shard_map/ppermute | solution.py:143
  186.9 29.0 %all-to-all-start.4 = ((bf16[4,80,640]{2,1,0:T(8,128)(2,1)}), bf16[4,80,640]{2,1,0:T(8,128)(2,1)S(1)}, u32[]{:S(2)}, u32[]{:S(2)}) async-start(bf16[4,80,640]{2,1,0:T(8,128)(2,1)} %bitcast.26), calls=%async_computation.4 | async-start | bytes 819200 | tf_op jit(solution)/shard_map/all_to_all | solution.py:51
  216.0 40.7 %copy-start.4 = (bf16[320,800]{1,0:T(8,128)(2,1)S(1)}, bf16[320,800]{1,0:T(8,128)(2,1)}, u32[]{:S(2)}) copy-start(bf16[320,800]{1,0:T(8,128)(2,1)} %total.1) | copy-start | bytes 1536004
  228.5 28.2 %copy-start.3 = (bf16[1280,800]{1,0:T(8,128)(2,1)S(1)}, bf16[1280,800]{1,0:T(8,128)(2,1)}, u32[]{:S(2)}) copy-start(bf16[1280,800]{1,0:T(8,128)(2,1)} %all-gather.13.cloned.1.call-done.refs_2_) | copy-start | bytes 6144004
  228.7 28.1 %copy-start.2 = (bf16[1280,800]{1,0:T(8,128)(2,1)S(1)}, bf16[1280,800]{1,0:T(8,128)(2,1)}, u32[]{:S(2)}) copy-start(bf16[1280,800]{1,0:T(8,128)(2,1)} %all-gather.9.cloned.1.call-done.refs_1_) | copy-start | bytes 6144004
  228.8 27.9 %copy-start.1 = (bf16[1280,800]{1,0:T(8,128)(2,1)S(1)}, bf16[1280,800]{1,0:T(8,128)(2,1)}, u32[]{:S(2)}) copy-start(bf16[1280,800]{1,0:T(8,128)(2,1)} %all-gather.11.cloned.1.call-done.refs_3_) | copy-start | bytes 6144004
  246.1 13.7 %collective-permute-start.5 = (bf16[320,2560]{1,0:T(8,128)(2,1)S(1)}, bf16[320,2560]{1,0:T(8,128)(2,1)S(1)}, u32[]{:S(2)}, u32[]{:S(2)}) collective-permute-start(bf16[320,2560]{1,0:T(8,128)(2,1)S(1)} %bitcast.58), channel_id=1, source_target_pairs={{1,0},{0,1},{3,2},{2,3},{5,4},{4,5},{7,6},{6,7},{9,8},{8,9},{11,10... | collective-permute-start | bytes 4915208 | tf_op jit(solution)/shard_map/ppermute | solution.py:23
Sparse Core Ops, SparseCore 0:
  9.5 45.4 all-gather.6
  68.3 44.5 all-gather.10
  115.0 40.2 all-gather.8
  157.2 42.5 all-gather.12

commit v13 on v11

--- a/solution.py
+++ b/solution.py
@@ -148,11 +148,11 @@
     )
     square = matmul_over_c(left, *columns(right))
     square = exchanged_sum(square.reshape(4, slab, pair), "zh")
-    square, opposite = lax.optimization_barrier((square, opposite))
     polynomial = (QUINTIC_B * turned.astype(F32) + QUINTIC_C * square).astype(BF16)
 
     polynomial = lax.all_gather(polynomial, "zl", axis=0, tiled=False)
     polynomial = jnp.concatenate(rolled([polynomial[i] for i in range(4)], h), axis=1)
+    polynomial, opposite = lax.optimization_barrier((polynomial, opposite))
     polynomial = gathered(polynomial, "y").reshape(rows, 4 * pair)
     swapped = take(polynomial, "c", 1)
 

time: 270 us -> 285 us (1.056)
  waiting for transfers between devices: 92 us -> 99.8 us
  blocking collectives: 79.8 us -> 86.6 us
    all_to_all x1, waiting for transfers between devices: 0.01 us -> 7.65 us  [gathered(): return lax.all_to_all(spread, axis, split_axis=0, concat_axis=0, tiled=True)]
    all_to_all x1, blocking collectives: 16.1 us -> 22.7 us  [gathered(): return lax.all_to_all(spread, axis, split_axis=0, concat_axis=0, tiled=True)]
    ppermute x3, starting transfers between devices: 26.4 us -> 22.9 us  [take(): lax.ppermute(value, axis, [((i + distance) % n, i) for i in range(n)])]
  transfers between devices with their start and end apart: 14 -> 14, of which waited for: 5 -> 6; matrix products, arithmetic and copies ran while one was open for 6% -> 6% of each run, Pallas kernels for 1% -> 1%
where the time goes in v13:
time: 285 us; the launch traced here: 284 us
  waiting for transfers between devices  99.8 us (35%)
  blocking collectives  86.6 us (30%)
  starting transfers between devices  59.6 us (21%)
  between operations  13.4 us (5%)
  matrix products  10.4 us (4%)
  Pallas kernels  5.26 us (2%)
  other arithmetic  5.12 us (2%)
  local copies, waits for them, and re-layouts  4.26 us (1%)
    ppermute x3, waiting for transfers between devices, take(): lax.ppermute(value, axis, [((i + distance) % n, i) for i in range(n)])  44.8 us
    all_to_all x3, waiting for transfers between devices, exchanged(): return lax.all_to_all(value, axis, split_axis=0, concat_axis=0, tiled=True)  26.6 us
    ppermute x3, starting transfers between devices, take(): lax.ppermute(value, axis, [((i + distance) % n, i) for i in range(n)])  22.9 us
    all_to_all x1, blocking collectives, gathered(): return lax.all_to_all(spread, axis, split_axis=0, concat_axis=0, tiled=True)  22.7 us
    all_gather x1, blocking collectives, local(): left = lax.all_gather(gram, 'zl', axis=0, tiled=True)  22.4 us
    all_to_all x3, starting transfers between devices, exchanged(): return lax.all_to_all(value, axis, split_axis=0, concat_axis=0, tiled=True)  21.1 us
    all_to_all x1, blocking collectives, exchanged(): return lax.all_to_all(value, axis, split_axis=0, concat_axis=0, tiled=True)  20.2 us
    ppermute x2, waiting for transfers between devices, shifted(): return lax.ppermute(value, ('zh', 'c'), route)  17.7 us
  transfers between devices with their start and end apart: 14, of which 6 were waited for; matrix products, arithmetic and copies ran while one was open for 6% of the time, Pallas kernels for 1%

profile of v13, /device:TPU:1, one launch (start us, length us, event | category | flops | bytes accessed | tf_op | source)
XLA Modules:
  0.0 284.3 jit_solution(17330551918834412341)
XLA Ops:
  6.5 0.7 all-gather.8.cloned.1.call-update
  7.3 0.0 all-gather.10.cloned.1.call-start
  7.3 13.3 %collective-permute-start = (bf16[320,800]{1,0:T(8,128)(2,1)}, bf16[320,800]{1,0:T(8,128)(2,1)S(1)}, u32[]{:S(2)}, u32[]{:S(2)}) collective-permute-start(bf16[320,800]{1,0:T(8,128)(2,1)} %total.1), channel_id=1, source_target_pairs={{32,0},{64,32},{96,64},{0,96},{33,1},{65,33},{97,65},{1,97},{34,2}... | collective-permute-start | bytes 1536008 | tf_op jit(solution)/shard_map/ppermute | solution.py:23
  20.6 1.9 collective-permute-start.1
  22.5 44.7 %collective-permute-done = bf16[320,800]{1,0:T(8,128)(2,1)S(1)} collective-permute-done((bf16[320,800]{1,0:T(8,128)(2,1)}, bf16[320,800]{1,0:T(8,128)(2,1)S(1)}, u32[]{:S(2)}, u32[]{:S(2)}) %collective-permute-start) | collective-permute-done | bytes 512032 | tf_op jit(solution)/shard_map/ppermute | solution.py:23
  67.3 0.8 copy-done.5
  68.1 1.6 pad_maximum_fusion
  69.8 0.3 copy-done
  70.1 4.0 %convolution_convert_fusion = bf16[2,640,960]{1,2,0:T(8,128)(2,1)} fusion(bf16[2,640,800]{2,1,0:T(8,128)(2,1)S(1)} %bitcast.57, bf16[960,800,1]{1,0,2:T(8,128)(2,1)S(1)} %bitcast.67), kind=kOutput, calls=%fused_computation | convolution fusion | flops 1967308800 | bytes 6041600 | tf_op jit(solution)/shard_map/rn,csn->crs/dot_general | solution.py:110
  74.1 8.3 %all-to-all-start = ((bf16[8,240,640]{2,1,0:T(8,128)(2,1)}), bf16[8,240,640]{2,1,0:T(8,128)(2,1)}, u32[]{:S(2)}, u32[]{:S(2)}) async-start(bf16[8,240,640]{2,1,0:T(8,128)(2,1)} %bitcast.65), calls=%async_computation | async-start | bytes 4915200 | tf_op jit(solution)/shard_map/all_to_all | solution.py:51
  82.5 0.9 slice_select_fusion
  83.4 7.9 %collective-permute-start.2 = (bf16[160,800]{1,0:T(8,128)(2,1)}, bf16[160,800]{1,0:T(8,128)(2,1)S(1)}, u32[]{:S(2)}, u32[]{:S(2)}) collective-permute-start(bf16[160,800]{1,0:T(8,128)(2,1)} %get-tuple-element.24), channel_id=1, source_target_pairs={{0,32},{1,97},{32,64},{33,1},{64,96},{65,33},{96,0},{97,65},{2,34}... | collective-permute-start | bytes 768008 | tf_op jit(solution)/shard_map/ppermute | solution.py:32
  91.2 1.9 collective-permute-start.3
  93.2 17.7 %collective-permute-done.2 = bf16[160,800]{1,0:T(8,128)(2,1)S(1)} collective-permute-done((bf16[160,800]{1,0:T(8,128)(2,1)}, bf16[160,800]{1,0:T(8,128)(2,1)S(1)}, u32[]{:S(2)}, u32[]{:S(2)}) %collective-permute-start.2) | collective-permute-done | bytes 256032 | tf_op jit(solution)/shard_map/ppermute | solution.py:32
  111.0 0.7 convolution_convert_fusion.1
  111.7 2.7 all-gather
  114.4 1.5 fusion
  116.0 4.6 %all-to-all-start.1 = ((bf16[4,80,640]{2,1,0:T(8,128)(2,1)}), bf16[4,80,640]{2,1,0:T(8,128)(2,1)S(1)}, u32[]{:S(2)}, u32[]{:S(2)}) async-start(bf16[4,80,640]{2,1,0:T(8,128)(2,1)} %bitcast.16), calls=%async_computation.1 | async-start | bytes 819200 | tf_op jit(solution)/shard_map/all_to_all | solution.py:51
  120.5 0.7 all-gather.12.cloned.1.call-update
  121.3 2.1 reduce_sum.45
  123.4 4.5 %all-to-all-done.1 = bf16[4,80,640]{2,1,0:T(8,128)(2,1)S(1)} async-done(((bf16[4,80,640]{2,1,0:T(8,128)(2,1)}), bf16[4,80,640]{2,1,0:T(8,128)(2,1)S(1)}, u32[]{:S(2)}, u32[]{:S(2)}) %all-to-all-start.1) | async-done | bytes 409632 | tf_op jit(solution)/shard_map/all_to_all | solution.py:51
  127.9 0.1 reduce_sum.46
  128.0 0.1 select_bitcast_fusion.3
  128.1 0.1 pad_maximum_fusion.1
  128.1 20.2 %all_to_all.30 = bf16[4,80,640]{2,1,0:T(8,128)(2,1)S(1)} all-to-all(bf16[4,80,640]{2,1,0:T(8,128)(2,1)S(1)} %pad_maximum_fusion.1), channel_id=1, replica_groups=mesh['x'=4,'zh'=4,'zl'=4,'y'=4,'c'=2] {'zl'}, dimensions={0} | all-to-all | bytes 819200 | tf_op jit(solution)/shard_map/all_to_all | solution.py:51
  148.3 0.1 reduce_sum.47
  148.4 1.3 broadcast_in_dim.4
  149.7 5.1 %all-to-all-start.3 = ((bf16[16,80,640]{2,1,0:T(8,128)(2,1)}), bf16[16,80,640]{2,1,0:T(8,128)(2,1)}, u32[]{:S(2)}, u32[]{:S(2)}) async-start(bf16[16,80,640]{2,1,0:T(8,128)(2,1)} %broadcast_in_dim.4), calls=%async_computation.3 | async-start | bytes 3276800 | tf_op jit(solution)/shard_map/all_to_all | solution.py:43
  154.8 0.0 all-gather.14.cloned.1.call-start
  154.9 0.5 all-gather.14.cloned.1.call-update
  155.4 0.7 collective-permute-start.4
  156.1 22.4 %all_gather.36 = bf16[320,640]{1,0:T(8,128)(2,1)S(1)} all-gather(bf16[80,640]{1,0:T(8,128)(2,1)S(1)} %reduce_sum.47), channel_id=1, replica_groups=mesh['x'=4,'zh'=4,'zl'=4,'y'=4,'c'=2] {'zl'}, dimensions={0}, use_global_device_ids=true | all-gather | bytes 512000 | tf_op jit(solution)/shard_map/all_gather | solution.py:144
  178.4 1.1 all-gather.12.cloned.1.call-done.refs_3_
  179.5 7.7 %all-to-all-done.3 = bf16[16,80,640]{2,1,0:T(8,128)(2,1)} async-done(((bf16[16,80,640]{2,1,0:T(8,128)(2,1)}), bf16[16,80,640]{2,1,0:T(8,128)(2,1)}, u32[]{:S(2)}, u32[]{:S(2)}) %all-to-all-start.3) | async-done | bytes 1638432 | tf_op jit(solution)/shard_map/all_to_all | solution.py:43
  187.2 1.7 convolution_convert_fusion.2
  188.9 4.2 %all-gather.1 = bf16[640,640]{1,0:T(8,128)(2,1)S(1)} all-gather(bf16[320,640]{1,0:T(8,128)(2,1)S(1)} %convolution_convert_fusion.2), channel_id=3, replica_groups=mesh['x'=4,'zh'=4,'zl'=4,'y'=4,'c'=2] {'c'}, dimensions={0}, use_global_device_ids=true | all-gather | bytes 1228800 | tf_op jit(solution)/shard_map/all_gather | solution.py:60
  193.0 2.4 fusion.1
  195.5 8.2 %all-to-all-start.4 = ((bf16[4,80,640]{2,1,0:T(8,128)(2,1)}), bf16[4,80,640]{2,1,0:T(8,128)(2,1)S(1)}, u32[]{:S(2)}, u32[]{:S(2)}) async-start(bf16[4,80,640]{2,1,0:T(8,128)(2,1)} %bitcast.27), calls=%async_computation.4 | async-start | bytes 819200 | tf_op jit(solution)/shard_map/all_to_all | solution.py:51
  203.6 22.1 %all-to-all-done.4 = bf16[4,80,640]{2,1,0:T(8,128)(2,1)S(1)} async-done(((bf16[4,80,640]{2,1,0:T(8,128)(2,1)}), bf16[4,80,640]{2,1,0:T(8,128)(2,1)S(1)}, u32[]{:S(2)}, u32[]{:S(2)}) %all-to-all-start.4) | async-done | bytes 409632 | tf_op jit(solution)/shard_map/all_to_all | solution.py:51
  225.7 0.1 convert_reduce_fusion
  225.8 14.4 %all-gather.2 = bf16[320,640]{1,0:T(8,128)(2,1)S(1)} all-gather(bf16[80,640]{1,0:T(8,128)(2,1)S(1)} %add_convert_fusion), channel_id=4, replica_groups=mesh['x'=4,'zh'=4,'zl'=4,'y'=4,'c'=2] {'zl'}, dimensions={0}, use_global_device_ids=true | all-gather | bytes 512000 | tf_op jit(solution)/shard_map/all_gather | solution.py:153
  240.2 0.1 select_select_fusion.3
  240.4 0.1 broadcast_in_dim.5
  240.5 22.7 %all_to_all.31 = bf16[4,80,2560]{2,1,0:T(8,128)(2,1)S(1)} all-to-all(bf16[4,80,2560]{2,1,0:T(8,128)(2,1)S(1)} %broadcast_in_dim.5), channel_id=1, replica_groups=mesh['x'=4,'zh'=4,'zl'=4,'y'=4,'c'=2] {'y'}, dimensions={0} | all-to-all | bytes 3276800 | tf_op jit(solution)/shard_map/all_to_all | solution.py:43
  263.2 7.7 %collective-permute-start.5 = (bf16[320,2560]{1,0:T(8,128)(2,1)S(1)}, bf16[320,2560]{1,0:T(8,128)(2,1)S(1)}, u32[]{:S(2)}, u32[]{:S(2)}) collective-permute-start(bf16[320,2560]{1,0:T(8,128)(2,1)S(1)} %bitcast.60), channel_id=1, source_target_pairs={{1,0},{0,1},{3,2},{2,3},{5,4},{4,5},{7,6},{6,7},{9,8},{8,9},{11,10... | collective-permute-start | bytes 4915208 | tf_op jit(solution)/shard_map/ppermute | solution.py:23
  270.9 1.6 copy-done.3
  272.5 2.1 shard_map.17.total
  274.7 3.1 %shard_map.18 = f32[320,800]{1,0:T(8,128)} custom-call(f32[320,800]{1,0:T(8,128)S(1)} %shard_map.17.total, bf16[320,2560]{1,0:T(8,128)(2,1)S(1)} %collective-permute-done.5.left, bf16[1280,800]{1,0:T(8,128)(2,1)S(1)} %copy-done, bf16[1280,800]{1,0:T(8,128)(2,1)S(1)} %copy-done.1, bf16[1280,800]{1,0:T(8,128)(2,1)S(1)} %copy-done.3, ...), custom_call_target="tpu_custom_call" | custom-call | flops 1310720000 | bytes 3686400 | tf_op jit(solution)/shard_map/pallas_call | solution.py:85
  (30 shorter events, 0.2 us)
Async XLA Ops:
  6.5 60.8 %all-gather.8.cloned.1.call-start = ((), (), s32[]{:S(2)}) async-start(), calls=%async_computation.6 | async-start | bytes 2867200 | tf_op jit(solution)/shard_map/all_gather | solution.py:119
  7.3 171.2 %all-gather.10.cloned.1.call-start = ((), (), s32[]{:S(2)}) async-start(), calls=%async_computation.7 | async-start | bytes 2867200 | tf_op jit(solution)/shard_map/all_gather | solution.py:121
  7.3 60.0 %collective-permute-start = (bf16[320,800]{1,0:T(8,128)(2,1)}, bf16[320,800]{1,0:T(8,128)(2,1)S(1)}, u32[]{:S(2)}, u32[]{:S(2)}) collective-permute-start(bf16[320,800]{1,0:T(8,128)(2,1)} %total.1), channel_id=1, source_target_pairs={{32,0},{64,32},{96,64},{0,96},{33,1},{65,33},{97,65},{1,97},{34,2}... | collective-permute-start | bytes 1536008 | tf_op jit(solution)/shard_map/ppermute | solution.py:23
  20.6 46.7 %collective-permute-start.1 = (bf16[320,800]{1,0:T(8,128)(2,1)}, bf16[320,800]{1,0:T(8,128)(2,1)S(1)}, u32[]{:S(2)}, u32[]{:S(2)}) collective-permute-start(bf16[320,800]{1,0:T(8,128)(2,1)} %total.1), channel_id=1, source_target_pairs={{96,0},{0,32},{32,64},{64,96},{97,1},{1,33},{33,65},{65,97},{98,2}... | collective-permute-start | bytes 1536008 | tf_op jit(solution)/shard_map/ppermute | solution.py:23
  67.3 0.8 copy-start.5
  67.3 15.2 %copy-start.7 = (bf16[320,800]{1,0:T(8,128)(2,1)}, bf16[320,800]{1,0:T(8,128)(2,1)S(1)}, u32[]{:S(2)}) copy-start(bf16[320,800]{1,0:T(8,128)(2,1)S(1)} %collective-permute-done.1) | copy-start | bytes 1536004
  68.1 2.0 copy-start
  74.1 8.3 %copy-start.6 = (bf16[320,800]{1,0:T(8,128)(2,1)S(1)}, bf16[320,800]{1,0:T(8,128)(2,1)}, u32[]{:S(2)}) copy-start(bf16[320,800]{1,0:T(8,128)(2,1)} %copy-done.5) | copy-start | bytes 1536004
  74.1 41.8 %all-to-all-start = ((bf16[8,240,640]{2,1,0:T(8,128)(2,1)}), bf16[8,240,640]{2,1,0:T(8,128)(2,1)}, u32[]{:S(2)}, u32[]{:S(2)}) async-start(bf16[8,240,640]{2,1,0:T(8,128)(2,1)} %bitcast.65), calls=%async_computation | async-start | bytes 4915200 | tf_op jit(solution)/shard_map/all_to_all | solution.py:51
  83.4 27.5 %collective-permute-start.2 = (bf16[160,800]{1,0:T(8,128)(2,1)}, bf16[160,800]{1,0:T(8,128)(2,1)S(1)}, u32[]{:S(2)}, u32[]{:S(2)}) collective-permute-start(bf16[160,800]{1,0:T(8,128)(2,1)} %get-tuple-element.24), channel_id=1, source_target_pairs={{0,32},{1,97},{32,64},{33,1},{64,96},{65,33},{96,0},{97,65},{2,34}... | collective-permute-start | bytes 768008 | tf_op jit(solution)/shard_map/ppermute | solution.py:32
  91.2 19.7 %collective-permute-start.3 = (bf16[160,800]{1,0:T(8,128)(2,1)}, bf16[160,800]{1,0:T(8,128)(2,1)S(1)}, u32[]{:S(2)}, u32[]{:S(2)}) collective-permute-start(bf16[160,800]{1,0:T(8,128)(2,1)} %get-tuple-element.25), channel_id=1, source_target_pairs={{0,96},{1,33},{32,0},{33,65},{64,32},{65,97},{96,64},{97,1},{2,98}... | collective-permute-start | bytes 768008 | tf_op jit(solution)/shard_map/ppermute | solution.py:32
  111.0 3.5 %copy-start.8 = (bf16[320,800]{1,0:T(8,128)(2,1)}, bf16[320,800]{1,0:T(8,128)(2,1)S(1)}, u32[]{:S(2)}) copy-start(bf16[320,800]{1,0:T(8,128)(2,1)S(1)} %constant_dynamic-update-slice_fusion) | copy-start | bytes 1536004
  116.0 12.0 %all-to-all-start.1 = ((bf16[4,80,640]{2,1,0:T(8,128)(2,1)}), bf16[4,80,640]{2,1,0:T(8,128)(2,1)S(1)}, u32[]{:S(2)}, u32[]{:S(2)}) async-start(bf16[4,80,640]{2,1,0:T(8,128)(2,1)} %bitcast.16), calls=%async_computation.1 | async-start | bytes 819200 | tf_op jit(solution)/shard_map/all_to_all | solution.py:51
  120.5 59.0 %all-gather.12.cloned.1.call-start = ((), (), s32[]{:S(2)}) async-start(), calls=%async_computation.8 | async-start | bytes 2867200 | tf_op jit(solution)/shard_map/all_gather | solution.py:122
  149.7 37.5 %all-to-all-start.3 = ((bf16[16,80,640]{2,1,0:T(8,128)(2,1)}), bf16[16,80,640]{2,1,0:T(8,128)(2,1)}, u32[]{:S(2)}, u32[]{:S(2)}) async-start(bf16[16,80,640]{2,1,0:T(8,128)(2,1)} %broadcast_in_dim.4), calls=%async_computation.3 | async-start | bytes 3276800 | tf_op jit(solution)/shard_map/all_to_all | solution.py:43
  154.8 85.5 %all-gather.14.cloned.1.call-start = ((), (), s32[]{:S(2)}) async-start(), calls=%async_computation.9 | async-start | bytes 2867200 | tf_op jit(solution)/shard_map/all_gather | solution.py:137
  155.4 24.1 %collective-permute-start.4 = (bf16[80,640]{1,0:T(8,128)(2,1)S(1)}, bf16[80,640]{1,0:T(8,128)(2,1)S(1)}, u32[]{:S(2)}, u32[]{:S(2)}) collective-permute-start(bf16[80,640]{1,0:T(8,128)(2,1)S(1)} %reduce_sum.47), channel_id=1, source_target_pairs={{0,0},{32,8},{64,16},{96,24},{8,32},{40,40},{72,48},{104,56},{16,6... | collective-permute-start | bytes 307208 | tf_op jit(solution)/shard_map/ppermute | solution.py:143
  195.5 30.2 %all-to-all-start.4 = ((bf16[4,80,640]{2,1,0:T(8,128)(2,1)}), bf16[4,80,640]{2,1,0:T(8,128)(2,1)S(1)}, u32[]{:S(2)}, u32[]{:S(2)}) async-start(bf16[4,80,640]{2,1,0:T(8,128)(2,1)} %bitcast.27), calls=%async_computation.4 | async-start | bytes 819200 | tf_op jit(solution)/shard_map/all_to_all | solution.py:51
  240.3 30.5 %copy-start.2 = (bf16[1280,800]{1,0:T(8,128)(2,1)S(1)}, bf16[1280,800]{1,0:T(8,128)(2,1)}, u32[]{:S(2)}) copy-start(bf16[1280,800]{1,0:T(8,128)(2,1)} %all-gather.12.cloned.1.call-done.refs_3_) | copy-start | bytes 6144004
  240.5 30.4 %copy-start.1 = (bf16[1280,800]{1,0:T(8,128)(2,1)S(1)}, bf16[1280,800]{1,0:T(8,128)(2,1)}, u32[]{:S(2)}) copy-start(bf16[1280,800]{1,0:T(8,128)(2,1)} %all-gather.10.cloned.1.call-done.refs_1_) | copy-start | bytes 6144004
  240.5 30.4 %copy-start.4 = (bf16[320,800]{1,0:T(8,128)(2,1)S(1)}, bf16[320,800]{1,0:T(8,128)(2,1)}, u32[]{:S(2)}) copy-start(bf16[320,800]{1,0:T(8,128)(2,1)} %total.1) | copy-start | bytes 1536004
  263.2 11.5 %collective-permute-start.5 = (bf16[320,2560]{1,0:T(8,128)(2,1)S(1)}, bf16[320,2560]{1,0:T(8,128)(2,1)S(1)}, u32[]{:S(2)}, u32[]{:S(2)}) collective-permute-start(bf16[320,2560]{1,0:T(8,128)(2,1)S(1)} %bitcast.60), channel_id=1, source_target_pairs={{1,0},{0,1},{3,2},{2,3},{5,4},{4,5},{7,6},{6,7},{9,8},{8,9},{11,10... | collective-permute-start | bytes 4915208 | tf_op jit(solution)/shard_map/ppermute | solution.py:23
  270.9 1.6 copy-start.3
Sparse Core Ops, SparseCore 0:
  9.5 45.4 all-gather.7
  68.2 43.7 all-gather.9
  123.4 56.0 all-gather.11
  181.5 44.9 all-gather.13
